TPU v7x, 32 devices: a whole 2x2x4 slice. The times are simulated.
32 devices in a mesh: groups: 2 (over y), expert: 4 (over z), dp: 4 (over x, core).
Axes of the slice: x: 2, y: 2, z: 4, core: 2. Of those that a mesh axis runs over, the one named last changes fastest.
Arguments:
- tokens: bfloat16 [1024, 2560], P(('groups', 'expert'), 'dp'), parts along dimension 0, may hold values from -6 to 6
- out_grad: bfloat16 [1024, 2560], P(('groups', 'expert'), 'dp'), parts along dimension 0, may hold values from -6 to 6
- gate_weights: float32 [1024, 2], P(('groups', 'expert')), parts along dimension 0, may hold values from 0.1 to 0.5
- expert_ids: int32 [1024, 2], P(('groups', 'expert')), parts along dimension 0, may hold values from 0 to 3, as said below
- replica_plan: int32 [4, 2], P('groups'), parts along dimension 0, may hold values from 0 to 3, as said below
- cap_blocks: int32 [8], P('groups'), parts along dimension 0, may hold values from 1 to 2, as said below
- gate_weight: bfloat16 [4, 2560, 768], P('expert', 'dp'), may hold values from -0.125 to 0.125
- up_weight: bfloat16 [4, 2560, 768], P('expert', 'dp'), may hold values from -0.125 to 0.125
- down_weight: bfloat16 [4, 768, 2560], P('expert', None, 'dp'), may hold values from -0.21875 to 0.21875
Outputs:
- mixed: bfloat16 [1024, 2560], P(('groups', 'expert'), 'dp'), parts along dimension 0
- token_grad: bfloat16 [1024, 2560], P(('groups', 'expert'), 'dp'), parts along dimension 0
- gate_grad: bfloat16 [8, 2560, 768], P(('groups', 'expert'), 'dp'), parts along dimension 0
- up_grad: bfloat16 [8, 2560, 768], P(('groups', 'expert'), 'dp'), parts along dimension 0
- down_grad: bfloat16 [8, 768, 2560], P(('groups', 'expert'), None, 'dp'), parts along dimension 0
There are 2 independent parts, one for each index of `groups`. A program takes and returns all parts, laid end to end along the dimension named above; an argument that names none is the same for every part. Nothing has to cross between parts.
Inputs may be any that keep to these rules, and one draw needn't show every extreme that they name: `expert_ids`: each row names 2 different experts. `replica_plan`: every number 0 to 3 appears once; entry [i, 0] is the i-th hot expert and the rest of row i are the expert devices that hold its replicas. `cap_blocks`: capacity of expert device d for rows of its own expert from one source, in blocks of 4 rows.
All inputs are finite; a program needn't handle non-finite values.
Results may differ from a plain program's by a relative error of at most 0.018.
Values may be sent and summed in bfloat16 or wider, within the bound.
No kernel may reach another device: no remote copies, remote signals or barrier semaphores. Data moves between devices by JAX's collectives and lax.ppermute only.
A program may use at most 128 MiB of HBM per device.

v0:
```python
import jax
import jax.numpy as jnp
from jax import lax
from jax.sharding import PartitionSpec as P

BLK = 4
MAXB = 2
SPARE = 2


def broadcast(block, axis, holder):
    block = jnp.where(lax.axis_index(axis) == holder, block, jnp.zeros_like(block))
    return lax.psum(block, axis)


def routing(expert_ids, replica_plan, cap_blocks, token_index):
    host_count = replica_plan.shape[1]
    experts = cap_blocks.shape[0]
    host_slot = token_index % host_count
    is_first = expert_ids == replica_plan[0, 0]
    is_second = expert_ids == replica_plan[1, 0]
    first_host = replica_plan[0][host_slot][:, None]
    second_host = replica_plan[1][host_slot][:, None]
    target = jnp.where(is_first, first_host, jnp.where(is_second, second_host, expert_ids))
    spare_kind = ((is_first | is_second) & (host_slot[:, None] > 0)).astype(jnp.int32)
    bucket = (target * 2 + spare_kind).reshape(-1)
    onehot = (bucket[:, None] == jnp.arange(2 * experts, dtype=jnp.int32)[None, :]).astype(
        jnp.int32
    )
    before = jnp.cumsum(onehot, axis=0) - onehot
    position = jnp.sum(before * onehot, axis=1).reshape(target.shape)
    capacity = jnp.where(spare_kind == 1, SPARE, cap_blocks[target] * BLK)
    accepted = position < capacity
    return (target, spare_kind, position, accepted)


def silu_parts(preact):
    sigma = jax.nn.sigmoid(preact)
    return (preact * sigma, sigma * (1.0 + preact * (1.0 - sigma)))


def shards(
    tokens,
    out_grad,
    gate_weights,
    expert_ids,
    replica_plan,
    cap_blocks,
    gate_weight,
    up_weight,
    down_weight,
):
    n_expert = lax.axis_size("expert")
    device = lax.axis_index("expert")
    local_count, feature = tokens.shape
    choose = expert_ids.shape[1]
    own_cap = MAXB * BLK
    token_index = device * local_count + jnp.arange(local_count, dtype=jnp.int32)
    target, spare_kind, position, accepted = routing(
        expert_ids, replica_plan, cap_blocks, token_index
    )
    pair_ids = jnp.arange(local_count * choose, dtype=jnp.int32)
    sentinel = local_count * choose
    own_keep = (accepted & (spare_kind == 0)).reshape(-1)
    spare_keep = (accepted & (spare_kind == 1)).reshape(-1)
    flat_target = target.reshape(-1)
    flat_position = position.reshape(-1)
    own_slots = jnp.where(own_keep, flat_target * own_cap + flat_position, n_expert * own_cap)
    spare_slots = jnp.where(spare_keep, flat_target * SPARE + flat_position, n_expert * SPARE)
    own_table = (
        jnp.full((n_expert * own_cap,), sentinel, jnp.int32)
        .at[own_slots]
        .set(pair_ids, mode="drop")
    )
    spare_table = (
        jnp.full((n_expert * SPARE,), sentinel, jnp.int32)
        .at[spare_slots]
        .set(pair_ids, mode="drop")
    )
    padded_tokens = jnp.concatenate([tokens, jnp.zeros((1, feature), jnp.bfloat16)], axis=0)
    padded_grads = jnp.concatenate([out_grad, jnp.zeros((1, feature), jnp.bfloat16)], axis=0)
    padded_gates = jnp.concatenate([gate_weights.reshape(-1), jnp.zeros((1,), jnp.float32)], axis=0)

    def pair_rows(table, count):
        token_rows = table // choose
        rows = padded_tokens[token_rows].reshape(n_expert, count, feature)
        cotangent = (
            padded_gates[table][:, None] * padded_grads[token_rows].astype(jnp.float32)
        ).astype(jnp.bfloat16)
        return (rows, cotangent.reshape(n_expert, count, feature))

    own_send, own_cot_send = pair_rows(own_table, own_cap)
    spare_send, spare_cot_send = pair_rows(spare_table, SPARE)
    own_recv, spare_recv = (
        lax.all_to_all(own_send, "expert", split_axis=0, concat_axis=0, tiled=True),
        lax.all_to_all(spare_send, "expert", split_axis=0, concat_axis=0, tiled=True),
    )
    own_weights = (gate_weight[0], up_weight[0], down_weight[0])
    copies = []
    for which in range(2):
        copies.append(
            (
                broadcast(own_weights[0], "expert", replica_plan[which, 0]),
                broadcast(own_weights[1], "expert", replica_plan[which, 0]),
                broadcast(own_weights[2], "expert", replica_plan[which, 0]),
            )
        )
    in_first = jnp.any(replica_plan[0] == device)

    def choose_copy(first_copy, second_copy):
        return jnp.where(in_first, first_copy, second_copy)

    spare_weights = jax.tree.map(choose_copy, copies[0], copies[1])
    own_rows = own_recv.reshape(-1, feature)
    spare_rows = spare_recv.reshape(-1, feature)
    own_gate = jnp.dot(own_rows, own_weights[0], preferred_element_type=jnp.float32)
    own_up = jnp.dot(own_rows, own_weights[1], preferred_element_type=jnp.float32)
    spare_gate = jnp.dot(spare_rows, spare_weights[0], preferred_element_type=jnp.float32)
    spare_up = jnp.dot(spare_rows, spare_weights[1], preferred_element_type=jnp.float32)
    own_gate, own_up, spare_gate, spare_up = (
        lax.psum_scatter(
            own_gate.astype(jnp.bfloat16), "dp", scatter_dimension=1, tiled=True
        ).astype(jnp.float32),
        lax.psum_scatter(own_up.astype(jnp.bfloat16), "dp", scatter_dimension=1, tiled=True).astype(
            jnp.float32
        ),
        lax.psum_scatter(
            spare_gate.astype(jnp.bfloat16), "dp", scatter_dimension=1, tiled=True
        ).astype(jnp.float32),
        lax.psum_scatter(
            spare_up.astype(jnp.bfloat16), "dp", scatter_dimension=1, tiled=True
        ).astype(jnp.float32),
    )
    own_active, own_slope = silu_parts(own_gate)
    spare_active, spare_slope = silu_parts(spare_gate)
    own_hidden = (own_active * own_up).astype(jnp.bfloat16)
    spare_hidden = (spare_active * spare_up).astype(jnp.bfloat16)
    own_hidden_full, spare_hidden_full = (
        lax.all_gather(own_hidden, "dp", axis=1, tiled=True),
        lax.all_gather(spare_hidden, "dp", axis=1, tiled=True),
    )
    own_out = jnp.dot(own_hidden_full, own_weights[2], preferred_element_type=jnp.float32).astype(
        jnp.bfloat16
    )
    spare_out = jnp.dot(
        spare_hidden_full, spare_weights[2], preferred_element_type=jnp.float32
    ).astype(jnp.bfloat16)
    own_out = own_out.reshape(n_expert, own_cap, feature)
    spare_out = spare_out.reshape(n_expert, SPARE, feature)
    own_back, spare_back = (
        lax.all_to_all(own_out, "expert", split_axis=0, concat_axis=0, tiled=True),
        lax.all_to_all(spare_out, "expert", split_axis=0, concat_axis=0, tiled=True),
    )
    own_cot_rows, spare_cot_rows = (
        lax.all_to_all(own_cot_send, "expert", split_axis=0, concat_axis=0, tiled=True),
        lax.all_to_all(spare_cot_send, "expert", split_axis=0, concat_axis=0, tiled=True),
    )
    own_cot = own_cot_rows.reshape(-1, feature)
    spare_cot = spare_cot_rows.reshape(-1, feature)
    own_down_part = jnp.dot(own_hidden_full.T, own_cot, preferred_element_type=jnp.float32)
    spare_down_part = jnp.dot(spare_hidden_full.T, spare_cot, preferred_element_type=jnp.float32)
    own_back_hidden = jnp.dot(own_cot, own_weights[2].T, preferred_element_type=jnp.float32)
    spare_back_hidden = jnp.dot(spare_cot, spare_weights[2].T, preferred_element_type=jnp.float32)
    own_back_hidden, spare_back_hidden = (
        lax.psum_scatter(
            own_back_hidden.astype(jnp.bfloat16), "dp", scatter_dimension=1, tiled=True
        ).astype(jnp.float32),
        lax.psum_scatter(
            spare_back_hidden.astype(jnp.bfloat16), "dp", scatter_dimension=1, tiled=True
        ).astype(jnp.float32),
    )
    own_gate_grad = (own_back_hidden * own_up * own_slope).astype(jnp.bfloat16)
    own_up_grad = (own_back_hidden * own_active).astype(jnp.bfloat16)
    spare_gate_grad = (spare_back_hidden * spare_up * spare_slope).astype(jnp.bfloat16)
    spare_up_grad = (spare_back_hidden * spare_active).astype(jnp.bfloat16)
    own_gate_full, own_up_full, spare_gate_full, spare_up_full = (
        lax.all_gather(own_gate_grad, "dp", axis=1, tiled=True),
        lax.all_gather(own_up_grad, "dp", axis=1, tiled=True),
        lax.all_gather(spare_gate_grad, "dp", axis=1, tiled=True),
        lax.all_gather(spare_up_grad, "dp", axis=1, tiled=True),
    )
    own_gate_part = jnp.dot(own_rows.T, own_gate_full, preferred_element_type=jnp.float32)
    own_up_part = jnp.dot(own_rows.T, own_up_full, preferred_element_type=jnp.float32)
    spare_gate_part = jnp.dot(spare_rows.T, spare_gate_full, preferred_element_type=jnp.float32)
    spare_up_part = jnp.dot(spare_rows.T, spare_up_full, preferred_element_type=jnp.float32)
    own_input = jnp.dot(own_gate_full, own_weights[0].T, preferred_element_type=jnp.float32)
    own_input = (
        own_input + jnp.dot(own_up_full, own_weights[1].T, preferred_element_type=jnp.float32)
    ).astype(jnp.bfloat16)
    spare_input = jnp.dot(spare_gate_full, spare_weights[0].T, preferred_element_type=jnp.float32)
    spare_input = (
        spare_input + jnp.dot(spare_up_full, spare_weights[1].T, preferred_element_type=jnp.float32)
    ).astype(jnp.bfloat16)
    own_input = own_input.reshape(n_expert, own_cap, feature)
    spare_input = spare_input.reshape(n_expert, SPARE, feature)
    own_input_back, spare_input_back = (
        lax.all_to_all(own_input, "expert", split_axis=0, concat_axis=0, tiled=True),
        lax.all_to_all(spare_input, "expert", split_axis=0, concat_axis=0, tiled=True),
    )
    place = jnp.where(in_first, 0, 1).astype(jnp.int32)

    def stacked(partial_value):
        return jnp.zeros((2,) + partial_value.shape, jnp.float32).at[place].set(partial_value)

    hot_gate, hot_up, hot_down = (
        lax.psum(stacked(spare_gate_part).astype(jnp.bfloat16), "expert").astype(jnp.float32),
        lax.psum(stacked(spare_up_part).astype(jnp.bfloat16), "expert").astype(jnp.float32),
        lax.psum(stacked(spare_down_part).astype(jnp.bfloat16), "expert").astype(jnp.float32),
    )
    owner_first = device == replica_plan[0, 0]
    owner_second = device == replica_plan[1, 0]

    def finish(own_part, hot_part):
        total = (
            own_part
            + jnp.where(owner_first, hot_part[0], 0.0)
            + jnp.where(owner_second, hot_part[1], 0.0)
        )
        return total.astype(jnp.bfloat16)[None]

    own_pick = accepted & (spare_kind == 0)
    spare_pick = accepted & (spare_kind == 1)
    own_pos = jnp.where(own_pick, target * own_cap + position, 0)
    spare_pos = jnp.where(spare_pick, target * SPARE + position, 0)

    def combine(own_flat, spare_flat):
        own_vals = own_flat.reshape(-1, feature)[own_pos]
        spare_vals = spare_flat.reshape(-1, feature)[spare_pos]
        picked = jnp.where(
            own_pick[..., None],
            own_vals,
            jnp.where(spare_pick[..., None], spare_vals, jnp.zeros_like(own_vals)),
        )
        return picked.astype(jnp.float32)

    mixed = jnp.sum(gate_weights[..., None] * combine(own_back, spare_back), axis=1).astype(
        jnp.bfloat16
    )
    token_grad = jnp.sum(combine(own_input_back, spare_input_back), axis=1).astype(jnp.bfloat16)
    return (
        mixed,
        token_grad,
        finish(own_gate_part, hot_gate),
        finish(own_up_part, hot_up),
        finish(own_down_part, hot_down),
    )


def solution(mesh):
    return jax.shard_map(
        shards,
        mesh=mesh,
        in_specs=(
            P(("groups", "expert"), "dp"),
            P(("groups", "expert"), "dp"),
            P(("groups", "expert"), None),
            P(("groups", "expert"), None),
            P("groups", None),
            P("groups"),
            P("expert", "dp", None),
            P("expert", "dp", None),
            P("expert", None, "dp"),
        ),
        out_specs=(
            P(("groups", "expert"), "dp"),
            P(("groups", "expert"), "dp"),
            P(("groups", "expert"), "dp", None),
            P(("groups", "expert"), "dp", None),
            P(("groups", "expert"), None, "dp"),
        ),
        check_vma=False,
    )
```

profile of v0, /device:TPU:0, one launch (start us, length us, event | category | flops | bytes accessed | tf_op | source)
XLA Modules:
  0.0 596.6 jit_solution(17549083196930659713)
XLA Ops:
  7.2 1.4 fusion.86
  9.9 2.6 bitcast_select_fusion.2
  12.5 1.4 bitcast_select_fusion.4
  14.1 1.4 bitcast_select_fusion
  15.6 2.7 fusion.71
  23.1 2.6 compare_select_fusion.2
  27.1 1.4 scatter_custom_fusion.1
  30.6 6.3 %all-to-all-start.6 = ((bf16[4,2,640]{2,1,0:T(2,128)(2,1)}), bf16[4,2,640]{2,1,0:T(2,128)(2,1)S(1)}, u32[]{:S(2)}, u32[]{:S(2)}) async-start(bf16[4,2,640]{2,1,0:T(2,128)(2,1)} %multiply_convert_fusion), calls=%async_computation.6 | async-start | bytes 20480 | tf_op jit(solution)/shard_map/all_to_all | solution.py:156
  36.9 1.4 scatter_custom_fusion
  43.0 5.1 all-to-all-start.2
  50.1 6.2 %all-to-all-done.2 = bf16[4,2,640]{2,1,0:T(2,128)(2,1)S(1)} async-done(((bf16[4,2,640]{2,1,0:T(2,128)(2,1)}), bf16[4,2,640]{2,1,0:T(2,128)(2,1)S(1)}, u32[]{:S(2)}, u32[]{:S(2)}) %all-to-all-start.2) | async-done | bytes 10272 | tf_op jit(solution)/shard_map/all_to_all | solution.py:96
  56.2 3.3 all-to-all-start.4
  59.6 171.9 %all-reduce.9.cloned.1.call-done = (bf16[640,768]{1,0:T(8,128)(2,1)}, bf16[640,768]{1,0:T(8,128)(2,1)}, bf16[640,768]{1,0:T(8,128)(2,1)}, bf16[640,768]{1,0:T(8,...) async-done(((bf16[640,768]{1,0:T(8,128)(2,1)}, bf16[640,768]{1,0:T(8,128)(2,1)}, bf16[640,768]{1,0:T(8,128)(2,1)}, bf16[640,768]{1,0:T(8,128)(2,1)}, ...) | async-done | bytes 5898256 | tf_op jit(solution)/shard_map/psum | solution.py:13
  231.5 2.3 convolution_convert_fusion.4
  234.7 2.1 convolution_convert_fusion.6
  237.8 2.2 convolution_convert_fusion.5
  240.8 3.3 all-to-all-start
  245.4 4.3 all-to-all-done
  252.1 1.4 reduce-scatter.29.cloned.1.call-done
  254.3 21.4 %reduce-scatter.23.cloned.1.call-done = bf16[192,8]{1,0:T(8,128)(2,1)} async-done(((bf16[768,8]{1,0:T(8,128)(2,1)}), bf16[192,8]{1,0:T(8,128)(2,1)}) %reduce-scatter.23.cloned.1.call-update) | async-done | bytes 3088
  276.5 21.2 %reduce-scatter.25.cloned.1.call-done = bf16[192,8]{1,0:T(8,128)(2,1)} async-done(((bf16[768,8]{1,0:T(8,128)(2,1)}), bf16[192,8]{1,0:T(8,128)(2,1)}) %reduce-scatter.25.cloned.1.call-update) | async-done | bytes 3088
  298.6 5.2 all-gather.1
  303.9 5.2 all-gather.4
  309.1 5.2 all-gather.5
  315.6 1.5 broadcast.355.clone.1
  317.1 2.0 bitcast_dynamic-update-slice_fusion.1
  319.1 1.5 broadcast_in_dim.123
  320.6 2.0 bitcast_dynamic-update-slice_fusion
  324.0 18.9 %reduce-scatter.19.cloned.1.call-done = bf16[192,32]{1,0:T(8,128)(2,1)} async-done(((bf16[768,32]{1,0:T(8,128)(2,1)}), bf16[192,32]{1,0:T(8,128)(2,1)}) %reduce-scatter.19.cloned.1.call-update) | async-done | bytes 12304
  343.8 21.9 %reduce-scatter.21.cloned.1.call-done = bf16[192,32]{1,0:T(8,128)(2,1)} async-done(((bf16[768,32]{1,0:T(8,128)(2,1)}), bf16[192,32]{1,0:T(8,128)(2,1)}) %reduce-scatter.21.cloned.1.call-update) | async-done | bytes 12304
  366.6 5.2 all-gather
  373.0 4.6 all-to-all-start.1
  377.6 5.2 all-gather.2
  382.9 5.4 all-gather.3
  391.2 5.1 all-to-all-start.5
  396.3 2.1 convolution_convert_fusion.7
  399.0 3.7 all-to-all-done.5
  402.8 5.8 all-to-all-start.3
  410.2 5.1 all-to-all-done.3
  415.3 3.3 all-to-all-start.7
  422.6 1.8 all-to-all-done.7
  425.8 2.0 fusion.30
  427.7 2.3 multiply_reduce_fusion
  430.0 151.2 %all-reduce.7.cloned.1.call-done = (bf16[2,640,768]{2,1,0:T(8,128)(2,1)}, bf16[2,640,768]{2,1,0:T(8,128)(2,1)}, bf16[2,768,640]{2,1,0:T(8,128)(2,1)}) async-done(((bf16[2,640,768]{2,1,0:T(8,128)(2,1)}, bf16[2,640,768]{2,1,0:T(8,128)(2,1)}, bf16[2,768,640]{2,1,0:T(8,128)(2,1)}), (bf16[2,640,768]{2,1,0:T(8,128)(2,1)}, bf16[2,640,768]{2,1,0:T(8,128)(2,1)}, ...) | async-done | bytes 5898256 | tf_op jit(solution)/shard_map/psum | solution.py:206
  581.2 2.0 convert_element_type.167
  585.1 1.5 fusion.15
  586.6 1.5 fusion.16
  588.2 1.6 fusion.17
  (166 shorter events, 41.5 us)
Async XLA Ops:
  7.2 5.4 copy-start.1
  7.2 224.3 %all-reduce.9.cloned.1.call-start = ((), (), s32[]{:S(2)}) async-start(), calls=%async_computation.21 | async-start | bytes 11796480 | tf_op jit(solution)/shard_map/psum | solution.py:13
  12.5 1.6 copy-start
  15.5 2.8 copy-start.14
  15.5 6.9 %copy-start.13 = (s32[4]{0:T(128)S(1)}, s32[4]{0:T(128)}, u32[]{:S(2)}) copy-start(s32[4]{0:T(128)} %param.20) | copy-start | bytes 52
  15.5 11.2 %copy-start.16 = (f32[128,2]{0,1:T(2,128)S(1)}, f32[128,2]{0,1:T(2,128)}, u32[]{:S(2)}) copy-start(f32[128,2]{0,1:T(2,128)} %param.17) | copy-start | bytes 3076
  15.5 11.5 %copy-start.11 = (bf16[128,640]{1,0:T(8,128)(2,1)S(1)}, bf16[128,640]{1,0:T(8,128)(2,1)}, u32[]{:S(2)}) copy-start(bf16[128,640]{1,0:T(8,128)(2,1)} %param.16) | copy-start | bytes 491524
  15.6 24.9 %copy-start.15 = (s32[2,2]{1,0:T(2,128)S(1)}, s32[2,2]{1,0:T(2,128)}, u32[]{:S(2)}) copy-start(s32[2,2]{1,0:T(2,128)} %param.19) | copy-start | bytes 52
  15.6 25.6 %copy-start.12 = (bf16[128,640]{1,0:T(8,128)(2,1)S(1)}, bf16[128,640]{1,0:T(8,128)(2,1)}, u32[]{:S(2)}) copy-start(bf16[128,640]{1,0:T(8,128)(2,1)} %param.15) | copy-start | bytes 491524
  15.6 32.5 %copy-start.17 = (s32[3]{0:T(128)S(1)}, s32[3]{0:T(128)}, u32[]{:S(2)}) copy-start(s32[3]{0:T(128)} %constant.153.clone.1) | copy-start | bytes 40
  30.6 12.4 %all-to-all-start.6 = ((bf16[4,2,640]{2,1,0:T(2,128)(2,1)}), bf16[4,2,640]{2,1,0:T(2,128)(2,1)S(1)}, u32[]{:S(2)}, u32[]{:S(2)}) async-start(bf16[4,2,640]{2,1,0:T(2,128)(2,1)} %multiply_convert_fusion), calls=%async_computation.6 | async-start | bytes 20480 | tf_op jit(solution)/shard_map/all_to_all | solution.py:156
  43.0 13.3 %all-to-all-start.2 = ((bf16[4,2,640]{2,1,0:T(2,128)(2,1)}), bf16[4,2,640]{2,1,0:T(2,128)(2,1)S(1)}, u32[]{:S(2)}, u32[]{:S(2)}) async-start(bf16[4,2,640]{2,1,0:T(2,128)(2,1)} %reshape.357), calls=%async_computation.2 | async-start | bytes 20480 | tf_op jit(solution)/shard_map/all_to_all | solution.py:96
  56.2 184.5 %all-to-all-start.4 = ((bf16[4,8,640]{2,1,0:T(8,128)(2,1)}), bf16[4,8,640]{2,1,0:T(8,128)(2,1)S(1)}, u32[]{:S(2)}, u32[]{:S(2)}) async-start(bf16[4,8,640]{2,1,0:T(8,128)(2,1)} %fusion.31), calls=%async_computation.4 | async-start | bytes 81920 | tf_op jit(solution)/shard_map/all_to_all | solution.py:155
  59.5 193.9 %reduce-scatter.29.cloned.1.call-start = ((), (), s32[]{:S(2)}) async-start(), calls=%async_computation.19 | async-start | bytes 245760
  231.5 3.2 copy-start.4
  234.7 41.0 %reduce-scatter.23.cloned.1.call-start = ((), (), s32[]{:S(2)}) async-start(), calls=%async_computation.16 | async-start | bytes 245760
  237.7 60.0 %reduce-scatter.25.cloned.1.call-start = ((), (), s32[]{:S(2)}) async-start(), calls=%async_computation.17 | async-start | bytes 245760
  239.9 11.0 %copy-start.2 = (bf16[1,640,768]{2,1,0:T(8,128)(2,1)S(1)}, bf16[1,640,768]{2,1,0:T(8,128)(2,1)}, u32[]{:S(2)}) copy-start(bf16[1,640,768]{2,1,0:T(8,128)(2,1)} %param.22) | copy-start | bytes 2949124
  240.8 8.9 %all-to-all-start = ((bf16[4,8,640]{2,1,0:T(8,128)(2,1)}), bf16[4,8,640]{2,1,0:T(8,128)(2,1)S(1)}, u32[]{:S(2)}, u32[]{:S(2)}) async-start(bf16[4,8,640]{2,1,0:T(8,128)(2,1)} %bitcast.14), calls=%async_computation | async-start | bytes 81920 | tf_op jit(solution)/shard_map/all_to_all | solution.py:95
  244.1 79.0 %reduce-scatter.27.cloned.1.call-start = ((), (), s32[]{:S(2)}) async-start(), calls=%async_computation.18 | async-start | bytes 245760
  245.4 97.5 %reduce-scatter.19.cloned.1.call-start = ((), (), s32[]{:S(2)}) async-start(), calls=%async_computation.14 | async-start | bytes 245760
  250.8 114.9 %reduce-scatter.21.cloned.1.call-start = ((), (), s32[]{:S(2)}) async-start(), calls=%async_computation.15 | async-start | bytes 245760
  252.0 329.2 %all-reduce.7.cloned.1.call-start = ((), (), s32[]{:S(2)}) async-start(), calls=%async_computation.20 | async-start | bytes 11796480 | tf_op jit(solution)/shard_map/psum | solution.py:206
  315.6 3.5 copy-start.3
  373.0 18.2 %all-to-all-start.1 = ((bf16[4,8,640]{2,1,0:T(8,128)(2,1)}), bf16[4,8,640]{2,1,0:T(8,128)(2,1)S(1)}, u32[]{:S(2)}, u32[]{:S(2)}) async-start(bf16[4,8,640]{2,1,0:T(8,128)(2,1)} %fusion.19), calls=%async_computation.1 | async-start | bytes 81920 | tf_op jit(solution)/shard_map/all_to_all | solution.py:151
  388.5 1.5 copy-start.5
  388.5 1.5 copy-start.6
  390.0 18.5 %copy-start.7 = (bf16[640,768]{1,0:T(8,128)(2,1)S(1)}, bf16[640,768]{1,0:T(8,128)(2,1)}, u32[]{:S(2)}) copy-start(bf16[640,768]{1,0:T(8,128)(2,1)} %get-tuple-element.44) | copy-start | bytes 2949124
  390.0 18.5 %copy-start.8 = (bf16[640,768]{1,0:T(8,128)(2,1)S(1)}, bf16[640,768]{1,0:T(8,128)(2,1)}, u32[]{:S(2)}) copy-start(bf16[640,768]{1,0:T(8,128)(2,1)} %get-tuple-element.45) | copy-start | bytes 2949124
  391.2 11.6 %all-to-all-start.5 = ((bf16[4,8,640]{2,1,0:T(8,128)(2,1)}), bf16[4,8,640]{2,1,0:T(8,128)(2,1)S(1)}, u32[]{:S(2)}, u32[]{:S(2)}) async-start(bf16[4,8,640]{2,1,0:T(8,128)(2,1)} %fusion.20), calls=%async_computation.5 | async-start | bytes 81920 | tf_op jit(solution)/shard_map/all_to_all | solution.py:197
  402.8 12.6 %all-to-all-start.3 = ((bf16[4,2,640]{2,1,0:T(2,128)(2,1)}), bf16[4,2,640]{2,1,0:T(2,128)(2,1)S(1)}, u32[]{:S(2)}, u32[]{:S(2)}) async-start(bf16[4,2,640]{2,1,0:T(2,128)(2,1)} %reshape.359), calls=%async_computation.3 | async-start | bytes 20480 | tf_op jit(solution)/shard_map/all_to_all | solution.py:152
  415.3 9.1 %all-to-all-start.7 = ((bf16[4,2,640]{2,1,0:T(2,128)(2,1)}), bf16[4,2,640]{2,1,0:T(2,128)(2,1)S(1)}, u32[]{:S(2)}, u32[]{:S(2)}) async-start(bf16[4,2,640]{2,1,0:T(2,128)(2,1)} %reshape.366), calls=%async_computation.7 | async-start | bytes 20480 | tf_op jit(solution)/shard_map/all_to_all | solution.py:198
  581.2 2.1 copy-start.10
  583.3 1.5 copy-start.9
Sparse Core Ops, SparseCore 0:
  15.7 215.7 all-reduce.8
  234.8 18.5 reduce-scatter.28
  255.9 19.7 reduce-scatter.22
  277.9 19.7 reduce-scatter.24
  300.6 19.7 reduce-scatter.26
  323.2 19.6 reduce-scatter.18
  345.9 19.7 reduce-scatter.20
  368.3 212.8 all-reduce.6
where the time goes:
time: 598 us; the launch traced here: 597 us
  waiting for transfers between devices  429 us (72%)
  starting transfers between devices  37.1 us (6%)
  local copies, waits for them, and re-layouts  35.1 us (6%)
  blocking collectives  31.4 us (5%)
  matrix products  23.7 us (4%)
  other arithmetic  23.6 us (4%)
  between operations  16.5 us (3%)
    psum x1, waiting for transfers between devices, broadcast(): return lax.psum(block, axis)  172 us
    psum x1, waiting for transfers between devices, shards(): lax.psum(stacked(spare_gate_part).astype(jnp.bfloat16), 'expert')  151 us
    unnamed x14, waiting for transfers between devices  85 us
    unnamed x55, local copies, waits for them, and re-layouts  12.4 us
  transfers between devices with their start and end apart: 16, of which 12 were waited for; matrix products, arithmetic and copies ran while one was open for 11% of the time, Pallas kernels for 0%

commit v1 on v0

v1 whole, which is shorter than its diff:
```python
import functools

import jax
import jax.numpy as jnp
from jax import lax
from jax.experimental import pallas as pl
from jax.experimental.pallas import tpu as pltpu
from jax.sharding import PartitionSpec as P

BLK = 4
MAXB = 2
SPARE = 2
OWN = BLK * MAXB
GROUP = 4
TILE = 256
VMEM_LIMIT = 32 * 1024 * 1024

BF16 = jnp.bfloat16
F32 = jnp.float32
I32 = jnp.int32


def matmul(left, right, left_dim, right_dim):
    return lax.dot_general(
        left, right, (((left_dim,), (right_dim,)), ((), ())), preferred_element_type=F32
    )


def params():
    return pltpu.CompilerParams(vmem_limit_bytes=VMEM_LIMIT)


def dispatch_kernel(
    experts, hosts, slots, block, plan_ref, caps_ref, ids_ref, gates_ref, tok_ref, grad_ref, send_ref, pick_ref
):
    choose, count = ids_ref.shape
    row = lax.broadcasted_iota(I32, (block, count), 0)
    col = lax.broadcasted_iota(I32, (block, count), 1)
    is_cot = row >= slots
    slot = jnp.where(is_cot, row - slots, row)
    valid = row < 2 * slots
    is_spare = slot >= OWN
    spare_slot = jnp.maximum(slot - OWN, 0)
    replica = jnp.where(is_spare, 1 + lax.div(spare_slot, SPARE), 0)
    position = jnp.where(is_spare, lax.rem(spare_slot, SPARE), slot)
    token_slot = lax.rem(col, hosts)
    members, weights, limits = [], [], []
    for expert in range(experts):
        hot = (plan_ref[0, 0] == expert) | (plan_ref[1, 0] == expert)
        wanted = token_slot * hot.astype(I32)
        here = jnp.zeros((1, count), F32)
        weight = jnp.zeros((1, count), F32)
        for k in range(choose):
            chosen = ids_ref[k : k + 1, :] == expert
            here = jnp.where(chosen, 1.0, here)
            weight = jnp.where(chosen, gates_ref[k : k + 1, :], weight)
        fits = valid & (replica == wanted)
        members.append(jnp.where(fits, jnp.broadcast_to(here, fits.shape), 0.0))
        weights.append(jnp.broadcast_to(weight, fits.shape))
        room = jnp.where(is_spare, SPARE, caps_ref[expert] * BLK)
        limits.append(jnp.where(position < room, position, -1))
    member = jnp.concatenate(members, axis=0)
    weight = jnp.concatenate(weights, axis=0)
    limit = jnp.concatenate(limits, axis=0).astype(F32)
    cots = jnp.concatenate([is_cot.astype(F32)] * experts, axis=0)
    earlier = (
        lax.broadcasted_iota(I32, (count, count), 0) < lax.broadcasted_iota(I32, (count, count), 1)
    )
    before = matmul(member.astype(BF16), earlier.astype(F32).astype(BF16), 1, 0)
    taken = jnp.where(before == limit, member, 0.0)
    pick_cot = taken * cots
    pick_tok = taken - pick_cot
    gate = jnp.sum(taken * weight, axis=1, keepdims=True)
    pick_cot = pick_cot.astype(BF16)
    rows = matmul(pick_tok.astype(BF16), tok_ref[...], 1, 0)
    cotangents = gate * matmul(pick_cot, grad_ref[...], 1, 0)
    send_ref[...] = (rows + cotangents).astype(BF16)
    scaled = pick_tok * weight
    high = scaled.astype(BF16)
    pick_ref[0] = high
    pick_ref[1] = (scaled - high.astype(F32)).astype(BF16)
    pick_ref[2] = pick_cot


def dispatch(plan, caps, ids, gates, tokens, grads, experts, slots, block):
    count, feature = tokens.shape
    smem = pl.BlockSpec(memory_space=pltpu.SMEM)
    vmem = pl.BlockSpec(memory_space=pltpu.VMEM)
    return pl.pallas_call(
        functools.partial(dispatch_kernel, experts, plan.shape[1], slots, block),
        out_shape=(
            jax.ShapeDtypeStruct((experts * block, feature), BF16),
            jax.ShapeDtypeStruct((3, experts * block, count), BF16),
        ),
        in_specs=[smem, smem, vmem, vmem, vmem, vmem],
        out_specs=(vmem, vmem),
        compiler_params=params(),
        name="dispatch",
    )(plan, caps, ids, gates, tokens, grads)


def partial_kernel(
    group, slots, block, recv_ref, gate_ref, up_ref, down_ref, rows_ref, cots_ref, part_ref, wide, flat
):
    wide[...] = recv_ref[...].astype(F32)
    for s in range(group):
        flat[0, s * slots : (s + 1) * slots, :] = wide[s * block : s * block + slots, :]
        flat[1, s * slots : (s + 1) * slots, :] = wide[s * block + slots : s * block + 2 * slots, :]
    rows = flat[0].astype(BF16)
    cots = flat[1].astype(BF16)
    rows_ref[...] = rows
    cots_ref[...] = cots
    hidden = gate_ref.shape[1]
    part_ref[:, :hidden] = matmul(rows, gate_ref[...], 1, 0).astype(BF16)
    part_ref[:, hidden : 2 * hidden] = matmul(rows, up_ref[...], 1, 0).astype(BF16)
    part_ref[:, 2 * hidden :] = matmul(cots, down_ref[...], 1, 1).astype(BF16)


def partials(recv, gate, up, down, experts, slots, block):
    feature, hidden = gate.shape
    tile, big = GROUP * slots, GROUP * block
    total = experts * slots

    def whole(shape):
        return pl.BlockSpec(shape, lambda i: (0, 0))

    def by_rows(rows, width):
        return pl.BlockSpec((rows, width), lambda i: (i, 0))

    return pl.pallas_call(
        functools.partial(partial_kernel, GROUP, slots, block),
        grid=(experts // GROUP,),
        out_shape=(
            jax.ShapeDtypeStruct((total, feature), BF16),
            jax.ShapeDtypeStruct((total, feature), BF16),
            jax.ShapeDtypeStruct((total, 3 * hidden), BF16),
        ),
        in_specs=[
            by_rows(big, feature),
            whole((feature, hidden)),
            whole((feature, hidden)),
            whole((hidden, feature)),
        ],
        out_specs=(by_rows(tile, feature), by_rows(tile, feature), by_rows(tile, 3 * hidden)),
        scratch_shapes=[pltpu.VMEM((big, feature), F32), pltpu.VMEM((2, tile, feature), F32)],
        compiler_params=params(),
        name="partials",
    )(recv, gate, up, down)


def middle_kernel(
    group, slots, block, parts_ref, gate_ref, up_ref, down_ref, back_ref, hidden_ref, gg_ref, ug_ref, flat, wide
):
    width = gate_ref.shape[1]
    total = parts_ref[0].astype(F32)
    for j in range(1, parts_ref.shape[0]):
        total = total + parts_ref[j].astype(F32)
    gate_pre, up_pre, hidden_grad = (total[:, i * width : (i + 1) * width] for i in range(3))
    sigma = jax.nn.sigmoid(gate_pre)
    active = gate_pre * sigma
    slope = sigma * (1.0 + gate_pre * (1.0 - sigma))
    hidden = (active * up_pre).astype(BF16)
    gg = (hidden_grad * up_pre * slope).astype(BF16)
    ug = (hidden_grad * active).astype(BF16)
    hidden_ref[...] = hidden
    gg_ref[...] = gg
    ug_ref[...] = ug
    flat[0] = matmul(hidden, down_ref[...], 1, 0)
    flat[1] = matmul(gg, gate_ref[...], 1, 1) + matmul(ug, up_ref[...], 1, 1)
    wide[...] = jnp.zeros_like(wide)
    for s in range(group):
        wide[s * block : s * block + slots, :] = flat[0, s * slots : (s + 1) * slots, :]
        wide[s * block + slots : s * block + 2 * slots, :] = flat[1, s * slots : (s + 1) * slots, :]
    back_ref[...] = wide[...].astype(BF16)


def middle(parts, gate, up, down, experts, slots, block):
    feature, hidden = gate.shape
    tile, big = GROUP * slots, GROUP * block
    total = experts * slots

    def whole(shape):
        return pl.BlockSpec(shape, lambda i: (0, 0))

    def by_rows(rows, width):
        return pl.BlockSpec((rows, width), lambda i: (i, 0))

    return pl.pallas_call(
        functools.partial(middle_kernel, GROUP, slots, block),
        grid=(experts // GROUP,),
        out_shape=(
            jax.ShapeDtypeStruct((experts * block, feature), BF16),
            jax.ShapeDtypeStruct((total, hidden), BF16),
            jax.ShapeDtypeStruct((total, hidden), BF16),
            jax.ShapeDtypeStruct((total, hidden), BF16),
        ),
        in_specs=[
            pl.BlockSpec((parts.shape[0], tile, 3 * hidden), lambda i: (0, i, 0)),
            whole((feature, hidden)),
            whole((feature, hidden)),
            whole((hidden, feature)),
        ],
        out_specs=(
            by_rows(big, feature),
            by_rows(tile, hidden),
            by_rows(tile, hidden),
            by_rows(tile, hidden),
        ),
        scratch_shapes=[pltpu.VMEM((2, tile, feature), F32), pltpu.VMEM((big, feature), F32)],
        compiler_params=params(),
        name="middle",
    )(parts, gate, up, down)


def grads_kernel(rows_ref, cots_ref, hidden_ref, gg_ref, ug_ref, gate_ref, up_ref, down_ref):
    gate_ref[...] = matmul(rows_ref[...], gg_ref[...], 0, 0).astype(BF16)
    up_ref[...] = matmul(rows_ref[...], ug_ref[...], 0, 0).astype(BF16)
    down_ref[...] = matmul(hidden_ref[...], cots_ref[...], 0, 0).astype(BF16)


def weight_grads(rows, cots, hidden, gg, ug):
    total, feature = rows.shape
    width = hidden.shape[1]
    tile = TILE if width % TILE == 0 else width

    def whole(shape):
        return pl.BlockSpec(shape, lambda i: (0, 0))

    def by_columns(count):
        return pl.BlockSpec((count, tile), lambda i: (0, i))

    return pl.pallas_call(
        grads_kernel,
        grid=(width // tile,),
        out_shape=(
            jax.ShapeDtypeStruct((feature, width), BF16),
            jax.ShapeDtypeStruct((feature, width), BF16),
            jax.ShapeDtypeStruct((width, feature), BF16),
        ),
        in_specs=[
            whole((total, feature)),
            whole((total, feature)),
            by_columns(total),
            by_columns(total),
            by_columns(total),
        ],
        out_specs=(
            by_columns(feature),
            by_columns(feature),
            pl.BlockSpec((tile, feature), lambda i: (i, 0)),
        ),
        compiler_params=params(),
        cost_estimate=pl.CostEstimate(
            flops=6 * total * feature * width,
            bytes_accessed=6 * feature * width,
            transcendentals=0,
        ),
        name="weight_grads",
    )(rows, cots, hidden, gg, ug)


def combine_kernel(back_ref, pick_ref, mixed_ref, token_ref):
    back = back_ref[...]
    mixed = matmul(pick_ref[0], back, 0, 0) + matmul(pick_ref[1], back, 0, 0)
    mixed_ref[...] = mixed.astype(BF16)
    token_ref[...] = matmul(pick_ref[2], back, 0, 0).astype(BF16)


def combine(back, pick):
    feature, count = back.shape[1], pick.shape[2]
    vmem = pl.BlockSpec(memory_space=pltpu.VMEM)
    shape = jax.ShapeDtypeStruct((count, feature), BF16)
    return pl.pallas_call(
        combine_kernel,
        out_shape=(shape, shape),
        in_specs=[vmem, vmem],
        out_specs=(vmem, vmem),
        compiler_params=params(),
        name="combine",
    )(back, pick)


def over_experts(array, experts):
    blocks = array.reshape(experts, -1, array.shape[1])
    return lax.all_to_all(blocks, "expert", split_axis=0, concat_axis=0, tiled=True).reshape(array.shape)


def shards(
    tokens,
    out_grad,
    gate_weights,
    expert_ids,
    replica_plan,
    cap_blocks,
    gate_weight,
    up_weight,
    down_weight,
):
    experts = lax.axis_size("expert")
    hosts = replica_plan.shape[1]
    assert tokens.shape[0] % hosts == 0 and experts % GROUP == 0
    slots = OWN + SPARE * (hosts - 1)
    block = -(-2 * slots // 8) * 8
    gate, up, down = gate_weight[0], up_weight[0], down_weight[0]
    send, pick = dispatch(
        replica_plan, cap_blocks, expert_ids.T, gate_weights.T, tokens, out_grad, experts, slots, block
    )
    recv = over_experts(send, experts)
    rows, cots, part = partials(recv, gate, up, down, experts, slots, block)
    parts = lax.all_gather(part, "dp")
    back, hidden, gg, ug = middle(parts, gate, up, down, experts, slots, block)
    returned = over_experts(back, experts)
    gate_grad, up_grad, down_grad = weight_grads(rows, cots, hidden, gg, ug)
    mixed, token_grad = combine(returned, pick)
    return mixed, token_grad, gate_grad[None], up_grad[None], down_grad[None]


def solution(mesh):
    return jax.shard_map(
        shards,
        mesh=mesh,
        in_specs=(
            P(("groups", "expert"), "dp"),
            P(("groups", "expert"), "dp"),
            P(("groups", "expert"), None),
            P(("groups", "expert"), None),
            P("groups", None),
            P("groups"),
            P("expert", "dp", None),
            P("expert", "dp", None),
            P("expert", None, "dp"),
        ),
        out_specs=(
            P(("groups", "expert"), "dp"),
            P(("groups", "expert"), "dp"),
            P(("groups", "expert"), "dp", None),
            P(("groups", "expert"), "dp", None),
            P(("groups", "expert"), None, "dp"),
        ),
        check_vma=False,
    )
```

time: 598 us -> 41.6 us (0.07)
  waiting for transfers between devices: 429 us -> 3.6 us
  starting transfers between devices: 37.1 us -> 3.32 us
  local copies, waits for them, and re-layouts: 35.1 us -> 6.13 us
  matrix products: 23.7 us -> 0 us
  other arithmetic: 23.6 us -> 0 us
  between operations: 16.5 us -> 0.7 us
  blocking collectives: 31.4 us -> 20.6 us
  Pallas kernels: 0 us -> 6.84 us
    psum x2 -> x0, waiting for transfers between devices: 323 us -> none  [the longest x1 172 us: broadcast(): return lax.psum(block, axis)]
    unnamed x14 -> x0, waiting for transfers between devices: 85 us -> none
    all_to_all x8 -> x1, starting transfers between devices: 36.7 us -> 3.32 us  [over_experts(): lax.all_to_all(blocks, 'expert', split_axis=0, concat_axis=0, tiled=True)]
    dot_general x18 -> x0, matrix products: 23.7 us -> none  [the longest x1 2.3 us: shards(): jnp.dot(spare_cot, spare_weights[2].T, preferred_element_type=jnp.float32)]
    all_gather x6 -> x1, blocking collectives: 31.4 us -> 8.46 us  [shards(): parts = lax.all_gather(part, 'dp')]
    all_to_all x8 -> x1, waiting for transfers between devices: 21.1 us -> 3.6 us  [over_experts(): lax.all_to_all(blocks, 'expert', split_axis=0, concat_axis=0, tiled=True)]
    all_to_all x0 -> x1, blocking collectives: none -> 12.1 us  [over_experts(): lax.all_to_all(blocks, 'expert', split_axis=0, concat_axis=0, tiled=True)]
    gather x16 -> x0, local copies, waits for them, and re-layouts: 11.8 us -> none  [the longest x4 2.67 us: combine(): spare_vals = spare_flat.reshape(-1, feature)[spare_pos]]
  transfers between devices with their start and end apart: 16 -> 1, of which waited for: 12 -> 1; matrix products, arithmetic and copies ran while one was open for 11% -> 0% of each run, Pallas kernels for 0% -> 7%
where the time goes in v1:
time: 41.6 us; the launch traced here: 41.2 us
  blocking collectives  20.6 us (50%)
  Pallas kernels  6.84 us (16%)
  local copies, waits for them, and re-layouts  6.13 us (15%)
  waiting for transfers between devices  3.6 us (9%)
  starting transfers between devices  3.32 us (8%)
  between operations  0.7 us (2%)
    all_to_all x1, blocking collectives, over_experts(): lax.all_to_all(blocks, 'expert', split_axis=0, concat_axis=0, tiled=True)  12.1 us
    all_gather x1, blocking collectives, shards(): parts = lax.all_gather(part, 'dp')  8.46 us
    unnamed x24, local copies, waits for them, and re-layouts  6.13 us
    all_to_all x1, waiting for transfers between devices, over_experts(): lax.all_to_all(blocks, 'expert', split_axis=0, concat_axis=0, tiled=True)  3.6 us
    all_to_all x1, starting transfers between devices, over_experts(): lax.all_to_all(blocks, 'expert', split_axis=0, concat_axis=0, tiled=True)  3.32 us
    pallas_call x1, Pallas kernels, weight_grads(): pl.pallas_call(grads_kernel, grid=(width // tile,), out_shape=(jax.ShapeD...  2.7 us
    pallas_call x1, Pallas kernels, middle(): pl.pallas_call(functools.partial(middle_kernel, GROUP, slots, block), gri...  1.51 us
    pallas_call x1, Pallas kernels, combine(): pl.pallas_call(combine_kernel, out_shape=(shape, shape), in_specs=[vmem,...  1.01 us
  transfers between devices with their start and end apart: 1, of which 1 were waited for; matrix products, arithmetic and copies ran while one was open for 0% of the time, Pallas kernels for 7%

profile of v1, /device:TPU:0, one launch (start us, length us, event | category | flops | bytes accessed | tf_op | source)
XLA Modules:
  0.0 41.2 jit_solution(17988924078086898659)
XLA Ops:
  0.6 0.0 copy-start.9
  0.6 0.0 copy-start.10
  0.7 0.0 copy-start.8
  0.7 0.0 copy-start.11
  0.7 0.6 %copy-done.9 = s32[128,2]{0,1:T(2,128)S(1)} copy-done((s32[128,2]{0,1:T(2,128)S(1)}, s32[128,2]{0,1:T(2,128)}, u32[]{:S(2)}) %copy-start.9) | copy-done | bytes 1048
  1.3 0.0 copy-done.10
  1.3 0.0 copy-done.8
  1.3 0.0 copy-done.11
  1.3 0.0 copy-start.6
  1.3 0.9 %copy-done.6 = bf16[128,640]{1,0:T(8,128)(2,1)S(1)} copy-done((bf16[128,640]{1,0:T(8,128)(2,1)S(1)}, bf16[128,640]{1,0:T(8,128)(2,1)}, u32[]{:S(2)}) %copy-start.6) | copy-done | bytes 163864
  2.3 0.0 copy-start.7
  2.3 0.9 %copy-done.7 = bf16[128,640]{1,0:T(8,128)(2,1)S(1)} copy-done((bf16[128,640]{1,0:T(8,128)(2,1)S(1)}, bf16[128,640]{1,0:T(8,128)(2,1)}, u32[]{:S(2)}) %copy-start.7) | copy-done | bytes 163864
  3.2 0.9 %dispatch.1 = (bf16[96,640]{1,0:T(8,128)(2,1)S(1)}, bf16[3,96,128]{2,1,0:T(8,128)(2,1)S(1)}) custom-call(s32[2,2]{1,0:T(2,128)S(1)} %copy-done.8, s32[4]{0:T(128)S(1)} %copy-done.11, s32[2,128]{1,0:T(2,128)S(1)} %bitcast.23, f32[2,128]{1,0:T(2,128)S(1)} %bitcast.24, bf16[128,640]{1,0:T(8,128)(2,1)S(1)} %copy-done.6, bf16[128,640]{1,0:T(8,128)(2,1)S(1)} %copy-done.7), custom_call_target="tpu_custom_call" | custom-call | tf_op jit(solution)/shard_map/dispatch/pallas_call | solution.py:89
  4.1 12.1 %all_to_all.10 = bf16[4,24,640]{2,1,0:T(8,128)(2,1)S(1)} all-to-all(bf16[4,24,640]{2,1,0:T(8,128)(2,1)S(1)} %bitcast.22), channel_id=1, replica_groups=mesh['groups'=2,'expert'=4,'dp'=4] {'expert'}, dimensions={0} | all-to-all | bytes 245760 | tf_op jit(solution)/shard_map/all_to_all | solution.py:285
  16.2 0.0 copy-start
  16.2 1.2 %copy-done = bf16[1,640,768]{2,1,0:T(8,128)(2,1)S(1)} copy-done((bf16[1,640,768]{2,1,0:T(8,128)(2,1)S(1)}, bf16[1,640,768]{2,1,0:T(8,128)(2,1)}, u32[]{:S(2)}) %copy-start) | copy-done | bytes 983064
  17.4 0.0 copy-start.2
  17.4 1.2 %copy-done.2 = bf16[1,640,768]{2,1,0:T(8,128)(2,1)S(1)} copy-done((bf16[1,640,768]{2,1,0:T(8,128)(2,1)S(1)}, bf16[1,640,768]{2,1,0:T(8,128)(2,1)}, u32[]{:S(2)}) %copy-start.2) | copy-done | bytes 983064
  18.6 0.0 copy-start.4
  18.6 1.2 %copy-done.4 = bf16[1,768,640]{2,1,0:T(8,128)(2,1)S(1)} copy-done((bf16[1,768,640]{2,1,0:T(8,128)(2,1)S(1)}, bf16[1,768,640]{2,1,0:T(8,128)(2,1)}, u32[]{:S(2)}) %copy-start.4) | copy-done | bytes 983064
  19.8 0.0 copy-start.1
  19.8 0.0 copy-start.3
  19.8 0.0 copy-start.5
  19.8 0.7 %partials.1 = (bf16[40,640]{1,0:T(8,128)(2,1)S(1)}, bf16[40,640]{1,0:T(8,128)(2,1)S(1)}, bf16[40,2304]{1,0:T(8,128)(2,1)S(1)}) custom-call(bf16[96,640]{1,0:T(8,128)(2,1)S(1)} %bitcast.21, bf16[640,768]{1,0:T(8,128)(2,1)S(1)} %bitcast.13, bf16[640,768]{1,0:T(8,128)(2,1)S(1)} %bitcast.15, bf16[768,640]{1,0:T(8,128)(2,1)S(1)} %bitcast.17), custom_call_target="tpu_custom_call" | custom-call | tf_op jit(solution)/shard_map/partials/pallas_call | solution.py:130
  20.5 8.5 %all-gather = bf16[160,2304]{1,0:T(8,128)(2,1)S(1)} all-gather(bf16[40,2304]{1,0:T(8,128)(2,1)S(1)} %get-tuple-element.20), channel_id=2, replica_groups=mesh['groups'=2,'expert'=4,'dp'=4] {'dp'}, dimensions={0}, use_global_device_ids=true | all-gather | bytes 921600 | tf_op jit(solution)/shard_map/all_gather | solution.py:310
  29.0 0.0 copy-done.1
  29.0 0.0 copy-done.3
  29.0 0.0 copy-done.5
  29.0 1.5 %middle.1 = (bf16[96,640]{1,0:T(8,128)(2,1)}, bf16[40,768]{1,0:T(8,128)(2,1)S(1)}, bf16[40,768]{1,0:T(8,128)(2,1)S(1)}, bf16[40,768]{1,0:T(8,128)(2,1)S(1)}) custom-call(bf16[4,40,2304]{2,1,0:T(8,128)(2,1)S(1)} %bitcast.19, bf16[640,768]{1,0:T(8,128)(2,1)S(1)} %bitcast.14, bf16[640,768]{1,0:T(8,128)(2,1)S(1)} %bitcast.16, bf16[768,640]{1,0:T(8,128)(2,1)S(1)} %bitcast.18), custom_call_target="tpu_custom_call" | custom-call | tf_op jit(solution)/shard_map/middle/pallas_call | solution.py:188
  30.5 3.3 %all-to-all-start.1 = ((bf16[4,24,640]{2,1,0:T(8,128)(2,1)}), bf16[4,24,640]{2,1,0:T(8,128)(2,1)S(1)}, u32[]{:S(2)}, u32[]{:S(2)}) async-start(bf16[4,24,640]{2,1,0:T(8,128)(2,1)} %bitcast.8), calls=%async_computation.1 | async-start | bytes 245760 | tf_op jit(solution)/shard_map/all_to_all | solution.py:285
  33.8 2.7 %weight_grads.1 = (bf16[640,768]{1,0:T(8,128)(2,1)}, bf16[640,768]{1,0:T(8,128)(2,1)}, bf16[768,640]{1,0:T(8,128)(2,1)}) custom-call(bf16[40,640]{1,0:T(8,128)(2,1)S(1)} %get-tuple-element.25.rows_ref, bf16[40,640]{1,0:T(8,128)(2,1)S(1)} %get-tuple-element.26.cots_ref, bf16[40,768]{1,0:T(8,128)(2,1)S(1)} %get-tuple-element.27.hidden_ref, ...), custom_call_target="tpu_custom_call" | custom-call | flops 117964800 | bytes 2949120 | tf_op jit(solution)/shard_map/weight_grads/pallas_call | solution.py:232
  36.5 3.6 %all-to-all-done.1 = bf16[4,24,640]{2,1,0:T(8,128)(2,1)S(1)} async-done(((bf16[4,24,640]{2,1,0:T(8,128)(2,1)}), bf16[4,24,640]{2,1,0:T(8,128)(2,1)S(1)}, u32[]{:S(2)}, u32[]{:S(2)}) %all-to-all-start.1) | async-done | bytes 122912 | tf_op jit(solution)/shard_map/all_to_all | solution.py:285
  40.1 1.0 %combine.1 = (bf16[128,640]{1,0:T(8,128)(2,1)}, bf16[128,640]{1,0:T(8,128)(2,1)}) custom-call(bf16[96,640]{1,0:T(8,128)(2,1)S(1)} %bitcast.20, bf16[3,96,128]{2,1,0:T(8,128)(2,1)S(1)} %get-tuple-element.22.pick_ref), custom_call_target="tpu_custom_call" | custom-call | tf_op jit(solution)/shard_map/combine/pallas_call | solution.py:273
Async XLA Ops:
  0.6 0.7 %copy-start.9 = (s32[128,2]{0,1:T(2,128)S(1)}, s32[128,2]{0,1:T(2,128)}, u32[]{:S(2)}) copy-start(s32[128,2]{0,1:T(2,128)} %param.12) | copy-start | bytes 3076
  0.6 0.7 %copy-start.10 = (f32[128,2]{0,1:T(2,128)S(1)}, f32[128,2]{0,1:T(2,128)}, u32[]{:S(2)}) copy-start(f32[128,2]{0,1:T(2,128)} %param.11) | copy-start | bytes 3076
  0.7 0.7 %copy-start.8 = (s32[2,2]{1,0:T(2,128)S(1)}, s32[2,2]{1,0:T(2,128)}, u32[]{:S(2)}) copy-start(s32[2,2]{1,0:T(2,128)} %plan_ref.1) | copy-start | bytes 52
  0.7 0.7 %copy-start.11 = (s32[4]{0:T(128)S(1)}, s32[4]{0:T(128)}, u32[]{:S(2)}) copy-start(s32[4]{0:T(128)} %caps_ref.1) | copy-start | bytes 52
  1.3 0.9 %copy-start.6 = (bf16[128,640]{1,0:T(8,128)(2,1)S(1)}, bf16[128,640]{1,0:T(8,128)(2,1)}, u32[]{:S(2)}) copy-start(bf16[128,640]{1,0:T(8,128)(2,1)} %tok_ref.1) | copy-start | bytes 491524
  2.3 0.9 %copy-start.7 = (bf16[128,640]{1,0:T(8,128)(2,1)S(1)}, bf16[128,640]{1,0:T(8,128)(2,1)}, u32[]{:S(2)}) copy-start(bf16[128,640]{1,0:T(8,128)(2,1)} %grad_ref.1) | copy-start | bytes 491524
  16.2 1.2 %copy-start = (bf16[1,640,768]{2,1,0:T(8,128)(2,1)S(1)}, bf16[1,640,768]{2,1,0:T(8,128)(2,1)}, u32[]{:S(2)}) copy-start(bf16[1,640,768]{2,1,0:T(8,128)(2,1)} %param.15) | copy-start | bytes 2949124
  17.4 1.2 %copy-start.2 = (bf16[1,640,768]{2,1,0:T(8,128)(2,1)S(1)}, bf16[1,640,768]{2,1,0:T(8,128)(2,1)}, u32[]{:S(2)}) copy-start(bf16[1,640,768]{2,1,0:T(8,128)(2,1)} %param.16) | copy-start | bytes 2949124
  18.6 1.2 %copy-start.4 = (bf16[1,768,640]{2,1,0:T(8,128)(2,1)S(1)}, bf16[1,768,640]{2,1,0:T(8,128)(2,1)}, u32[]{:S(2)}) copy-start(bf16[1,768,640]{2,1,0:T(8,128)(2,1)} %param.17) | copy-start | bytes 2949124
  19.8 9.2 %copy-start.1 = (bf16[1,640,768]{2,1,0:T(8,128)(2,1)S(1)}, bf16[1,640,768]{2,1,0:T(8,128)(2,1)}, u32[]{:S(2)}) copy-start(bf16[1,640,768]{2,1,0:T(8,128)(2,1)} %param.15) | copy-start | bytes 2949124
  19.8 9.2 %copy-start.3 = (bf16[1,640,768]{2,1,0:T(8,128)(2,1)S(1)}, bf16[1,640,768]{2,1,0:T(8,128)(2,1)}, u32[]{:S(2)}) copy-start(bf16[1,640,768]{2,1,0:T(8,128)(2,1)} %param.16) | copy-start | bytes 2949124
  19.8 9.2 %copy-start.5 = (bf16[1,768,640]{2,1,0:T(8,128)(2,1)S(1)}, bf16[1,768,640]{2,1,0:T(8,128)(2,1)}, u32[]{:S(2)}) copy-start(bf16[1,768,640]{2,1,0:T(8,128)(2,1)} %param.17) | copy-start | bytes 2949124
  30.5 9.6 %all-to-all-start.1 = ((bf16[4,24,640]{2,1,0:T(8,128)(2,1)}), bf16[4,24,640]{2,1,0:T(8,128)(2,1)S(1)}, u32[]{:S(2)}, u32[]{:S(2)}) async-start(bf16[4,24,640]{2,1,0:T(8,128)(2,1)} %bitcast.8), calls=%async_computation.1 | async-start | bytes 245760 | tf_op jit(solution)/shard_map/all_to_all | solution.py:285

commit v2 on v1

--- a/solution.py
+++ b/solution.py
@@ -30,9 +30,26 @@
     return pltpu.CompilerParams(vmem_limit_bytes=VMEM_LIMIT)
 
 
-def dispatch_kernel(
-    experts, hosts, slots, block, plan_ref, caps_ref, ids_ref, gates_ref, tok_ref, grad_ref, send_ref, pick_ref
-):
+def dispatch_kernel(experts, hosts, slots, block, pieces, *refs):
+    plan_hbm, caps_hbm, ids_hbm, gates_hbm, tok_hbm, grad_hbm = refs[:6]
+    send_refs, pick_ref = refs[6 : 6 + pieces], refs[6 + pieces]
+    plan_ref, caps_ref, ids_ref, gates_ref, tok_ref, grad_ref, sems = refs[7 + pieces :]
+    copies = [
+        pltpu.make_async_copy(source, target, sems.at[i])
+        for i, (source, target) in enumerate(
+            (
+                (ids_hbm, ids_ref),
+                (plan_hbm, plan_ref),
+                (caps_hbm, caps_ref),
+                (gates_hbm, gates_ref),
+                (tok_hbm, tok_ref),
+                (grad_hbm, grad_ref),
+            )
+        )
+    ]
+    for copy in copies:
+        copy.start()
+    me = lax.axis_index("expert")
     choose, count = ids_ref.shape
     row = lax.broadcasted_iota(I32, (block, count), 0)
     col = lax.broadcasted_iota(I32, (block, count), 1)
@@ -44,8 +61,16 @@
     replica = jnp.where(is_spare, 1 + lax.div(spare_slot, SPARE), 0)
     position = jnp.where(is_spare, lax.rem(spare_slot, SPARE), slot)
     token_slot = lax.rem(col, hosts)
+    earlier = (
+        lax.broadcasted_iota(I32, (count, count), 0) < lax.broadcasted_iota(I32, (count, count), 1)
+    )
+    earlier = earlier.astype(F32).astype(BF16)
+    cots = jnp.concatenate([is_cot.astype(F32)] * experts, axis=0)
+    for copy in copies[:4]:
+        copy.wait()
     members, weights, limits = [], [], []
-    for expert in range(experts):
+    for index in range(experts):
+        expert = index if pieces == 1 else lax.rem(me + index, experts)
         hot = (plan_ref[0, 0] == expert) | (plan_ref[1, 0] == expert)
         wanted = token_slot * hot.astype(I32)
         here = jnp.zeros((1, count), F32)
@@ -62,47 +87,88 @@
     member = jnp.concatenate(members, axis=0)
     weight = jnp.concatenate(weights, axis=0)
     limit = jnp.concatenate(limits, axis=0).astype(F32)
-    cots = jnp.concatenate([is_cot.astype(F32)] * experts, axis=0)
-    earlier = (
-        lax.broadcasted_iota(I32, (count, count), 0) < lax.broadcasted_iota(I32, (count, count), 1)
-    )
-    before = matmul(member.astype(BF16), earlier.astype(F32).astype(BF16), 1, 0)
+    before = matmul(member.astype(BF16), earlier, 1, 0)
     taken = jnp.where(before == limit, member, 0.0)
     pick_cot = taken * cots
     pick_tok = taken - pick_cot
     gate = jnp.sum(taken * weight, axis=1, keepdims=True)
-    pick_cot = pick_cot.astype(BF16)
-    rows = matmul(pick_tok.astype(BF16), tok_ref[...], 1, 0)
-    cotangents = gate * matmul(pick_cot, grad_ref[...], 1, 0)
-    send_ref[...] = (rows + cotangents).astype(BF16)
     scaled = pick_tok * weight
     high = scaled.astype(BF16)
+    pick_cot = pick_cot.astype(BF16)
     pick_ref[0] = high
     pick_ref[1] = (scaled - high.astype(F32)).astype(BF16)
     pick_ref[2] = pick_cot
-
-
-def dispatch(plan, caps, ids, gates, tokens, grads, experts, slots, block):
+    for copy in copies[4:]:
+        copy.wait()
+    rows = matmul(pick_tok.astype(BF16), tok_ref[...], 1, 0)
+    cotangents = gate * matmul(pick_cot, grad_ref[...], 1, 0)
+    send = (rows + cotangents).astype(BF16)
+    size = send.shape[0] // pieces
+    for i, send_ref in enumerate(send_refs):
+        send_ref[...] = send[i * size : (i + 1) * size]
+
+
+def dispatch(plan, caps, ids, gates, tokens, grads, experts, slots, block, pieces):
     count, feature = tokens.shape
-    smem = pl.BlockSpec(memory_space=pltpu.SMEM)
+    vmem = pl.BlockSpec(memory_space=pltpu.VMEM)
+    size = experts * block // pieces
+    outs = pl.pallas_call(
+        functools.partial(dispatch_kernel, experts, plan.shape[1], slots, block, pieces),
+        out_shape=(jax.ShapeDtypeStruct((size, feature), BF16),) * pieces
+        + (jax.ShapeDtypeStruct((3, experts * block, count), BF16),),
+        in_specs=[pl.BlockSpec(memory_space=pltpu.HBM)] * 6,
+        out_specs=(vmem,) * (pieces + 1),
+        scratch_shapes=[
+            pltpu.SMEM(plan.shape, I32),
+            pltpu.SMEM(caps.shape, I32),
+            pltpu.VMEM(ids.shape, I32),
+            pltpu.VMEM(gates.shape, F32),
+            pltpu.VMEM(tokens.shape, BF16),
+            pltpu.VMEM(grads.shape, BF16),
+            pltpu.SemaphoreType.DMA((6,)),
+        ],
+        compiler_params=params(),
+        name="dispatch",
+    )(plan, caps, ids, gates, tokens, grads)
+    return outs[:pieces], outs[pieces]
+
+
+def load_kernel(gate_hbm, up_hbm, down_hbm, pick_ref, gate_ref, up_ref, down_ref, sems):
+    copies = [
+        pltpu.make_async_copy(source, target, sems.at[i])
+        for i, (source, target) in enumerate(
+            ((gate_hbm, gate_ref), (up_hbm, up_ref), (down_hbm, down_ref))
+        )
+    ]
+    for copy in copies:
+        copy.start()
+    for copy in copies:
+        copy.wait()
+
+
+def load_weights(gate, up, down, pick):
+    hbm = pl.BlockSpec(memory_space=pltpu.HBM)
     vmem = pl.BlockSpec(memory_space=pltpu.VMEM)
     return pl.pallas_call(
-        functools.partial(dispatch_kernel, experts, plan.shape[1], slots, block),
-        out_shape=(
-            jax.ShapeDtypeStruct((experts * block, feature), BF16),
-            jax.ShapeDtypeStruct((3, experts * block, count), BF16),
-        ),
-        in_specs=[smem, smem, vmem, vmem, vmem, vmem],
-        out_specs=(vmem, vmem),
-        compiler_params=params(),
-        name="dispatch",
-    )(plan, caps, ids, gates, tokens, grads)
-
-
-def partial_kernel(
-    group, slots, block, recv_ref, gate_ref, up_ref, down_ref, rows_ref, cots_ref, part_ref, wide, flat
-):
-    wide[...] = recv_ref[...].astype(F32)
+        load_kernel,
+        out_shape=tuple(pltpu.VMEM(w.shape, BF16) for w in (gate, up, down)),
+        in_specs=[hbm, hbm, hbm, pl.BlockSpec(memory_space=pl.ANY)],
+        out_specs=(vmem, vmem, vmem),
+        scratch_shapes=[pltpu.SemaphoreType.DMA((3,))],
+        compiler_params=params(),
+        cost_estimate=pl.CostEstimate(
+            flops=0, bytes_accessed=2 * 3 * gate.size * 2, transcendentals=0
+        ),
+        name="load_weights",
+    )(gate, up, down, pick)
+
+
+def partial_kernel(group, slots, block, pieces, *refs):
+    recv_refs = refs[:pieces]
+    gate_ref, up_ref, down_ref, rows_ref, cots_ref, part_ref, wide, flat = refs[pieces:]
+    size = group * block // pieces
+    for i, recv_ref in enumerate(recv_refs):
+        wide[i * size : (i + 1) * size, :] = recv_ref[...].astype(F32)
     for s in range(group):
         flat[0, s * slots : (s + 1) * slots, :] = wide[s * block : s * block + slots, :]
         flat[1, s * slots : (s + 1) * slots, :] = wide[s * block + slots : s * block + 2 * slots, :]
@@ -116,7 +182,8 @@
     part_ref[:, 2 * hidden :] = matmul(cots, down_ref[...], 1, 1).astype(BF16)
 
 
-def partials(recv, gate, up, down, experts, slots, block):
+def partials(recvs, gate, up, down, experts, slots, block):
+    pieces = len(recvs)
     feature, hidden = gate.shape
     tile, big = GROUP * slots, GROUP * block
     total = experts * slots
@@ -128,15 +195,15 @@
         return pl.BlockSpec((rows, width), lambda i: (i, 0))
 
     return pl.pallas_call(
-        functools.partial(partial_kernel, GROUP, slots, block),
+        functools.partial(partial_kernel, GROUP, slots, block, pieces),
         grid=(experts // GROUP,),
         out_shape=(
             jax.ShapeDtypeStruct((total, feature), BF16),
             jax.ShapeDtypeStruct((total, feature), BF16),
             jax.ShapeDtypeStruct((total, 3 * hidden), BF16),
         ),
-        in_specs=[
-            by_rows(big, feature),
+        in_specs=[by_rows(big // pieces, feature)] * pieces
+        + [
             whole((feature, hidden)),
             whole((feature, hidden)),
             whole((hidden, feature)),
@@ -145,12 +212,13 @@
         scratch_shapes=[pltpu.VMEM((big, feature), F32), pltpu.VMEM((2, tile, feature), F32)],
         compiler_params=params(),
         name="partials",
-    )(recv, gate, up, down)
-
-
-def middle_kernel(
-    group, slots, block, parts_ref, gate_ref, up_ref, down_ref, back_ref, hidden_ref, gg_ref, ug_ref, flat, wide
-):
+    )(*recvs, gate, up, down)
+
+
+def middle_kernel(group, slots, block, pieces, *refs):
+    parts_ref, gate_ref, up_ref, down_ref = refs[:4]
+    back_refs = refs[4 : 4 + pieces]
+    hidden_ref, gg_ref, ug_ref, flat, wide = refs[4 + pieces :]
     width = gate_ref.shape[1]
     total = parts_ref[0].astype(F32)
     for j in range(1, parts_ref.shape[0]):
@@ -171,10 +239,12 @@
     for s in range(group):
         wide[s * block : s * block + slots, :] = flat[0, s * slots : (s + 1) * slots, :]
         wide[s * block + slots : s * block + 2 * slots, :] = flat[1, s * slots : (s + 1) * slots, :]
-    back_ref[...] = wide[...].astype(BF16)
-
-
-def middle(parts, gate, up, down, experts, slots, block):
+    size = group * block // pieces
+    for i, back_ref in enumerate(back_refs):
+        back_ref[...] = wide[i * size : (i + 1) * size, :].astype(BF16)
+
+
+def middle(parts, gate, up, down, experts, slots, block, pieces):
     feature, hidden = gate.shape
     tile, big = GROUP * slots, GROUP * block
     total = experts * slots
@@ -185,31 +255,23 @@
     def by_rows(rows, width):
         return pl.BlockSpec((rows, width), lambda i: (i, 0))
 
-    return pl.pallas_call(
-        functools.partial(middle_kernel, GROUP, slots, block),
+    outs = pl.pallas_call(
+        functools.partial(middle_kernel, GROUP, slots, block, pieces),
         grid=(experts // GROUP,),
-        out_shape=(
-            jax.ShapeDtypeStruct((experts * block, feature), BF16),
-            jax.ShapeDtypeStruct((total, hidden), BF16),
-            jax.ShapeDtypeStruct((total, hidden), BF16),
-            jax.ShapeDtypeStruct((total, hidden), BF16),
-        ),
+        out_shape=(jax.ShapeDtypeStruct((experts * block // pieces, feature), BF16),) * pieces
+        + (jax.ShapeDtypeStruct((total, hidden), BF16),) * 3,
         in_specs=[
             pl.BlockSpec((parts.shape[0], tile, 3 * hidden), lambda i: (0, i, 0)),
             whole((feature, hidden)),
             whole((feature, hidden)),
             whole((hidden, feature)),
         ],
-        out_specs=(
-            by_rows(big, feature),
-            by_rows(tile, hidden),
-            by_rows(tile, hidden),
-            by_rows(tile, hidden),
-        ),
+        out_specs=(by_rows(big // pieces, feature),) * pieces + (by_rows(tile, hidden),) * 3,
         scratch_shapes=[pltpu.VMEM((2, tile, feature), F32), pltpu.VMEM((big, feature), F32)],
         compiler_params=params(),
         name="middle",
     )(parts, gate, up, down)
+    return outs[:pieces], *outs[pieces:]
 
 
 def grads_kernel(rows_ref, cots_ref, hidden_ref, gg_ref, ug_ref, gate_ref, up_ref, down_ref):
@@ -259,30 +321,41 @@
     )(rows, cots, hidden, gg, ug)
 
 
-def combine_kernel(back_ref, pick_ref, mixed_ref, token_ref):
-    back = back_ref[...]
+def combine_kernel(pieces, *refs):
+    back_refs = refs[:pieces]
+    pick_ref, mixed_ref, token_ref = refs[pieces:]
+    back = jnp.concatenate([back_ref[...] for back_ref in back_refs], axis=0)
     mixed = matmul(pick_ref[0], back, 0, 0) + matmul(pick_ref[1], back, 0, 0)
     mixed_ref[...] = mixed.astype(BF16)
     token_ref[...] = matmul(pick_ref[2], back, 0, 0).astype(BF16)
 
 
-def combine(back, pick):
-    feature, count = back.shape[1], pick.shape[2]
+def combine(backs, pick):
+    feature, count = backs[0].shape[1], pick.shape[2]
     vmem = pl.BlockSpec(memory_space=pltpu.VMEM)
     shape = jax.ShapeDtypeStruct((count, feature), BF16)
     return pl.pallas_call(
-        combine_kernel,
+        functools.partial(combine_kernel, len(backs)),
         out_shape=(shape, shape),
-        in_specs=[vmem, vmem],
+        in_specs=[vmem] * (len(backs) + 1),
         out_specs=(vmem, vmem),
         compiler_params=params(),
         name="combine",
-    )(back, pick)
-
-
-def over_experts(array, experts):
-    blocks = array.reshape(experts, -1, array.shape[1])
-    return lax.all_to_all(blocks, "expert", split_axis=0, concat_axis=0, tiled=True).reshape(array.shape)
+    )(*backs, pick)
+
+
+def over_experts(arrays, experts, sign):
+    if len(arrays) == 1:
+        array = arrays[0]
+        blocks = array.reshape(experts, -1, array.shape[1])
+        moved = lax.all_to_all(blocks, "expert", split_axis=0, concat_axis=0, tiled=True)
+        return [moved.reshape(array.shape)]
+    return [arrays[0]] + [
+        lax.ppermute(
+            arrays[shift], "expert", [(i, (i + sign * shift) % experts) for i in range(experts)]
+        )
+        for shift in range(1, experts)
+    ]
 
 
 def shards(
@@ -301,15 +374,26 @@
     assert tokens.shape[0] % hosts == 0 and experts % GROUP == 0
     slots = OWN + SPARE * (hosts - 1)
     block = -(-2 * slots // 8) * 8
+    pieces = experts if experts <= GROUP else 1
     gate, up, down = gate_weight[0], up_weight[0], down_weight[0]
-    send, pick = dispatch(
-        replica_plan, cap_blocks, expert_ids.T, gate_weights.T, tokens, out_grad, experts, slots, block
+    sends, pick = dispatch(
+        replica_plan,
+        cap_blocks,
+        expert_ids.T,
+        gate_weights.T,
+        tokens,
+        out_grad,
+        experts,
+        slots,
+        block,
+        pieces,
     )
-    recv = over_experts(send, experts)
-    rows, cots, part = partials(recv, gate, up, down, experts, slots, block)
+    recvs = over_experts(sends, experts, 1)
+    gate, up, down = load_weights(gate, up, down, pick)
+    rows, cots, part = partials(recvs, gate, up, down, experts, slots, block)
     parts = lax.all_gather(part, "dp")
-    back, hidden, gg, ug = middle(parts, gate, up, down, experts, slots, block)
-    returned = over_experts(back, experts)
+    backs, hidden, gg, ug = middle(parts, gate, up, down, experts, slots, block, pieces)
+    returned = over_experts(backs, experts, -1)
     gate_grad, up_grad, down_grad = weight_grads(rows, cots, hidden, gg, ug)
     mixed, token_grad = combine(returned, pick)
     return mixed, token_grad, gate_grad[None], up_grad[None], down_grad[None]

time: 41.6 us -> 35 us (0.84)
  blocking collectives: 20.6 us -> 8.33 us
  starting transfers between devices: 3.32 us -> 9.43 us
  waiting for transfers between devices: 3.6 us -> 2.78 us
  Pallas kernels: 6.84 us -> 7.28 us
    all_to_all x1 -> x0, blocking collectives: 12.1 us -> none  [over_experts(): lax.all_to_all(blocks, 'expert', split_axis=0, concat_axis=0, tiled=True)]
    ppermute x0 -> x6, starting transfers between devices: none -> 9.43 us  [over_experts(): lax.ppermute(arrays[shift], 'expert', [(i, (i + sign * shift) % experts)...]
    all_to_all x1 -> x0, waiting for transfers between devices: 3.6 us -> none  [over_experts(): lax.all_to_all(blocks, 'expert', split_axis=0, concat_axis=0, tiled=True)]
    all_to_all x1 -> x0, starting transfers between devices: 3.32 us -> none  [over_experts(): lax.all_to_all(blocks, 'expert', split_axis=0, concat_axis=0, tiled=True)]
    ppermute x0 -> x6, waiting for transfers between devices: none -> 2.78 us  [over_experts(): lax.ppermute(arrays[shift], 'expert', [(i, (i + sign * shift) % experts)...]
    pallas_call x3 -> x4, Pallas kernels: 3.25 us -> 3.53 us  [the longest x1 1.01 us: combine(): pl.pallas_call(functools.partial(combine_kernel, len(backs)), out_shape=(...]
    unnamed x24 -> x18, local copies, waits for them, and re-layouts: 6.13 us -> 6.12 us
  transfers between devices with their start and end apart: 1 -> 6, of which waited for: 1 -> 2; matrix products, arithmetic and copies ran while one was open for 0% -> 0% of each run, Pallas kernels for 7% -> 10%
where the time goes in v2:
time: 35 us; the launch traced here: 34.7 us
  starting transfers between devices  9.43 us (27%)
  blocking collectives  8.33 us (24%)
  Pallas kernels  7.28 us (21%)
  local copies, waits for them, and re-layouts  6.12 us (17%)
  waiting for transfers between devices  2.78 us (8%)
  between operations  0.73 us (2%)
    ppermute x6, starting transfers between devices, over_experts(): lax.ppermute(arrays[shift], 'expert', [(i, (i + sign * shift) % experts)...  9.43 us
    all_gather x1, blocking collectives, shards(): parts = lax.all_gather(part, 'dp')  8.33 us
    unnamed x18, local copies, waits for them, and re-layouts  6.12 us
    ppermute x6, waiting for transfers between devices, over_experts(): lax.ppermute(arrays[shift], 'expert', [(i, (i + sign * shift) % experts)...  2.78 us
    pallas_call x1, Pallas kernels, weight_grads(): pl.pallas_call(grads_kernel, grid=(width // tile,), out_shape=(jax.ShapeD...  2.69 us
    pallas_call x1, Pallas kernels, dispatch(): pl.pallas_call(functools.partial(dispatch_kernel, experts, plan.shape[1],...  1.06 us
    pallas_call x1, Pallas kernels, combine(): pl.pallas_call(functools.partial(combine_kernel, len(backs)), out_shape=(...  1.01 us
    pallas_call x1, Pallas kernels, load_weights(): pl.pallas_call(load_kernel, out_shape=tuple((pltpu.VMEM(w.shape, BF16) fo...  0.95 us
  transfers between devices with their start and end apart: 6, of which 2 were waited for; matrix products, arithmetic and copies ran while one was open for 0% of the time, Pallas kernels for 10%

profile of v2, /device:TPU:0, one launch (start us, length us, event | category | flops | bytes accessed | tf_op | source)
XLA Modules:
  0.0 34.7 jit_solution(5789699543346505134)
XLA Ops:
  0.6 0.0 copy-start.6
  0.6 0.0 copy-start.7
  0.7 0.0 copy-start.5
  0.7 0.0 copy-start.8
  0.7 0.6 %copy-done.6 = s32[128,2]{0,1:T(2,128)S(1)} copy-done((s32[128,2]{0,1:T(2,128)S(1)}, s32[128,2]{0,1:T(2,128)}, u32[]{:S(2)}) %copy-start.6) | copy-done | bytes 1048
  1.3 0.0 copy-done.7
  1.3 0.0 copy-done.5
  1.3 0.0 copy-done.8
  1.3 0.0 copy-start.3
  1.3 0.9 %copy-done.3 = bf16[128,640]{1,0:T(8,128)(2,1)S(1)} copy-done((bf16[128,640]{1,0:T(8,128)(2,1)S(1)}, bf16[128,640]{1,0:T(8,128)(2,1)}, u32[]{:S(2)}) %copy-start.3) | copy-done | bytes 163864
  2.3 0.0 copy-start.4
  2.3 0.9 %copy-done.4 = bf16[128,640]{1,0:T(8,128)(2,1)S(1)} copy-done((bf16[128,640]{1,0:T(8,128)(2,1)S(1)}, bf16[128,640]{1,0:T(8,128)(2,1)}, u32[]{:S(2)}) %copy-start.4) | copy-done | bytes 163864
  3.2 1.1 %dispatch.1 = (bf16[24,640]{1,0:T(8,128)(2,1)S(1)}, bf16[24,640]{1,0:T(8,128)(2,1)S(1)}, bf16[24,640]{1,0:T(8,128)(2,1)S(1)}, bf16[24,640]{1,0:T(8,128)(2,1)S(1)}, bf16[3,96,128]{2,1,0:T(8,128)(2,1)S(1)}) custom-call(s32[2,2]{1,0:T(2,128)S(1)} %copy-done.5, s32[4]{0:T(128)S(1)} %copy-done.8, s32[2,128]{1,0:T(2,128)S(1)} %bitcast.13, f32[2,128]{1,0:T(2,128)S(1)} %bitcast.14, ...), custom_call_target="tpu_custom_call" | custom-call | tf_op jit(solution)/shard_map/dispatch/pallas_call | solution.py:115
  4.3 3.1 %collective-permute-start = (bf16[24,640]{1,0:T(8,128)(2,1)S(1)}, bf16[24,640]{1,0:T(8,128)(2,1)S(1)}, u32[]{:S(2)}, u32[]{:S(2)}) collective-permute-start(bf16[24,640]{1,0:T(8,128)(2,1)S(1)} %get-tuple-element.29), channel_id=1, source_target_pairs={{0,4},{4,8},{8,12},{12,0},{1,5},{5,9},{9,13},{13,1},{2,6},{6,10},{... | collective-permute-start | bytes 92168 | tf_op jit(solution)/shard_map/ppermute | solution.py:354
  7.3 2.6 %collective-permute-start.1 = (bf16[24,640]{1,0:T(8,128)(2,1)S(1)}, bf16[24,640]{1,0:T(8,128)(2,1)S(1)}, u32[]{:S(2)}, u32[]{:S(2)}) collective-permute-start(bf16[24,640]{1,0:T(8,128)(2,1)S(1)} %get-tuple-element.30), channel_id=1, source_target_pairs={{0,8},{4,12},{8,0},{12,4},{1,9},{5,13},{9,1},{13,5},{2,10},{6,14},... | collective-permute-start | bytes 92168 | tf_op jit(solution)/shard_map/ppermute | solution.py:354
  9.9 1.3 %collective-permute-start.2 = (bf16[24,640]{1,0:T(8,128)(2,1)S(1)}, bf16[24,640]{1,0:T(8,128)(2,1)S(1)}, u32[]{:S(2)}, u32[]{:S(2)}) collective-permute-start(bf16[24,640]{1,0:T(8,128)(2,1)S(1)} %get-tuple-element.31), channel_id=1, source_target_pairs={{0,12},{4,0},{8,4},{12,8},{1,13},{5,1},{9,5},{13,9},{2,14},{6,2},{... | collective-permute-start | bytes 92168 | tf_op jit(solution)/shard_map/ppermute | solution.py:354
  11.3 0.0 copy-start
  11.3 1.2 %copy-done = bf16[1,640,768]{2,1,0:T(8,128)(2,1)S(1)} copy-done((bf16[1,640,768]{2,1,0:T(8,128)(2,1)S(1)}, bf16[1,640,768]{2,1,0:T(8,128)(2,1)}, u32[]{:S(2)}) %copy-start) | copy-done | bytes 983064
  12.5 0.0 copy-start.1
  12.5 1.2 %copy-done.1 = bf16[1,640,768]{2,1,0:T(8,128)(2,1)S(1)} copy-done((bf16[1,640,768]{2,1,0:T(8,128)(2,1)S(1)}, bf16[1,640,768]{2,1,0:T(8,128)(2,1)}, u32[]{:S(2)}) %copy-start.1) | copy-done | bytes 983064
  13.7 0.0 copy-start.2
  13.7 1.2 %copy-done.2 = bf16[1,768,640]{2,1,0:T(8,128)(2,1)S(1)} copy-done((bf16[1,768,640]{2,1,0:T(8,128)(2,1)S(1)}, bf16[1,768,640]{2,1,0:T(8,128)(2,1)}, u32[]{:S(2)}) %copy-start.2) | copy-done | bytes 983064
  14.9 0.9 %load_weights.1 = (bf16[640,768]{1,0:T(8,128)(2,1)S(1)}, bf16[640,768]{1,0:T(8,128)(2,1)S(1)}, bf16[768,640]{1,0:T(8,128)(2,1)S(1)}) custom-call(bf16[640,768]{1,0:T(8,128)(2,1)S(1)} %bitcast.10, bf16[640,768]{1,0:T(8,128)(2,1)S(1)} %bitcast.11, bf16[768,640]{1,0:T(8,128)(2,1)S(1)} %bitcast.12, bf16[3,96,128]{2,1,0:T(8,128)(2,1)S(1)} %get-tuple-element.32.pick_ref.refs_4_), custom_call_target="tpu_custom_call" | custom-call | bytes 5898240 | tf_op jit(solution)/shard_map/load_weights/pallas_call | solution.py:152
  15.8 0.0 collective-permute-done.refs_1_
  15.8 0.0 collective-permute-done.1.refs_2_
  15.8 0.0 collective-permute-done.2.refs_3_
  15.9 0.7 %partials.1 = (bf16[40,640]{1,0:T(8,128)(2,1)S(1)}, bf16[40,640]{1,0:T(8,128)(2,1)S(1)}, bf16[40,2304]{1,0:T(8,128)(2,1)S(1)}) custom-call(bf16[24,640]{1,0:T(8,128)(2,1)S(1)} %get-tuple-element.28.refs_0_, bf16[24,640]{1,0:T(8,128)(2,1)S(1)} %collective-permute-done.refs_1_, bf16[24,640]{1,0:T(8,128)(2,1)S(1)} %collective-permute-done.1.refs_2_, ...), custom_call_target="tpu_custom_call" | custom-call | tf_op jit(solution)/shard_map/partials/pallas_call | solution.py:197
  16.6 8.3 %all-gather = bf16[160,2304]{1,0:T(8,128)(2,1)S(1)} all-gather(bf16[40,2304]{1,0:T(8,128)(2,1)S(1)} %get-tuple-element.36), channel_id=2, replica_groups=mesh['groups'=2,'expert'=4,'dp'=4] {'dp'}, dimensions={0}, use_global_device_ids=true | all-gather | bytes 921600 | tf_op jit(solution)/shard_map/all_gather | solution.py:394
  24.9 0.9 %middle.1 = (bf16[24,640]{1,0:T(8,128)(2,1)S(1)}, bf16[24,640]{1,0:T(8,128)(2,1)S(1)}, bf16[24,640]{1,0:T(8,128)(2,1)S(1)}, bf16[24,640]{1,0:T(8,128)(2,1)S(1)},...) custom-call(bf16[4,40,2304]{2,1,0:T(8,128)(2,1)S(1)} %bitcast.9, ...), custom_call_target="tpu_custom_call" | custom-call | tf_op jit(solution)/shard_map/middle/pallas_call | solution.py:258
  25.8 1.2 %collective-permute-start.3 = (bf16[24,640]{1,0:T(8,128)(2,1)S(1)}, bf16[24,640]{1,0:T(8,128)(2,1)S(1)}, u32[]{:S(2)}, u32[]{:S(2)}) collective-permute-start(bf16[24,640]{1,0:T(8,128)(2,1)S(1)} %get-tuple-element.38), channel_id=1, source_target_pairs={{0,12},{4,0},{8,4},{12,8},{1,13},{5,1},{9,5},{13,9},{2,14},{6,2},{... | collective-permute-start | bytes 92168 | tf_op jit(solution)/shard_map/ppermute | solution.py:354
  26.9 1.0 %collective-permute-start.4 = (bf16[24,640]{1,0:T(8,128)(2,1)S(1)}, bf16[24,640]{1,0:T(8,128)(2,1)S(1)}, u32[]{:S(2)}, u32[]{:S(2)}) collective-permute-start(bf16[24,640]{1,0:T(8,128)(2,1)S(1)} %get-tuple-element.39), channel_id=1, source_target_pairs={{0,8},{4,12},{8,0},{12,4},{1,9},{5,13},{9,1},{13,5},{2,10},{6,14},... | collective-permute-start | bytes 92168 | tf_op jit(solution)/shard_map/ppermute | solution.py:354
  28.0 0.2 collective-permute-start.5
  28.2 2.7 %weight_grads.1 = (bf16[640,768]{1,0:T(8,128)(2,1)}, bf16[640,768]{1,0:T(8,128)(2,1)}, bf16[768,640]{1,0:T(8,128)(2,1)}) custom-call(bf16[40,640]{1,0:T(8,128)(2,1)S(1)} %get-tuple-element.43.rows_ref, bf16[40,640]{1,0:T(8,128)(2,1)S(1)} %get-tuple-element.44.cots_ref, bf16[40,768]{1,0:T(8,128)(2,1)S(1)} %get-tuple-element.45.hidden_ref, ...), custom_call_target="tpu_custom_call" | custom-call | flops 117964800 | bytes 2949120 | tf_op jit(solution)/shard_map/weight_grads/pallas_call | solution.py:294
  30.9 0.0 collective-permute-done.3.refs_1_
  30.9 0.8 %collective-permute-done.4.refs_2_ = bf16[24,640]{1,0:T(8,128)(2,1)S(1)} collective-permute-done((bf16[24,640]{1,0:T(8,128)(2,1)S(1)}, bf16[24,640]{1,0:T(8,128)(2,1)S(1)}, u32[]{:S(2)}, u32[]{:S(2)}) %collective-permute-start.4) | collective-permute-done | bytes 30752 | tf_op jit(solution)/shard_map/ppermute | solution.py:354
  31.7 1.9 %collective-permute-done.5.refs_3_ = bf16[24,640]{1,0:T(8,128)(2,1)S(1)} collective-permute-done((bf16[24,640]{1,0:T(8,128)(2,1)S(1)}, bf16[24,640]{1,0:T(8,128)(2,1)S(1)}, u32[]{:S(2)}, u32[]{:S(2)}) %collective-permute-start.5) | collective-permute-done | bytes 30752 | tf_op jit(solution)/shard_map/ppermute | solution.py:354
  33.7 1.0 %combine.1 = (bf16[128,640]{1,0:T(8,128)(2,1)}, bf16[128,640]{1,0:T(8,128)(2,1)}) custom-call(bf16[24,640]{1,0:T(8,128)(2,1)S(1)} %get-tuple-element.37.refs_0_, bf16[24,640]{1,0:T(8,128)(2,1)S(1)} %collective-permute-done.3.refs_1_, bf16[24,640]{1,0:T(8,128)(2,1)S(1)} %collective-permute-done.4.refs_2_, bf16[24,640]{1,0:T(8,128)(2,1)S(1)} %collective-permute-done.5.refs_3_, ...), custom_call_target="tpu_custom_call" | custom-call | tf_op jit(solution)/shard_map/combine/pallas_call | solution.py:337
Async XLA Ops:
  0.6 0.7 %copy-start.6 = (s32[128,2]{0,1:T(2,128)S(1)}, s32[128,2]{0,1:T(2,128)}, u32[]{:S(2)}) copy-start(s32[128,2]{0,1:T(2,128)} %param.12) | copy-start | bytes 3076
  0.6 0.7 %copy-start.7 = (f32[128,2]{0,1:T(2,128)S(1)}, f32[128,2]{0,1:T(2,128)}, u32[]{:S(2)}) copy-start(f32[128,2]{0,1:T(2,128)} %param.11) | copy-start | bytes 3076
  0.7 0.7 %copy-start.5 = (s32[2,2]{1,0:T(2,128)S(1)}, s32[2,2]{1,0:T(2,128)}, u32[]{:S(2)}) copy-start(s32[2,2]{1,0:T(2,128)} %refs_0_.1) | copy-start | bytes 52
  0.7 0.7 %copy-start.8 = (s32[4]{0:T(128)S(1)}, s32[4]{0:T(128)}, u32[]{:S(2)}) copy-start(s32[4]{0:T(128)} %refs_1_.1) | copy-start | bytes 52
  1.3 0.9 %copy-start.3 = (bf16[128,640]{1,0:T(8,128)(2,1)S(1)}, bf16[128,640]{1,0:T(8,128)(2,1)}, u32[]{:S(2)}) copy-start(bf16[128,640]{1,0:T(8,128)(2,1)} %refs_4_.1) | copy-start | bytes 491524
  2.3 0.9 %copy-start.4 = (bf16[128,640]{1,0:T(8,128)(2,1)S(1)}, bf16[128,640]{1,0:T(8,128)(2,1)}, u32[]{:S(2)}) copy-start(bf16[128,640]{1,0:T(8,128)(2,1)} %refs_5_.1) | copy-start | bytes 491524
  4.3 11.6 %collective-permute-start = (bf16[24,640]{1,0:T(8,128)(2,1)S(1)}, bf16[24,640]{1,0:T(8,128)(2,1)S(1)}, u32[]{:S(2)}, u32[]{:S(2)}) collective-permute-start(bf16[24,640]{1,0:T(8,128)(2,1)S(1)} %get-tuple-element.29), channel_id=1, source_target_pairs={{0,4},{4,8},{8,12},{12,0},{1,5},{5,9},{9,13},{13,1},{2,6},{6,10},{... | collective-permute-start | bytes 92168 | tf_op jit(solution)/shard_map/ppermute | solution.py:354
  7.3 8.5 %collective-permute-start.1 = (bf16[24,640]{1,0:T(8,128)(2,1)S(1)}, bf16[24,640]{1,0:T(8,128)(2,1)S(1)}, u32[]{:S(2)}, u32[]{:S(2)}) collective-permute-start(bf16[24,640]{1,0:T(8,128)(2,1)S(1)} %get-tuple-element.30), channel_id=1, source_target_pairs={{0,8},{4,12},{8,0},{12,4},{1,9},{5,13},{9,1},{13,5},{2,10},{6,14},... | collective-permute-start | bytes 92168 | tf_op jit(solution)/shard_map/ppermute | solution.py:354
  9.9 5.9 %collective-permute-start.2 = (bf16[24,640]{1,0:T(8,128)(2,1)S(1)}, bf16[24,640]{1,0:T(8,128)(2,1)S(1)}, u32[]{:S(2)}, u32[]{:S(2)}) collective-permute-start(bf16[24,640]{1,0:T(8,128)(2,1)S(1)} %get-tuple-element.31), channel_id=1, source_target_pairs={{0,12},{4,0},{8,4},{12,8},{1,13},{5,1},{9,5},{13,9},{2,14},{6,2},{... | collective-permute-start | bytes 92168 | tf_op jit(solution)/shard_map/ppermute | solution.py:354
  11.3 1.2 %copy-start = (bf16[1,640,768]{2,1,0:T(8,128)(2,1)S(1)}, bf16[1,640,768]{2,1,0:T(8,128)(2,1)}, u32[]{:S(2)}) copy-start(bf16[1,640,768]{2,1,0:T(8,128)(2,1)} %param.15) | copy-start | bytes 2949124
  12.5 1.2 %copy-start.1 = (bf16[1,640,768]{2,1,0:T(8,128)(2,1)S(1)}, bf16[1,640,768]{2,1,0:T(8,128)(2,1)}, u32[]{:S(2)}) copy-start(bf16[1,640,768]{2,1,0:T(8,128)(2,1)} %param.16) | copy-start | bytes 2949124
  13.7 1.2 %copy-start.2 = (bf16[1,768,640]{2,1,0:T(8,128)(2,1)S(1)}, bf16[1,768,640]{2,1,0:T(8,128)(2,1)}, u32[]{:S(2)}) copy-start(bf16[1,768,640]{2,1,0:T(8,128)(2,1)} %param.17) | copy-start | bytes 2949124
  25.8 5.1 %collective-permute-start.3 = (bf16[24,640]{1,0:T(8,128)(2,1)S(1)}, bf16[24,640]{1,0:T(8,128)(2,1)S(1)}, u32[]{:S(2)}, u32[]{:S(2)}) collective-permute-start(bf16[24,640]{1,0:T(8,128)(2,1)S(1)} %get-tuple-element.38), channel_id=1, source_target_pairs={{0,12},{4,0},{8,4},{12,8},{1,13},{5,1},{9,5},{13,9},{2,14},{6,2},{... | collective-permute-start | bytes 92168 | tf_op jit(solution)/shard_map/ppermute | solution.py:354
  26.9 4.8 %collective-permute-start.4 = (bf16[24,640]{1,0:T(8,128)(2,1)S(1)}, bf16[24,640]{1,0:T(8,128)(2,1)S(1)}, u32[]{:S(2)}, u32[]{:S(2)}) collective-permute-start(bf16[24,640]{1,0:T(8,128)(2,1)S(1)} %get-tuple-element.39), channel_id=1, source_target_pairs={{0,8},{4,12},{8,0},{12,4},{1,9},{5,13},{9,1},{13,5},{2,10},{6,14},... | collective-permute-start | bytes 92168 | tf_op jit(solution)/shard_map/ppermute | solution.py:354
  28.0 5.7 %collective-permute-start.5 = (bf16[24,640]{1,0:T(8,128)(2,1)S(1)}, bf16[24,640]{1,0:T(8,128)(2,1)S(1)}, u32[]{:S(2)}, u32[]{:S(2)}) collective-permute-start(bf16[24,640]{1,0:T(8,128)(2,1)S(1)} %get-tuple-element.40), channel_id=1, source_target_pairs={{0,4},{4,8},{8,12},{12,0},{1,5},{5,9},{9,13},{13,1},{2,6},{6,10},{... | collective-permute-start | bytes 92168 | tf_op jit(solution)/shard_map/ppermute | solution.py:354

commit v3 on v2

--- a/solution.py
+++ b/solution.py
@@ -12,7 +12,8 @@
 SPARE = 2
 OWN = BLK * MAXB
 GROUP = 4
-TILE = 256
+CHUNK = 128
+LOADS = 4
 VMEM_LIMIT = 32 * 1024 * 1024
 
 BF16 = jnp.bfloat16
@@ -28,6 +29,14 @@
 
 def params():
     return pltpu.CompilerParams(vmem_limit_bytes=VMEM_LIMIT)
+
+
+def in_hbm(array):
+    return pltpu.with_memory_space_constraint(array, pltpu.HBM)
+
+
+def spans(extent, size):
+    return [(start, min(size, extent - start)) for start in range(0, extent, size)]
 
 
 def dispatch_kernel(experts, hosts, slots, block, pieces, *refs):
@@ -129,17 +138,18 @@
         ],
         compiler_params=params(),
         name="dispatch",
-    )(plan, caps, ids, gates, tokens, grads)
+    )(*(in_hbm(array) for array in (plan, caps, ids, gates, tokens, grads)))
     return outs[:pieces], outs[pieces]
 
 
 def load_kernel(gate_hbm, up_hbm, down_hbm, pick_ref, gate_ref, up_ref, down_ref, sems):
-    copies = [
-        pltpu.make_async_copy(source, target, sems.at[i])
-        for i, (source, target) in enumerate(
-            ((gate_hbm, gate_ref), (up_hbm, up_ref), (down_hbm, down_ref))
-        )
-    ]
+    copies = []
+    for source, target in ((gate_hbm, gate_ref), (up_hbm, up_ref), (down_hbm, down_ref)):
+        for start, size in spans(source.shape[0], source.shape[0] // LOADS):
+            rows = pl.ds(start, size)
+            copies.append(
+                pltpu.make_async_copy(source.at[rows], target.at[rows], sems.at[len(copies)])
+            )
     for copy in copies:
         copy.start()
     for copy in copies:
@@ -149,18 +159,19 @@
 def load_weights(gate, up, down, pick):
     hbm = pl.BlockSpec(memory_space=pltpu.HBM)
     vmem = pl.BlockSpec(memory_space=pltpu.VMEM)
+    assert all(w.shape[0] % (16 * LOADS) == 0 for w in (gate, up, down))
     return pl.pallas_call(
         load_kernel,
         out_shape=tuple(pltpu.VMEM(w.shape, BF16) for w in (gate, up, down)),
         in_specs=[hbm, hbm, hbm, pl.BlockSpec(memory_space=pl.ANY)],
         out_specs=(vmem, vmem, vmem),
-        scratch_shapes=[pltpu.SemaphoreType.DMA((3,))],
+        scratch_shapes=[pltpu.SemaphoreType.DMA((3 * LOADS,))],
         compiler_params=params(),
         cost_estimate=pl.CostEstimate(
             flops=0, bytes_accessed=2 * 3 * gate.size * 2, transcendentals=0
         ),
         name="load_weights",
-    )(gate, up, down, pick)
+    )(in_hbm(gate), in_hbm(up), in_hbm(down), pick)
 
 
 def partial_kernel(group, slots, block, pieces, *refs):
@@ -274,43 +285,39 @@
     return outs[:pieces], *outs[pieces:]
 
 
-def grads_kernel(rows_ref, cots_ref, hidden_ref, gg_ref, ug_ref, gate_ref, up_ref, down_ref):
-    gate_ref[...] = matmul(rows_ref[...], gg_ref[...], 0, 0).astype(BF16)
-    up_ref[...] = matmul(rows_ref[...], ug_ref[...], 0, 0).astype(BF16)
-    down_ref[...] = matmul(hidden_ref[...], cots_ref[...], 0, 0).astype(BF16)
+def grads_kernel(
+    rows_ref, cots_ref, hidden_ref, gg_ref, ug_ref, gate_hbm, up_hbm, down_hbm, gate_ref, up_ref, down_ref, sems
+):
+    copies = []
+    for left_ref, right_ref, out_ref, out_hbm in (
+        (rows_ref, gg_ref, gate_ref, gate_hbm),
+        (rows_ref, ug_ref, up_ref, up_hbm),
+        (hidden_ref, cots_ref, down_ref, down_hbm),
+    ):
+        for start, size in spans(out_ref.shape[0], CHUNK):
+            rows = pl.ds(start, size)
+            out_ref[rows, :] = matmul(left_ref[:, rows], right_ref[...], 0, 0).astype(BF16)
+            copies.append(
+                pltpu.make_async_copy(out_ref.at[rows], out_hbm.at[rows], sems.at[len(copies)])
+            )
+            copies[-1].start()
+    for copy in copies:
+        copy.wait()
 
 
 def weight_grads(rows, cots, hidden, gg, ug):
     total, feature = rows.shape
     width = hidden.shape[1]
-    tile = TILE if width % TILE == 0 else width
-
-    def whole(shape):
-        return pl.BlockSpec(shape, lambda i: (0, 0))
-
-    def by_columns(count):
-        return pl.BlockSpec((count, tile), lambda i: (0, i))
-
+    vmem = pl.BlockSpec(memory_space=pltpu.VMEM)
+    hbm = pl.BlockSpec(memory_space=pltpu.HBM)
+    shapes = ((feature, width), (feature, width), (width, feature))
     return pl.pallas_call(
         grads_kernel,
-        grid=(width // tile,),
-        out_shape=(
-            jax.ShapeDtypeStruct((feature, width), BF16),
-            jax.ShapeDtypeStruct((feature, width), BF16),
-            jax.ShapeDtypeStruct((width, feature), BF16),
-        ),
-        in_specs=[
-            whole((total, feature)),
-            whole((total, feature)),
-            by_columns(total),
-            by_columns(total),
-            by_columns(total),
-        ],
-        out_specs=(
-            by_columns(feature),
-            by_columns(feature),
-            pl.BlockSpec((tile, feature), lambda i: (i, 0)),
-        ),
+        out_shape=tuple(jax.ShapeDtypeStruct(shape, BF16) for shape in shapes),
+        in_specs=[vmem] * 5,
+        out_specs=(hbm,) * 3,
+        scratch_shapes=[pltpu.VMEM(shape, BF16) for shape in shapes]
+        + [pltpu.SemaphoreType.DMA((sum(len(spans(shape[0], CHUNK)) for shape in shapes),))],
         compiler_params=params(),
         cost_estimate=pl.CostEstimate(
             flops=6 * total * feature * width,
@@ -323,22 +330,34 @@
 
 def combine_kernel(pieces, *refs):
     back_refs = refs[:pieces]
-    pick_ref, mixed_ref, token_ref = refs[pieces:]
+    pick_ref, mixed_hbm, token_hbm, mixed_ref, token_ref, sems = refs[pieces:]
     back = jnp.concatenate([back_ref[...] for back_ref in back_refs], axis=0)
+    token_ref[...] = matmul(pick_ref[2], back, 0, 0).astype(BF16)
+    token_copy = pltpu.make_async_copy(token_ref, token_hbm, sems.at[0])
+    token_copy.start()
     mixed = matmul(pick_ref[0], back, 0, 0) + matmul(pick_ref[1], back, 0, 0)
     mixed_ref[...] = mixed.astype(BF16)
-    token_ref[...] = matmul(pick_ref[2], back, 0, 0).astype(BF16)
+    mixed_copy = pltpu.make_async_copy(mixed_ref, mixed_hbm, sems.at[1])
+    mixed_copy.start()
+    token_copy.wait()
+    mixed_copy.wait()
 
 
 def combine(backs, pick):
     feature, count = backs[0].shape[1], pick.shape[2]
     vmem = pl.BlockSpec(memory_space=pltpu.VMEM)
-    shape = jax.ShapeDtypeStruct((count, feature), BF16)
+    hbm = pl.BlockSpec(memory_space=pltpu.HBM)
+    shape = (count, feature)
     return pl.pallas_call(
         functools.partial(combine_kernel, len(backs)),
-        out_shape=(shape, shape),
+        out_shape=(jax.ShapeDtypeStruct(shape, BF16),) * 2,
         in_specs=[vmem] * (len(backs) + 1),
-        out_specs=(vmem, vmem),
+        out_specs=(hbm, hbm),
+        scratch_shapes=[
+            pltpu.VMEM(shape, BF16),
+            pltpu.VMEM(shape, BF16),
+            pltpu.SemaphoreType.DMA((2,)),
+        ],
         compiler_params=params(),
         name="combine",
     )(*backs, pick)

time: 35 us -> 31.5 us (0.900)
  local copies, waits for them, and re-layouts: 6.12 us -> 0 us
  starting transfers between devices: 9.43 us -> 10.9 us
  waiting for transfers between devices: 2.78 us -> 3.57 us
  Pallas kernels: 7.28 us -> 7.87 us
    unnamed x18 -> x0, local copies, waits for them, and re-layouts: 6.12 us -> none
    ppermute x6, starting transfers between devices: 9.43 us -> 10.9 us  [over_experts(): lax.ppermute(arrays[shift], 'expert', [(i, (i + sign * shift) % experts)...]
    pallas_call x1, Pallas kernels: 0.95 us -> 2 us  [load_weights(): pl.pallas_call(load_kernel, out_shape=tuple((pltpu.VMEM(w.shape, BF16) fo...]
    ppermute x6, waiting for transfers between devices: 2.78 us -> 3.57 us  [over_experts(): lax.ppermute(arrays[shift], 'expert', [(i, (i + sign * shift) % experts)...]
    pallas_call x1, Pallas kernels: 2.69 us -> 1.98 us  [weight_grads(): pl.pallas_call(grads_kernel, out_shape=tuple((jax.ShapeDtypeStruct(shape,...]
  transfers between devices with their start and end apart: 6 -> 6, of which waited for: 2 -> 3; matrix products, arithmetic and copies ran while one was open for 0% -> 0% of each run, Pallas kernels for 10% -> 13%
where the time goes in v3:
time: 31.5 us; the launch traced here: 31.3 us
  starting transfers between devices  10.9 us (35%)
  blocking collectives  8.33 us (26%)
  Pallas kernels  7.87 us (25%)
  waiting for transfers between devices  3.57 us (11%)
  between operations  0.7 us (2%)
    ppermute x6, starting transfers between devices, over_experts(): lax.ppermute(arrays[shift], 'expert', [(i, (i + sign * shift) % experts)...  10.9 us
    all_gather x1, blocking collectives, shards(): parts = lax.all_gather(part, 'dp')  8.33 us
    ppermute x6, waiting for transfers between devices, over_experts(): lax.ppermute(arrays[shift], 'expert', [(i, (i + sign * shift) % experts)...  3.57 us
    pallas_call x1, Pallas kernels, load_weights(): pl.pallas_call(load_kernel, out_shape=tuple((pltpu.VMEM(w.shape, BF16) fo...  2 us
    pallas_call x1, Pallas kernels, weight_grads(): pl.pallas_call(grads_kernel, out_shape=tuple((jax.ShapeDtypeStruct(shape,...  1.98 us
    pallas_call x1, Pallas kernels, dispatch(): pl.pallas_call(functools.partial(dispatch_kernel, experts, plan.shape[1],...  1.33 us
    pallas_call x1, Pallas kernels, combine(): pl.pallas_call(functools.partial(combine_kernel, len(backs)), out_shape=(...  1.01 us
    pallas_call x1, Pallas kernels, middle(): pl.pallas_call(functools.partial(middle_kernel, GROUP, slots, block, piec...  0.83 us
  transfers between devices with their start and end apart: 6, of which 3 were waited for; matrix products, arithmetic and copies ran while one was open for 0% of the time, Pallas kernels for 13%

profile of v3, /device:TPU:0, one launch (start us, length us, event | category | flops | bytes accessed | tf_op | source)
XLA Modules:
  0.0 31.3 jit_solution(8431660008059685026)
XLA Ops:
  0.6 1.3 %dispatch.1 = (bf16[24,640]{1,0:T(8,128)(2,1)S(1)}, bf16[24,640]{1,0:T(8,128)(2,1)S(1)}, bf16[24,640]{1,0:T(8,128)(2,1)S(1)}, bf16[24,640]{1,0:T(8,128)(2,1)S(1)}, bf16[3,96,128]{2,1,0:T(8,128)(2,1)S(1)}) custom-call(s32[2,2]{1,0:T(2,128)} %refs_0_.1, s32[4]{0:T(128)} %refs_1_.1, s32[2,128]{1,0:T(2,128)} %bitcast.13, f32[2,128]{1,0:T(2,128)} %bitcast.14, ...), custom_call_target="tpu_custom_call" | custom-call | tf_op jit(solution)/shard_map/dispatch/pallas_call | solution.py:124
  2.0 3.1 %collective-permute-start = (bf16[24,640]{1,0:T(8,128)(2,1)S(1)}, bf16[24,640]{1,0:T(8,128)(2,1)S(1)}, u32[]{:S(2)}, u32[]{:S(2)}) collective-permute-start(bf16[24,640]{1,0:T(8,128)(2,1)S(1)} %get-tuple-element.29), channel_id=1, source_target_pairs={{0,4},{4,8},{8,12},{12,0},{1,5},{5,9},{9,13},{13,1},{2,6},{6,10},{... | collective-permute-start | bytes 92168 | tf_op jit(solution)/shard_map/ppermute | solution.py:373
  5.1 2.6 %collective-permute-start.1 = (bf16[24,640]{1,0:T(8,128)(2,1)S(1)}, bf16[24,640]{1,0:T(8,128)(2,1)S(1)}, u32[]{:S(2)}, u32[]{:S(2)}) collective-permute-start(bf16[24,640]{1,0:T(8,128)(2,1)S(1)} %get-tuple-element.30), channel_id=1, source_target_pairs={{0,8},{4,12},{8,0},{12,4},{1,9},{5,13},{9,1},{13,5},{2,10},{6,14},... | collective-permute-start | bytes 92168 | tf_op jit(solution)/shard_map/ppermute | solution.py:373
  7.6 1.3 %collective-permute-start.2 = (bf16[24,640]{1,0:T(8,128)(2,1)S(1)}, bf16[24,640]{1,0:T(8,128)(2,1)S(1)}, u32[]{:S(2)}, u32[]{:S(2)}) collective-permute-start(bf16[24,640]{1,0:T(8,128)(2,1)S(1)} %get-tuple-element.31), channel_id=1, source_target_pairs={{0,12},{4,0},{8,4},{12,8},{1,13},{5,1},{9,5},{13,9},{2,14},{6,2},{... | collective-permute-start | bytes 92168 | tf_op jit(solution)/shard_map/ppermute | solution.py:373
  9.0 2.0 %load_weights.1 = (bf16[640,768]{1,0:T(8,128)(2,1)S(1)}, bf16[640,768]{1,0:T(8,128)(2,1)S(1)}, bf16[768,640]{1,0:T(8,128)(2,1)S(1)}) custom-call(bf16[640,768]{1,0:T(8,128)(2,1)} %bitcast.10, bf16[640,768]{1,0:T(8,128)(2,1)} %bitcast.11, bf16[768,640]{1,0:T(8,128)(2,1)} %bitcast.12, bf16[3,96,128]{2,1,0:T(8,128)(2,1)S(1)} %get-tuple-element.32.pick_ref.refs_4_), custom_call_target="tpu_custom_call" | custom-call | bytes 5898240 | tf_op jit(solution)/shard_map/load_weights/pallas_call | solution.py:163
  11.0 0.0 collective-permute-done.refs_1_
  11.0 0.0 collective-permute-done.1.refs_2_
  11.0 0.5 %collective-permute-done.2.refs_3_ = bf16[24,640]{1,0:T(8,128)(2,1)S(1)} collective-permute-done((bf16[24,640]{1,0:T(8,128)(2,1)S(1)}, bf16[24,640]{1,0:T(8,128)(2,1)S(1)}, u32[]{:S(2)}, u32[]{:S(2)}) %collective-permute-start.2) | collective-permute-done | bytes 30752 | tf_op jit(solution)/shard_map/ppermute | solution.py:373
  11.5 0.7 %partials.1 = (bf16[40,640]{1,0:T(8,128)(2,1)S(1)}, bf16[40,640]{1,0:T(8,128)(2,1)S(1)}, bf16[40,2304]{1,0:T(8,128)(2,1)S(1)}) custom-call(bf16[24,640]{1,0:T(8,128)(2,1)S(1)} %get-tuple-element.28.refs_0_, bf16[24,640]{1,0:T(8,128)(2,1)S(1)} %collective-permute-done.refs_1_, bf16[24,640]{1,0:T(8,128)(2,1)S(1)} %collective-permute-done.1.refs_2_, ...), custom_call_target="tpu_custom_call" | custom-call | tf_op jit(solution)/shard_map/partials/pallas_call | solution.py:208
  12.3 8.3 %all-gather = bf16[160,2304]{1,0:T(8,128)(2,1)S(1)} all-gather(bf16[40,2304]{1,0:T(8,128)(2,1)S(1)} %get-tuple-element.36), channel_id=2, replica_groups=mesh['groups'=2,'expert'=4,'dp'=4] {'dp'}, dimensions={0}, use_global_device_ids=true | all-gather | bytes 921600 | tf_op jit(solution)/shard_map/all_gather | solution.py:413
  20.6 0.8 %middle.1 = (bf16[24,640]{1,0:T(8,128)(2,1)S(1)}, bf16[24,640]{1,0:T(8,128)(2,1)S(1)}, bf16[24,640]{1,0:T(8,128)(2,1)S(1)}, bf16[24,640]{1,0:T(8,128)(2,1)S(1)},...) custom-call(bf16[4,40,2304]{2,1,0:T(8,128)(2,1)S(1)} %bitcast.9, ...), custom_call_target="tpu_custom_call" | custom-call | tf_op jit(solution)/shard_map/middle/pallas_call | solution.py:269
  21.4 3.2 %collective-permute-start.3 = (bf16[24,640]{1,0:T(8,128)(2,1)S(1)}, bf16[24,640]{1,0:T(8,128)(2,1)S(1)}, u32[]{:S(2)}, u32[]{:S(2)}) collective-permute-start(bf16[24,640]{1,0:T(8,128)(2,1)S(1)} %get-tuple-element.38), channel_id=1, source_target_pairs={{0,12},{4,0},{8,4},{12,8},{1,13},{5,1},{9,5},{13,9},{2,14},{6,2},{... | collective-permute-start | bytes 92168 | tf_op jit(solution)/shard_map/ppermute | solution.py:373
  24.6 0.0 collective-permute-start.4
  24.6 0.6 %collective-permute-start.5 = (bf16[24,640]{1,0:T(8,128)(2,1)S(1)}, bf16[24,640]{1,0:T(8,128)(2,1)S(1)}, u32[]{:S(2)}, u32[]{:S(2)}) collective-permute-start(bf16[24,640]{1,0:T(8,128)(2,1)S(1)} %get-tuple-element.40), channel_id=1, source_target_pairs={{0,4},{4,8},{8,12},{12,0},{1,5},{5,9},{9,13},{13,1},{2,6},{6,10},{... | collective-permute-start | bytes 92168 | tf_op jit(solution)/shard_map/ppermute | solution.py:373
  25.3 2.0 %weight_grads.1 = (bf16[640,768]{1,0:T(8,128)(2,1)}, bf16[640,768]{1,0:T(8,128)(2,1)}, bf16[768,640]{1,0:T(8,128)(2,1)}) custom-call(bf16[40,640]{1,0:T(8,128)(2,1)S(1)} %get-tuple-element.43.rows_ref, bf16[40,640]{1,0:T(8,128)(2,1)S(1)} %get-tuple-element.44.cots_ref, bf16[40,768]{1,0:T(8,128)(2,1)S(1)} %get-tuple-element.45.hidden_ref, ...), custom_call_target="tpu_custom_call" | custom-call | flops 117964800 | bytes 2949120 | tf_op jit(solution)/shard_map/weight_grads/pallas_call | solution.py:314
  27.3 0.0 collective-permute-done.3.refs_1_
  27.3 2.5 %collective-permute-done.4.refs_2_ = bf16[24,640]{1,0:T(8,128)(2,1)S(1)} collective-permute-done((bf16[24,640]{1,0:T(8,128)(2,1)S(1)}, bf16[24,640]{1,0:T(8,128)(2,1)S(1)}, u32[]{:S(2)}, u32[]{:S(2)}) %collective-permute-start.4) | collective-permute-done | bytes 30752 | tf_op jit(solution)/shard_map/ppermute | solution.py:373
  29.8 0.6 %collective-permute-done.5.refs_3_ = bf16[24,640]{1,0:T(8,128)(2,1)S(1)} collective-permute-done((bf16[24,640]{1,0:T(8,128)(2,1)S(1)}, bf16[24,640]{1,0:T(8,128)(2,1)S(1)}, u32[]{:S(2)}, u32[]{:S(2)}) %collective-permute-start.5) | collective-permute-done | bytes 30752 | tf_op jit(solution)/shard_map/ppermute | solution.py:373
  30.3 1.0 %combine.1 = (bf16[128,640]{1,0:T(8,128)(2,1)}, bf16[128,640]{1,0:T(8,128)(2,1)}) custom-call(bf16[24,640]{1,0:T(8,128)(2,1)S(1)} %get-tuple-element.37.refs_0_, bf16[24,640]{1,0:T(8,128)(2,1)S(1)} %collective-permute-done.3.refs_1_, bf16[24,640]{1,0:T(8,128)(2,1)S(1)} %collective-permute-done.4.refs_2_, bf16[24,640]{1,0:T(8,128)(2,1)S(1)} %collective-permute-done.5.refs_3_, ...), custom_call_target="tpu_custom_call" | custom-call | tf_op jit(solution)/shard_map/combine/pallas_call | solution.py:351
Async XLA Ops:
  2.0 9.0 %collective-permute-start = (bf16[24,640]{1,0:T(8,128)(2,1)S(1)}, bf16[24,640]{1,0:T(8,128)(2,1)S(1)}, u32[]{:S(2)}, u32[]{:S(2)}) collective-permute-start(bf16[24,640]{1,0:T(8,128)(2,1)S(1)} %get-tuple-element.29), channel_id=1, source_target_pairs={{0,4},{4,8},{8,12},{12,0},{1,5},{5,9},{9,13},{13,1},{2,6},{6,10},{... | collective-permute-start | bytes 92168 | tf_op jit(solution)/shard_map/ppermute | solution.py:373
  5.1 6.0 %collective-permute-start.1 = (bf16[24,640]{1,0:T(8,128)(2,1)S(1)}, bf16[24,640]{1,0:T(8,128)(2,1)S(1)}, u32[]{:S(2)}, u32[]{:S(2)}) collective-permute-start(bf16[24,640]{1,0:T(8,128)(2,1)S(1)} %get-tuple-element.30), channel_id=1, source_target_pairs={{0,8},{4,12},{8,0},{12,4},{1,9},{5,13},{9,1},{13,5},{2,10},{6,14},... | collective-permute-start | bytes 92168 | tf_op jit(solution)/shard_map/ppermute | solution.py:373
  7.6 3.9 %collective-permute-start.2 = (bf16[24,640]{1,0:T(8,128)(2,1)S(1)}, bf16[24,640]{1,0:T(8,128)(2,1)S(1)}, u32[]{:S(2)}, u32[]{:S(2)}) collective-permute-start(bf16[24,640]{1,0:T(8,128)(2,1)S(1)} %get-tuple-element.31), channel_id=1, source_target_pairs={{0,12},{4,0},{8,4},{12,8},{1,13},{5,1},{9,5},{13,9},{2,14},{6,2},{... | collective-permute-start | bytes 92168 | tf_op jit(solution)/shard_map/ppermute | solution.py:373
  21.4 5.8 %collective-permute-start.3 = (bf16[24,640]{1,0:T(8,128)(2,1)S(1)}, bf16[24,640]{1,0:T(8,128)(2,1)S(1)}, u32[]{:S(2)}, u32[]{:S(2)}) collective-permute-start(bf16[24,640]{1,0:T(8,128)(2,1)S(1)} %get-tuple-element.38), channel_id=1, source_target_pairs={{0,12},{4,0},{8,4},{12,8},{1,13},{5,1},{9,5},{13,9},{2,14},{6,2},{... | collective-permute-start | bytes 92168 | tf_op jit(solution)/shard_map/ppermute | solution.py:373
  24.6 5.1 %collective-permute-start.4 = (bf16[24,640]{1,0:T(8,128)(2,1)S(1)}, bf16[24,640]{1,0:T(8,128)(2,1)S(1)}, u32[]{:S(2)}, u32[]{:S(2)}) collective-permute-start(bf16[24,640]{1,0:T(8,128)(2,1)S(1)} %get-tuple-element.39), channel_id=1, source_target_pairs={{0,8},{4,12},{8,0},{12,4},{1,9},{5,13},{9,1},{13,5},{2,10},{6,14},... | collective-permute-start | bytes 92168 | tf_op jit(solution)/shard_map/ppermute | solution.py:373
  24.6 5.7 %collective-permute-start.5 = (bf16[24,640]{1,0:T(8,128)(2,1)S(1)}, bf16[24,640]{1,0:T(8,128)(2,1)S(1)}, u32[]{:S(2)}, u32[]{:S(2)}) collective-permute-start(bf16[24,640]{1,0:T(8,128)(2,1)S(1)} %get-tuple-element.40), channel_id=1, source_target_pairs={{0,4},{4,8},{8,12},{12,0},{1,5},{5,9},{9,13},{13,1},{2,6},{6,10},{... | collective-permute-start | bytes 92168 | tf_op jit(solution)/shard_map/ppermute | solution.py:373

commit v4 on v3

--- a/solution.py
+++ b/solution.py
@@ -79,7 +79,7 @@
         copy.wait()
     members, weights, limits = [], [], []
     for index in range(experts):
-        expert = index if pieces == 1 else lax.rem(me + index, experts)
+        expert = index if pieces == 1 else me ^ index
         hot = (plan_ref[0, 0] == expert) | (plan_ref[1, 0] == expert)
         wanted = token_slot * hot.astype(I32)
         here = jnp.zeros((1, count), F32)
@@ -227,13 +227,11 @@
 
 
 def middle_kernel(group, slots, block, pieces, *refs):
-    parts_ref, gate_ref, up_ref, down_ref = refs[:4]
-    back_refs = refs[4 : 4 + pieces]
-    hidden_ref, gg_ref, ug_ref, flat, wide = refs[4 + pieces :]
+    near_ref, far_ref, gate_ref, up_ref, down_ref = refs[:5]
+    back_refs = refs[5 : 5 + pieces]
+    hidden_ref, gg_ref, ug_ref, flat, wide = refs[5 + pieces :]
     width = gate_ref.shape[1]
-    total = parts_ref[0].astype(F32)
-    for j in range(1, parts_ref.shape[0]):
-        total = total + parts_ref[j].astype(F32)
+    total = near_ref[...].astype(F32) + far_ref[...].astype(F32)
     gate_pre, up_pre, hidden_grad = (total[:, i * width : (i + 1) * width] for i in range(3))
     sigma = jax.nn.sigmoid(gate_pre)
     active = gate_pre * sigma
@@ -272,7 +270,8 @@
         out_shape=(jax.ShapeDtypeStruct((experts * block // pieces, feature), BF16),) * pieces
         + (jax.ShapeDtypeStruct((total, hidden), BF16),) * 3,
         in_specs=[
-            pl.BlockSpec((parts.shape[0], tile, 3 * hidden), lambda i: (0, i, 0)),
+            by_rows(tile, 3 * hidden),
+            by_rows(tile, 3 * hidden),
             whole((feature, hidden)),
             whole((feature, hidden)),
             whole((hidden, feature)),
@@ -281,7 +280,7 @@
         scratch_shapes=[pltpu.VMEM((2, tile, feature), F32), pltpu.VMEM((big, feature), F32)],
         compiler_params=params(),
         name="middle",
-    )(parts, gate, up, down)
+    )(*parts, gate, up, down)
     return outs[:pieces], *outs[pieces:]
 
 
@@ -363,18 +362,43 @@
     )(*backs, pick)
 
 
-def over_experts(arrays, experts, sign):
+def swapped(array, axis, distance):
+    return lax.ppermute(array, axis, [(i, i ^ distance) for i in range(lax.axis_size(axis))])
+
+
+def over_experts(arrays, experts):
     if len(arrays) == 1:
         array = arrays[0]
         blocks = array.reshape(experts, -1, array.shape[1])
         moved = lax.all_to_all(blocks, "expert", split_axis=0, concat_axis=0, tiled=True)
         return [moved.reshape(array.shape)]
-    return [arrays[0]] + [
-        lax.ppermute(
-            arrays[shift], "expert", [(i, (i + sign * shift) % experts) for i in range(experts)]
-        )
-        for shift in range(1, experts)
-    ]
+    return [arrays[0]] + [swapped(arrays[d], "expert", d) for d in range(1, experts)]
+
+
+def add_kernel(left_ref, right_ref, sum_ref):
+    sum_ref[...] = (left_ref[...].astype(F32) + right_ref[...].astype(F32)).astype(BF16)
+
+
+def add(left, right, tile):
+    spec = pl.BlockSpec((tile, left.shape[1]), lambda i: (i, 0))
+    return pl.pallas_call(
+        add_kernel,
+        grid=(left.shape[0] // tile,),
+        out_shape=jax.ShapeDtypeStruct(left.shape, BF16),
+        in_specs=[spec, spec],
+        out_specs=spec,
+        compiler_params=params(),
+        name="add",
+    )(left, right)
+
+
+def halves_over_dp(part, tile):
+    last = lax.axis_size("dp") // 2
+    distance = 1
+    while distance < last:
+        part = add(part, swapped(part, "dp", distance), tile)
+        distance *= 2
+    return part, swapped(part, "dp", last)
 
 
 def shards(
@@ -391,6 +415,7 @@
     experts = lax.axis_size("expert")
     hosts = replica_plan.shape[1]
     assert tokens.shape[0] % hosts == 0 and experts % GROUP == 0
+    assert all(n & (n - 1) == 0 for n in (experts, lax.axis_size("dp")))
     slots = OWN + SPARE * (hosts - 1)
     block = -(-2 * slots // 8) * 8
     pieces = experts if experts <= GROUP else 1
@@ -407,12 +432,12 @@
         block,
         pieces,
     )
-    recvs = over_experts(sends, experts, 1)
+    recvs = over_experts(sends, experts)
     gate, up, down = load_weights(gate, up, down, pick)
     rows, cots, part = partials(recvs, gate, up, down, experts, slots, block)
-    parts = lax.all_gather(part, "dp")
+    parts = halves_over_dp(part, GROUP * slots)
     backs, hidden, gg, ug = middle(parts, gate, up, down, experts, slots, block, pieces)
-    returned = over_experts(backs, experts, -1)
+    returned = over_experts(backs, experts)
     gate_grad, up_grad, down_grad = weight_grads(rows, cots, hidden, gg, ug)
     mixed, token_grad = combine(returned, pick)
     return mixed, token_grad, gate_grad[None], up_grad[None], down_grad[None]

time: 31.5 us -> 31 us (0.984)
  blocking collectives: 8.33 us -> 0 us
  waiting for transfers between devices: 3.57 us -> 10.5 us
  starting transfers between devices: 10.9 us -> 11.8 us
    all_gather x1 -> x0, blocking collectives: 8.33 us -> none  [shards(): parts = lax.all_gather(part, 'dp')]
    ppermute x6 -> x8, waiting for transfers between devices: 3.57 us -> 10.5 us  [swapped(): lax.ppermute(array, axis, [(i, i ^ distance) for i in range(lax.axis_size...]
    ppermute x6 -> x8, starting transfers between devices: 10.9 us -> 11.8 us  [swapped(): lax.ppermute(array, axis, [(i, i ^ distance) for i in range(lax.axis_size...]
  transfers between devices with their start and end apart: 6 -> 8, of which waited for: 3 -> 5; matrix products, arithmetic and copies ran while one was open for 0% -> 0% of each run, Pallas kernels for 13% -> 13%
where the time goes in v4:
time: 31 us; the launch traced here: 30.9 us
  starting transfers between devices  11.8 us (38%)
  waiting for transfers between devices  10.5 us (34%)
  Pallas kernels  7.91 us (26%)
  between operations  0.72 us (2%)
    ppermute x8, starting transfers between devices, swapped(): lax.ppermute(array, axis, [(i, i ^ distance) for i in range(lax.axis_size...  11.8 us
    ppermute x8, waiting for transfers between devices, swapped(): lax.ppermute(array, axis, [(i, i ^ distance) for i in range(lax.axis_size...  10.5 us
    pallas_call x1, Pallas kernels, load_weights(): pl.pallas_call(load_kernel, out_shape=tuple((pltpu.VMEM(w.shape, BF16) fo...  2 us
    pallas_call x1, Pallas kernels, weight_grads(): pl.pallas_call(grads_kernel, out_shape=tuple((jax.ShapeDtypeStruct(shape,...  1.97 us
    pallas_call x1, Pallas kernels, dispatch(): pl.pallas_call(functools.partial(dispatch_kernel, experts, plan.shape[1],...  1.33 us
    pallas_call x1, Pallas kernels, combine(): pl.pallas_call(functools.partial(combine_kernel, len(backs)), out_shape=(...  1.01 us
    pallas_call x1, Pallas kernels, middle(): pl.pallas_call(functools.partial(middle_kernel, GROUP, slots, block, piec...  0.83 us
    pallas_call x1, Pallas kernels, partials(): pl.pallas_call(functools.partial(partial_kernel, GROUP, slots, block, pie...  0.72 us
  transfers between devices with their start and end apart: 8, of which 5 were waited for; matrix products, arithmetic and copies ran while one was open for 0% of the time, Pallas kernels for 13%

profile of v4, /device:TPU:0, one launch (start us, length us, event | category | flops | bytes accessed | tf_op | source)
XLA Modules:
  0.0 30.9 jit_solution(10590949194096090825)
XLA Ops:
  0.6 1.3 %dispatch.1 = (bf16[24,640]{1,0:T(8,128)(2,1)S(1)}, bf16[24,640]{1,0:T(8,128)(2,1)S(1)}, bf16[24,640]{1,0:T(8,128)(2,1)S(1)}, bf16[24,640]{1,0:T(8,128)(2,1)S(1)}, bf16[3,96,128]{2,1,0:T(8,128)(2,1)S(1)}) custom-call(s32[2,2]{1,0:T(2,128)} %refs_0_.1, s32[4]{0:T(128)} %refs_1_.1, s32[2,128]{1,0:T(2,128)} %bitcast.11, f32[2,128]{1,0:T(2,128)} %bitcast.12, ...), custom_call_target="tpu_custom_call" | custom-call | tf_op jit(solution)/shard_map/dispatch/pallas_call | solution.py:124
  2.0 3.1 %collective-permute-start = (bf16[24,640]{1,0:T(8,128)(2,1)S(1)}, bf16[24,640]{1,0:T(8,128)(2,1)S(1)}, u32[]{:S(2)}, u32[]{:S(2)}) collective-permute-start(bf16[24,640]{1,0:T(8,128)(2,1)S(1)} %get-tuple-element.29), channel_id=1, source_target_pairs={{0,4},{4,0},{8,12},{12,8},{1,5},{5,1},{9,13},{13,9},{2,6},{6,2},{1... | collective-permute-start | bytes 92168 | tf_op jit(solution)/shard_map/ppermute | solution.py:366
  5.1 2.6 %collective-permute-start.1 = (bf16[24,640]{1,0:T(8,128)(2,1)S(1)}, bf16[24,640]{1,0:T(8,128)(2,1)S(1)}, u32[]{:S(2)}, u32[]{:S(2)}) collective-permute-start(bf16[24,640]{1,0:T(8,128)(2,1)S(1)} %get-tuple-element.30), channel_id=1, source_target_pairs={{0,8},{4,12},{8,0},{12,4},{1,9},{5,13},{9,1},{13,5},{2,10},{6,14},... | collective-permute-start | bytes 92168 | tf_op jit(solution)/shard_map/ppermute | solution.py:366
  7.7 0.0 collective-permute-start.2
  7.7 2.0 %load_weights.1 = (bf16[640,768]{1,0:T(8,128)(2,1)S(1)}, bf16[640,768]{1,0:T(8,128)(2,1)S(1)}, bf16[768,640]{1,0:T(8,128)(2,1)S(1)}) custom-call(bf16[640,768]{1,0:T(8,128)(2,1)} %bitcast.8, bf16[640,768]{1,0:T(8,128)(2,1)} %bitcast.9, bf16[768,640]{1,0:T(8,128)(2,1)} %bitcast.10, bf16[3,96,128]{2,1,0:T(8,128)(2,1)S(1)} %get-tuple-element.32.pick_ref.refs_4_), custom_call_target="tpu_custom_call" | custom-call | bytes 5898240 | tf_op jit(solution)/shard_map/load_weights/pallas_call | solution.py:163
  9.7 0.0 collective-permute-done.refs_1_
  9.7 0.7 %collective-permute-done.1.refs_2_ = bf16[24,640]{1,0:T(8,128)(2,1)S(1)} collective-permute-done((bf16[24,640]{1,0:T(8,128)(2,1)S(1)}, bf16[24,640]{1,0:T(8,128)(2,1)S(1)}, u32[]{:S(2)}, u32[]{:S(2)}) %collective-permute-start.1) | collective-permute-done | bytes 30752 | tf_op jit(solution)/shard_map/ppermute | solution.py:366
  10.4 3.0 %collective-permute-done.2.refs_3_ = bf16[24,640]{1,0:T(8,128)(2,1)S(1)} collective-permute-done((bf16[24,640]{1,0:T(8,128)(2,1)S(1)}, bf16[24,640]{1,0:T(8,128)(2,1)S(1)}, u32[]{:S(2)}, u32[]{:S(2)}) %collective-permute-start.2) | collective-permute-done | bytes 30752 | tf_op jit(solution)/shard_map/ppermute | solution.py:366
  13.3 0.7 %partials.1 = (bf16[40,640]{1,0:T(8,128)(2,1)S(1)}, bf16[40,640]{1,0:T(8,128)(2,1)S(1)}, bf16[40,2304]{1,0:T(8,128)(2,1)S(1)}) custom-call(bf16[24,640]{1,0:T(8,128)(2,1)S(1)} %get-tuple-element.28.refs_0_, bf16[24,640]{1,0:T(8,128)(2,1)S(1)} %collective-permute-done.refs_1_, bf16[24,640]{1,0:T(8,128)(2,1)S(1)} %collective-permute-done.1.refs_2_, ...), custom_call_target="tpu_custom_call" | custom-call | tf_op jit(solution)/shard_map/partials/pallas_call | solution.py:208
  14.1 0.1 collective-permute-start.3
  14.2 1.4 %collective-permute-done.3.right_ref = bf16[40,2304]{1,0:T(8,128)(2,1)S(1)} collective-permute-done((bf16[40,2304]{1,0:T(8,128)(2,1)S(1)}, bf16[40,2304]{1,0:T(8,128)(2,1)S(1)}, u32[]{:S(2)}, u32[]{:S(2)}) %collective-permute-start.3) | collective-permute-done | bytes 184352 | tf_op jit(solution)/shard_map/ppermute | solution.py:366
  15.6 1.6 %collective-permute-start.4 = (bf16[40,2304]{1,0:T(8,128)(2,1)S(1)}, bf16[40,2304]{1,0:T(8,128)(2,1)S(1)}, u32[]{:S(2)}, u32[]{:S(2)}) collective-permute-start(bf16[40,2304]{1,0:T(8,128)(2,1)S(1)} %add.1.refs_0_), channel_id=1, source_target_pairs={{0,2},{1,3},{2,0},{3,1},{4,6},{5,7},{6,4},{7,5},{8,10},{9,11},{10,... | collective-permute-start | bytes 552968 | tf_op jit(solution)/shard_map/ppermute | solution.py:366
  17.2 5.2 %collective-permute-done.4.refs_1_ = bf16[40,2304]{1,0:T(8,128)(2,1)S(1)} collective-permute-done((bf16[40,2304]{1,0:T(8,128)(2,1)S(1)}, bf16[40,2304]{1,0:T(8,128)(2,1)S(1)}, u32[]{:S(2)}, u32[]{:S(2)}) %collective-permute-start.4) | collective-permute-done | bytes 184352 | tf_op jit(solution)/shard_map/ppermute | solution.py:366
  22.4 0.8 %middle.1 = (bf16[24,640]{1,0:T(8,128)(2,1)S(1)}, bf16[24,640]{1,0:T(8,128)(2,1)S(1)}, bf16[24,640]{1,0:T(8,128)(2,1)S(1)}, bf16[24,640]{1,0:T(8,128)(2,1)S(1)},...) custom-call(bf16[40,2304]{1,0:T(8,128)(2,1)S(1)} %add.1.refs_0_, ...), custom_call_target="tpu_custom_call" | custom-call | tf_op jit(solution)/shard_map/middle/pallas_call | solution.py:267
  23.2 0.1 collective-permute-start.5
  23.3 0.9 %collective-permute-start.6 = (bf16[24,640]{1,0:T(8,128)(2,1)S(1)}, bf16[24,640]{1,0:T(8,128)(2,1)S(1)}, u32[]{:S(2)}, u32[]{:S(2)}) collective-permute-start(bf16[24,640]{1,0:T(8,128)(2,1)S(1)} %get-tuple-element.39), channel_id=1, source_target_pairs={{0,8},{4,12},{8,0},{12,4},{1,9},{5,13},{9,1},{13,5},{2,10},{6,14},... | collective-permute-start | bytes 92168 | tf_op jit(solution)/shard_map/ppermute | solution.py:366
  24.2 3.5 %collective-permute-start.7 = (bf16[24,640]{1,0:T(8,128)(2,1)S(1)}, bf16[24,640]{1,0:T(8,128)(2,1)S(1)}, u32[]{:S(2)}, u32[]{:S(2)}) collective-permute-start(bf16[24,640]{1,0:T(8,128)(2,1)S(1)} %get-tuple-element.40), channel_id=1, source_target_pairs={{0,12},{4,8},{8,4},{12,0},{1,13},{5,9},{9,5},{13,1},{2,14},{6,10},... | collective-permute-start | bytes 92168 | tf_op jit(solution)/shard_map/ppermute | solution.py:366
  27.6 2.0 %weight_grads.1 = (bf16[640,768]{1,0:T(8,128)(2,1)}, bf16[640,768]{1,0:T(8,128)(2,1)}, bf16[768,640]{1,0:T(8,128)(2,1)}) custom-call(bf16[40,640]{1,0:T(8,128)(2,1)S(1)} %get-tuple-element.43.rows_ref, bf16[40,640]{1,0:T(8,128)(2,1)S(1)} %get-tuple-element.44.cots_ref, bf16[40,768]{1,0:T(8,128)(2,1)S(1)} %get-tuple-element.45.hidden_ref, ...), custom_call_target="tpu_custom_call" | custom-call | flops 117964800 | bytes 2949120 | tf_op jit(solution)/shard_map/weight_grads/pallas_call | solution.py:313
  29.6 0.0 collective-permute-done.5.refs_1_
  29.6 0.0 collective-permute-done.6.refs_2_
  29.6 0.2 collective-permute-done.7.refs_3_
  29.8 1.0 %combine.1 = (bf16[128,640]{1,0:T(8,128)(2,1)}, bf16[128,640]{1,0:T(8,128)(2,1)}) custom-call(bf16[24,640]{1,0:T(8,128)(2,1)S(1)} %get-tuple-element.37.refs_0_, bf16[24,640]{1,0:T(8,128)(2,1)S(1)} %collective-permute-done.5.refs_1_, bf16[24,640]{1,0:T(8,128)(2,1)S(1)} %collective-permute-done.6.refs_2_, bf16[24,640]{1,0:T(8,128)(2,1)S(1)} %collective-permute-done.7.refs_3_, ...), custom_call_target="tpu_custom_call" | custom-call | tf_op jit(solution)/shard_map/combine/pallas_call | solution.py:350
  (1 shorter events, 0.0 us)
Async XLA Ops:
  2.0 7.7 %collective-permute-start = (bf16[24,640]{1,0:T(8,128)(2,1)S(1)}, bf16[24,640]{1,0:T(8,128)(2,1)S(1)}, u32[]{:S(2)}, u32[]{:S(2)}) collective-permute-start(bf16[24,640]{1,0:T(8,128)(2,1)S(1)} %get-tuple-element.29), channel_id=1, source_target_pairs={{0,4},{4,0},{8,12},{12,8},{1,5},{5,1},{9,13},{13,9},{2,6},{6,2},{1... | collective-permute-start | bytes 92168 | tf_op jit(solution)/shard_map/ppermute | solution.py:366
  5.1 5.3 %collective-permute-start.1 = (bf16[24,640]{1,0:T(8,128)(2,1)S(1)}, bf16[24,640]{1,0:T(8,128)(2,1)S(1)}, u32[]{:S(2)}, u32[]{:S(2)}) collective-permute-start(bf16[24,640]{1,0:T(8,128)(2,1)S(1)} %get-tuple-element.30), channel_id=1, source_target_pairs={{0,8},{4,12},{8,0},{12,4},{1,9},{5,13},{9,1},{13,5},{2,10},{6,14},... | collective-permute-start | bytes 92168 | tf_op jit(solution)/shard_map/ppermute | solution.py:366
  7.7 5.7 %collective-permute-start.2 = (bf16[24,640]{1,0:T(8,128)(2,1)S(1)}, bf16[24,640]{1,0:T(8,128)(2,1)S(1)}, u32[]{:S(2)}, u32[]{:S(2)}) collective-permute-start(bf16[24,640]{1,0:T(8,128)(2,1)S(1)} %get-tuple-element.31), channel_id=1, source_target_pairs={{0,12},{4,8},{8,4},{12,0},{1,13},{5,9},{9,5},{13,1},{2,14},{6,10},... | collective-permute-start | bytes 92168 | tf_op jit(solution)/shard_map/ppermute | solution.py:366
  14.1 1.5 %collective-permute-start.3 = (bf16[40,2304]{1,0:T(8,128)(2,1)S(1)}, bf16[40,2304]{1,0:T(8,128)(2,1)S(1)}, u32[]{:S(2)}, u32[]{:S(2)}) collective-permute-start(bf16[40,2304]{1,0:T(8,128)(2,1)S(1)} %get-tuple-element.36.left_ref), channel_id=1, source_target_pairs={{0,1},{1,0},{2,3},{3,2},{4,5},{5,4},{6,7},{7,6},{8,9},{9,8},{10,11... | collective-permute-start | bytes 552968 | tf_op jit(solution)/shard_map/ppermute | solution.py:366
  15.6 6.7 %collective-permute-start.4 = (bf16[40,2304]{1,0:T(8,128)(2,1)S(1)}, bf16[40,2304]{1,0:T(8,128)(2,1)S(1)}, u32[]{:S(2)}, u32[]{:S(2)}) collective-permute-start(bf16[40,2304]{1,0:T(8,128)(2,1)S(1)} %add.1.refs_0_), channel_id=1, source_target_pairs={{0,2},{1,3},{2,0},{3,1},{4,6},{5,7},{6,4},{7,5},{8,10},{9,11},{10,... | collective-permute-start | bytes 552968 | tf_op jit(solution)/shard_map/ppermute | solution.py:366
  23.2 6.4 %collective-permute-start.5 = (bf16[24,640]{1,0:T(8,128)(2,1)S(1)}, bf16[24,640]{1,0:T(8,128)(2,1)S(1)}, u32[]{:S(2)}, u32[]{:S(2)}) collective-permute-start(bf16[24,640]{1,0:T(8,128)(2,1)S(1)} %get-tuple-element.38), channel_id=1, source_target_pairs={{0,4},{4,0},{8,12},{12,8},{1,5},{5,1},{9,13},{13,9},{2,6},{6,2},{1... | collective-permute-start | bytes 92168 | tf_op jit(solution)/shard_map/ppermute | solution.py:366
  23.3 6.4 %collective-permute-start.6 = (bf16[24,640]{1,0:T(8,128)(2,1)S(1)}, bf16[24,640]{1,0:T(8,128)(2,1)S(1)}, u32[]{:S(2)}, u32[]{:S(2)}) collective-permute-start(bf16[24,640]{1,0:T(8,128)(2,1)S(1)} %get-tuple-element.39), channel_id=1, source_target_pairs={{0,8},{4,12},{8,0},{12,4},{1,9},{5,13},{9,1},{13,5},{2,10},{6,14},... | collective-permute-start | bytes 92168 | tf_op jit(solution)/shard_map/ppermute | solution.py:366
  24.2 5.7 %collective-permute-start.7 = (bf16[24,640]{1,0:T(8,128)(2,1)S(1)}, bf16[24,640]{1,0:T(8,128)(2,1)S(1)}, u32[]{:S(2)}, u32[]{:S(2)}) collective-permute-start(bf16[24,640]{1,0:T(8,128)(2,1)S(1)} %get-tuple-element.40), channel_id=1, source_target_pairs={{0,12},{4,8},{8,4},{12,0},{1,13},{5,9},{9,5},{13,1},{2,14},{6,10},... | collective-permute-start | bytes 92168 | tf_op jit(solution)/shard_map/ppermute | solution.py:366

commit v5 on v3

--- a/solution.py
+++ b/solution.py
@@ -79,7 +79,7 @@
         copy.wait()
     members, weights, limits = [], [], []
     for index in range(experts):
-        expert = index if pieces == 1 else lax.rem(me + index, experts)
+        expert = index if pieces == 1 else me ^ index
         hot = (plan_ref[0, 0] == expert) | (plan_ref[1, 0] == expert)
         wanted = token_slot * hot.astype(I32)
         here = jnp.zeros((1, count), F32)
@@ -174,9 +174,24 @@
     )(in_hbm(gate), in_hbm(up), in_hbm(down), pick)
 
 
-def partial_kernel(group, slots, block, pieces, *refs):
+def half_columns(which, width):
+    half = width // 2
+    side = lax.rem(lax.axis_index("dp") + which, 2)
+    return pl.ds(pl.multiple_of(side * half, half), half)
+
+
+def half_partials(which, rows, cots, gate_ref, up_ref, down_ref, part_ref):
+    width = gate_ref.shape[1]
+    half = width // 2
+    units = half_columns(which, width)
+    part_ref[:, :half] = matmul(rows, gate_ref[:, units], 1, 0).astype(BF16)
+    part_ref[:, half : 2 * half] = matmul(rows, up_ref[:, units], 1, 0).astype(BF16)
+    part_ref[:, 2 * half :] = matmul(cots, down_ref[units, :], 1, 1).astype(BF16)
+
+
+def give_kernel(group, slots, block, pieces, *refs):
     recv_refs = refs[:pieces]
-    gate_ref, up_ref, down_ref, rows_ref, cots_ref, part_ref, wide, flat = refs[pieces:]
+    gate_ref, up_ref, down_ref, rows_ref, cots_ref, give_ref, wide, flat = refs[pieces:]
     size = group * block // pieces
     for i, recv_ref in enumerate(recv_refs):
         wide[i * size : (i + 1) * size, :] = recv_ref[...].astype(F32)
@@ -187,65 +202,49 @@
     cots = flat[1].astype(BF16)
     rows_ref[...] = rows
     cots_ref[...] = cots
-    hidden = gate_ref.shape[1]
-    part_ref[:, :hidden] = matmul(rows, gate_ref[...], 1, 0).astype(BF16)
-    part_ref[:, hidden : 2 * hidden] = matmul(rows, up_ref[...], 1, 0).astype(BF16)
-    part_ref[:, 2 * hidden :] = matmul(cots, down_ref[...], 1, 1).astype(BF16)
-
-
-def partials(recvs, gate, up, down, experts, slots, block):
-    pieces = len(recvs)
-    feature, hidden = gate.shape
-    tile, big = GROUP * slots, GROUP * block
-    total = experts * slots
-
-    def whole(shape):
-        return pl.BlockSpec(shape, lambda i: (0, 0))
-
-    def by_rows(rows, width):
-        return pl.BlockSpec((rows, width), lambda i: (i, 0))
-
-    return pl.pallas_call(
-        functools.partial(partial_kernel, GROUP, slots, block, pieces),
-        grid=(experts // GROUP,),
-        out_shape=(
-            jax.ShapeDtypeStruct((total, feature), BF16),
-            jax.ShapeDtypeStruct((total, feature), BF16),
-            jax.ShapeDtypeStruct((total, 3 * hidden), BF16),
-        ),
-        in_specs=[by_rows(big // pieces, feature)] * pieces
-        + [
-            whole((feature, hidden)),
-            whole((feature, hidden)),
-            whole((hidden, feature)),
-        ],
-        out_specs=(by_rows(tile, feature), by_rows(tile, feature), by_rows(tile, 3 * hidden)),
-        scratch_shapes=[pltpu.VMEM((big, feature), F32), pltpu.VMEM((2, tile, feature), F32)],
-        compiler_params=params(),
-        name="partials",
-    )(*recvs, gate, up, down)
-
-
-def middle_kernel(group, slots, block, pieces, *refs):
-    parts_ref, gate_ref, up_ref, down_ref = refs[:4]
-    back_refs = refs[4 : 4 + pieces]
-    hidden_ref, gg_ref, ug_ref, flat, wide = refs[4 + pieces :]
-    width = gate_ref.shape[1]
-    total = parts_ref[0].astype(F32)
-    for j in range(1, parts_ref.shape[0]):
-        total = total + parts_ref[j].astype(F32)
-    gate_pre, up_pre, hidden_grad = (total[:, i * width : (i + 1) * width] for i in range(3))
+    half_partials(1, rows, cots, gate_ref, up_ref, down_ref, give_ref)
+
+
+def keep_kernel(rows_ref, cots_ref, gate_ref, up_ref, down_ref, keep_ref):
+    half_partials(0, rows_ref[...], cots_ref[...], gate_ref, up_ref, down_ref, keep_ref)
+
+
+def add_kernel(left_ref, right_ref, sum_ref):
+    sum_ref[...] = (left_ref[...].astype(F32) + right_ref[...].astype(F32)).astype(BF16)
+
+
+def activate_kernel(near_ref, far_ref, mine_ref):
+    half = mine_ref.shape[1] // 3
+    total = near_ref[...].astype(F32) + far_ref[...].astype(F32)
+    gate_pre, up_pre, hidden_grad = (total[:, i * half : (i + 1) * half] for i in range(3))
     sigma = jax.nn.sigmoid(gate_pre)
     active = gate_pre * sigma
     slope = sigma * (1.0 + gate_pre * (1.0 - sigma))
-    hidden = (active * up_pre).astype(BF16)
-    gg = (hidden_grad * up_pre * slope).astype(BF16)
-    ug = (hidden_grad * active).astype(BF16)
-    hidden_ref[...] = hidden
-    gg_ref[...] = gg
-    ug_ref[...] = ug
-    flat[0] = matmul(hidden, down_ref[...], 1, 0)
-    flat[1] = matmul(gg, gate_ref[...], 1, 1) + matmul(ug, up_ref[...], 1, 1)
+    mine_ref[:, :half] = (active * up_pre).astype(BF16)
+    mine_ref[:, half : 2 * half] = (hidden_grad * up_pre * slope).astype(BF16)
+    mine_ref[:, 2 * half :] = (hidden_grad * active).astype(BF16)
+
+
+def half_outputs(which, acts_ref, gate_ref, up_ref, down_ref):
+    width = gate_ref.shape[1]
+    half = width // 2
+    units = half_columns(which, width)
+    outs = matmul(acts_ref[:, :half], down_ref[units, :], 1, 0)
+    ins = matmul(acts_ref[:, half : 2 * half], gate_ref[:, units], 1, 1)
+    return outs, ins + matmul(acts_ref[:, 2 * half :], up_ref[:, units], 1, 1)
+
+
+def own_kernel(mine_ref, gate_ref, up_ref, down_ref, outs_ref, ins_ref):
+    outs_ref[...], ins_ref[...] = half_outputs(0, mine_ref, gate_ref, up_ref, down_ref)
+
+
+def back_kernel(group, slots, block, pieces, *refs):
+    theirs_ref, outs_ref, ins_ref, gate_ref, up_ref, down_ref = refs[:6]
+    back_refs = refs[6 : 6 + pieces]
+    flat, wide = refs[6 + pieces :]
+    outs, ins = half_outputs(1, theirs_ref, gate_ref, up_ref, down_ref)
+    flat[0] = outs_ref[...] + outs
+    flat[1] = ins_ref[...] + ins
     wide[...] = jnp.zeros_like(wide)
     for s in range(group):
         wide[s * block : s * block + slots, :] = flat[0, s * slots : (s + 1) * slots, :]
@@ -255,69 +254,73 @@
         back_ref[...] = wide[i * size : (i + 1) * size, :].astype(BF16)
 
 
-def middle(parts, gate, up, down, experts, slots, block, pieces):
-    feature, hidden = gate.shape
-    tile, big = GROUP * slots, GROUP * block
-    total = experts * slots
+def by_rows(kernel, name, steps, arrays, weights, outs, scratch=(), flops=0):
+    def tiled(shape):
+        return pl.BlockSpec((shape[0] // steps, shape[1]), lambda i: (i, 0))
 
     def whole(shape):
         return pl.BlockSpec(shape, lambda i: (0, 0))
 
-    def by_rows(rows, width):
-        return pl.BlockSpec((rows, width), lambda i: (i, 0))
-
-    outs = pl.pallas_call(
-        functools.partial(middle_kernel, GROUP, slots, block, pieces),
-        grid=(experts // GROUP,),
-        out_shape=(jax.ShapeDtypeStruct((experts * block // pieces, feature), BF16),) * pieces
-        + (jax.ShapeDtypeStruct((total, hidden), BF16),) * 3,
-        in_specs=[
-            pl.BlockSpec((parts.shape[0], tile, 3 * hidden), lambda i: (0, i, 0)),
-            whole((feature, hidden)),
-            whole((feature, hidden)),
-            whole((hidden, feature)),
-        ],
-        out_specs=(by_rows(big // pieces, feature),) * pieces + (by_rows(tile, hidden),) * 3,
-        scratch_shapes=[pltpu.VMEM((2, tile, feature), F32), pltpu.VMEM((big, feature), F32)],
+    moved = sum(array.size * array.dtype.itemsize for array in (*arrays, *weights))
+    results = pl.pallas_call(
+        kernel,
+        grid=(steps,),
+        out_shape=tuple(jax.ShapeDtypeStruct(shape, dtype) for shape, dtype in outs),
+        in_specs=[tiled(array.shape) for array in arrays] + [whole(w.shape) for w in weights],
+        out_specs=tuple(tiled(shape) for shape, _ in outs),
+        scratch_shapes=list(scratch),
         compiler_params=params(),
-        name="middle",
-    )(parts, gate, up, down)
-    return outs[:pieces], *outs[pieces:]
+        cost_estimate=pl.CostEstimate(flops=flops, bytes_accessed=moved, transcendentals=0),
+        name=name,
+    )(*arrays, *weights)
+    return results if len(outs) > 1 else results[0]
 
 
 def grads_kernel(
-    rows_ref, cots_ref, hidden_ref, gg_ref, ug_ref, gate_hbm, up_hbm, down_hbm, gate_ref, up_ref, down_ref, sems
+    rows_ref, cots_ref, mine_ref, theirs_ref, gate_hbm, up_hbm, down_hbm, gate_ref, up_ref, down_ref, sems
 ):
+    width = gate_ref.shape[1]
+    half = width // 2
     copies = []
-    for left_ref, right_ref, out_ref, out_hbm in (
-        (rows_ref, gg_ref, gate_ref, gate_hbm),
-        (rows_ref, ug_ref, up_ref, up_hbm),
-        (hidden_ref, cots_ref, down_ref, down_hbm),
-    ):
+
+    def send(source, target, rows):
+        copies.append(
+            pltpu.make_async_copy(source.at[rows], target.at[rows], sems.at[len(copies)])
+        )
+        copies[-1].start()
+
+    sides = [(mine_ref, half_columns(0, width)), (theirs_ref, half_columns(1, width))]
+    for acts_ref, units in sides:
+        for start, size in spans(half, CHUNK):
+            rows = pl.ds(pl.multiple_of(units.start + start, 16), size)
+            hidden = acts_ref[:, start : start + size]
+            down_ref[rows, :] = matmul(hidden, cots_ref[...], 0, 0).astype(BF16)
+            send(down_ref, down_hbm, rows)
+    for place, out_ref, out_hbm in ((1, gate_ref, gate_hbm), (2, up_ref, up_hbm)):
         for start, size in spans(out_ref.shape[0], CHUNK):
             rows = pl.ds(start, size)
-            out_ref[rows, :] = matmul(left_ref[:, rows], right_ref[...], 0, 0).astype(BF16)
-            copies.append(
-                pltpu.make_async_copy(out_ref.at[rows], out_hbm.at[rows], sems.at[len(copies)])
-            )
-            copies[-1].start()
+            for acts_ref, units in sides:
+                grad = acts_ref[:, place * half : (place + 1) * half]
+                out_ref[rows, units] = matmul(rows_ref[:, rows], grad, 0, 0).astype(BF16)
+            send(out_ref, out_hbm, rows)
     for copy in copies:
         copy.wait()
 
 
-def weight_grads(rows, cots, hidden, gg, ug):
+def weight_grads(rows, cots, mine, theirs):
     total, feature = rows.shape
-    width = hidden.shape[1]
+    width = 2 * mine.shape[1] // 3
     vmem = pl.BlockSpec(memory_space=pltpu.VMEM)
     hbm = pl.BlockSpec(memory_space=pltpu.HBM)
     shapes = ((feature, width), (feature, width), (width, feature))
+    pieces = 2 * len(spans(feature, CHUNK)) + 2 * len(spans(width // 2, CHUNK))
     return pl.pallas_call(
         grads_kernel,
         out_shape=tuple(jax.ShapeDtypeStruct(shape, BF16) for shape in shapes),
-        in_specs=[vmem] * 5,
+        in_specs=[vmem] * 4,
         out_specs=(hbm,) * 3,
         scratch_shapes=[pltpu.VMEM(shape, BF16) for shape in shapes]
-        + [pltpu.SemaphoreType.DMA((sum(len(spans(shape[0], CHUNK)) for shape in shapes),))],
+        + [pltpu.SemaphoreType.DMA((pieces,))],
         compiler_params=params(),
         cost_estimate=pl.CostEstimate(
             flops=6 * total * feature * width,
@@ -325,7 +328,7 @@
             transcendentals=0,
         ),
         name="weight_grads",
-    )(rows, cots, hidden, gg, ug)
+    )(rows, cots, mine, theirs)
 
 
 def combine_kernel(pieces, *refs):
@@ -363,18 +366,17 @@
     )(*backs, pick)
 
 
-def over_experts(arrays, experts, sign):
+def swapped(array, axis, distance):
+    return lax.ppermute(array, axis, [(i, i ^ distance) for i in range(lax.axis_size(axis))])
+
+
+def over_experts(arrays, experts):
     if len(arrays) == 1:
         array = arrays[0]
         blocks = array.reshape(experts, -1, array.shape[1])
         moved = lax.all_to_all(blocks, "expert", split_axis=0, concat_axis=0, tiled=True)
         return [moved.reshape(array.shape)]
-    return [arrays[0]] + [
-        lax.ppermute(
-            arrays[shift], "expert", [(i, (i + sign * shift) % experts) for i in range(experts)]
-        )
-        for shift in range(1, experts)
-    ]
+    return [arrays[0]] + [swapped(arrays[d], "expert", d) for d in range(1, experts)]
 
 
 def shards(
@@ -391,6 +393,7 @@
     experts = lax.axis_size("expert")
     hosts = replica_plan.shape[1]
     assert tokens.shape[0] % hosts == 0 and experts % GROUP == 0
+    assert all(n >= 4 and n & (n - 1) == 0 for n in (experts, lax.axis_size("dp")))
     slots = OWN + SPARE * (hosts - 1)
     block = -(-2 * slots // 8) * 8
     pieces = experts if experts <= GROUP else 1
@@ -407,13 +410,52 @@
         block,
         pieces,
     )
-    recvs = over_experts(sends, experts, 1)
-    gate, up, down = load_weights(gate, up, down, pick)
-    rows, cots, part = partials(recvs, gate, up, down, experts, slots, block)
-    parts = lax.all_gather(part, "dp")
-    backs, hidden, gg, ug = middle(parts, gate, up, down, experts, slots, block, pieces)
-    returned = over_experts(backs, experts, -1)
-    gate_grad, up_grad, down_grad = weight_grads(rows, cots, hidden, gg, ug)
+    recvs = over_experts(sends, experts)
+    weights = load_weights(gate, up, down, pick)
+    feature, width = gate.shape
+    tile, big = GROUP * slots, GROUP * block
+    steps, total, half = experts // GROUP, experts * slots, 3 * width // 2
+    layout = (GROUP, slots, block, pieces)
+    flops = 3 * total * feature * width
+    scratch = [pltpu.VMEM((big, feature), F32), pltpu.VMEM((2, tile, feature), F32)]
+    rows, cots, give = by_rows(
+        functools.partial(give_kernel, *layout),
+        "give",
+        steps,
+        recvs,
+        weights,
+        [((total, feature), BF16), ((total, feature), BF16), ((total, half), BF16)],
+        scratch,
+        flops,
+    )
+    got = swapped(give, "dp", 1)
+    keep = by_rows(
+        keep_kernel, "keep", steps, [rows, cots], weights, [((total, half), BF16)], (), flops
+    )
+    near = by_rows(add_kernel, "add", steps, [keep, got], [], [((total, half), BF16)])
+    distance, last = 2, lax.axis_size("dp") // 2
+    while distance < last:
+        far = swapped(near, "dp", distance)
+        near = by_rows(add_kernel, "add", steps, [near, far], [], [((total, half), BF16)])
+        distance *= 2
+    far = swapped(near, "dp", last)
+    mine = by_rows(activate_kernel, "activate", steps, [near, far], [], [((total, half), BF16)])
+    theirs = swapped(mine, "dp", 1)
+    outs, ins = by_rows(
+        own_kernel, "own", steps, [mine], weights, [((total, feature), F32)] * 2, (), flops
+    )
+    backs = by_rows(
+        functools.partial(back_kernel, *layout),
+        "back",
+        steps,
+        [theirs, outs, ins],
+        weights,
+        [((experts * block // pieces, feature), BF16)] * pieces,
+        scratch[::-1],
+        flops,
+    )
+    returned = over_experts(backs if pieces > 1 else [backs], experts)
+    gate_grad, up_grad, down_grad = weight_grads(rows, cots, mine, theirs)
     mixed, token_grad = combine(returned, pick)
     return mixed, token_grad, gate_grad[None], up_grad[None], down_grad[None]
 

time: 31.5 us -> 29.8 us (0.946)
  blocking collectives: 8.33 us -> 0 us
  waiting for transfers between devices: 3.57 us -> 8.72 us
  starting transfers between devices: 10.9 us -> 11.8 us
  Pallas kernels: 7.87 us -> 8.34 us
    all_gather x1 -> x0, blocking collectives: 8.33 us -> none  [shards(): parts = lax.all_gather(part, 'dp')]
    ppermute x6 -> x9, waiting for transfers between devices: 3.57 us -> 8.72 us  [swapped(): lax.ppermute(array, axis, [(i, i ^ distance) for i in range(lax.axis_size...]
    ppermute x6 -> x9, starting transfers between devices: 10.9 us -> 11.8 us  [swapped(): lax.ppermute(array, axis, [(i, i ^ distance) for i in range(lax.axis_size...]
    pallas_call x2 -> x6, Pallas kernels: 1.55 us -> 2.03 us  [by_rows(): pl.pallas_call(kernel, grid=(steps,), out_shape=tuple((jax.ShapeDtypeStru...]
  transfers between devices with their start and end apart: 6 -> 9, of which waited for: 3 -> 6; matrix products, arithmetic and copies ran while one was open for 0% -> 0% of each run, Pallas kernels for 13% -> 17%
where the time goes in v5:
time: 29.8 us; the launch traced here: 29.6 us
  starting transfers between devices  11.8 us (40%)
  waiting for transfers between devices  8.72 us (29%)
  Pallas kernels  8.34 us (28%)
  between operations  0.74 us (2%)
    ppermute x9, starting transfers between devices, swapped(): lax.ppermute(array, axis, [(i, i ^ distance) for i in range(lax.axis_size...  11.8 us
    ppermute x9, waiting for transfers between devices, swapped(): lax.ppermute(array, axis, [(i, i ^ distance) for i in range(lax.axis_size...  8.72 us
    pallas_call x6, Pallas kernels, by_rows(): pl.pallas_call(kernel, grid=(steps,), out_shape=tuple((jax.ShapeDtypeStru...  2.03 us
    pallas_call x1, Pallas kernels, load_weights(): pl.pallas_call(load_kernel, out_shape=tuple((pltpu.VMEM(w.shape, BF16) fo...  2 us
    pallas_call x1, Pallas kernels, weight_grads(): pl.pallas_call(grads_kernel, out_shape=tuple((jax.ShapeDtypeStruct(shape,...  1.96 us
    pallas_call x1, Pallas kernels, dispatch(): pl.pallas_call(functools.partial(dispatch_kernel, experts, plan.shape[1],...  1.33 us
    pallas_call x1, Pallas kernels, combine(): pl.pallas_call(functools.partial(combine_kernel, len(backs)), out_shape=(...  1.01 us
  transfers between devices with their start and end apart: 9, of which 6 were waited for; matrix products, arithmetic and copies ran while one was open for 0% of the time, Pallas kernels for 17%

profile of v5, /device:TPU:0, one launch (start us, length us, event | category | flops | bytes accessed | tf_op | source)
XLA Modules:
  0.0 29.6 jit_solution(14543673515331114689)
XLA Ops:
  0.6 1.3 %dispatch.1 = (bf16[24,640]{1,0:T(8,128)(2,1)S(1)}, bf16[24,640]{1,0:T(8,128)(2,1)S(1)}, bf16[24,640]{1,0:T(8,128)(2,1)S(1)}, bf16[24,640]{1,0:T(8,128)(2,1)S(1)}, bf16[3,96,128]{2,1,0:T(8,128)(2,1)S(1)}) custom-call(s32[2,2]{1,0:T(2,128)} %refs_0_.1, s32[4]{0:T(128)} %refs_1_.1, s32[2,128]{1,0:T(2,128)} %bitcast.11, f32[2,128]{1,0:T(2,128)} %bitcast.12, ...), custom_call_target="tpu_custom_call" | custom-call | tf_op jit(solution)/shard_map/dispatch/pallas_call | solution.py:124
  2.0 3.1 %collective-permute-start = (bf16[24,640]{1,0:T(8,128)(2,1)S(1)}, bf16[24,640]{1,0:T(8,128)(2,1)S(1)}, u32[]{:S(2)}, u32[]{:S(2)}) collective-permute-start(bf16[24,640]{1,0:T(8,128)(2,1)S(1)} %get-tuple-element.28), channel_id=1, source_target_pairs={{0,4},{4,0},{8,12},{12,8},{1,5},{5,1},{9,13},{13,9},{2,6},{6,2},{1... | collective-permute-start | bytes 92168 | tf_op jit(solution)/shard_map/ppermute | solution.py:370
  5.1 2.6 %collective-permute-start.1 = (bf16[24,640]{1,0:T(8,128)(2,1)S(1)}, bf16[24,640]{1,0:T(8,128)(2,1)S(1)}, u32[]{:S(2)}, u32[]{:S(2)}) collective-permute-start(bf16[24,640]{1,0:T(8,128)(2,1)S(1)} %get-tuple-element.29), channel_id=1, source_target_pairs={{0,8},{4,12},{8,0},{12,4},{1,9},{5,13},{9,1},{13,5},{2,10},{6,14},... | collective-permute-start | bytes 92168 | tf_op jit(solution)/shard_map/ppermute | solution.py:370
  7.7 0.0 collective-permute-start.2
  7.7 2.0 %load_weights.1 = (bf16[640,768]{1,0:T(8,128)(2,1)S(1)}, bf16[640,768]{1,0:T(8,128)(2,1)S(1)}, bf16[768,640]{1,0:T(8,128)(2,1)S(1)}) custom-call(bf16[640,768]{1,0:T(8,128)(2,1)} %bitcast.8, bf16[640,768]{1,0:T(8,128)(2,1)} %bitcast.9, bf16[768,640]{1,0:T(8,128)(2,1)} %bitcast.10, bf16[3,96,128]{2,1,0:T(8,128)(2,1)S(1)} %get-tuple-element.31.pick_ref.refs_4_), custom_call_target="tpu_custom_call" | custom-call | bytes 5898240 | tf_op jit(solution)/shard_map/load_weights/pallas_call | solution.py:163
  9.7 0.0 collective-permute-done.refs_1_
  9.7 0.7 %collective-permute-done.1.refs_2_ = bf16[24,640]{1,0:T(8,128)(2,1)S(1)} collective-permute-done((bf16[24,640]{1,0:T(8,128)(2,1)S(1)}, bf16[24,640]{1,0:T(8,128)(2,1)S(1)}, u32[]{:S(2)}, u32[]{:S(2)}) %collective-permute-start.1) | collective-permute-done | bytes 30752 | tf_op jit(solution)/shard_map/ppermute | solution.py:370
  10.4 3.0 %collective-permute-done.2.refs_3_ = bf16[24,640]{1,0:T(8,128)(2,1)S(1)} collective-permute-done((bf16[24,640]{1,0:T(8,128)(2,1)S(1)}, bf16[24,640]{1,0:T(8,128)(2,1)S(1)}, u32[]{:S(2)}, u32[]{:S(2)}) %collective-permute-start.2) | collective-permute-done | bytes 30752 | tf_op jit(solution)/shard_map/ppermute | solution.py:370
  13.3 0.5 %give.1 = (bf16[40,640]{1,0:T(8,128)(2,1)S(1)}, bf16[40,640]{1,0:T(8,128)(2,1)S(1)}, bf16[40,1152]{1,0:T(8,128)(2,1)S(1)}) custom-call(bf16[24,640]{1,0:T(8,128)(2,1)S(1)} %get-tuple-element.27.refs_0_, bf16[24,640]{1,0:T(8,128)(2,1)S(1)} %collective-permute-done.refs_1_, bf16[24,640]{1,0:T(8,128)(2,1)S(1)} %collective-permute-done.1.refs_2_, ...), custom_call_target="tpu_custom_call" | custom-call | flops 58982400 | bytes 3072000 | tf_op jit(solution)/shard_map/give/pallas_call | solution.py:265
  13.8 0.1 collective-permute-start.3
  13.9 0.4 %keep.1.left_ref = bf16[40,1152]{1,0:T(8,128)(2,1)S(1)} custom-call(bf16[40,640]{1,0:T(8,128)(2,1)S(1)} %get-tuple-element.35.rows_ref, bf16[40,640]{1,0:T(8,128)(2,1)S(1)} %get-tuple-element.36.cots_ref, bf16[640,768]{1,0:T(8,128)(2,1)S(1)} %get-tuple-element.32.refs_4_.gate_ref.refs_3_, bf16[640,768]{1,0:T(8,128)(2,1)S(1)} %get-tuple-element.33.refs_5_.up_ref.refs_4_, ...), custom_call_target="tpu_custom_call" | custom-call | flops 58982400 | bytes 3051520 | tf_op jit(solution)/shard_map/keep/pallas_call | solution.py:265
  14.3 0.8 %collective-permute-done.3.right_ref = bf16[40,1152]{1,0:T(8,128)(2,1)S(1)} collective-permute-done((bf16[40,1152]{1,0:T(8,128)(2,1)S(1)}, bf16[40,1152]{1,0:T(8,128)(2,1)S(1)}, u32[]{:S(2)}, u32[]{:S(2)}) %collective-permute-start.3) | collective-permute-done | bytes 92192 | tf_op jit(solution)/shard_map/ppermute | solution.py:370
  15.2 1.6 %collective-permute-start.4 = (bf16[40,1152]{1,0:T(8,128)(2,1)S(1)}, bf16[40,1152]{1,0:T(8,128)(2,1)S(1)}, u32[]{:S(2)}, u32[]{:S(2)}) collective-permute-start(bf16[40,1152]{1,0:T(8,128)(2,1)S(1)} %add.1.near_ref), channel_id=1, source_target_pairs={{0,2},{1,3},{2,0},{3,1},{4,6},{5,7},{6,4},{7,5},{8,10},{9,11},{10,... | collective-permute-start | bytes 276488 | tf_op jit(solution)/shard_map/ppermute | solution.py:370
  16.8 3.2 %collective-permute-done.4.far_ref = bf16[40,1152]{1,0:T(8,128)(2,1)S(1)} collective-permute-done((bf16[40,1152]{1,0:T(8,128)(2,1)S(1)}, bf16[40,1152]{1,0:T(8,128)(2,1)S(1)}, u32[]{:S(2)}, u32[]{:S(2)}) %collective-permute-start.4) | collective-permute-done | bytes 92192 | tf_op jit(solution)/shard_map/ppermute | solution.py:370
  20.0 0.1 activate.1.mine_ref
  20.0 0.1 collective-permute-start.5
  20.1 0.5 %own.1 = (f32[40,640]{1,0:T(8,128)S(1)}, f32[40,640]{1,0:T(8,128)S(1)}) custom-call(bf16[40,1152]{1,0:T(8,128)(2,1)S(1)} %activate.1.mine_ref, bf16[640,768]{1,0:T(8,128)(2,1)S(1)} %get-tuple-element.32.refs_4_.gate_ref.refs_3_, bf16[640,768]{1,0:T(8,128)(2,1)S(1)} %get-tuple-element.33.refs_5_.up_ref.refs_4_, ...), custom_call_target="tpu_custom_call" | custom-call | flops 58982400 | bytes 3041280 | tf_op jit(solution)/shard_map/own/pallas_call | solution.py:265
  20.6 0.8 %collective-permute-done.5.refs_0_.theirs_ref = bf16[40,1152]{1,0:T(8,128)(2,1)S(1)} collective-permute-done((bf16[40,1152]{1,0:T(8,128)(2,1)S(1)}, bf16[40,1152]{1,0:T(8,128)(2,1)S(1)}, u32[]{:S(2)}, u32[]{:S(2)}) %collective-permute-start.5) | collective-permute-done | bytes 92192 | tf_op jit(solution)/shard_map/ppermute | solution.py:370
  21.4 0.6 %back.1 = (bf16[24,640]{1,0:T(8,128)(2,1)S(1)}, bf16[24,640]{1,0:T(8,128)(2,1)S(1)}, bf16[24,640]{1,0:T(8,128)(2,1)S(1)}, bf16[24,640]{1,0:T(8,128)(2,1)S(1)}) custom-call(bf16[40,1152]{1,0:T(8,128)(2,1)S(1)} %collective-permute-done.5.refs_0_.theirs_ref, f32[40,640]{1,0:T(8,128)S(1)} %get-tuple-element.38.refs_1_, f32[40,640]{1,0:T(8,128)S(1)} %get-tuple-element.39.refs_2_, ...), custom_call_target="tpu_custom_call" | custom-call | flops 58982400 | bytes 3246080 | tf_op jit(solution)/shard_map/back/pallas_call | solution.py:265
  22.0 0.1 collective-permute-start.6
  22.0 0.9 %collective-permute-start.7 = (bf16[24,640]{1,0:T(8,128)(2,1)S(1)}, bf16[24,640]{1,0:T(8,128)(2,1)S(1)}, u32[]{:S(2)}, u32[]{:S(2)}) collective-permute-start(bf16[24,640]{1,0:T(8,128)(2,1)S(1)} %get-tuple-element.42), channel_id=1, source_target_pairs={{0,8},{4,12},{8,0},{12,4},{1,9},{5,13},{9,1},{13,5},{2,10},{6,14},... | collective-permute-start | bytes 92168 | tf_op jit(solution)/shard_map/ppermute | solution.py:370
  22.9 3.5 %collective-permute-start.8 = (bf16[24,640]{1,0:T(8,128)(2,1)S(1)}, bf16[24,640]{1,0:T(8,128)(2,1)S(1)}, u32[]{:S(2)}, u32[]{:S(2)}) collective-permute-start(bf16[24,640]{1,0:T(8,128)(2,1)S(1)} %get-tuple-element.43), channel_id=1, source_target_pairs={{0,12},{4,8},{8,4},{12,0},{1,13},{5,9},{9,5},{13,1},{2,14},{6,10},... | collective-permute-start | bytes 92168 | tf_op jit(solution)/shard_map/ppermute | solution.py:370
  26.4 2.0 %weight_grads.1 = (bf16[640,768]{1,0:T(8,128)(2,1)}, bf16[640,768]{1,0:T(8,128)(2,1)}, bf16[768,640]{1,0:T(8,128)(2,1)}) custom-call(bf16[40,640]{1,0:T(8,128)(2,1)S(1)} %get-tuple-element.35.rows_ref, bf16[40,640]{1,0:T(8,128)(2,1)S(1)} %get-tuple-element.36.cots_ref, bf16[40,1152]{1,0:T(8,128)(2,1)S(1)} %activate.1.mine_ref, ...), custom_call_target="tpu_custom_call" | custom-call | flops 117964800 | bytes 2949120 | tf_op jit(solution)/shard_map/weight_grads/pallas_call | solution.py:317
  28.4 0.0 collective-permute-done.6.refs_1_
  28.4 0.0 collective-permute-done.7.refs_2_
  28.4 0.2 collective-permute-done.8.refs_3_
  28.6 1.0 %combine.1 = (bf16[128,640]{1,0:T(8,128)(2,1)}, bf16[128,640]{1,0:T(8,128)(2,1)}) custom-call(bf16[24,640]{1,0:T(8,128)(2,1)S(1)} %get-tuple-element.40.refs_0_, bf16[24,640]{1,0:T(8,128)(2,1)S(1)} %collective-permute-done.6.refs_1_, bf16[24,640]{1,0:T(8,128)(2,1)S(1)} %collective-permute-done.7.refs_2_, bf16[24,640]{1,0:T(8,128)(2,1)S(1)} %collective-permute-done.8.refs_3_, ...), custom_call_target="tpu_custom_call" | custom-call | tf_op jit(solution)/shard_map/combine/pallas_call | solution.py:354
  (1 shorter events, 0.0 us)
Async XLA Ops:
  2.0 7.7 %collective-permute-start = (bf16[24,640]{1,0:T(8,128)(2,1)S(1)}, bf16[24,640]{1,0:T(8,128)(2,1)S(1)}, u32[]{:S(2)}, u32[]{:S(2)}) collective-permute-start(bf16[24,640]{1,0:T(8,128)(2,1)S(1)} %get-tuple-element.28), channel_id=1, source_target_pairs={{0,4},{4,0},{8,12},{12,8},{1,5},{5,1},{9,13},{13,9},{2,6},{6,2},{1... | collective-permute-start | bytes 92168 | tf_op jit(solution)/shard_map/ppermute | solution.py:370
  5.1 5.3 %collective-permute-start.1 = (bf16[24,640]{1,0:T(8,128)(2,1)S(1)}, bf16[24,640]{1,0:T(8,128)(2,1)S(1)}, u32[]{:S(2)}, u32[]{:S(2)}) collective-permute-start(bf16[24,640]{1,0:T(8,128)(2,1)S(1)} %get-tuple-element.29), channel_id=1, source_target_pairs={{0,8},{4,12},{8,0},{12,4},{1,9},{5,13},{9,1},{13,5},{2,10},{6,14},... | collective-permute-start | bytes 92168 | tf_op jit(solution)/shard_map/ppermute | solution.py:370
  7.7 5.7 %collective-permute-start.2 = (bf16[24,640]{1,0:T(8,128)(2,1)S(1)}, bf16[24,640]{1,0:T(8,128)(2,1)S(1)}, u32[]{:S(2)}, u32[]{:S(2)}) collective-permute-start(bf16[24,640]{1,0:T(8,128)(2,1)S(1)} %get-tuple-element.30), channel_id=1, source_target_pairs={{0,12},{4,8},{8,4},{12,0},{1,13},{5,9},{9,5},{13,1},{2,14},{6,10},... | collective-permute-start | bytes 92168 | tf_op jit(solution)/shard_map/ppermute | solution.py:370
  13.8 1.4 %collective-permute-start.3 = (bf16[40,1152]{1,0:T(8,128)(2,1)S(1)}, bf16[40,1152]{1,0:T(8,128)(2,1)S(1)}, u32[]{:S(2)}, u32[]{:S(2)}) collective-permute-start(bf16[40,1152]{1,0:T(8,128)(2,1)S(1)} %get-tuple-element.37), channel_id=1, source_target_pairs={{0,1},{1,0},{2,3},{3,2},{4,5},{5,4},{6,7},{7,6},{8,9},{9,8},{10,11... | collective-permute-start | bytes 276488 | tf_op jit(solution)/shard_map/ppermute | solution.py:370
  15.2 4.8 %collective-permute-start.4 = (bf16[40,1152]{1,0:T(8,128)(2,1)S(1)}, bf16[40,1152]{1,0:T(8,128)(2,1)S(1)}, u32[]{:S(2)}, u32[]{:S(2)}) collective-permute-start(bf16[40,1152]{1,0:T(8,128)(2,1)S(1)} %add.1.near_ref), channel_id=1, source_target_pairs={{0,2},{1,3},{2,0},{3,1},{4,6},{5,7},{6,4},{7,5},{8,10},{9,11},{10,... | collective-permute-start | bytes 276488 | tf_op jit(solution)/shard_map/ppermute | solution.py:370
  20.0 1.4 %collective-permute-start.5 = (bf16[40,1152]{1,0:T(8,128)(2,1)S(1)}, bf16[40,1152]{1,0:T(8,128)(2,1)S(1)}, u32[]{:S(2)}, u32[]{:S(2)}) collective-permute-start(bf16[40,1152]{1,0:T(8,128)(2,1)S(1)} %activate.1.mine_ref), channel_id=1, source_target_pairs={{0,1},{1,0},{2,3},{3,2},{4,5},{5,4},{6,7},{7,6},{8,9},{9,8},{10,11... | collective-permute-start | bytes 276488 | tf_op jit(solution)/shard_map/ppermute | solution.py:370
  22.0 6.4 %collective-permute-start.6 = (bf16[24,640]{1,0:T(8,128)(2,1)S(1)}, bf16[24,640]{1,0:T(8,128)(2,1)S(1)}, u32[]{:S(2)}, u32[]{:S(2)}) collective-permute-start(bf16[24,640]{1,0:T(8,128)(2,1)S(1)} %get-tuple-element.41), channel_id=1, source_target_pairs={{0,4},{4,0},{8,12},{12,8},{1,5},{5,1},{9,13},{13,9},{2,6},{6,2},{1... | collective-permute-start | bytes 92168 | tf_op jit(solution)/shard_map/ppermute | solution.py:370
  22.0 6.4 %collective-permute-start.7 = (bf16[24,640]{1,0:T(8,128)(2,1)S(1)}, bf16[24,640]{1,0:T(8,128)(2,1)S(1)}, u32[]{:S(2)}, u32[]{:S(2)}) collective-permute-start(bf16[24,640]{1,0:T(8,128)(2,1)S(1)} %get-tuple-element.42), channel_id=1, source_target_pairs={{0,8},{4,12},{8,0},{12,4},{1,9},{5,13},{9,1},{13,5},{2,10},{6,14},... | collective-permute-start | bytes 92168 | tf_op jit(solution)/shard_map/ppermute | solution.py:370
  22.9 5.7 %collective-permute-start.8 = (bf16[24,640]{1,0:T(8,128)(2,1)S(1)}, bf16[24,640]{1,0:T(8,128)(2,1)S(1)}, u32[]{:S(2)}, u32[]{:S(2)}) collective-permute-start(bf16[24,640]{1,0:T(8,128)(2,1)S(1)} %get-tuple-element.43), channel_id=1, source_target_pairs={{0,12},{4,8},{8,4},{12,0},{1,13},{5,9},{9,5},{13,1},{2,14},{6,10},... | collective-permute-start | bytes 92168 | tf_op jit(solution)/shard_map/ppermute | solution.py:370

commit v6 on v5

--- a/solution.py
+++ b/solution.py
@@ -376,7 +376,8 @@
         blocks = array.reshape(experts, -1, array.shape[1])
         moved = lax.all_to_all(blocks, "expert", split_axis=0, concat_axis=0, tiled=True)
         return [moved.reshape(array.shape)]
-    return [arrays[0]] + [swapped(arrays[d], "expert", d) for d in range(1, experts)]
+    moved = {d: swapped(arrays[d], "expert", d) for d in reversed(range(1, experts))}
+    return [arrays[0]] + [moved[d] for d in range(1, experts)]
 
 
 def shards(

time: 29.8 us -> 29.8 us (level)
  no operation moved by 1% of the time
where the time goes in v6:
time: 29.8 us; the launch traced here: 29.6 us
  starting transfers between devices  11.8 us (40%)
  waiting for transfers between devices  8.72 us (29%)
  Pallas kernels  8.34 us (28%)
  between operations  0.74 us (2%)
    ppermute x9, starting transfers between devices, swapped(): lax.ppermute(array, axis, [(i, i ^ distance) for i in range(lax.axis_size...  11.8 us
    ppermute x9, waiting for transfers between devices, swapped(): lax.ppermute(array, axis, [(i, i ^ distance) for i in range(lax.axis_size...  8.72 us
    pallas_call x6, Pallas kernels, by_rows(): pl.pallas_call(kernel, grid=(steps,), out_shape=tuple((jax.ShapeDtypeStru...  2.03 us
    pallas_call x1, Pallas kernels, load_weights(): pl.pallas_call(load_kernel, out_shape=tuple((pltpu.VMEM(w.shape, BF16) fo...  2 us
    pallas_call x1, Pallas kernels, weight_grads(): pl.pallas_call(grads_kernel, out_shape=tuple((jax.ShapeDtypeStruct(shape,...  1.96 us
    pallas_call x1, Pallas kernels, dispatch(): pl.pallas_call(functools.partial(dispatch_kernel, experts, plan.shape[1],...  1.33 us
    pallas_call x1, Pallas kernels, combine(): pl.pallas_call(functools.partial(combine_kernel, len(backs)), out_shape=(...  1.01 us
  transfers between devices with their start and end apart: 9, of which 6 were waited for; matrix products, arithmetic and copies ran while one was open for 0% of the time, Pallas kernels for 17%

profile of v6, /device:TPU:0, one launch (start us, length us, event | category | flops | bytes accessed | tf_op | source)
XLA Modules:
  0.0 29.6 jit_solution(14543673515331114689)
XLA Ops:
  0.6 1.3 %dispatch.1 = (bf16[24,640]{1,0:T(8,128)(2,1)S(1)}, bf16[24,640]{1,0:T(8,128)(2,1)S(1)}, bf16[24,640]{1,0:T(8,128)(2,1)S(1)}, bf16[24,640]{1,0:T(8,128)(2,1)S(1)}, bf16[3,96,128]{2,1,0:T(8,128)(2,1)S(1)}) custom-call(s32[2,2]{1,0:T(2,128)} %refs_0_.1, s32[4]{0:T(128)} %refs_1_.1, s32[2,128]{1,0:T(2,128)} %bitcast.11, f32[2,128]{1,0:T(2,128)} %bitcast.12, ...), custom_call_target="tpu_custom_call" | custom-call | tf_op jit(solution)/shard_map/dispatch/pallas_call | solution.py:124
  2.0 3.1 %collective-permute-start = (bf16[24,640]{1,0:T(8,128)(2,1)S(1)}, bf16[24,640]{1,0:T(8,128)(2,1)S(1)}, u32[]{:S(2)}, u32[]{:S(2)}) collective-permute-start(bf16[24,640]{1,0:T(8,128)(2,1)S(1)} %get-tuple-element.28), channel_id=1, source_target_pairs={{0,4},{4,0},{8,12},{12,8},{1,5},{5,1},{9,13},{13,9},{2,6},{6,2},{1... | collective-permute-start | bytes 92168 | tf_op jit(solution)/shard_map/ppermute | solution.py:370
  5.1 2.6 %collective-permute-start.1 = (bf16[24,640]{1,0:T(8,128)(2,1)S(1)}, bf16[24,640]{1,0:T(8,128)(2,1)S(1)}, u32[]{:S(2)}, u32[]{:S(2)}) collective-permute-start(bf16[24,640]{1,0:T(8,128)(2,1)S(1)} %get-tuple-element.29), channel_id=1, source_target_pairs={{0,8},{4,12},{8,0},{12,4},{1,9},{5,13},{9,1},{13,5},{2,10},{6,14},... | collective-permute-start | bytes 92168 | tf_op jit(solution)/shard_map/ppermute | solution.py:370
  7.7 0.0 collective-permute-start.2
  7.7 2.0 %load_weights.1 = (bf16[640,768]{1,0:T(8,128)(2,1)S(1)}, bf16[640,768]{1,0:T(8,128)(2,1)S(1)}, bf16[768,640]{1,0:T(8,128)(2,1)S(1)}) custom-call(bf16[640,768]{1,0:T(8,128)(2,1)} %bitcast.8, bf16[640,768]{1,0:T(8,128)(2,1)} %bitcast.9, bf16[768,640]{1,0:T(8,128)(2,1)} %bitcast.10, bf16[3,96,128]{2,1,0:T(8,128)(2,1)S(1)} %get-tuple-element.31.pick_ref.refs_4_), custom_call_target="tpu_custom_call" | custom-call | bytes 5898240 | tf_op jit(solution)/shard_map/load_weights/pallas_call | solution.py:163
  9.7 0.0 collective-permute-done.refs_1_
  9.7 0.7 %collective-permute-done.1.refs_2_ = bf16[24,640]{1,0:T(8,128)(2,1)S(1)} collective-permute-done((bf16[24,640]{1,0:T(8,128)(2,1)S(1)}, bf16[24,640]{1,0:T(8,128)(2,1)S(1)}, u32[]{:S(2)}, u32[]{:S(2)}) %collective-permute-start.1) | collective-permute-done | bytes 30752 | tf_op jit(solution)/shard_map/ppermute | solution.py:370
  10.4 3.0 %collective-permute-done.2.refs_3_ = bf16[24,640]{1,0:T(8,128)(2,1)S(1)} collective-permute-done((bf16[24,640]{1,0:T(8,128)(2,1)S(1)}, bf16[24,640]{1,0:T(8,128)(2,1)S(1)}, u32[]{:S(2)}, u32[]{:S(2)}) %collective-permute-start.2) | collective-permute-done | bytes 30752 | tf_op jit(solution)/shard_map/ppermute | solution.py:370
  13.3 0.5 %give.1 = (bf16[40,640]{1,0:T(8,128)(2,1)S(1)}, bf16[40,640]{1,0:T(8,128)(2,1)S(1)}, bf16[40,1152]{1,0:T(8,128)(2,1)S(1)}) custom-call(bf16[24,640]{1,0:T(8,128)(2,1)S(1)} %get-tuple-element.27.refs_0_, bf16[24,640]{1,0:T(8,128)(2,1)S(1)} %collective-permute-done.refs_1_, bf16[24,640]{1,0:T(8,128)(2,1)S(1)} %collective-permute-done.1.refs_2_, ...), custom_call_target="tpu_custom_call" | custom-call | flops 58982400 | bytes 3072000 | tf_op jit(solution)/shard_map/give/pallas_call | solution.py:265
  13.8 0.1 collective-permute-start.3
  13.9 0.4 %keep.1.left_ref = bf16[40,1152]{1,0:T(8,128)(2,1)S(1)} custom-call(bf16[40,640]{1,0:T(8,128)(2,1)S(1)} %get-tuple-element.35.rows_ref, bf16[40,640]{1,0:T(8,128)(2,1)S(1)} %get-tuple-element.36.cots_ref, bf16[640,768]{1,0:T(8,128)(2,1)S(1)} %get-tuple-element.32.refs_4_.gate_ref.refs_3_, bf16[640,768]{1,0:T(8,128)(2,1)S(1)} %get-tuple-element.33.refs_5_.up_ref.refs_4_, ...), custom_call_target="tpu_custom_call" | custom-call | flops 58982400 | bytes 3051520 | tf_op jit(solution)/shard_map/keep/pallas_call | solution.py:265
  14.3 0.8 %collective-permute-done.3.right_ref = bf16[40,1152]{1,0:T(8,128)(2,1)S(1)} collective-permute-done((bf16[40,1152]{1,0:T(8,128)(2,1)S(1)}, bf16[40,1152]{1,0:T(8,128)(2,1)S(1)}, u32[]{:S(2)}, u32[]{:S(2)}) %collective-permute-start.3) | collective-permute-done | bytes 92192 | tf_op jit(solution)/shard_map/ppermute | solution.py:370
  15.2 1.6 %collective-permute-start.4 = (bf16[40,1152]{1,0:T(8,128)(2,1)S(1)}, bf16[40,1152]{1,0:T(8,128)(2,1)S(1)}, u32[]{:S(2)}, u32[]{:S(2)}) collective-permute-start(bf16[40,1152]{1,0:T(8,128)(2,1)S(1)} %add.1.near_ref), channel_id=1, source_target_pairs={{0,2},{1,3},{2,0},{3,1},{4,6},{5,7},{6,4},{7,5},{8,10},{9,11},{10,... | collective-permute-start | bytes 276488 | tf_op jit(solution)/shard_map/ppermute | solution.py:370
  16.8 3.2 %collective-permute-done.4.far_ref = bf16[40,1152]{1,0:T(8,128)(2,1)S(1)} collective-permute-done((bf16[40,1152]{1,0:T(8,128)(2,1)S(1)}, bf16[40,1152]{1,0:T(8,128)(2,1)S(1)}, u32[]{:S(2)}, u32[]{:S(2)}) %collective-permute-start.4) | collective-permute-done | bytes 92192 | tf_op jit(solution)/shard_map/ppermute | solution.py:370
  20.0 0.1 activate.1.mine_ref
  20.0 0.1 collective-permute-start.5
  20.1 0.5 %own.1 = (f32[40,640]{1,0:T(8,128)S(1)}, f32[40,640]{1,0:T(8,128)S(1)}) custom-call(bf16[40,1152]{1,0:T(8,128)(2,1)S(1)} %activate.1.mine_ref, bf16[640,768]{1,0:T(8,128)(2,1)S(1)} %get-tuple-element.32.refs_4_.gate_ref.refs_3_, bf16[640,768]{1,0:T(8,128)(2,1)S(1)} %get-tuple-element.33.refs_5_.up_ref.refs_4_, ...), custom_call_target="tpu_custom_call" | custom-call | flops 58982400 | bytes 3041280 | tf_op jit(solution)/shard_map/own/pallas_call | solution.py:265
  20.6 0.8 %collective-permute-done.5.refs_0_.theirs_ref = bf16[40,1152]{1,0:T(8,128)(2,1)S(1)} collective-permute-done((bf16[40,1152]{1,0:T(8,128)(2,1)S(1)}, bf16[40,1152]{1,0:T(8,128)(2,1)S(1)}, u32[]{:S(2)}, u32[]{:S(2)}) %collective-permute-start.5) | collective-permute-done | bytes 92192 | tf_op jit(solution)/shard_map/ppermute | solution.py:370
  21.4 0.6 %back.1 = (bf16[24,640]{1,0:T(8,128)(2,1)S(1)}, bf16[24,640]{1,0:T(8,128)(2,1)S(1)}, bf16[24,640]{1,0:T(8,128)(2,1)S(1)}, bf16[24,640]{1,0:T(8,128)(2,1)S(1)}) custom-call(bf16[40,1152]{1,0:T(8,128)(2,1)S(1)} %collective-permute-done.5.refs_0_.theirs_ref, f32[40,640]{1,0:T(8,128)S(1)} %get-tuple-element.38.refs_1_, f32[40,640]{1,0:T(8,128)S(1)} %get-tuple-element.39.refs_2_, ...), custom_call_target="tpu_custom_call" | custom-call | flops 58982400 | bytes 3246080 | tf_op jit(solution)/shard_map/back/pallas_call | solution.py:265
  22.0 0.1 collective-permute-start.6
  22.0 0.9 %collective-permute-start.7 = (bf16[24,640]{1,0:T(8,128)(2,1)S(1)}, bf16[24,640]{1,0:T(8,128)(2,1)S(1)}, u32[]{:S(2)}, u32[]{:S(2)}) collective-permute-start(bf16[24,640]{1,0:T(8,128)(2,1)S(1)} %get-tuple-element.42), channel_id=1, source_target_pairs={{0,8},{4,12},{8,0},{12,4},{1,9},{5,13},{9,1},{13,5},{2,10},{6,14},... | collective-permute-start | bytes 92168 | tf_op jit(solution)/shard_map/ppermute | solution.py:370
  22.9 3.5 %collective-permute-start.8 = (bf16[24,640]{1,0:T(8,128)(2,1)S(1)}, bf16[24,640]{1,0:T(8,128)(2,1)S(1)}, u32[]{:S(2)}, u32[]{:S(2)}) collective-permute-start(bf16[24,640]{1,0:T(8,128)(2,1)S(1)} %get-tuple-element.43), channel_id=1, source_target_pairs={{0,12},{4,8},{8,4},{12,0},{1,13},{5,9},{9,5},{13,1},{2,14},{6,10},... | collective-permute-start | bytes 92168 | tf_op jit(solution)/shard_map/ppermute | solution.py:370
  26.4 2.0 %weight_grads.1 = (bf16[640,768]{1,0:T(8,128)(2,1)}, bf16[640,768]{1,0:T(8,128)(2,1)}, bf16[768,640]{1,0:T(8,128)(2,1)}) custom-call(bf16[40,640]{1,0:T(8,128)(2,1)S(1)} %get-tuple-element.35.rows_ref, bf16[40,640]{1,0:T(8,128)(2,1)S(1)} %get-tuple-element.36.cots_ref, bf16[40,1152]{1,0:T(8,128)(2,1)S(1)} %activate.1.mine_ref, ...), custom_call_target="tpu_custom_call" | custom-call | flops 117964800 | bytes 2949120 | tf_op jit(solution)/shard_map/weight_grads/pallas_call | solution.py:317
  28.4 0.0 collective-permute-done.6.refs_1_
  28.4 0.0 collective-permute-done.7.refs_2_
  28.4 0.2 collective-permute-done.8.refs_3_
  28.6 1.0 %combine.1 = (bf16[128,640]{1,0:T(8,128)(2,1)}, bf16[128,640]{1,0:T(8,128)(2,1)}) custom-call(bf16[24,640]{1,0:T(8,128)(2,1)S(1)} %get-tuple-element.40.refs_0_, bf16[24,640]{1,0:T(8,128)(2,1)S(1)} %collective-permute-done.6.refs_1_, bf16[24,640]{1,0:T(8,128)(2,1)S(1)} %collective-permute-done.7.refs_2_, bf16[24,640]{1,0:T(8,128)(2,1)S(1)} %collective-permute-done.8.refs_3_, ...), custom_call_target="tpu_custom_call" | custom-call | tf_op jit(solution)/shard_map/combine/pallas_call | solution.py:354
  (1 shorter events, 0.0 us)
Async XLA Ops:
  2.0 7.7 %collective-permute-start = (bf16[24,640]{1,0:T(8,128)(2,1)S(1)}, bf16[24,640]{1,0:T(8,128)(2,1)S(1)}, u32[]{:S(2)}, u32[]{:S(2)}) collective-permute-start(bf16[24,640]{1,0:T(8,128)(2,1)S(1)} %get-tuple-element.28), channel_id=1, source_target_pairs={{0,4},{4,0},{8,12},{12,8},{1,5},{5,1},{9,13},{13,9},{2,6},{6,2},{1... | collective-permute-start | bytes 92168 | tf_op jit(solution)/shard_map/ppermute | solution.py:370
  5.1 5.3 %collective-permute-start.1 = (bf16[24,640]{1,0:T(8,128)(2,1)S(1)}, bf16[24,640]{1,0:T(8,128)(2,1)S(1)}, u32[]{:S(2)}, u32[]{:S(2)}) collective-permute-start(bf16[24,640]{1,0:T(8,128)(2,1)S(1)} %get-tuple-element.29), channel_id=1, source_target_pairs={{0,8},{4,12},{8,0},{12,4},{1,9},{5,13},{9,1},{13,5},{2,10},{6,14},... | collective-permute-start | bytes 92168 | tf_op jit(solution)/shard_map/ppermute | solution.py:370
  7.7 5.7 %collective-permute-start.2 = (bf16[24,640]{1,0:T(8,128)(2,1)S(1)}, bf16[24,640]{1,0:T(8,128)(2,1)S(1)}, u32[]{:S(2)}, u32[]{:S(2)}) collective-permute-start(bf16[24,640]{1,0:T(8,128)(2,1)S(1)} %get-tuple-element.30), channel_id=1, source_target_pairs={{0,12},{4,8},{8,4},{12,0},{1,13},{5,9},{9,5},{13,1},{2,14},{6,10},... | collective-permute-start | bytes 92168 | tf_op jit(solution)/shard_map/ppermute | solution.py:370
  13.8 1.4 %collective-permute-start.3 = (bf16[40,1152]{1,0:T(8,128)(2,1)S(1)}, bf16[40,1152]{1,0:T(8,128)(2,1)S(1)}, u32[]{:S(2)}, u32[]{:S(2)}) collective-permute-start(bf16[40,1152]{1,0:T(8,128)(2,1)S(1)} %get-tuple-element.37), channel_id=1, source_target_pairs={{0,1},{1,0},{2,3},{3,2},{4,5},{5,4},{6,7},{7,6},{8,9},{9,8},{10,11... | collective-permute-start | bytes 276488 | tf_op jit(solution)/shard_map/ppermute | solution.py:370
  15.2 4.8 %collective-permute-start.4 = (bf16[40,1152]{1,0:T(8,128)(2,1)S(1)}, bf16[40,1152]{1,0:T(8,128)(2,1)S(1)}, u32[]{:S(2)}, u32[]{:S(2)}) collective-permute-start(bf16[40,1152]{1,0:T(8,128)(2,1)S(1)} %add.1.near_ref), channel_id=1, source_target_pairs={{0,2},{1,3},{2,0},{3,1},{4,6},{5,7},{6,4},{7,5},{8,10},{9,11},{10,... | collective-permute-start | bytes 276488 | tf_op jit(solution)/shard_map/ppermute | solution.py:370
  20.0 1.4 %collective-permute-start.5 = (bf16[40,1152]{1,0:T(8,128)(2,1)S(1)}, bf16[40,1152]{1,0:T(8,128)(2,1)S(1)}, u32[]{:S(2)}, u32[]{:S(2)}) collective-permute-start(bf16[40,1152]{1,0:T(8,128)(2,1)S(1)} %activate.1.mine_ref), channel_id=1, source_target_pairs={{0,1},{1,0},{2,3},{3,2},{4,5},{5,4},{6,7},{7,6},{8,9},{9,8},{10,11... | collective-permute-start | bytes 276488 | tf_op jit(solution)/shard_map/ppermute | solution.py:370
  22.0 6.4 %collective-permute-start.6 = (bf16[24,640]{1,0:T(8,128)(2,1)S(1)}, bf16[24,640]{1,0:T(8,128)(2,1)S(1)}, u32[]{:S(2)}, u32[]{:S(2)}) collective-permute-start(bf16[24,640]{1,0:T(8,128)(2,1)S(1)} %get-tuple-element.41), channel_id=1, source_target_pairs={{0,4},{4,0},{8,12},{12,8},{1,5},{5,1},{9,13},{13,9},{2,6},{6,2},{1... | collective-permute-start | bytes 92168 | tf_op jit(solution)/shard_map/ppermute | solution.py:370
  22.0 6.4 %collective-permute-start.7 = (bf16[24,640]{1,0:T(8,128)(2,1)S(1)}, bf16[24,640]{1,0:T(8,128)(2,1)S(1)}, u32[]{:S(2)}, u32[]{:S(2)}) collective-permute-start(bf16[24,640]{1,0:T(8,128)(2,1)S(1)} %get-tuple-element.42), channel_id=1, source_target_pairs={{0,8},{4,12},{8,0},{12,4},{1,9},{5,13},{9,1},{13,5},{2,10},{6,14},... | collective-permute-start | bytes 92168 | tf_op jit(solution)/shard_map/ppermute | solution.py:370
  22.9 5.7 %collective-permute-start.8 = (bf16[24,640]{1,0:T(8,128)(2,1)S(1)}, bf16[24,640]{1,0:T(8,128)(2,1)S(1)}, u32[]{:S(2)}, u32[]{:S(2)}) collective-permute-start(bf16[24,640]{1,0:T(8,128)(2,1)S(1)} %get-tuple-element.43), channel_id=1, source_target_pairs={{0,12},{4,8},{8,4},{12,0},{1,13},{5,9},{9,5},{13,1},{2,14},{6,10},... | collective-permute-start | bytes 92168 | tf_op jit(solution)/shard_map/ppermute | solution.py:370

commit v7 on v5

--- a/solution.py
+++ b/solution.py
@@ -37,6 +37,10 @@
 
 def spans(extent, size):
     return [(start, min(size, extent - start)) for start in range(0, extent, size)]
+
+
+def distance(index, experts):
+    return (experts - index) % experts
 
 
 def dispatch_kernel(experts, hosts, slots, block, pieces, *refs):
@@ -79,7 +83,7 @@
         copy.wait()
     members, weights, limits = [], [], []
     for index in range(experts):
-        expert = index if pieces == 1 else me ^ index
+        expert = index if pieces == 1 else me ^ distance(index, experts)
         hot = (plan_ref[0, 0] == expert) | (plan_ref[1, 0] == expert)
         wanted = token_slot * hot.astype(I32)
         here = jnp.zeros((1, count), F32)
@@ -376,7 +380,8 @@
         blocks = array.reshape(experts, -1, array.shape[1])
         moved = lax.all_to_all(blocks, "expert", split_axis=0, concat_axis=0, tiled=True)
         return [moved.reshape(array.shape)]
-    return [arrays[0]] + [swapped(arrays[d], "expert", d) for d in range(1, experts)]
+    moved = [swapped(arrays[i], "expert", distance(i, experts)) for i in range(1, experts)]
+    return [arrays[0]] + moved
 
 
 def shards(
@@ -433,11 +438,11 @@
         keep_kernel, "keep", steps, [rows, cots], weights, [((total, half), BF16)], (), flops
     )
     near = by_rows(add_kernel, "add", steps, [keep, got], [], [((total, half), BF16)])
-    distance, last = 2, lax.axis_size("dp") // 2
-    while distance < last:
-        far = swapped(near, "dp", distance)
+    step, last = 2, lax.axis_size("dp") // 2
+    while step < last:
+        far = swapped(near, "dp", step)
         near = by_rows(add_kernel, "add", steps, [near, far], [], [((total, half), BF16)])
-        distance *= 2
+        step *= 2
     far = swapped(near, "dp", last)
     mine = by_rows(activate_kernel, "activate", steps, [near, far], [], [((total, half), BF16)])
     theirs = swapped(mine, "dp", 1)

time: 29.8 us -> 28.4 us (0.953)
  waiting for transfers between devices: 8.72 us -> 7.23 us
    ppermute x9, waiting for transfers between devices: 8.72 us -> 7.23 us  [swapped(): lax.ppermute(array, axis, [(i, i ^ distance) for i in range(lax.axis_size...]
where the time goes in v7:
time: 28.4 us; the launch traced here: 28.2 us
  starting transfers between devices  11.9 us (42%)
  Pallas kernels  8.33 us (29%)
  waiting for transfers between devices  7.23 us (25%)
  between operations  0.73 us (3%)
    ppermute x9, starting transfers between devices, swapped(): lax.ppermute(array, axis, [(i, i ^ distance) for i in range(lax.axis_size...  11.9 us
    ppermute x9, waiting for transfers between devices, swapped(): lax.ppermute(array, axis, [(i, i ^ distance) for i in range(lax.axis_size...  7.23 us
    pallas_call x6, Pallas kernels, by_rows(): pl.pallas_call(kernel, grid=(steps,), out_shape=tuple((jax.ShapeDtypeStru...  2.03 us
    pallas_call x1, Pallas kernels, load_weights(): pl.pallas_call(load_kernel, out_shape=tuple((pltpu.VMEM(w.shape, BF16) fo...  2 us
    pallas_call x1, Pallas kernels, weight_grads(): pl.pallas_call(grads_kernel, out_shape=tuple((jax.ShapeDtypeStruct(shape,...  1.96 us
    pallas_call x1, Pallas kernels, dispatch(): pl.pallas_call(functools.partial(dispatch_kernel, experts, plan.shape[1],...  1.33 us
    pallas_call x1, Pallas kernels, combine(): pl.pallas_call(functools.partial(combine_kernel, len(backs)), out_shape=(...  1 us
  transfers between devices with their start and end apart: 9, of which 6 were waited for; matrix products, arithmetic and copies ran while one was open for 0% of the time, Pallas kernels for 17%

profile of v7, /device:TPU:0, one launch (start us, length us, event | category | flops | bytes accessed | tf_op | source)
XLA Modules:
  0.0 28.2 jit_solution(16966220491622362735)
XLA Ops:
  0.6 1.3 %dispatch.1 = (bf16[24,640]{1,0:T(8,128)(2,1)S(1)}, bf16[24,640]{1,0:T(8,128)(2,1)S(1)}, bf16[24,640]{1,0:T(8,128)(2,1)S(1)}, bf16[24,640]{1,0:T(8,128)(2,1)S(1)}, bf16[3,96,128]{2,1,0:T(8,128)(2,1)S(1)}) custom-call(s32[2,2]{1,0:T(2,128)} %refs_0_.1, s32[4]{0:T(128)} %refs_1_.1, s32[2,128]{1,0:T(2,128)} %bitcast.11, f32[2,128]{1,0:T(2,128)} %bitcast.12, ...), custom_call_target="tpu_custom_call" | custom-call | tf_op jit(solution)/shard_map/dispatch/pallas_call | solution.py:128
  2.0 5.1 %collective-permute-start = (bf16[24,640]{1,0:T(8,128)(2,1)S(1)}, bf16[24,640]{1,0:T(8,128)(2,1)S(1)}, u32[]{:S(2)}, u32[]{:S(2)}) collective-permute-start(bf16[24,640]{1,0:T(8,128)(2,1)S(1)} %get-tuple-element.28), channel_id=1, source_target_pairs={{0,12},{4,8},{8,4},{12,0},{1,13},{5,9},{9,5},{13,1},{2,14},{6,10},... | collective-permute-start | bytes 92168 | tf_op jit(solution)/shard_map/ppermute | solution.py:374
  7.1 0.0 collective-permute-start.1
  7.1 0.6 %collective-permute-start.2 = (bf16[24,640]{1,0:T(8,128)(2,1)S(1)}, bf16[24,640]{1,0:T(8,128)(2,1)S(1)}, u32[]{:S(2)}, u32[]{:S(2)}) collective-permute-start(bf16[24,640]{1,0:T(8,128)(2,1)S(1)} %get-tuple-element.30), channel_id=1, source_target_pairs={{0,4},{4,0},{8,12},{12,8},{1,5},{5,1},{9,13},{13,9},{2,6},{6,2},{1... | collective-permute-start | bytes 92168 | tf_op jit(solution)/shard_map/ppermute | solution.py:374
  7.7 2.0 %load_weights.1 = (bf16[640,768]{1,0:T(8,128)(2,1)S(1)}, bf16[640,768]{1,0:T(8,128)(2,1)S(1)}, bf16[768,640]{1,0:T(8,128)(2,1)S(1)}) custom-call(bf16[640,768]{1,0:T(8,128)(2,1)} %bitcast.8, bf16[640,768]{1,0:T(8,128)(2,1)} %bitcast.9, bf16[768,640]{1,0:T(8,128)(2,1)} %bitcast.10, bf16[3,96,128]{2,1,0:T(8,128)(2,1)S(1)} %get-tuple-element.31.pick_ref.refs_4_), custom_call_target="tpu_custom_call" | custom-call | bytes 5898240 | tf_op jit(solution)/shard_map/load_weights/pallas_call | solution.py:167
  9.7 0.0 collective-permute-done.refs_1_
  9.8 2.1 %collective-permute-done.1.refs_2_ = bf16[24,640]{1,0:T(8,128)(2,1)S(1)} collective-permute-done((bf16[24,640]{1,0:T(8,128)(2,1)S(1)}, bf16[24,640]{1,0:T(8,128)(2,1)S(1)}, u32[]{:S(2)}, u32[]{:S(2)}) %collective-permute-start.1) | collective-permute-done | bytes 30752 | tf_op jit(solution)/shard_map/ppermute | solution.py:374
  11.9 0.0 collective-permute-done.2.refs_3_
  11.9 0.5 %give.1 = (bf16[40,640]{1,0:T(8,128)(2,1)S(1)}, bf16[40,640]{1,0:T(8,128)(2,1)S(1)}, bf16[40,1152]{1,0:T(8,128)(2,1)S(1)}) custom-call(bf16[24,640]{1,0:T(8,128)(2,1)S(1)} %get-tuple-element.27.refs_0_, bf16[24,640]{1,0:T(8,128)(2,1)S(1)} %collective-permute-done.refs_1_, bf16[24,640]{1,0:T(8,128)(2,1)S(1)} %collective-permute-done.1.refs_2_, ...), custom_call_target="tpu_custom_call" | custom-call | flops 58982400 | bytes 3072000 | tf_op jit(solution)/shard_map/give/pallas_call | solution.py:269
  12.4 0.1 collective-permute-start.3
  12.4 0.4 %keep.1.left_ref = bf16[40,1152]{1,0:T(8,128)(2,1)S(1)} custom-call(bf16[40,640]{1,0:T(8,128)(2,1)S(1)} %get-tuple-element.35.rows_ref, bf16[40,640]{1,0:T(8,128)(2,1)S(1)} %get-tuple-element.36.cots_ref, bf16[640,768]{1,0:T(8,128)(2,1)S(1)} %get-tuple-element.32.refs_4_.gate_ref.refs_3_, bf16[640,768]{1,0:T(8,128)(2,1)S(1)} %get-tuple-element.33.refs_5_.up_ref.refs_4_, ...), custom_call_target="tpu_custom_call" | custom-call | flops 58982400 | bytes 3051520 | tf_op jit(solution)/shard_map/keep/pallas_call | solution.py:269
  12.9 0.8 %collective-permute-done.3.right_ref = bf16[40,1152]{1,0:T(8,128)(2,1)S(1)} collective-permute-done((bf16[40,1152]{1,0:T(8,128)(2,1)S(1)}, bf16[40,1152]{1,0:T(8,128)(2,1)S(1)}, u32[]{:S(2)}, u32[]{:S(2)}) %collective-permute-start.3) | collective-permute-done | bytes 92192 | tf_op jit(solution)/shard_map/ppermute | solution.py:374
  13.7 1.6 %collective-permute-start.4 = (bf16[40,1152]{1,0:T(8,128)(2,1)S(1)}, bf16[40,1152]{1,0:T(8,128)(2,1)S(1)}, u32[]{:S(2)}, u32[]{:S(2)}) collective-permute-start(bf16[40,1152]{1,0:T(8,128)(2,1)S(1)} %add.1.near_ref), channel_id=1, source_target_pairs={{0,2},{1,3},{2,0},{3,1},{4,6},{5,7},{6,4},{7,5},{8,10},{9,11},{10,... | collective-permute-start | bytes 276488 | tf_op jit(solution)/shard_map/ppermute | solution.py:374
  15.3 3.2 %collective-permute-done.4.far_ref = bf16[40,1152]{1,0:T(8,128)(2,1)S(1)} collective-permute-done((bf16[40,1152]{1,0:T(8,128)(2,1)S(1)}, bf16[40,1152]{1,0:T(8,128)(2,1)S(1)}, u32[]{:S(2)}, u32[]{:S(2)}) %collective-permute-start.4) | collective-permute-done | bytes 92192 | tf_op jit(solution)/shard_map/ppermute | solution.py:374
  18.5 0.1 activate.1.mine_ref
  18.6 0.1 collective-permute-start.5
  18.7 0.5 %own.1 = (f32[40,640]{1,0:T(8,128)S(1)}, f32[40,640]{1,0:T(8,128)S(1)}) custom-call(bf16[40,1152]{1,0:T(8,128)(2,1)S(1)} %activate.1.mine_ref, bf16[640,768]{1,0:T(8,128)(2,1)S(1)} %get-tuple-element.32.refs_4_.gate_ref.refs_3_, bf16[640,768]{1,0:T(8,128)(2,1)S(1)} %get-tuple-element.33.refs_5_.up_ref.refs_4_, ...), custom_call_target="tpu_custom_call" | custom-call | flops 58982400 | bytes 3041280 | tf_op jit(solution)/shard_map/own/pallas_call | solution.py:269
  19.2 0.8 %collective-permute-done.5.refs_0_.theirs_ref = bf16[40,1152]{1,0:T(8,128)(2,1)S(1)} collective-permute-done((bf16[40,1152]{1,0:T(8,128)(2,1)S(1)}, bf16[40,1152]{1,0:T(8,128)(2,1)S(1)}, u32[]{:S(2)}, u32[]{:S(2)}) %collective-permute-start.5) | collective-permute-done | bytes 92192 | tf_op jit(solution)/shard_map/ppermute | solution.py:374
  19.9 0.6 %back.1 = (bf16[24,640]{1,0:T(8,128)(2,1)S(1)}, bf16[24,640]{1,0:T(8,128)(2,1)S(1)}, bf16[24,640]{1,0:T(8,128)(2,1)S(1)}, bf16[24,640]{1,0:T(8,128)(2,1)S(1)}) custom-call(bf16[40,1152]{1,0:T(8,128)(2,1)S(1)} %collective-permute-done.5.refs_0_.theirs_ref, f32[40,640]{1,0:T(8,128)S(1)} %get-tuple-element.38.refs_1_, f32[40,640]{1,0:T(8,128)S(1)} %get-tuple-element.39.refs_2_, ...), custom_call_target="tpu_custom_call" | custom-call | flops 58982400 | bytes 3246080 | tf_op jit(solution)/shard_map/back/pallas_call | solution.py:269
  20.5 1.7 %collective-permute-start.6 = (bf16[24,640]{1,0:T(8,128)(2,1)S(1)}, bf16[24,640]{1,0:T(8,128)(2,1)S(1)}, u32[]{:S(2)}, u32[]{:S(2)}) collective-permute-start(bf16[24,640]{1,0:T(8,128)(2,1)S(1)} %get-tuple-element.41), channel_id=1, source_target_pairs={{0,12},{4,8},{8,4},{12,0},{1,13},{5,9},{9,5},{13,1},{2,14},{6,10},... | collective-permute-start | bytes 92168 | tf_op jit(solution)/shard_map/ppermute | solution.py:374
  22.2 0.5 %collective-permute-start.7 = (bf16[24,640]{1,0:T(8,128)(2,1)S(1)}, bf16[24,640]{1,0:T(8,128)(2,1)S(1)}, u32[]{:S(2)}, u32[]{:S(2)}) collective-permute-start(bf16[24,640]{1,0:T(8,128)(2,1)S(1)} %get-tuple-element.42), channel_id=1, source_target_pairs={{0,8},{4,12},{8,0},{12,4},{1,9},{5,13},{9,1},{13,5},{2,10},{6,14},... | collective-permute-start | bytes 92168 | tf_op jit(solution)/shard_map/ppermute | solution.py:374
  22.7 2.3 %collective-permute-start.8 = (bf16[24,640]{1,0:T(8,128)(2,1)S(1)}, bf16[24,640]{1,0:T(8,128)(2,1)S(1)}, u32[]{:S(2)}, u32[]{:S(2)}) collective-permute-start(bf16[24,640]{1,0:T(8,128)(2,1)S(1)} %get-tuple-element.43), channel_id=1, source_target_pairs={{0,4},{4,0},{8,12},{12,8},{1,5},{5,1},{9,13},{13,9},{2,6},{6,2},{1... | collective-permute-start | bytes 92168 | tf_op jit(solution)/shard_map/ppermute | solution.py:374
  25.0 2.0 %weight_grads.1 = (bf16[640,768]{1,0:T(8,128)(2,1)}, bf16[640,768]{1,0:T(8,128)(2,1)}, bf16[768,640]{1,0:T(8,128)(2,1)}) custom-call(bf16[40,640]{1,0:T(8,128)(2,1)S(1)} %get-tuple-element.35.rows_ref, bf16[40,640]{1,0:T(8,128)(2,1)S(1)} %get-tuple-element.36.cots_ref, bf16[40,1152]{1,0:T(8,128)(2,1)S(1)} %activate.1.mine_ref, ...), custom_call_target="tpu_custom_call" | custom-call | flops 117964800 | bytes 2949120 | tf_op jit(solution)/shard_map/weight_grads/pallas_call | solution.py:321
  26.9 0.0 collective-permute-done.6.refs_1_
  26.9 0.1 collective-permute-done.7.refs_2_
  27.0 0.1 collective-permute-done.8.refs_3_
  27.2 1.0 %combine.1 = (bf16[128,640]{1,0:T(8,128)(2,1)}, bf16[128,640]{1,0:T(8,128)(2,1)}) custom-call(bf16[24,640]{1,0:T(8,128)(2,1)S(1)} %get-tuple-element.40.refs_0_, bf16[24,640]{1,0:T(8,128)(2,1)S(1)} %collective-permute-done.6.refs_1_, bf16[24,640]{1,0:T(8,128)(2,1)S(1)} %collective-permute-done.7.refs_2_, bf16[24,640]{1,0:T(8,128)(2,1)S(1)} %collective-permute-done.8.refs_3_, ...), custom_call_target="tpu_custom_call" | custom-call | tf_op jit(solution)/shard_map/combine/pallas_call | solution.py:358
  (1 shorter events, 0.0 us)
Async XLA Ops:
  2.0 7.8 %collective-permute-start = (bf16[24,640]{1,0:T(8,128)(2,1)S(1)}, bf16[24,640]{1,0:T(8,128)(2,1)S(1)}, u32[]{:S(2)}, u32[]{:S(2)}) collective-permute-start(bf16[24,640]{1,0:T(8,128)(2,1)S(1)} %get-tuple-element.28), channel_id=1, source_target_pairs={{0,12},{4,8},{8,4},{12,0},{1,13},{5,9},{9,5},{13,1},{2,14},{6,10},... | collective-permute-start | bytes 92168 | tf_op jit(solution)/shard_map/ppermute | solution.py:374
  7.1 4.8 %collective-permute-start.1 = (bf16[24,640]{1,0:T(8,128)(2,1)S(1)}, bf16[24,640]{1,0:T(8,128)(2,1)S(1)}, u32[]{:S(2)}, u32[]{:S(2)}) collective-permute-start(bf16[24,640]{1,0:T(8,128)(2,1)S(1)} %get-tuple-element.29), channel_id=1, source_target_pairs={{0,8},{4,12},{8,0},{12,4},{1,9},{5,13},{9,1},{13,5},{2,10},{6,14},... | collective-permute-start | bytes 92168 | tf_op jit(solution)/shard_map/ppermute | solution.py:374
  7.1 4.8 %collective-permute-start.2 = (bf16[24,640]{1,0:T(8,128)(2,1)S(1)}, bf16[24,640]{1,0:T(8,128)(2,1)S(1)}, u32[]{:S(2)}, u32[]{:S(2)}) collective-permute-start(bf16[24,640]{1,0:T(8,128)(2,1)S(1)} %get-tuple-element.30), channel_id=1, source_target_pairs={{0,4},{4,0},{8,12},{12,8},{1,5},{5,1},{9,13},{13,9},{2,6},{6,2},{1... | collective-permute-start | bytes 92168 | tf_op jit(solution)/shard_map/ppermute | solution.py:374
  12.4 1.4 %collective-permute-start.3 = (bf16[40,1152]{1,0:T(8,128)(2,1)S(1)}, bf16[40,1152]{1,0:T(8,128)(2,1)S(1)}, u32[]{:S(2)}, u32[]{:S(2)}) collective-permute-start(bf16[40,1152]{1,0:T(8,128)(2,1)S(1)} %get-tuple-element.37), channel_id=1, source_target_pairs={{0,1},{1,0},{2,3},{3,2},{4,5},{5,4},{6,7},{7,6},{8,9},{9,8},{10,11... | collective-permute-start | bytes 276488 | tf_op jit(solution)/shard_map/ppermute | solution.py:374
  13.7 4.8 %collective-permute-start.4 = (bf16[40,1152]{1,0:T(8,128)(2,1)S(1)}, bf16[40,1152]{1,0:T(8,128)(2,1)S(1)}, u32[]{:S(2)}, u32[]{:S(2)}) collective-permute-start(bf16[40,1152]{1,0:T(8,128)(2,1)S(1)} %add.1.near_ref), channel_id=1, source_target_pairs={{0,2},{1,3},{2,0},{3,1},{4,6},{5,7},{6,4},{7,5},{8,10},{9,11},{10,... | collective-permute-start | bytes 276488 | tf_op jit(solution)/shard_map/ppermute | solution.py:374
  18.6 1.4 %collective-permute-start.5 = (bf16[40,1152]{1,0:T(8,128)(2,1)S(1)}, bf16[40,1152]{1,0:T(8,128)(2,1)S(1)}, u32[]{:S(2)}, u32[]{:S(2)}) collective-permute-start(bf16[40,1152]{1,0:T(8,128)(2,1)S(1)} %activate.1.mine_ref), channel_id=1, source_target_pairs={{0,1},{1,0},{2,3},{3,2},{4,5},{5,4},{6,7},{7,6},{8,9},{9,8},{10,11... | collective-permute-start | bytes 276488 | tf_op jit(solution)/shard_map/ppermute | solution.py:374
  20.5 6.4 %collective-permute-start.6 = (bf16[24,640]{1,0:T(8,128)(2,1)S(1)}, bf16[24,640]{1,0:T(8,128)(2,1)S(1)}, u32[]{:S(2)}, u32[]{:S(2)}) collective-permute-start(bf16[24,640]{1,0:T(8,128)(2,1)S(1)} %get-tuple-element.41), channel_id=1, source_target_pairs={{0,12},{4,8},{8,4},{12,0},{1,13},{5,9},{9,5},{13,1},{2,14},{6,10},... | collective-permute-start | bytes 92168 | tf_op jit(solution)/shard_map/ppermute | solution.py:374
  22.2 4.8 %collective-permute-start.7 = (bf16[24,640]{1,0:T(8,128)(2,1)S(1)}, bf16[24,640]{1,0:T(8,128)(2,1)S(1)}, u32[]{:S(2)}, u32[]{:S(2)}) collective-permute-start(bf16[24,640]{1,0:T(8,128)(2,1)S(1)} %get-tuple-element.42), channel_id=1, source_target_pairs={{0,8},{4,12},{8,0},{12,4},{1,9},{5,13},{9,1},{13,5},{2,10},{6,14},... | collective-permute-start | bytes 92168 | tf_op jit(solution)/shard_map/ppermute | solution.py:374
  22.7 4.5 %collective-permute-start.8 = (bf16[24,640]{1,0:T(8,128)(2,1)S(1)}, bf16[24,640]{1,0:T(8,128)(2,1)S(1)}, u32[]{:S(2)}, u32[]{:S(2)}) collective-permute-start(bf16[24,640]{1,0:T(8,128)(2,1)S(1)} %get-tuple-element.43), channel_id=1, source_target_pairs={{0,4},{4,0},{8,12},{12,8},{1,5},{5,1},{9,13},{13,9},{2,6},{6,2},{1... | collective-permute-start | bytes 92168 | tf_op jit(solution)/shard_map/ppermute | solution.py:374

commit v8 on v7

--- a/solution.py
+++ b/solution.py
@@ -45,8 +45,9 @@
 
 def dispatch_kernel(experts, hosts, slots, block, pieces, *refs):
     plan_hbm, caps_hbm, ids_hbm, gates_hbm, tok_hbm, grad_hbm = refs[:6]
-    send_refs, pick_ref = refs[6 : 6 + pieces], refs[6 + pieces]
-    plan_ref, caps_ref, ids_ref, gates_ref, tok_ref, grad_ref, sems = refs[7 + pieces :]
+    send_refs = refs[6 : 6 + pieces]
+    scaled_ref, pick_ref, plan_ref, caps_ref, ids_ref, gates_ref, both_ref, sems = refs[6 + pieces :]
+    choose, count = ids_ref.shape
     copies = [
         pltpu.make_async_copy(source, target, sems.at[i])
         for i, (source, target) in enumerate(
@@ -55,15 +56,14 @@
                 (plan_hbm, plan_ref),
                 (caps_hbm, caps_ref),
                 (gates_hbm, gates_ref),
-                (tok_hbm, tok_ref),
-                (grad_hbm, grad_ref),
+                (tok_hbm, both_ref.at[pl.ds(0, count)]),
+                (grad_hbm, both_ref.at[pl.ds(count, count)]),
             )
         )
     ]
     for copy in copies:
         copy.start()
     me = lax.axis_index("expert")
-    choose, count = ids_ref.shape
     row = lax.broadcasted_iota(I32, (block, count), 0)
     col = lax.broadcasted_iota(I32, (block, count), 1)
     is_cot = row >= slots
@@ -104,18 +104,14 @@
     taken = jnp.where(before == limit, member, 0.0)
     pick_cot = taken * cots
     pick_tok = taken - pick_cot
-    gate = jnp.sum(taken * weight, axis=1, keepdims=True)
-    scaled = pick_tok * weight
-    high = scaled.astype(BF16)
-    pick_cot = pick_cot.astype(BF16)
-    pick_ref[0] = high
-    pick_ref[1] = (scaled - high.astype(F32)).astype(BF16)
-    pick_ref[2] = pick_cot
+    picks = jnp.concatenate([pick_tok.astype(BF16), pick_cot.astype(BF16)], axis=1)
+    gate = jnp.sum(pick_cot * weight, axis=1, keepdims=True)
+    scale = jnp.where(cots[:, :1] > 0.0, gate, 1.0)
+    scaled_ref[...] = pick_tok * weight
+    pick_ref[...] = pick_cot
     for copy in copies[4:]:
         copy.wait()
-    rows = matmul(pick_tok.astype(BF16), tok_ref[...], 1, 0)
-    cotangents = gate * matmul(pick_cot, grad_ref[...], 1, 0)
-    send = (rows + cotangents).astype(BF16)
+    send = (scale * matmul(picks, both_ref[...], 1, 0)).astype(BF16)
     size = send.shape[0] // pieces
     for i, send_ref in enumerate(send_refs):
         send_ref[...] = send[i * size : (i + 1) * size]
@@ -128,25 +124,26 @@
     outs = pl.pallas_call(
         functools.partial(dispatch_kernel, experts, plan.shape[1], slots, block, pieces),
         out_shape=(jax.ShapeDtypeStruct((size, feature), BF16),) * pieces
-        + (jax.ShapeDtypeStruct((3, experts * block, count), BF16),),
+        + (jax.ShapeDtypeStruct((experts * block, count), F32),) * 2,
         in_specs=[pl.BlockSpec(memory_space=pltpu.HBM)] * 6,
-        out_specs=(vmem,) * (pieces + 1),
+        out_specs=(vmem,) * (pieces + 2),
         scratch_shapes=[
             pltpu.SMEM(plan.shape, I32),
             pltpu.SMEM(caps.shape, I32),
             pltpu.VMEM(ids.shape, I32),
             pltpu.VMEM(gates.shape, F32),
-            pltpu.VMEM(tokens.shape, BF16),
-            pltpu.VMEM(grads.shape, BF16),
+            pltpu.VMEM((2 * count, feature), BF16),
             pltpu.SemaphoreType.DMA((6,)),
         ],
         compiler_params=params(),
         name="dispatch",
     )(*(in_hbm(array) for array in (plan, caps, ids, gates, tokens, grads)))
-    return outs[:pieces], outs[pieces]
-
-
-def load_kernel(gate_hbm, up_hbm, down_hbm, pick_ref, gate_ref, up_ref, down_ref, sems):
+    return outs[:pieces], outs[pieces:]
+
+
+def load_kernel(
+    gate_hbm, up_hbm, down_hbm, scaled_ref, pick_ref, gate_ref, up_ref, down_ref, merge_ref, sems
+):
     copies = []
     for source, target in ((gate_hbm, gate_ref), (up_hbm, up_ref), (down_hbm, down_ref)):
         for start, size in spans(source.shape[0], source.shape[0] // LOADS):
@@ -156,26 +153,33 @@
             )
     for copy in copies:
         copy.start()
+    scaled = scaled_ref[...].T
+    count = scaled.shape[0]
+    high = scaled.astype(BF16)
+    merge_ref[:count, :] = high
+    merge_ref[count : 2 * count, :] = (scaled - high.astype(F32)).astype(BF16)
+    merge_ref[2 * count :, :] = pick_ref[...].T.astype(BF16)
     for copy in copies:
         copy.wait()
 
 
-def load_weights(gate, up, down, pick):
+def load_weights(gate, up, down, scaled, pick):
     hbm = pl.BlockSpec(memory_space=pltpu.HBM)
     vmem = pl.BlockSpec(memory_space=pltpu.VMEM)
     assert all(w.shape[0] % (16 * LOADS) == 0 for w in (gate, up, down))
+    merge = jax.ShapeDtypeStruct((3 * pick.shape[1], pick.shape[0]), BF16)
     return pl.pallas_call(
         load_kernel,
-        out_shape=tuple(pltpu.VMEM(w.shape, BF16) for w in (gate, up, down)),
-        in_specs=[hbm, hbm, hbm, pl.BlockSpec(memory_space=pl.ANY)],
-        out_specs=(vmem, vmem, vmem),
+        out_shape=tuple(pltpu.VMEM(w.shape, BF16) for w in (gate, up, down)) + (merge,),
+        in_specs=[hbm, hbm, hbm, vmem, vmem],
+        out_specs=(vmem,) * 4,
         scratch_shapes=[pltpu.SemaphoreType.DMA((3 * LOADS,))],
         compiler_params=params(),
         cost_estimate=pl.CostEstimate(
             flops=0, bytes_accessed=2 * 3 * gate.size * 2, transcendentals=0
         ),
         name="load_weights",
-    )(in_hbm(gate), in_hbm(up), in_hbm(down), pick)
+    )(in_hbm(gate), in_hbm(up), in_hbm(down), scaled, pick)
 
 
 def half_columns(which, width):
@@ -335,39 +339,47 @@
     )(rows, cots, mine, theirs)
 
 
-def combine_kernel(pieces, *refs):
+def combine_kernel(columns, pieces, *refs):
     back_refs = refs[:pieces]
-    pick_ref, mixed_hbm, token_hbm, mixed_ref, token_ref, sems = refs[pieces:]
-    back = jnp.concatenate([back_ref[...] for back_ref in back_refs], axis=0)
-    token_ref[...] = matmul(pick_ref[2], back, 0, 0).astype(BF16)
-    token_copy = pltpu.make_async_copy(token_ref, token_hbm, sems.at[0])
-    token_copy.start()
-    mixed = matmul(pick_ref[0], back, 0, 0) + matmul(pick_ref[1], back, 0, 0)
-    mixed_ref[...] = mixed.astype(BF16)
-    mixed_copy = pltpu.make_async_copy(mixed_ref, mixed_hbm, sems.at[1])
-    mixed_copy.start()
-    token_copy.wait()
-    mixed_copy.wait()
-
-
-def combine(backs, pick):
-    feature, count = backs[0].shape[1], pick.shape[2]
+    merge_ref, mixed_hbm, token_hbm, mixed_ref, token_ref, sems = refs[pieces:]
+    count = mixed_ref.shape[0]
+    copies = []
+    for start, size in columns:
+        part = pl.ds(start, size)
+        back = jnp.concatenate([back_ref[:, part] for back_ref in back_refs], axis=0)
+        sums = matmul(merge_ref[...], back, 1, 0)
+        mixed_ref[:, part] = (sums[:count] + sums[count : 2 * count]).astype(BF16)
+        token_ref[:, part] = sums[2 * count :].astype(BF16)
+        for source, target in ((mixed_ref, mixed_hbm), (token_ref, token_hbm)):
+            copies.append(
+                pltpu.make_async_copy(
+                    source.at[:, part], target.at[:, part], sems.at[len(copies)]
+                )
+            )
+            copies[-1].start()
+    for copy in copies:
+        copy.wait()
+
+
+def combine(backs, merge):
+    feature, count = backs[0].shape[1], merge.shape[0] // 3
+    columns = spans(feature, 2 * CHUNK if feature % CHUNK == 0 else feature)
     vmem = pl.BlockSpec(memory_space=pltpu.VMEM)
     hbm = pl.BlockSpec(memory_space=pltpu.HBM)
     shape = (count, feature)
     return pl.pallas_call(
-        functools.partial(combine_kernel, len(backs)),
+        functools.partial(combine_kernel, columns, len(backs)),
         out_shape=(jax.ShapeDtypeStruct(shape, BF16),) * 2,
         in_specs=[vmem] * (len(backs) + 1),
         out_specs=(hbm, hbm),
         scratch_shapes=[
             pltpu.VMEM(shape, BF16),
             pltpu.VMEM(shape, BF16),
-            pltpu.SemaphoreType.DMA((2,)),
+            pltpu.SemaphoreType.DMA((2 * len(columns),)),
         ],
         compiler_params=params(),
         name="combine",
-    )(*backs, pick)
+    )(*backs, merge)
 
 
 def swapped(array, axis, distance):
@@ -403,7 +415,7 @@
     block = -(-2 * slots // 8) * 8
     pieces = experts if experts <= GROUP else 1
     gate, up, down = gate_weight[0], up_weight[0], down_weight[0]
-    sends, pick = dispatch(
+    sends, (scaled, pick) = dispatch(
         replica_plan,
         cap_blocks,
         expert_ids.T,
@@ -416,7 +428,7 @@
         pieces,
     )
     recvs = over_experts(sends, experts)
-    weights = load_weights(gate, up, down, pick)
+    *weights, merge = load_weights(gate, up, down, scaled, pick)
     feature, width = gate.shape
     tile, big = GROUP * slots, GROUP * block
     steps, total, half = experts // GROUP, experts * slots, 3 * width // 2
@@ -461,7 +473,7 @@
     )
     returned = over_experts(backs if pieces > 1 else [backs], experts)
     gate_grad, up_grad, down_grad = weight_grads(rows, cots, mine, theirs)
-    mixed, token_grad = combine(returned, pick)
+    mixed, token_grad = combine(returned, merge)
     return mixed, token_grad, gate_grad[None], up_grad[None], down_grad[None]
 
 

time: 28.4 us -> 28.3 us (level)
  no operation moved by 1% of the time
where the time goes in v8:
time: 28.3 us; the launch traced here: 28.2 us
  starting transfers between devices  11.9 us (42%)
  Pallas kernels  8.29 us (29%)
  waiting for transfers between devices  7.23 us (26%)
  between operations  0.73 us (3%)
    ppermute x9, starting transfers between devices, swapped(): lax.ppermute(array, axis, [(i, i ^ distance) for i in range(lax.axis_size...  11.9 us
    ppermute x9, waiting for transfers between devices, swapped(): lax.ppermute(array, axis, [(i, i ^ distance) for i in range(lax.axis_size...  7.23 us
    pallas_call x6, Pallas kernels, by_rows(): pl.pallas_call(kernel, grid=(steps,), out_shape=tuple((jax.ShapeDtypeStru...  2.03 us
    pallas_call x1, Pallas kernels, load_weights(): pl.pallas_call(load_kernel, out_shape=tuple((pltpu.VMEM(w.shape, BF16) fo...  2.01 us
    pallas_call x1, Pallas kernels, weight_grads(): pl.pallas_call(grads_kernel, out_shape=tuple((jax.ShapeDtypeStruct(shape,...  1.96 us
    pallas_call x1, Pallas kernels, dispatch(): pl.pallas_call(functools.partial(dispatch_kernel, experts, plan.shape[1],...  1.32 us
    pallas_call x1, Pallas kernels, combine(): pl.pallas_call(functools.partial(combine_kernel, columns, len(backs)), ou...  0.97 us
  transfers between devices with their start and end apart: 9, of which 6 were waited for; matrix products, arithmetic and copies ran while one was open for 0% of the time, Pallas kernels for 17%

profile of v8, /device:TPU:0, one launch (start us, length us, event | category | flops | bytes accessed | tf_op | source)
XLA Modules:
  0.0 28.2 jit_solution(13338505296692693509)
XLA Ops:
  0.6 1.3 %dispatch.1 = (bf16[24,640]{1,0:T(8,128)(2,1)S(1)}, bf16[24,640]{1,0:T(8,128)(2,1)S(1)}, bf16[24,640]{1,0:T(8,128)(2,1)S(1)}, bf16[24,640]{1,0:T(8,128)(2,1)S(1)...) custom-call(s32[2,2]{1,0:T(2,128)} %refs_0_.1, s32[4]{0:T(128)} %refs_1_.1, s32[2,128]{1,0:T(2,128)} %bitcast.11, ...), custom_call_target="tpu_custom_call" | custom-call | tf_op jit(solution)/shard_map/dispatch/pallas_call | solution.py:124
  2.0 5.1 %collective-permute-start = (bf16[24,640]{1,0:T(8,128)(2,1)S(1)}, bf16[24,640]{1,0:T(8,128)(2,1)S(1)}, u32[]{:S(2)}, u32[]{:S(2)}) collective-permute-start(bf16[24,640]{1,0:T(8,128)(2,1)S(1)} %get-tuple-element.30), channel_id=1, source_target_pairs={{0,12},{4,8},{8,4},{12,0},{1,13},{5,9},{9,5},{13,1},{2,14},{6,10},... | collective-permute-start | bytes 92168 | tf_op jit(solution)/shard_map/ppermute | solution.py:386
  7.1 0.0 collective-permute-start.1
  7.1 0.6 %collective-permute-start.2 = (bf16[24,640]{1,0:T(8,128)(2,1)S(1)}, bf16[24,640]{1,0:T(8,128)(2,1)S(1)}, u32[]{:S(2)}, u32[]{:S(2)}) collective-permute-start(bf16[24,640]{1,0:T(8,128)(2,1)S(1)} %get-tuple-element.32), channel_id=1, source_target_pairs={{0,4},{4,0},{8,12},{12,8},{1,5},{5,1},{9,13},{13,9},{2,6},{6,2},{1... | collective-permute-start | bytes 92168 | tf_op jit(solution)/shard_map/ppermute | solution.py:386
  7.7 2.0 %load_weights.1 = (bf16[640,768]{1,0:T(8,128)(2,1)S(1)}, bf16[640,768]{1,0:T(8,128)(2,1)S(1)}, bf16[768,640]{1,0:T(8,128)(2,1)S(1)}, bf16[384,96]{1,0:T(8,128)(2,1)S(1)}) custom-call(bf16[640,768]{1,0:T(8,128)(2,1)} %bitcast.8, bf16[640,768]{1,0:T(8,128)(2,1)} %bitcast.9, bf16[768,640]{1,0:T(8,128)(2,1)} %bitcast.10, ...), custom_call_target="tpu_custom_call" | custom-call | bytes 5898240 | tf_op jit(solution)/shard_map/load_weights/pallas_call | solution.py:171
  9.7 0.0 collective-permute-done.refs_1_
  9.7 2.1 %collective-permute-done.1.refs_2_ = bf16[24,640]{1,0:T(8,128)(2,1)S(1)} collective-permute-done((bf16[24,640]{1,0:T(8,128)(2,1)S(1)}, bf16[24,640]{1,0:T(8,128)(2,1)S(1)}, u32[]{:S(2)}, u32[]{:S(2)}) %collective-permute-start.1) | collective-permute-done | bytes 30752 | tf_op jit(solution)/shard_map/ppermute | solution.py:386
  11.9 0.0 collective-permute-done.2.refs_3_
  11.9 0.5 %give.1 = (bf16[40,640]{1,0:T(8,128)(2,1)S(1)}, bf16[40,640]{1,0:T(8,128)(2,1)S(1)}, bf16[40,1152]{1,0:T(8,128)(2,1)S(1)}) custom-call(bf16[24,640]{1,0:T(8,128)(2,1)S(1)} %get-tuple-element.29.refs_0_, bf16[24,640]{1,0:T(8,128)(2,1)S(1)} %collective-permute-done.refs_1_, bf16[24,640]{1,0:T(8,128)(2,1)S(1)} %collective-permute-done.1.refs_2_, ...), custom_call_target="tpu_custom_call" | custom-call | flops 58982400 | bytes 3072000 | tf_op jit(solution)/shard_map/give/pallas_call | solution.py:273
  12.3 0.1 collective-permute-start.3
  12.4 0.4 %keep.1.left_ref = bf16[40,1152]{1,0:T(8,128)(2,1)S(1)} custom-call(bf16[40,640]{1,0:T(8,128)(2,1)S(1)} %get-tuple-element.38.rows_ref, bf16[40,640]{1,0:T(8,128)(2,1)S(1)} %get-tuple-element.39.cots_ref, bf16[640,768]{1,0:T(8,128)(2,1)S(1)} %get-tuple-element.35.refs_4_.gate_ref.refs_3_, bf16[640,768]{1,0:T(8,128)(2,1)S(1)} %get-tuple-element.36.refs_5_.up_ref.refs_4_, ...), custom_call_target="tpu_custom_call" | custom-call | flops 58982400 | bytes 3051520 | tf_op jit(solution)/shard_map/keep/pallas_call | solution.py:273
  12.9 0.8 %collective-permute-done.3.right_ref = bf16[40,1152]{1,0:T(8,128)(2,1)S(1)} collective-permute-done((bf16[40,1152]{1,0:T(8,128)(2,1)S(1)}, bf16[40,1152]{1,0:T(8,128)(2,1)S(1)}, u32[]{:S(2)}, u32[]{:S(2)}) %collective-permute-start.3) | collective-permute-done | bytes 92192 | tf_op jit(solution)/shard_map/ppermute | solution.py:386
  13.7 1.6 %collective-permute-start.4 = (bf16[40,1152]{1,0:T(8,128)(2,1)S(1)}, bf16[40,1152]{1,0:T(8,128)(2,1)S(1)}, u32[]{:S(2)}, u32[]{:S(2)}) collective-permute-start(bf16[40,1152]{1,0:T(8,128)(2,1)S(1)} %add.1.near_ref), channel_id=1, source_target_pairs={{0,2},{1,3},{2,0},{3,1},{4,6},{5,7},{6,4},{7,5},{8,10},{9,11},{10,... | collective-permute-start | bytes 276488 | tf_op jit(solution)/shard_map/ppermute | solution.py:386
  15.3 3.2 %collective-permute-done.4.far_ref = bf16[40,1152]{1,0:T(8,128)(2,1)S(1)} collective-permute-done((bf16[40,1152]{1,0:T(8,128)(2,1)S(1)}, bf16[40,1152]{1,0:T(8,128)(2,1)S(1)}, u32[]{:S(2)}, u32[]{:S(2)}) %collective-permute-start.4) | collective-permute-done | bytes 92192 | tf_op jit(solution)/shard_map/ppermute | solution.py:386
  18.5 0.1 activate.1.mine_ref
  18.6 0.1 collective-permute-start.5
  18.6 0.5 %own.1 = (f32[40,640]{1,0:T(8,128)S(1)}, f32[40,640]{1,0:T(8,128)S(1)}) custom-call(bf16[40,1152]{1,0:T(8,128)(2,1)S(1)} %activate.1.mine_ref, bf16[640,768]{1,0:T(8,128)(2,1)S(1)} %get-tuple-element.35.refs_4_.gate_ref.refs_3_, bf16[640,768]{1,0:T(8,128)(2,1)S(1)} %get-tuple-element.36.refs_5_.up_ref.refs_4_, ...), custom_call_target="tpu_custom_call" | custom-call | flops 58982400 | bytes 3041280 | tf_op jit(solution)/shard_map/own/pallas_call | solution.py:273
  19.1 0.8 %collective-permute-done.5.refs_0_.theirs_ref = bf16[40,1152]{1,0:T(8,128)(2,1)S(1)} collective-permute-done((bf16[40,1152]{1,0:T(8,128)(2,1)S(1)}, bf16[40,1152]{1,0:T(8,128)(2,1)S(1)}, u32[]{:S(2)}, u32[]{:S(2)}) %collective-permute-start.5) | collective-permute-done | bytes 92192 | tf_op jit(solution)/shard_map/ppermute | solution.py:386
  19.9 0.6 %back.1 = (bf16[24,640]{1,0:T(8,128)(2,1)S(1)}, bf16[24,640]{1,0:T(8,128)(2,1)S(1)}, bf16[24,640]{1,0:T(8,128)(2,1)S(1)}, bf16[24,640]{1,0:T(8,128)(2,1)S(1)}) custom-call(bf16[40,1152]{1,0:T(8,128)(2,1)S(1)} %collective-permute-done.5.refs_0_.theirs_ref, f32[40,640]{1,0:T(8,128)S(1)} %get-tuple-element.41.refs_1_, f32[40,640]{1,0:T(8,128)S(1)} %get-tuple-element.42.refs_2_, ...), custom_call_target="tpu_custom_call" | custom-call | flops 58982400 | bytes 3246080 | tf_op jit(solution)/shard_map/back/pallas_call | solution.py:273
  20.5 1.7 %collective-permute-start.6 = (bf16[24,640]{1,0:T(8,128)(2,1)S(1)}, bf16[24,640]{1,0:T(8,128)(2,1)S(1)}, u32[]{:S(2)}, u32[]{:S(2)}) collective-permute-start(bf16[24,640]{1,0:T(8,128)(2,1)S(1)} %get-tuple-element.44), channel_id=1, source_target_pairs={{0,12},{4,8},{8,4},{12,0},{1,13},{5,9},{9,5},{13,1},{2,14},{6,10},... | collective-permute-start | bytes 92168 | tf_op jit(solution)/shard_map/ppermute | solution.py:386
  22.2 0.5 %collective-permute-start.7 = (bf16[24,640]{1,0:T(8,128)(2,1)S(1)}, bf16[24,640]{1,0:T(8,128)(2,1)S(1)}, u32[]{:S(2)}, u32[]{:S(2)}) collective-permute-start(bf16[24,640]{1,0:T(8,128)(2,1)S(1)} %get-tuple-element.45), channel_id=1, source_target_pairs={{0,8},{4,12},{8,0},{12,4},{1,9},{5,13},{9,1},{13,5},{2,10},{6,14},... | collective-permute-start | bytes 92168 | tf_op jit(solution)/shard_map/ppermute | solution.py:386
  22.7 2.3 %collective-permute-start.8 = (bf16[24,640]{1,0:T(8,128)(2,1)S(1)}, bf16[24,640]{1,0:T(8,128)(2,1)S(1)}, u32[]{:S(2)}, u32[]{:S(2)}) collective-permute-start(bf16[24,640]{1,0:T(8,128)(2,1)S(1)} %get-tuple-element.46), channel_id=1, source_target_pairs={{0,4},{4,0},{8,12},{12,8},{1,5},{5,1},{9,13},{13,9},{2,6},{6,2},{1... | collective-permute-start | bytes 92168 | tf_op jit(solution)/shard_map/ppermute | solution.py:386
  24.9 2.0 %weight_grads.1 = (bf16[640,768]{1,0:T(8,128)(2,1)}, bf16[640,768]{1,0:T(8,128)(2,1)}, bf16[768,640]{1,0:T(8,128)(2,1)}) custom-call(bf16[40,640]{1,0:T(8,128)(2,1)S(1)} %get-tuple-element.38.rows_ref, bf16[40,640]{1,0:T(8,128)(2,1)S(1)} %get-tuple-element.39.cots_ref, bf16[40,1152]{1,0:T(8,128)(2,1)S(1)} %activate.1.mine_ref, ...), custom_call_target="tpu_custom_call" | custom-call | flops 117964800 | bytes 2949120 | tf_op jit(solution)/shard_map/weight_grads/pallas_call | solution.py:325
  26.9 0.0 collective-permute-done.6.refs_1_
  26.9 0.1 collective-permute-done.7.refs_2_
  27.0 0.2 collective-permute-done.8.refs_3_
  27.2 1.0 %combine.1 = (bf16[128,640]{1,0:T(8,128)(2,1)}, bf16[128,640]{1,0:T(8,128)(2,1)}) custom-call(bf16[24,640]{1,0:T(8,128)(2,1)S(1)} %get-tuple-element.43.refs_0_, bf16[24,640]{1,0:T(8,128)(2,1)S(1)} %collective-permute-done.6.refs_1_, bf16[24,640]{1,0:T(8,128)(2,1)S(1)} %collective-permute-done.7.refs_2_, bf16[24,640]{1,0:T(8,128)(2,1)S(1)} %collective-permute-done.8.refs_3_, ...), custom_call_target="tpu_custom_call" | custom-call | tf_op jit(solution)/shard_map/combine/pallas_call | solution.py:370
  (1 shorter events, 0.0 us)
Async XLA Ops:
  2.0 7.8 %collective-permute-start = (bf16[24,640]{1,0:T(8,128)(2,1)S(1)}, bf16[24,640]{1,0:T(8,128)(2,1)S(1)}, u32[]{:S(2)}, u32[]{:S(2)}) collective-permute-start(bf16[24,640]{1,0:T(8,128)(2,1)S(1)} %get-tuple-element.30), channel_id=1, source_target_pairs={{0,12},{4,8},{8,4},{12,0},{1,13},{5,9},{9,5},{13,1},{2,14},{6,10},... | collective-permute-start | bytes 92168 | tf_op jit(solution)/shard_map/ppermute | solution.py:386
  7.1 4.8 %collective-permute-start.1 = (bf16[24,640]{1,0:T(8,128)(2,1)S(1)}, bf16[24,640]{1,0:T(8,128)(2,1)S(1)}, u32[]{:S(2)}, u32[]{:S(2)}) collective-permute-start(bf16[24,640]{1,0:T(8,128)(2,1)S(1)} %get-tuple-element.31), channel_id=1, source_target_pairs={{0,8},{4,12},{8,0},{12,4},{1,9},{5,13},{9,1},{13,5},{2,10},{6,14},... | collective-permute-start | bytes 92168 | tf_op jit(solution)/shard_map/ppermute | solution.py:386
  7.1 4.8 %collective-permute-start.2 = (bf16[24,640]{1,0:T(8,128)(2,1)S(1)}, bf16[24,640]{1,0:T(8,128)(2,1)S(1)}, u32[]{:S(2)}, u32[]{:S(2)}) collective-permute-start(bf16[24,640]{1,0:T(8,128)(2,1)S(1)} %get-tuple-element.32), channel_id=1, source_target_pairs={{0,4},{4,0},{8,12},{12,8},{1,5},{5,1},{9,13},{13,9},{2,6},{6,2},{1... | collective-permute-start | bytes 92168 | tf_op jit(solution)/shard_map/ppermute | solution.py:386
  12.3 1.4 %collective-permute-start.3 = (bf16[40,1152]{1,0:T(8,128)(2,1)S(1)}, bf16[40,1152]{1,0:T(8,128)(2,1)S(1)}, u32[]{:S(2)}, u32[]{:S(2)}) collective-permute-start(bf16[40,1152]{1,0:T(8,128)(2,1)S(1)} %get-tuple-element.40), channel_id=1, source_target_pairs={{0,1},{1,0},{2,3},{3,2},{4,5},{5,4},{6,7},{7,6},{8,9},{9,8},{10,11... | collective-permute-start | bytes 276488 | tf_op jit(solution)/shard_map/ppermute | solution.py:386
  13.7 4.8 %collective-permute-start.4 = (bf16[40,1152]{1,0:T(8,128)(2,1)S(1)}, bf16[40,1152]{1,0:T(8,128)(2,1)S(1)}, u32[]{:S(2)}, u32[]{:S(2)}) collective-permute-start(bf16[40,1152]{1,0:T(8,128)(2,1)S(1)} %add.1.near_ref), channel_id=1, source_target_pairs={{0,2},{1,3},{2,0},{3,1},{4,6},{5,7},{6,4},{7,5},{8,10},{9,11},{10,... | collective-permute-start | bytes 276488 | tf_op jit(solution)/shard_map/ppermute | solution.py:386
  18.6 1.4 %collective-permute-start.5 = (bf16[40,1152]{1,0:T(8,128)(2,1)S(1)}, bf16[40,1152]{1,0:T(8,128)(2,1)S(1)}, u32[]{:S(2)}, u32[]{:S(2)}) collective-permute-start(bf16[40,1152]{1,0:T(8,128)(2,1)S(1)} %activate.1.mine_ref), channel_id=1, source_target_pairs={{0,1},{1,0},{2,3},{3,2},{4,5},{5,4},{6,7},{7,6},{8,9},{9,8},{10,11... | collective-permute-start | bytes 276488 | tf_op jit(solution)/shard_map/ppermute | solution.py:386
  20.5 6.4 %collective-permute-start.6 = (bf16[24,640]{1,0:T(8,128)(2,1)S(1)}, bf16[24,640]{1,0:T(8,128)(2,1)S(1)}, u32[]{:S(2)}, u32[]{:S(2)}) collective-permute-start(bf16[24,640]{1,0:T(8,128)(2,1)S(1)} %get-tuple-element.44), channel_id=1, source_target_pairs={{0,12},{4,8},{8,4},{12,0},{1,13},{5,9},{9,5},{13,1},{2,14},{6,10},... | collective-permute-start | bytes 92168 | tf_op jit(solution)/shard_map/ppermute | solution.py:386
  22.2 4.8 %collective-permute-start.7 = (bf16[24,640]{1,0:T(8,128)(2,1)S(1)}, bf16[24,640]{1,0:T(8,128)(2,1)S(1)}, u32[]{:S(2)}, u32[]{:S(2)}) collective-permute-start(bf16[24,640]{1,0:T(8,128)(2,1)S(1)} %get-tuple-element.45), channel_id=1, source_target_pairs={{0,8},{4,12},{8,0},{12,4},{1,9},{5,13},{9,1},{13,5},{2,10},{6,14},... | collective-permute-start | bytes 92168 | tf_op jit(solution)/shard_map/ppermute | solution.py:386
  22.7 4.5 %collective-permute-start.8 = (bf16[24,640]{1,0:T(8,128)(2,1)S(1)}, bf16[24,640]{1,0:T(8,128)(2,1)S(1)}, u32[]{:S(2)}, u32[]{:S(2)}) collective-permute-start(bf16[24,640]{1,0:T(8,128)(2,1)S(1)} %get-tuple-element.46), channel_id=1, source_target_pairs={{0,4},{4,0},{8,12},{12,8},{1,5},{5,1},{9,13},{13,9},{2,6},{6,2},{1... | collective-permute-start | bytes 92168 | tf_op jit(solution)/shard_map/ppermute | solution.py:386

commit v9 on v8

--- a/solution.py
+++ b/solution.py
@@ -39,27 +39,28 @@
     return [(start, min(size, extent - start)) for start in range(0, extent, size)]
 
 
+def padded(rows):
+    return -(-rows // 8) * 8
+
+
 def distance(index, experts):
     return (experts - index) % experts
 
 
-def dispatch_kernel(experts, hosts, slots, block, pieces, *refs):
+def dispatch_kernel(experts, hosts, slots, chunks, pieces, *refs):
     plan_hbm, caps_hbm, ids_hbm, gates_hbm, tok_hbm, grad_hbm = refs[:6]
     send_refs = refs[6 : 6 + pieces]
-    scaled_ref, pick_ref, plan_ref, caps_ref, ids_ref, gates_ref, both_ref, sems = refs[6 + pieces :]
+    scaled_ref, pick_ref, plan_ref, caps_ref, ids_ref, gates_ref, both_ref, wide, sems = refs[6 + pieces :]
     choose, count = ids_ref.shape
+    block = padded(2 * slots)
+    pairs = [(ids_hbm, ids_ref), (plan_hbm, plan_ref), (caps_hbm, caps_ref), (gates_hbm, gates_ref)]
+    for place, source in enumerate((tok_hbm, grad_hbm)):
+        for start, size in spans(count, count // LOADS):
+            target = both_ref.at[pl.ds(place * count + start, size)]
+            pairs.append((source.at[pl.ds(start, size)], target))
     copies = [
         pltpu.make_async_copy(source, target, sems.at[i])
-        for i, (source, target) in enumerate(
-            (
-                (ids_hbm, ids_ref),
-                (plan_hbm, plan_ref),
-                (caps_hbm, caps_ref),
-                (gates_hbm, gates_ref),
-                (tok_hbm, both_ref.at[pl.ds(0, count)]),
-                (grad_hbm, both_ref.at[pl.ds(count, count)]),
-            )
-        )
+        for i, (source, target) in enumerate(pairs)
     ]
     for copy in copies:
         copy.start()
@@ -111,19 +112,26 @@
     pick_ref[...] = pick_cot
     for copy in copies[4:]:
         copy.wait()
-    send = (scale * matmul(picks, both_ref[...], 1, 0)).astype(BF16)
-    size = send.shape[0] // pieces
+    send = scale * matmul(picks, both_ref[...], 1, 0)
+    if pieces == 1:
+        send_refs[0][...] = send.astype(BF16)
+        return
+    width = send.shape[1] // chunks
     for i, send_ref in enumerate(send_refs):
-        send_ref[...] = send[i * size : (i + 1) * size]
-
-
-def dispatch(plan, caps, ids, gates, tokens, grads, experts, slots, block, pieces):
+        for j in range(chunks):
+            rows = send[i * block : i * block + 2 * slots, j * width : (j + 1) * width]
+            wide[2 * slots * j : 2 * slots * (j + 1), :] = rows
+        send_ref[...] = wide[...].astype(BF16)
+
+
+def dispatch(plan, caps, ids, gates, tokens, grads, experts, slots, chunks, pieces):
     count, feature = tokens.shape
     vmem = pl.BlockSpec(memory_space=pltpu.VMEM)
-    size = experts * block // pieces
+    block = padded(2 * slots)
+    sent = (experts * block, feature) if pieces == 1 else (2 * slots * chunks, feature // chunks)
     outs = pl.pallas_call(
-        functools.partial(dispatch_kernel, experts, plan.shape[1], slots, block, pieces),
-        out_shape=(jax.ShapeDtypeStruct((size, feature), BF16),) * pieces
+        functools.partial(dispatch_kernel, experts, plan.shape[1], slots, chunks, pieces),
+        out_shape=(jax.ShapeDtypeStruct(sent, BF16),) * pieces
         + (jax.ShapeDtypeStruct((experts * block, count), F32),) * 2,
         in_specs=[pl.BlockSpec(memory_space=pltpu.HBM)] * 6,
         out_specs=(vmem,) * (pieces + 2),
@@ -133,7 +141,8 @@
             pltpu.VMEM(ids.shape, I32),
             pltpu.VMEM(gates.shape, F32),
             pltpu.VMEM((2 * count, feature), BF16),
-            pltpu.SemaphoreType.DMA((6,)),
+            pltpu.VMEM((2 * slots * chunks, feature // chunks), F32),
+            pltpu.SemaphoreType.DMA((4 + 2 * LOADS,)),
         ],
         compiler_params=params(),
         name="dispatch",
@@ -197,15 +206,18 @@
     part_ref[:, 2 * half :] = matmul(cots, down_ref[units, :], 1, 1).astype(BF16)
 
 
-def give_kernel(group, slots, block, pieces, *refs):
+def give_kernel(slots, chunks, pieces, *refs):
     recv_refs = refs[:pieces]
     gate_ref, up_ref, down_ref, rows_ref, cots_ref, give_ref, wide, flat = refs[pieces:]
-    size = group * block // pieces
-    for i, recv_ref in enumerate(recv_refs):
-        wide[i * size : (i + 1) * size, :] = recv_ref[...].astype(F32)
+    group, block, width = wide.shape
     for s in range(group):
-        flat[0, s * slots : (s + 1) * slots, :] = wide[s * block : s * block + slots, :]
-        flat[1, s * slots : (s + 1) * slots, :] = wide[s * block + slots : s * block + 2 * slots, :]
+        recv_ref, start = (recv_refs[0], s * block) if pieces == 1 else (recv_refs[s], 0)
+        wide[s] = recv_ref[start : start + block, :].astype(F32)
+        for j in range(chunks):
+            columns = pl.ds(j * width, width)
+            for kind in range(2):
+                place = (2 * j + kind) * slots
+                flat[kind, s * slots : (s + 1) * slots, columns] = wide[s, place : place + slots, :]
     rows = flat[0].astype(BF16)
     cots = flat[1].astype(BF16)
     rows_ref[...] = rows
@@ -246,20 +258,24 @@
     outs_ref[...], ins_ref[...] = half_outputs(0, mine_ref, gate_ref, up_ref, down_ref)
 
 
-def back_kernel(group, slots, block, pieces, *refs):
+def back_kernel(slots, chunks, pieces, *refs):
     theirs_ref, outs_ref, ins_ref, gate_ref, up_ref, down_ref = refs[:6]
     back_refs = refs[6 : 6 + pieces]
     flat, wide = refs[6 + pieces :]
+    group, block, width = wide.shape
     outs, ins = half_outputs(1, theirs_ref, gate_ref, up_ref, down_ref)
     flat[0] = outs_ref[...] + outs
     flat[1] = ins_ref[...] + ins
-    wide[...] = jnp.zeros_like(wide)
+    if block > 2 * slots * chunks:
+        wide[...] = jnp.zeros_like(wide)
     for s in range(group):
-        wide[s * block : s * block + slots, :] = flat[0, s * slots : (s + 1) * slots, :]
-        wide[s * block + slots : s * block + 2 * slots, :] = flat[1, s * slots : (s + 1) * slots, :]
-    size = group * block // pieces
-    for i, back_ref in enumerate(back_refs):
-        back_ref[...] = wide[i * size : (i + 1) * size, :].astype(BF16)
+        for j in range(chunks):
+            columns = pl.ds(j * width, width)
+            for kind in range(2):
+                place = (2 * j + kind) * slots
+                wide[s, place : place + slots, :] = flat[kind, s * slots : (s + 1) * slots, columns]
+        back_ref, start = (back_refs[0], s * block) if pieces == 1 else (back_refs[s], 0)
+        back_ref[start : start + block, :] = wide[s].astype(BF16)
 
 
 def by_rows(kernel, name, steps, arrays, weights, outs, scratch=(), flops=0):
@@ -339,14 +355,22 @@
     )(rows, cots, mine, theirs)
 
 
-def combine_kernel(columns, pieces, *refs):
+def combine_kernel(columns, slots, chunks, pieces, *refs):
     back_refs = refs[:pieces]
-    merge_ref, mixed_hbm, token_hbm, mixed_ref, token_ref, sems = refs[pieces:]
+    merge_ref, mixed_hbm, token_hbm, mixed_ref, token_ref, wide, flat, sems = refs[pieces:]
+    if pieces > 1:
+        flat[...] = jnp.zeros_like(flat)
+        rows, width, block = 2 * slots, back_refs[0].shape[1], padded(2 * slots)
+        for i, back_ref in enumerate(back_refs):
+            wide[i] = back_ref[...].astype(F32)
+            for j in range(chunks):
+                part = pl.ds(j * width, width)
+                flat[i * block : i * block + rows, part] = wide[i, j * rows : (j + 1) * rows, :]
     count = mixed_ref.shape[0]
     copies = []
     for start, size in columns:
         part = pl.ds(start, size)
-        back = jnp.concatenate([back_ref[:, part] for back_ref in back_refs], axis=0)
+        back = back_refs[0][:, part] if pieces == 1 else flat[:, part].astype(BF16)
         sums = matmul(merge_ref[...], back, 1, 0)
         mixed_ref[:, part] = (sums[:count] + sums[count : 2 * count]).astype(BF16)
         token_ref[:, part] = sums[2 * count :].astype(BF16)
@@ -361,20 +385,22 @@
         copy.wait()
 
 
-def combine(backs, merge):
-    feature, count = backs[0].shape[1], merge.shape[0] // 3
+def combine(backs, merge, slots, chunks):
+    pieces, feature, count = len(backs), chunks * backs[0].shape[1], merge.shape[0] // 3
     columns = spans(feature, 2 * CHUNK if feature % CHUNK == 0 else feature)
     vmem = pl.BlockSpec(memory_space=pltpu.VMEM)
     hbm = pl.BlockSpec(memory_space=pltpu.HBM)
     shape = (count, feature)
+    staged = [(pieces, *backs[0].shape), (merge.shape[1], feature)] if pieces > 1 else [(8, 128)] * 2
     return pl.pallas_call(
-        functools.partial(combine_kernel, columns, len(backs)),
+        functools.partial(combine_kernel, columns, slots, chunks, pieces),
         out_shape=(jax.ShapeDtypeStruct(shape, BF16),) * 2,
-        in_specs=[vmem] * (len(backs) + 1),
+        in_specs=[vmem] * (pieces + 1),
         out_specs=(hbm, hbm),
         scratch_shapes=[
             pltpu.VMEM(shape, BF16),
             pltpu.VMEM(shape, BF16),
+            *(pltpu.VMEM(extent, F32) for extent in staged),
             pltpu.SemaphoreType.DMA((2 * len(columns),)),
         ],
         compiler_params=params(),
@@ -412,9 +438,11 @@
     assert tokens.shape[0] % hosts == 0 and experts % GROUP == 0
     assert all(n >= 4 and n & (n - 1) == 0 for n in (experts, lax.axis_size("dp")))
     slots = OWN + SPARE * (hosts - 1)
-    block = -(-2 * slots // 8) * 8
-    pieces = experts if experts <= GROUP else 1
     gate, up, down = gate_weight[0], up_weight[0], down_weight[0]
+    feature, width = gate.shape
+    pieces = experts if experts <= GROUP and feature % CHUNK == 0 else 1
+    chunks = feature // CHUNK if pieces > 1 else 1
+    block = 2 * slots * chunks if pieces > 1 else padded(2 * slots)
     sends, (scaled, pick) = dispatch(
         replica_plan,
         cap_blocks,
@@ -424,17 +452,18 @@
         out_grad,
         experts,
         slots,
-        block,
+        chunks,
         pieces,
     )
     recvs = over_experts(sends, experts)
     *weights, merge = load_weights(gate, up, down, scaled, pick)
-    feature, width = gate.shape
-    tile, big = GROUP * slots, GROUP * block
     steps, total, half = experts // GROUP, experts * slots, 3 * width // 2
-    layout = (GROUP, slots, block, pieces)
+    layout = (slots, chunks, pieces)
     flops = 3 * total * feature * width
-    scratch = [pltpu.VMEM((big, feature), F32), pltpu.VMEM((2, tile, feature), F32)]
+    scratch = [
+        pltpu.VMEM((GROUP, block, feature // chunks), F32),
+        pltpu.VMEM((2, GROUP * slots, feature), F32),
+    ]
     rows, cots, give = by_rows(
         functools.partial(give_kernel, *layout),
         "give",
@@ -467,13 +496,13 @@
         steps,
         [theirs, outs, ins],
         weights,
-        [((experts * block // pieces, feature), BF16)] * pieces,
+        [((experts * block // pieces, feature // chunks), BF16)] * pieces,
         scratch[::-1],
         flops,
     )
     returned = over_experts(backs if pieces > 1 else [backs], experts)
     gate_grad, up_grad, down_grad = weight_grads(rows, cots, mine, theirs)
-    mixed, token_grad = combine(returned, merge)
+    mixed, token_grad = combine(returned, merge, slots, chunks)
     return mixed, token_grad, gate_grad[None], up_grad[None], down_grad[None]
 
 

time: 28.3 us -> 28.3 us (level)
  transfers between devices with their start and end apart: 9 -> 9, of which waited for: 6 -> 5; matrix products, arithmetic and copies ran while one was open for 0% -> 0% of each run, Pallas kernels for 17% -> 17%
where the time goes in v9:
time: 28.3 us; the launch traced here: 28.1 us
  starting transfers between devices  11.9 us (42%)
  Pallas kernels  8.39 us (30%)
  waiting for transfers between devices  7.06 us (25%)
  between operations  0.73 us (3%)
    ppermute x9, starting transfers between devices, swapped(): lax.ppermute(array, axis, [(i, i ^ distance) for i in range(lax.axis_size...  11.9 us
    ppermute x9, waiting for transfers between devices, swapped(): lax.ppermute(array, axis, [(i, i ^ distance) for i in range(lax.axis_size...  7.06 us
    pallas_call x6, Pallas kernels, by_rows(): pl.pallas_call(kernel, grid=(steps,), out_shape=tuple((jax.ShapeDtypeStru...  2.03 us
    pallas_call x1, Pallas kernels, load_weights(): pl.pallas_call(load_kernel, out_shape=tuple((pltpu.VMEM(w.shape, BF16) fo...  2.01 us
    pallas_call x1, Pallas kernels, weight_grads(): pl.pallas_call(grads_kernel, out_shape=tuple((jax.ShapeDtypeStruct(shape,...  1.97 us
    pallas_call x1, Pallas kernels, dispatch(): pl.pallas_call(functools.partial(dispatch_kernel, experts, plan.shape[1],...  1.39 us
    pallas_call x1, Pallas kernels, combine(): pl.pallas_call(functools.partial(combine_kernel, columns, slots, chunks,...  0.99 us
  transfers between devices with their start and end apart: 9, of which 5 were waited for; matrix products, arithmetic and copies ran while one was open for 0% of the time, Pallas kernels for 17%

profile of v9, /device:TPU:0, one launch (start us, length us, event | category | flops | bytes accessed | tf_op | source)
XLA Modules:
  0.0 28.1 jit_solution(6945555009560311838)
XLA Ops:
  0.6 1.4 %dispatch.1 = (bf16[100,128]{1,0:T(8,128)(2,1)S(1)}, bf16[100,128]{1,0:T(8,128)(2,1)S(1)}, bf16[100,128]{1,0:T(8,128)(2,1)S(1)}, bf16[100,128]{1,0:T(8,128)(2,1)...) custom-call(s32[2,2]{1,0:T(2,128)} %refs_0_.1, s32[4]{0:T(128)} %refs_1_.1, s32[2,128]{1,0:T(2,128)} %bitcast.11, ...), custom_call_target="tpu_custom_call" | custom-call | tf_op jit(solution)/shard_map/dispatch/pallas_call | solution.py:132
  2.0 5.1 %collective-permute-start = (bf16[100,128]{1,0:T(8,128)(2,1)S(1)}, bf16[100,128]{1,0:T(8,128)(2,1)S(1)}, u32[]{:S(2)}, u32[]{:S(2)}) collective-permute-start(bf16[100,128]{1,0:T(8,128)(2,1)S(1)} %get-tuple-element.30), channel_id=1, source_target_pairs={{0,12},{4,8},{8,4},{12,0},{1,13},{5,9},{9,5},{13,1},{2,14},{6,10},... | collective-permute-start | bytes 76808 | tf_op jit(solution)/shard_map/ppermute | solution.py:412
  7.1 0.0 collective-permute-start.1
  7.1 0.6 %collective-permute-start.2 = (bf16[100,128]{1,0:T(8,128)(2,1)S(1)}, bf16[100,128]{1,0:T(8,128)(2,1)S(1)}, u32[]{:S(2)}, u32[]{:S(2)}) collective-permute-start(bf16[100,128]{1,0:T(8,128)(2,1)S(1)} %get-tuple-element.32), channel_id=1, source_target_pairs={{0,4},{4,0},{8,12},{12,8},{1,5},{5,1},{9,13},{13,9},{2,6},{6,2},{1... | collective-permute-start | bytes 76808 | tf_op jit(solution)/shard_map/ppermute | solution.py:412
  7.8 2.0 %load_weights.1 = (bf16[640,768]{1,0:T(8,128)(2,1)S(1)}, bf16[640,768]{1,0:T(8,128)(2,1)S(1)}, bf16[768,640]{1,0:T(8,128)(2,1)S(1)}, bf16[384,96]{1,0:T(8,128)(2,1)S(1)}) custom-call(bf16[640,768]{1,0:T(8,128)(2,1)} %bitcast.8, bf16[640,768]{1,0:T(8,128)(2,1)} %bitcast.9, bf16[768,640]{1,0:T(8,128)(2,1)} %bitcast.10, ...), custom_call_target="tpu_custom_call" | custom-call | bytes 5898240 | tf_op jit(solution)/shard_map/load_weights/pallas_call | solution.py:180
  9.8 0.0 collective-permute-done.refs_1_
  9.8 2.1 %collective-permute-done.1.refs_2_ = bf16[100,128]{1,0:T(8,128)(2,1)S(1)} collective-permute-done((bf16[100,128]{1,0:T(8,128)(2,1)S(1)}, bf16[100,128]{1,0:T(8,128)(2,1)S(1)}, u32[]{:S(2)}, u32[]{:S(2)}) %collective-permute-start.1) | collective-permute-done | bytes 25632 | tf_op jit(solution)/shard_map/ppermute | solution.py:412
  11.9 0.0 collective-permute-done.2.refs_3_
  11.9 0.5 %give.1 = (bf16[40,640]{1,0:T(8,128)(2,1)S(1)}, bf16[40,640]{1,0:T(8,128)(2,1)S(1)}, bf16[40,1152]{1,0:T(8,128)(2,1)S(1)}) custom-call(bf16[100,128]{1,0:T(8,128)(2,1)S(1)} %get-tuple-element.29.refs_0_, bf16[100,128]{1,0:T(8,128)(2,1)S(1)} %collective-permute-done.refs_1_, bf16[100,128]{1,0:T(8,128)(2,1)S(1)} %collective-permute-done.1.refs_2_, ...), custom_call_target="tpu_custom_call" | custom-call | flops 58982400 | bytes 3051520 | tf_op jit(solution)/shard_map/give/pallas_call | solution.py:289
  12.4 0.1 collective-permute-start.3
  12.5 0.4 %keep.1.left_ref = bf16[40,1152]{1,0:T(8,128)(2,1)S(1)} custom-call(bf16[40,640]{1,0:T(8,128)(2,1)S(1)} %get-tuple-element.38.rows_ref, bf16[40,640]{1,0:T(8,128)(2,1)S(1)} %get-tuple-element.39.cots_ref, bf16[640,768]{1,0:T(8,128)(2,1)S(1)} %get-tuple-element.35.refs_4_.gate_ref.refs_3_, bf16[640,768]{1,0:T(8,128)(2,1)S(1)} %get-tuple-element.36.refs_5_.up_ref.refs_4_, ...), custom_call_target="tpu_custom_call" | custom-call | flops 58982400 | bytes 3051520 | tf_op jit(solution)/shard_map/keep/pallas_call | solution.py:289
  12.9 0.8 %collective-permute-done.3.right_ref = bf16[40,1152]{1,0:T(8,128)(2,1)S(1)} collective-permute-done((bf16[40,1152]{1,0:T(8,128)(2,1)S(1)}, bf16[40,1152]{1,0:T(8,128)(2,1)S(1)}, u32[]{:S(2)}, u32[]{:S(2)}) %collective-permute-start.3) | collective-permute-done | bytes 92192 | tf_op jit(solution)/shard_map/ppermute | solution.py:412
  13.8 1.6 %collective-permute-start.4 = (bf16[40,1152]{1,0:T(8,128)(2,1)S(1)}, bf16[40,1152]{1,0:T(8,128)(2,1)S(1)}, u32[]{:S(2)}, u32[]{:S(2)}) collective-permute-start(bf16[40,1152]{1,0:T(8,128)(2,1)S(1)} %add.1.near_ref), channel_id=1, source_target_pairs={{0,2},{1,3},{2,0},{3,1},{4,6},{5,7},{6,4},{7,5},{8,10},{9,11},{10,... | collective-permute-start | bytes 276488 | tf_op jit(solution)/shard_map/ppermute | solution.py:412
  15.3 3.2 %collective-permute-done.4.far_ref = bf16[40,1152]{1,0:T(8,128)(2,1)S(1)} collective-permute-done((bf16[40,1152]{1,0:T(8,128)(2,1)S(1)}, bf16[40,1152]{1,0:T(8,128)(2,1)S(1)}, u32[]{:S(2)}, u32[]{:S(2)}) %collective-permute-start.4) | collective-permute-done | bytes 92192 | tf_op jit(solution)/shard_map/ppermute | solution.py:412
  18.5 0.1 activate.1.mine_ref
  18.6 0.1 collective-permute-start.5
  18.7 0.5 %own.1 = (f32[40,640]{1,0:T(8,128)S(1)}, f32[40,640]{1,0:T(8,128)S(1)}) custom-call(bf16[40,1152]{1,0:T(8,128)(2,1)S(1)} %activate.1.mine_ref, bf16[640,768]{1,0:T(8,128)(2,1)S(1)} %get-tuple-element.35.refs_4_.gate_ref.refs_3_, bf16[640,768]{1,0:T(8,128)(2,1)S(1)} %get-tuple-element.36.refs_5_.up_ref.refs_4_, ...), custom_call_target="tpu_custom_call" | custom-call | flops 58982400 | bytes 3041280 | tf_op jit(solution)/shard_map/own/pallas_call | solution.py:289
  19.2 0.8 %collective-permute-done.5.refs_0_.theirs_ref = bf16[40,1152]{1,0:T(8,128)(2,1)S(1)} collective-permute-done((bf16[40,1152]{1,0:T(8,128)(2,1)S(1)}, bf16[40,1152]{1,0:T(8,128)(2,1)S(1)}, u32[]{:S(2)}, u32[]{:S(2)}) %collective-permute-start.5) | collective-permute-done | bytes 92192 | tf_op jit(solution)/shard_map/ppermute | solution.py:412
  20.0 0.5 %back.1 = (bf16[100,128]{1,0:T(8,128)(2,1)S(1)}, bf16[100,128]{1,0:T(8,128)(2,1)S(1)}, bf16[100,128]{1,0:T(8,128)(2,1)S(1)}, bf16[100,128]{1,0:T(8,128)(2,1)S(1)}) custom-call(bf16[40,1152]{1,0:T(8,128)(2,1)S(1)} %collective-permute-done.5.refs_0_.theirs_ref, f32[40,640]{1,0:T(8,128)S(1)} %get-tuple-element.41.refs_1_, ...), custom_call_target="tpu_custom_call" | custom-call | flops 58982400 | bytes 3246080 | tf_op jit(solution)/shard_map/back/pallas_call | solution.py:289
  20.5 1.8 %collective-permute-start.6 = (bf16[100,128]{1,0:T(8,128)(2,1)S(1)}, bf16[100,128]{1,0:T(8,128)(2,1)S(1)}, u32[]{:S(2)}, u32[]{:S(2)}) collective-permute-start(bf16[100,128]{1,0:T(8,128)(2,1)S(1)} %get-tuple-element.44), channel_id=1, source_target_pairs={{0,12},{4,8},{8,4},{12,0},{1,13},{5,9},{9,5},{13,1},{2,14},{6,10},... | collective-permute-start | bytes 76808 | tf_op jit(solution)/shard_map/ppermute | solution.py:412
  22.3 0.4 %collective-permute-start.7 = (bf16[100,128]{1,0:T(8,128)(2,1)S(1)}, bf16[100,128]{1,0:T(8,128)(2,1)S(1)}, u32[]{:S(2)}, u32[]{:S(2)}) collective-permute-start(bf16[100,128]{1,0:T(8,128)(2,1)S(1)} %get-tuple-element.45), channel_id=1, source_target_pairs={{0,8},{4,12},{8,0},{12,4},{1,9},{5,13},{9,1},{13,5},{2,10},{6,14},... | collective-permute-start | bytes 76808 | tf_op jit(solution)/shard_map/ppermute | solution.py:412
  22.7 2.3 %collective-permute-start.8 = (bf16[100,128]{1,0:T(8,128)(2,1)S(1)}, bf16[100,128]{1,0:T(8,128)(2,1)S(1)}, u32[]{:S(2)}, u32[]{:S(2)}) collective-permute-start(bf16[100,128]{1,0:T(8,128)(2,1)S(1)} %get-tuple-element.46), channel_id=1, source_target_pairs={{0,4},{4,0},{8,12},{12,8},{1,5},{5,1},{9,13},{13,9},{2,6},{6,2},{1... | collective-permute-start | bytes 76808 | tf_op jit(solution)/shard_map/ppermute | solution.py:412
  25.0 2.0 %weight_grads.1 = (bf16[640,768]{1,0:T(8,128)(2,1)}, bf16[640,768]{1,0:T(8,128)(2,1)}, bf16[768,640]{1,0:T(8,128)(2,1)}) custom-call(bf16[40,640]{1,0:T(8,128)(2,1)S(1)} %get-tuple-element.38.rows_ref, bf16[40,640]{1,0:T(8,128)(2,1)S(1)} %get-tuple-element.39.cots_ref, bf16[40,1152]{1,0:T(8,128)(2,1)S(1)} %activate.1.mine_ref, ...), custom_call_target="tpu_custom_call" | custom-call | flops 117964800 | bytes 2949120 | tf_op jit(solution)/shard_map/weight_grads/pallas_call | solution.py:341
  26.9 0.0 collective-permute-done.6.refs_1_
  27.0 0.1 collective-permute-done.7.refs_2_
  27.0 0.0 collective-permute-done.8.refs_3_
  27.1 1.0 %combine.1 = (bf16[128,640]{1,0:T(8,128)(2,1)}, bf16[128,640]{1,0:T(8,128)(2,1)}) custom-call(bf16[100,128]{1,0:T(8,128)(2,1)S(1)} %get-tuple-element.43.refs_0_, bf16[100,128]{1,0:T(8,128)(2,1)S(1)} %collective-permute-done.6.refs_1_, bf16[100,128]{1,0:T(8,128)(2,1)S(1)} %collective-permute-done.7.refs_2_, ...), custom_call_target="tpu_custom_call" | custom-call | tf_op jit(solution)/shard_map/combine/pallas_call | solution.py:395
  (1 shorter events, 0.0 us)
Async XLA Ops:
  2.0 7.8 %collective-permute-start = (bf16[100,128]{1,0:T(8,128)(2,1)S(1)}, bf16[100,128]{1,0:T(8,128)(2,1)S(1)}, u32[]{:S(2)}, u32[]{:S(2)}) collective-permute-start(bf16[100,128]{1,0:T(8,128)(2,1)S(1)} %get-tuple-element.30), channel_id=1, source_target_pairs={{0,12},{4,8},{8,4},{12,0},{1,13},{5,9},{9,5},{13,1},{2,14},{6,10},... | collective-permute-start | bytes 76808 | tf_op jit(solution)/shard_map/ppermute | solution.py:412
  7.1 4.7 %collective-permute-start.1 = (bf16[100,128]{1,0:T(8,128)(2,1)S(1)}, bf16[100,128]{1,0:T(8,128)(2,1)S(1)}, u32[]{:S(2)}, u32[]{:S(2)}) collective-permute-start(bf16[100,128]{1,0:T(8,128)(2,1)S(1)} %get-tuple-element.31), channel_id=1, source_target_pairs={{0,8},{4,12},{8,0},{12,4},{1,9},{5,13},{9,1},{13,5},{2,10},{6,14},... | collective-permute-start | bytes 76808 | tf_op jit(solution)/shard_map/ppermute | solution.py:412
  7.1 4.7 %collective-permute-start.2 = (bf16[100,128]{1,0:T(8,128)(2,1)S(1)}, bf16[100,128]{1,0:T(8,128)(2,1)S(1)}, u32[]{:S(2)}, u32[]{:S(2)}) collective-permute-start(bf16[100,128]{1,0:T(8,128)(2,1)S(1)} %get-tuple-element.32), channel_id=1, source_target_pairs={{0,4},{4,0},{8,12},{12,8},{1,5},{5,1},{9,13},{13,9},{2,6},{6,2},{1... | collective-permute-start | bytes 76808 | tf_op jit(solution)/shard_map/ppermute | solution.py:412
  12.4 1.4 %collective-permute-start.3 = (bf16[40,1152]{1,0:T(8,128)(2,1)S(1)}, bf16[40,1152]{1,0:T(8,128)(2,1)S(1)}, u32[]{:S(2)}, u32[]{:S(2)}) collective-permute-start(bf16[40,1152]{1,0:T(8,128)(2,1)S(1)} %get-tuple-element.40), channel_id=1, source_target_pairs={{0,1},{1,0},{2,3},{3,2},{4,5},{5,4},{6,7},{7,6},{8,9},{9,8},{10,11... | collective-permute-start | bytes 276488 | tf_op jit(solution)/shard_map/ppermute | solution.py:412
  13.8 4.8 %collective-permute-start.4 = (bf16[40,1152]{1,0:T(8,128)(2,1)S(1)}, bf16[40,1152]{1,0:T(8,128)(2,1)S(1)}, u32[]{:S(2)}, u32[]{:S(2)}) collective-permute-start(bf16[40,1152]{1,0:T(8,128)(2,1)S(1)} %add.1.near_ref), channel_id=1, source_target_pairs={{0,2},{1,3},{2,0},{3,1},{4,6},{5,7},{6,4},{7,5},{8,10},{9,11},{10,... | collective-permute-start | bytes 276488 | tf_op jit(solution)/shard_map/ppermute | solution.py:412
  18.6 1.4 %collective-permute-start.5 = (bf16[40,1152]{1,0:T(8,128)(2,1)S(1)}, bf16[40,1152]{1,0:T(8,128)(2,1)S(1)}, u32[]{:S(2)}, u32[]{:S(2)}) collective-permute-start(bf16[40,1152]{1,0:T(8,128)(2,1)S(1)} %activate.1.mine_ref), channel_id=1, source_target_pairs={{0,1},{1,0},{2,3},{3,2},{4,5},{5,4},{6,7},{7,6},{8,9},{9,8},{10,11... | collective-permute-start | bytes 276488 | tf_op jit(solution)/shard_map/ppermute | solution.py:412
  20.5 6.4 %collective-permute-start.6 = (bf16[100,128]{1,0:T(8,128)(2,1)S(1)}, bf16[100,128]{1,0:T(8,128)(2,1)S(1)}, u32[]{:S(2)}, u32[]{:S(2)}) collective-permute-start(bf16[100,128]{1,0:T(8,128)(2,1)S(1)} %get-tuple-element.44), channel_id=1, source_target_pairs={{0,12},{4,8},{8,4},{12,0},{1,13},{5,9},{9,5},{13,1},{2,14},{6,10},... | collective-permute-start | bytes 76808 | tf_op jit(solution)/shard_map/ppermute | solution.py:412
  22.3 4.8 %collective-permute-start.7 = (bf16[100,128]{1,0:T(8,128)(2,1)S(1)}, bf16[100,128]{1,0:T(8,128)(2,1)S(1)}, u32[]{:S(2)}, u32[]{:S(2)}) collective-permute-start(bf16[100,128]{1,0:T(8,128)(2,1)S(1)} %get-tuple-element.45), channel_id=1, source_target_pairs={{0,8},{4,12},{8,0},{12,4},{1,9},{5,13},{9,1},{13,5},{2,10},{6,14},... | collective-permute-start | bytes 76808 | tf_op jit(solution)/shard_map/ppermute | solution.py:412
  22.7 4.4 %collective-permute-start.8 = (bf16[100,128]{1,0:T(8,128)(2,1)S(1)}, bf16[100,128]{1,0:T(8,128)(2,1)S(1)}, u32[]{:S(2)}, u32[]{:S(2)}) collective-permute-start(bf16[100,128]{1,0:T(8,128)(2,1)S(1)} %get-tuple-element.46), channel_id=1, source_target_pairs={{0,4},{4,0},{8,12},{12,8},{1,5},{5,1},{9,13},{13,9},{2,6},{6,2},{1... | collective-permute-start | bytes 76808 | tf_op jit(solution)/shard_map/ppermute | solution.py:412

commit v10 on v9

--- a/solution.py
+++ b/solution.py
@@ -14,6 +14,8 @@
 GROUP = 4
 CHUNK = 128
 LOADS = 4
+COST_F = 4_000_000_000
+COST_B = 12_000_000
 VMEM_LIMIT = 32 * 1024 * 1024
 
 BF16 = jnp.bfloat16
@@ -145,50 +147,31 @@
             pltpu.SemaphoreType.DMA((4 + 2 * LOADS,)),
         ],
         compiler_params=params(),
+        cost_estimate=pl.CostEstimate(flops=COST_F, bytes_accessed=COST_B, transcendentals=0),
         name="dispatch",
     )(*(in_hbm(array) for array in (plan, caps, ids, gates, tokens, grads)))
     return outs[:pieces], outs[pieces:]
 
 
-def load_kernel(
-    gate_hbm, up_hbm, down_hbm, scaled_ref, pick_ref, gate_ref, up_ref, down_ref, merge_ref, sems
-):
-    copies = []
-    for source, target in ((gate_hbm, gate_ref), (up_hbm, up_ref), (down_hbm, down_ref)):
-        for start, size in spans(source.shape[0], source.shape[0] // LOADS):
-            rows = pl.ds(start, size)
-            copies.append(
-                pltpu.make_async_copy(source.at[rows], target.at[rows], sems.at[len(copies)])
-            )
-    for copy in copies:
-        copy.start()
+def merge_kernel(scaled_ref, pick_ref, merge_ref):
     scaled = scaled_ref[...].T
     count = scaled.shape[0]
     high = scaled.astype(BF16)
     merge_ref[:count, :] = high
     merge_ref[count : 2 * count, :] = (scaled - high.astype(F32)).astype(BF16)
     merge_ref[2 * count :, :] = pick_ref[...].T.astype(BF16)
-    for copy in copies:
-        copy.wait()
-
-
-def load_weights(gate, up, down, scaled, pick):
-    hbm = pl.BlockSpec(memory_space=pltpu.HBM)
+
+
+def merged(scaled, pick):
     vmem = pl.BlockSpec(memory_space=pltpu.VMEM)
-    assert all(w.shape[0] % (16 * LOADS) == 0 for w in (gate, up, down))
-    merge = jax.ShapeDtypeStruct((3 * pick.shape[1], pick.shape[0]), BF16)
     return pl.pallas_call(
-        load_kernel,
-        out_shape=tuple(pltpu.VMEM(w.shape, BF16) for w in (gate, up, down)) + (merge,),
-        in_specs=[hbm, hbm, hbm, vmem, vmem],
-        out_specs=(vmem,) * 4,
-        scratch_shapes=[pltpu.SemaphoreType.DMA((3 * LOADS,))],
+        merge_kernel,
+        out_shape=jax.ShapeDtypeStruct((3 * pick.shape[1], pick.shape[0]), BF16),
+        in_specs=[vmem, vmem],
+        out_specs=vmem,
         compiler_params=params(),
-        cost_estimate=pl.CostEstimate(
-            flops=0, bytes_accessed=2 * 3 * gate.size * 2, transcendentals=0
-        ),
-        name="load_weights",
-    )(in_hbm(gate), in_hbm(up), in_hbm(down), scaled, pick)
+        name="merge",
+    )(scaled, pick)
 
 
 def half_columns(which, width):
@@ -456,7 +439,8 @@
         pieces,
     )
     recvs = over_experts(sends, experts)
-    *weights, merge = load_weights(gate, up, down, scaled, pick)
+    weights = (gate, up, down)
+    merge = merged(scaled, pick)
     steps, total, half = experts // GROUP, experts * slots, 3 * width // 2
     layout = (slots, chunks, pieces)
     flops = 3 * total * feature * width

time: 28.3 us -> 28.3 us (level)
  waiting for transfers between devices: 7.06 us -> 8.96 us
  Pallas kernels: 8.39 us -> 6.53 us
    pallas_call x1, Pallas kernels: 2.01 us -> 0.1 us  [merged(): pl.pallas_call(merge_kernel, out_shape=jax.ShapeDtypeStruct((3 * pick.sha...]
    ppermute x9, waiting for transfers between devices: 7.06 us -> 8.96 us  [swapped(): lax.ppermute(array, axis, [(i, i ^ distance) for i in range(lax.axis_size...]
  transfers between devices with their start and end apart: 9 -> 9, of which waited for: 5 -> 5; matrix products, arithmetic and copies ran while one was open for 0% -> 0% of each run, Pallas kernels for 17% -> 11%
where the time goes in v10:
time: 28.3 us; the launch traced here: 28.2 us
  starting transfers between devices  11.9 us (42%)
  waiting for transfers between devices  8.96 us (32%)
  Pallas kernels  6.53 us (23%)
  between operations  0.77 us (3%)
    ppermute x9, starting transfers between devices, swapped(): lax.ppermute(array, axis, [(i, i ^ distance) for i in range(lax.axis_size...  11.9 us
    ppermute x9, waiting for transfers between devices, swapped(): lax.ppermute(array, axis, [(i, i ^ distance) for i in range(lax.axis_size...  8.96 us
    pallas_call x6, Pallas kernels, by_rows(): pl.pallas_call(kernel, grid=(steps,), out_shape=tuple((jax.ShapeDtypeStru...  2.03 us
    pallas_call x1, Pallas kernels, weight_grads(): pl.pallas_call(grads_kernel, out_shape=tuple((jax.ShapeDtypeStruct(shape,...  1.97 us
    pallas_call x1, Pallas kernels, dispatch(): pl.pallas_call(functools.partial(dispatch_kernel, experts, plan.shape[1],...  1.43 us
    pallas_call x1, Pallas kernels, combine(): pl.pallas_call(functools.partial(combine_kernel, columns, slots, chunks,...  1 us
  transfers between devices with their start and end apart: 9, of which 5 were waited for; matrix products, arithmetic and copies ran while one was open for 0% of the time, Pallas kernels for 11%

profile of v10, /device:TPU:0, one launch (start us, length us, event | category | flops | bytes accessed | tf_op | source)
XLA Modules:
  0.0 28.2 jit_solution(10327166494573298408)
XLA Ops:
  0.6 0.0 copy-start
  0.6 0.0 copy-start.1
  0.7 0.0 copy-start.2
  0.7 1.4 %dispatch.1 = (bf16[100,128]{1,0:T(8,128)(2,1)S(1)}, bf16[100,128]{1,0:T(8,128)(2,1)S(1)}, bf16[100,128]{1,0:T(8,128)(2,1)S(1)}, bf16[100,128]{1,0:T(8,128)(2,1)...) custom-call(s32[2,2]{1,0:T(2,128)} %refs_0_.1, s32[4]{0:T(128)} %refs_1_.1, s32[2,128]{1,0:T(2,128)} %bitcast.20, ...), custom_call_target="tpu_custom_call" | custom-call | flops 4000000000 | bytes 12000000 | tf_op jit(solution)/shard_map/dispatch/pallas_call | solution.py:134
  2.1 5.1 %collective-permute-start = (bf16[100,128]{1,0:T(8,128)(2,1)S(1)}, bf16[100,128]{1,0:T(8,128)(2,1)S(1)}, u32[]{:S(2)}, u32[]{:S(2)}) collective-permute-start(bf16[100,128]{1,0:T(8,128)(2,1)S(1)} %get-tuple-element.26), channel_id=1, source_target_pairs={{0,12},{4,8},{8,4},{12,0},{1,13},{5,9},{9,5},{13,1},{2,14},{6,10},... | collective-permute-start | bytes 76808 | tf_op jit(solution)/shard_map/ppermute | solution.py:395
  7.2 0.0 collective-permute-start.1
  7.2 0.6 %collective-permute-start.2 = (bf16[100,128]{1,0:T(8,128)(2,1)S(1)}, bf16[100,128]{1,0:T(8,128)(2,1)S(1)}, u32[]{:S(2)}, u32[]{:S(2)}) collective-permute-start(bf16[100,128]{1,0:T(8,128)(2,1)S(1)} %get-tuple-element.28), channel_id=1, source_target_pairs={{0,4},{4,0},{8,12},{12,8},{1,5},{5,1},{9,13},{13,9},{2,6},{6,2},{1... | collective-permute-start | bytes 76808 | tf_op jit(solution)/shard_map/ppermute | solution.py:395
  7.9 1.2 %collective-permute-done.refs_1_ = bf16[100,128]{1,0:T(8,128)(2,1)S(1)} collective-permute-done((bf16[100,128]{1,0:T(8,128)(2,1)S(1)}, bf16[100,128]{1,0:T(8,128)(2,1)S(1)}, u32[]{:S(2)}, u32[]{:S(2)}) %collective-permute-start) | collective-permute-done | bytes 25632 | tf_op jit(solution)/shard_map/ppermute | solution.py:395
  9.0 2.9 %collective-permute-done.1.refs_2_ = bf16[100,128]{1,0:T(8,128)(2,1)S(1)} collective-permute-done((bf16[100,128]{1,0:T(8,128)(2,1)S(1)}, bf16[100,128]{1,0:T(8,128)(2,1)S(1)}, u32[]{:S(2)}, u32[]{:S(2)}) %collective-permute-start.1) | collective-permute-done | bytes 25632 | tf_op jit(solution)/shard_map/ppermute | solution.py:395
  12.0 0.0 collective-permute-done.2.refs_3_
  12.0 0.0 copy-done
  12.0 0.0 copy-done.1
  12.0 0.0 copy-done.2
  12.0 0.5 %give.1 = (bf16[40,640]{1,0:T(8,128)(2,1)S(1)}, bf16[40,640]{1,0:T(8,128)(2,1)S(1)}, bf16[40,1152]{1,0:T(8,128)(2,1)S(1)}) custom-call(bf16[100,128]{1,0:T(8,128)(2,1)S(1)} %get-tuple-element.25.refs_0_, bf16[100,128]{1,0:T(8,128)(2,1)S(1)} %collective-permute-done.refs_1_, bf16[100,128]{1,0:T(8,128)(2,1)S(1)} %collective-permute-done.1.refs_2_, ...), custom_call_target="tpu_custom_call" | custom-call | flops 58982400 | bytes 3051520 | tf_op jit(solution)/shard_map/give/pallas_call | solution.py:272
  12.5 0.1 collective-permute-start.3
  12.5 0.4 %keep.1.left_ref = bf16[40,1152]{1,0:T(8,128)(2,1)S(1)} custom-call(bf16[40,640]{1,0:T(8,128)(2,1)S(1)} %get-tuple-element.29.rows_ref, bf16[40,640]{1,0:T(8,128)(2,1)S(1)} %get-tuple-element.30.cots_ref, bf16[640,768]{1,0:T(8,128)(2,1)S(1)} %bitcast.9, bf16[640,768]{1,0:T(8,128)(2,1)S(1)} %bitcast.13, bf16[768,640]{1,0:T(8,128)(2,1)S(1)} %bitcast.17), custom_call_target="tpu_custom_call" | custom-call | flops 58982400 | bytes 3051520 | tf_op jit(solution)/shard_map/keep/pallas_call | solution.py:272
  13.0 0.8 %collective-permute-done.3.right_ref = bf16[40,1152]{1,0:T(8,128)(2,1)S(1)} collective-permute-done((bf16[40,1152]{1,0:T(8,128)(2,1)S(1)}, bf16[40,1152]{1,0:T(8,128)(2,1)S(1)}, u32[]{:S(2)}, u32[]{:S(2)}) %collective-permute-start.3) | collective-permute-done | bytes 92192 | tf_op jit(solution)/shard_map/ppermute | solution.py:395
  13.8 1.6 %collective-permute-start.4 = (bf16[40,1152]{1,0:T(8,128)(2,1)S(1)}, bf16[40,1152]{1,0:T(8,128)(2,1)S(1)}, u32[]{:S(2)}, u32[]{:S(2)}) collective-permute-start(bf16[40,1152]{1,0:T(8,128)(2,1)S(1)} %add.1.near_ref), channel_id=1, source_target_pairs={{0,2},{1,3},{2,0},{3,1},{4,6},{5,7},{6,4},{7,5},{8,10},{9,11},{10,... | collective-permute-start | bytes 276488 | tf_op jit(solution)/shard_map/ppermute | solution.py:395
  15.4 3.2 %collective-permute-done.4.far_ref = bf16[40,1152]{1,0:T(8,128)(2,1)S(1)} collective-permute-done((bf16[40,1152]{1,0:T(8,128)(2,1)S(1)}, bf16[40,1152]{1,0:T(8,128)(2,1)S(1)}, u32[]{:S(2)}, u32[]{:S(2)}) %collective-permute-start.4) | collective-permute-done | bytes 92192 | tf_op jit(solution)/shard_map/ppermute | solution.py:395
  18.6 0.1 activate.1.mine_ref
  18.7 0.1 collective-permute-start.5
  18.8 0.5 %own.1 = (f32[40,640]{1,0:T(8,128)S(1)}, f32[40,640]{1,0:T(8,128)S(1)}) custom-call(bf16[40,1152]{1,0:T(8,128)(2,1)S(1)} %activate.1.mine_ref, bf16[640,768]{1,0:T(8,128)(2,1)S(1)} %bitcast.10, bf16[640,768]{1,0:T(8,128)(2,1)S(1)} %bitcast.14, bf16[768,640]{1,0:T(8,128)(2,1)S(1)} %bitcast.18), custom_call_target="tpu_custom_call" | custom-call | flops 58982400 | bytes 3041280 | tf_op jit(solution)/shard_map/own/pallas_call | solution.py:272
  19.3 0.8 %collective-permute-done.5.refs_0_.theirs_ref = bf16[40,1152]{1,0:T(8,128)(2,1)S(1)} collective-permute-done((bf16[40,1152]{1,0:T(8,128)(2,1)S(1)}, bf16[40,1152]{1,0:T(8,128)(2,1)S(1)}, u32[]{:S(2)}, u32[]{:S(2)}) %collective-permute-start.5) | collective-permute-done | bytes 92192 | tf_op jit(solution)/shard_map/ppermute | solution.py:395
  20.0 0.5 %back.1 = (bf16[100,128]{1,0:T(8,128)(2,1)S(1)}, bf16[100,128]{1,0:T(8,128)(2,1)S(1)}, bf16[100,128]{1,0:T(8,128)(2,1)S(1)}, bf16[100,128]{1,0:T(8,128)(2,1)S(1)}) custom-call(bf16[40,1152]{1,0:T(8,128)(2,1)S(1)} %collective-permute-done.5.refs_0_.theirs_ref, f32[40,640]{1,0:T(8,128)S(1)} %get-tuple-element.32.refs_1_, ...), custom_call_target="tpu_custom_call" | custom-call | flops 58982400 | bytes 3246080 | tf_op jit(solution)/shard_map/back/pallas_call | solution.py:272
  20.6 1.5 %collective-permute-start.6 = (bf16[100,128]{1,0:T(8,128)(2,1)S(1)}, bf16[100,128]{1,0:T(8,128)(2,1)S(1)}, u32[]{:S(2)}, u32[]{:S(2)}) collective-permute-start(bf16[100,128]{1,0:T(8,128)(2,1)S(1)} %get-tuple-element.35), channel_id=1, source_target_pairs={{0,12},{4,8},{8,4},{12,0},{1,13},{5,9},{9,5},{13,1},{2,14},{6,10},... | collective-permute-start | bytes 76808 | tf_op jit(solution)/shard_map/ppermute | solution.py:395
  22.1 0.6 %collective-permute-start.7 = (bf16[100,128]{1,0:T(8,128)(2,1)S(1)}, bf16[100,128]{1,0:T(8,128)(2,1)S(1)}, u32[]{:S(2)}, u32[]{:S(2)}) collective-permute-start(bf16[100,128]{1,0:T(8,128)(2,1)S(1)} %get-tuple-element.36), channel_id=1, source_target_pairs={{0,8},{4,12},{8,0},{12,4},{1,9},{5,13},{9,1},{13,5},{2,10},{6,14},... | collective-permute-start | bytes 76808 | tf_op jit(solution)/shard_map/ppermute | solution.py:395
  22.8 2.3 %collective-permute-start.8 = (bf16[100,128]{1,0:T(8,128)(2,1)S(1)}, bf16[100,128]{1,0:T(8,128)(2,1)S(1)}, u32[]{:S(2)}, u32[]{:S(2)}) collective-permute-start(bf16[100,128]{1,0:T(8,128)(2,1)S(1)} %get-tuple-element.37), channel_id=1, source_target_pairs={{0,4},{4,0},{8,12},{12,8},{1,5},{5,1},{9,13},{13,9},{2,6},{6,2},{1... | collective-permute-start | bytes 76808 | tf_op jit(solution)/shard_map/ppermute | solution.py:395
  25.1 0.1 merge.1.refs_4_
  25.2 2.0 %weight_grads.1 = (bf16[640,768]{1,0:T(8,128)(2,1)}, bf16[640,768]{1,0:T(8,128)(2,1)}, bf16[768,640]{1,0:T(8,128)(2,1)}) custom-call(bf16[40,640]{1,0:T(8,128)(2,1)S(1)} %get-tuple-element.29.rows_ref, bf16[40,640]{1,0:T(8,128)(2,1)S(1)} %get-tuple-element.30.cots_ref, bf16[40,1152]{1,0:T(8,128)(2,1)S(1)} %activate.1.mine_ref, ...), custom_call_target="tpu_custom_call" | custom-call | flops 117964800 | bytes 2949120 | tf_op jit(solution)/shard_map/weight_grads/pallas_call | solution.py:324
  27.1 0.0 collective-permute-done.6.refs_1_
  27.1 0.0 collective-permute-done.7.refs_2_
  27.2 0.0 collective-permute-done.8.refs_3_
  27.2 1.0 %combine.1 = (bf16[128,640]{1,0:T(8,128)(2,1)}, bf16[128,640]{1,0:T(8,128)(2,1)}) custom-call(bf16[100,128]{1,0:T(8,128)(2,1)S(1)} %get-tuple-element.34.refs_0_, bf16[100,128]{1,0:T(8,128)(2,1)S(1)} %collective-permute-done.6.refs_1_, bf16[100,128]{1,0:T(8,128)(2,1)S(1)} %collective-permute-done.7.refs_2_, ...), custom_call_target="tpu_custom_call" | custom-call | tf_op jit(solution)/shard_map/combine/pallas_call | solution.py:378
  (1 shorter events, 0.0 us)
Async XLA Ops:
  0.6 11.3 %copy-start = (bf16[1,640,768]{2,1,0:T(8,128)(2,1)S(1)}, bf16[1,640,768]{2,1,0:T(8,128)(2,1)}, u32[]{:S(2)}) copy-start(bf16[1,640,768]{2,1,0:T(8,128)(2,1)} %param.15) | copy-start | bytes 2949124
  0.6 11.3 %copy-start.1 = (bf16[1,640,768]{2,1,0:T(8,128)(2,1)S(1)}, bf16[1,640,768]{2,1,0:T(8,128)(2,1)}, u32[]{:S(2)}) copy-start(bf16[1,640,768]{2,1,0:T(8,128)(2,1)} %param.16) | copy-start | bytes 2949124
  0.7 11.3 %copy-start.2 = (bf16[1,768,640]{2,1,0:T(8,128)(2,1)S(1)}, bf16[1,768,640]{2,1,0:T(8,128)(2,1)}, u32[]{:S(2)}) copy-start(bf16[1,768,640]{2,1,0:T(8,128)(2,1)} %param.17) | copy-start | bytes 2949124
  2.1 6.9 %collective-permute-start = (bf16[100,128]{1,0:T(8,128)(2,1)S(1)}, bf16[100,128]{1,0:T(8,128)(2,1)S(1)}, u32[]{:S(2)}, u32[]{:S(2)}) collective-permute-start(bf16[100,128]{1,0:T(8,128)(2,1)S(1)} %get-tuple-element.26), channel_id=1, source_target_pairs={{0,12},{4,8},{8,4},{12,0},{1,13},{5,9},{9,5},{13,1},{2,14},{6,10},... | collective-permute-start | bytes 76808 | tf_op jit(solution)/shard_map/ppermute | solution.py:395
  7.2 4.7 %collective-permute-start.1 = (bf16[100,128]{1,0:T(8,128)(2,1)S(1)}, bf16[100,128]{1,0:T(8,128)(2,1)S(1)}, u32[]{:S(2)}, u32[]{:S(2)}) collective-permute-start(bf16[100,128]{1,0:T(8,128)(2,1)S(1)} %get-tuple-element.27), channel_id=1, source_target_pairs={{0,8},{4,12},{8,0},{12,4},{1,9},{5,13},{9,1},{13,5},{2,10},{6,14},... | collective-permute-start | bytes 76808 | tf_op jit(solution)/shard_map/ppermute | solution.py:395
  7.2 4.7 %collective-permute-start.2 = (bf16[100,128]{1,0:T(8,128)(2,1)S(1)}, bf16[100,128]{1,0:T(8,128)(2,1)S(1)}, u32[]{:S(2)}, u32[]{:S(2)}) collective-permute-start(bf16[100,128]{1,0:T(8,128)(2,1)S(1)} %get-tuple-element.28), channel_id=1, source_target_pairs={{0,4},{4,0},{8,12},{12,8},{1,5},{5,1},{9,13},{13,9},{2,6},{6,2},{1... | collective-permute-start | bytes 76808 | tf_op jit(solution)/shard_map/ppermute | solution.py:395
  12.5 1.4 %collective-permute-start.3 = (bf16[40,1152]{1,0:T(8,128)(2,1)S(1)}, bf16[40,1152]{1,0:T(8,128)(2,1)S(1)}, u32[]{:S(2)}, u32[]{:S(2)}) collective-permute-start(bf16[40,1152]{1,0:T(8,128)(2,1)S(1)} %get-tuple-element.31), channel_id=1, source_target_pairs={{0,1},{1,0},{2,3},{3,2},{4,5},{5,4},{6,7},{7,6},{8,9},{9,8},{10,11... | collective-permute-start | bytes 276488 | tf_op jit(solution)/shard_map/ppermute | solution.py:395
  13.8 4.8 %collective-permute-start.4 = (bf16[40,1152]{1,0:T(8,128)(2,1)S(1)}, bf16[40,1152]{1,0:T(8,128)(2,1)S(1)}, u32[]{:S(2)}, u32[]{:S(2)}) collective-permute-start(bf16[40,1152]{1,0:T(8,128)(2,1)S(1)} %add.1.near_ref), channel_id=1, source_target_pairs={{0,2},{1,3},{2,0},{3,1},{4,6},{5,7},{6,4},{7,5},{8,10},{9,11},{10,... | collective-permute-start | bytes 276488 | tf_op jit(solution)/shard_map/ppermute | solution.py:395
  18.7 1.4 %collective-permute-start.5 = (bf16[40,1152]{1,0:T(8,128)(2,1)S(1)}, bf16[40,1152]{1,0:T(8,128)(2,1)S(1)}, u32[]{:S(2)}, u32[]{:S(2)}) collective-permute-start(bf16[40,1152]{1,0:T(8,128)(2,1)S(1)} %activate.1.mine_ref), channel_id=1, source_target_pairs={{0,1},{1,0},{2,3},{3,2},{4,5},{5,4},{6,7},{7,6},{8,9},{9,8},{10,11... | collective-permute-start | bytes 276488 | tf_op jit(solution)/shard_map/ppermute | solution.py:395
  20.6 6.5 %collective-permute-start.6 = (bf16[100,128]{1,0:T(8,128)(2,1)S(1)}, bf16[100,128]{1,0:T(8,128)(2,1)S(1)}, u32[]{:S(2)}, u32[]{:S(2)}) collective-permute-start(bf16[100,128]{1,0:T(8,128)(2,1)S(1)} %get-tuple-element.35), channel_id=1, source_target_pairs={{0,12},{4,8},{8,4},{12,0},{1,13},{5,9},{9,5},{13,1},{2,14},{6,10},... | collective-permute-start | bytes 76808 | tf_op jit(solution)/shard_map/ppermute | solution.py:395
  22.1 5.0 %collective-permute-start.7 = (bf16[100,128]{1,0:T(8,128)(2,1)S(1)}, bf16[100,128]{1,0:T(8,128)(2,1)S(1)}, u32[]{:S(2)}, u32[]{:S(2)}) collective-permute-start(bf16[100,128]{1,0:T(8,128)(2,1)S(1)} %get-tuple-element.36), channel_id=1, source_target_pairs={{0,8},{4,12},{8,0},{12,4},{1,9},{5,13},{9,1},{13,5},{2,10},{6,14},... | collective-permute-start | bytes 76808 | tf_op jit(solution)/shard_map/ppermute | solution.py:395
  22.8 4.4 %collective-permute-start.8 = (bf16[100,128]{1,0:T(8,128)(2,1)S(1)}, bf16[100,128]{1,0:T(8,128)(2,1)S(1)}, u32[]{:S(2)}, u32[]{:S(2)}) collective-permute-start(bf16[100,128]{1,0:T(8,128)(2,1)S(1)} %get-tuple-element.37), channel_id=1, source_target_pairs={{0,4},{4,0},{8,12},{12,8},{1,5},{5,1},{9,13},{13,9},{2,6},{6,2},{1... | collective-permute-start | bytes 76808 | tf_op jit(solution)/shard_map/ppermute | solution.py:395

commit v11 on v10

--- a/solution.py
+++ b/solution.py
@@ -84,11 +84,12 @@
     cots = jnp.concatenate([is_cot.astype(F32)] * experts, axis=0)
     for copy in copies[:4]:
         copy.wait()
+    places = lax.broadcasted_iota(I32, (1, experts), 1)
     members, weights, limits = [], [], []
     for index in range(experts):
         expert = index if pieces == 1 else me ^ distance(index, experts)
-        hot = (plan_ref[0, 0] == expert) | (plan_ref[1, 0] == expert)
-        wanted = token_slot * hot.astype(I32)
+        hot = (plan_ref[0:1, 0:1] == expert) | (plan_ref[1:2, 0:1] == expert)
+        wanted = jnp.where(hot, token_slot[:1], 0)
         here = jnp.zeros((1, count), F32)
         weight = jnp.zeros((1, count), F32)
         for k in range(choose):
@@ -98,7 +99,8 @@
         fits = valid & (replica == wanted)
         members.append(jnp.where(fits, jnp.broadcast_to(here, fits.shape), 0.0))
         weights.append(jnp.broadcast_to(weight, fits.shape))
-        room = jnp.where(is_spare, SPARE, caps_ref[expert] * BLK)
+        own_room = jnp.sum(jnp.where(places == expert, caps_ref[...], 0), axis=1, keepdims=True)
+        room = jnp.where(is_spare, SPARE, own_room * BLK)
         limits.append(jnp.where(position < room, position, -1))
     member = jnp.concatenate(members, axis=0)
     weight = jnp.concatenate(weights, axis=0)
@@ -138,8 +140,8 @@
         in_specs=[pl.BlockSpec(memory_space=pltpu.HBM)] * 6,
         out_specs=(vmem,) * (pieces + 2),
         scratch_shapes=[
-            pltpu.SMEM(plan.shape, I32),
-            pltpu.SMEM(caps.shape, I32),
+            pltpu.VMEM(plan.shape, I32),
+            pltpu.VMEM(caps.shape, I32),
             pltpu.VMEM(ids.shape, I32),
             pltpu.VMEM(gates.shape, F32),
             pltpu.VMEM((2 * count, feature), BF16),
@@ -151,27 +153,6 @@
         name="dispatch",
     )(*(in_hbm(array) for array in (plan, caps, ids, gates, tokens, grads)))
     return outs[:pieces], outs[pieces:]
-
-
-def merge_kernel(scaled_ref, pick_ref, merge_ref):
-    scaled = scaled_ref[...].T
-    count = scaled.shape[0]
-    high = scaled.astype(BF16)
-    merge_ref[:count, :] = high
-    merge_ref[count : 2 * count, :] = (scaled - high.astype(F32)).astype(BF16)
-    merge_ref[2 * count :, :] = pick_ref[...].T.astype(BF16)
-
-
-def merged(scaled, pick):
-    vmem = pl.BlockSpec(memory_space=pltpu.VMEM)
-    return pl.pallas_call(
-        merge_kernel,
-        out_shape=jax.ShapeDtypeStruct((3 * pick.shape[1], pick.shape[0]), BF16),
-        in_specs=[vmem, vmem],
-        out_specs=vmem,
-        compiler_params=params(),
-        name="merge",
-    )(scaled, pick)
 
 
 def half_columns(which, width):
@@ -237,8 +218,14 @@
     return outs, ins + matmul(acts_ref[:, 2 * half :], up_ref[:, units], 1, 1)
 
 
-def own_kernel(mine_ref, gate_ref, up_ref, down_ref, outs_ref, ins_ref):
+def own_kernel(mine_ref, scaled_ref, pick_ref, gate_ref, up_ref, down_ref, outs_ref, ins_ref, merge_ref):
     outs_ref[...], ins_ref[...] = half_outputs(0, mine_ref, gate_ref, up_ref, down_ref)
+    scaled = scaled_ref[...].T
+    count = scaled.shape[0]
+    high = scaled.astype(BF16)
+    merge_ref[:count, :] = high
+    merge_ref[count : 2 * count, :] = (scaled - high.astype(F32)).astype(BF16)
+    merge_ref[2 * count :, :] = pick_ref[...].T.astype(BF16)
 
 
 def back_kernel(slots, chunks, pieces, *refs):
@@ -354,7 +341,11 @@
     for start, size in columns:
         part = pl.ds(start, size)
         back = back_refs[0][:, part] if pieces == 1 else flat[:, part].astype(BF16)
-        sums = matmul(merge_ref[...], back, 1, 0)
+        depth = merge_ref.shape[1]
+        sums = sum(
+            matmul(merge_ref[3 * count * i : 3 * count * (i + 1), :], back[i * depth : (i + 1) * depth], 1, 0)
+            for i in range(back.shape[0] // depth)
+        )
         mixed_ref[:, part] = (sums[:count] + sums[count : 2 * count]).astype(BF16)
         token_ref[:, part] = sums[2 * count :].astype(BF16)
         for source, target in ((mixed_ref, mixed_hbm), (token_ref, token_hbm)):
@@ -368,8 +359,8 @@
         copy.wait()
 
 
-def combine(backs, merge, slots, chunks):
-    pieces, feature, count = len(backs), chunks * backs[0].shape[1], merge.shape[0] // 3
+def combine(backs, merge, count, slots, chunks):
+    pieces, feature = len(backs), chunks * backs[0].shape[1]
     columns = spans(feature, 2 * CHUNK if feature % CHUNK == 0 else feature)
     vmem = pl.BlockSpec(memory_space=pltpu.VMEM)
     hbm = pl.BlockSpec(memory_space=pltpu.HBM)
@@ -428,7 +419,7 @@
     block = 2 * slots * chunks if pieces > 1 else padded(2 * slots)
     sends, (scaled, pick) = dispatch(
         replica_plan,
-        cap_blocks,
+        cap_blocks[None],
         expert_ids.T,
         gate_weights.T,
         tokens,
@@ -440,7 +431,6 @@
     )
     recvs = over_experts(sends, experts)
     weights = (gate, up, down)
-    merge = merged(scaled, pick)
     steps, total, half = experts // GROUP, experts * slots, 3 * width // 2
     layout = (slots, chunks, pieces)
     flops = 3 * total * feature * width
@@ -471,8 +461,16 @@
     far = swapped(near, "dp", last)
     mine = by_rows(activate_kernel, "activate", steps, [near, far], [], [((total, half), BF16)])
     theirs = swapped(mine, "dp", 1)
-    outs, ins = by_rows(
-        own_kernel, "own", steps, [mine], weights, [((total, feature), F32)] * 2, (), flops
+    merge_shape = (steps * 3 * pick.shape[1], pick.shape[0] // steps)
+    outs, ins, merge = by_rows(
+        own_kernel,
+        "own",
+        steps,
+        [mine, scaled, pick],
+        weights,
+        [((total, feature), F32), ((total, feature), F32), (merge_shape, BF16)],
+        (),
+        flops,
     )
     backs = by_rows(
         functools.partial(back_kernel, *layout),
@@ -486,7 +484,7 @@
     )
     returned = over_experts(backs if pieces > 1 else [backs], experts)
     gate_grad, up_grad, down_grad = weight_grads(rows, cots, mine, theirs)
-    mixed, token_grad = combine(returned, merge, slots, chunks)
+    mixed, token_grad = combine(returned, merge, tokens.shape[0], slots, chunks)
     return mixed, token_grad, gate_grad[None], up_grad[None], down_grad[None]
 
 

time: 28.3 us -> 28.4 us (level)
  transfers between devices with their start and end apart: 9 -> 9, of which waited for: 5 -> 6; matrix products, arithmetic and copies ran while one was open for 0% -> 0% of each run, Pallas kernels for 11% -> 10%
where the time goes in v11:
time: 28.4 us; the launch traced here: 28.2 us
  starting transfers between devices  11.9 us (42%)
  waiting for transfers between devices  9.07 us (32%)
  Pallas kernels  6.49 us (23%)
  between operations  0.76 us (3%)
    ppermute x9, starting transfers between devices, swapped(): lax.ppermute(array, axis, [(i, i ^ distance) for i in range(lax.axis_size...  11.9 us
    ppermute x9, waiting for transfers between devices, swapped(): lax.ppermute(array, axis, [(i, i ^ distance) for i in range(lax.axis_size...  9.07 us
    pallas_call x6, Pallas kernels, by_rows(): pl.pallas_call(kernel, grid=(steps,), out_shape=tuple((jax.ShapeDtypeStru...  2.04 us
    pallas_call x1, Pallas kernels, weight_grads(): pl.pallas_call(grads_kernel, out_shape=tuple((jax.ShapeDtypeStruct(shape,...  1.95 us
    pallas_call x1, Pallas kernels, dispatch(): pl.pallas_call(functools.partial(dispatch_kernel, experts, plan.shape[1],...  1.5 us
    pallas_call x1, Pallas kernels, combine(): pl.pallas_call(functools.partial(combine_kernel, columns, slots, chunks,...  0.99 us
  transfers between devices with their start and end apart: 9, of which 6 were waited for; matrix products, arithmetic and copies ran while one was open for 0% of the time, Pallas kernels for 10%

profile of v11, /device:TPU:0, one launch (start us, length us, event | category | flops | bytes accessed | tf_op | source)
XLA Modules:
  0.0 28.2 jit_solution(4289627836283797503)
XLA Ops:
  0.6 0.0 copy-start
  0.6 0.0 copy-start.1
  0.7 0.0 copy-start.2
  0.7 1.5 %dispatch.1 = (bf16[100,128]{1,0:T(8,128)(2,1)S(1)}, bf16[100,128]{1,0:T(8,128)(2,1)S(1)}, bf16[100,128]{1,0:T(8,128)(2,1)S(1)}, bf16[100,128]{1,0:T(8,128)(2,1)...) custom-call(s32[2,2]{1,0:T(2,128)} %refs_0_.1, s32[1,4]{1,0:T(1,128)} %bitcast.23, s32[2,128]{1,0:T(2,128)} %bitcast.21, ...), custom_call_target="tpu_custom_call" | custom-call | flops 4000000000 | bytes 12000000 | tf_op jit(solution)/shard_map/dispatch/pallas_call | solution.py:136
  2.2 5.1 %collective-permute-start = (bf16[100,128]{1,0:T(8,128)(2,1)S(1)}, bf16[100,128]{1,0:T(8,128)(2,1)S(1)}, u32[]{:S(2)}, u32[]{:S(2)}) collective-permute-start(bf16[100,128]{1,0:T(8,128)(2,1)S(1)} %get-tuple-element.27), channel_id=1, source_target_pairs={{0,12},{4,8},{8,4},{12,0},{1,13},{5,9},{9,5},{13,1},{2,14},{6,10},... | collective-permute-start | bytes 76808 | tf_op jit(solution)/shard_map/ppermute | solution.py:386
  7.3 0.0 collective-permute-start.1
  7.3 0.6 %collective-permute-start.2 = (bf16[100,128]{1,0:T(8,128)(2,1)S(1)}, bf16[100,128]{1,0:T(8,128)(2,1)S(1)}, u32[]{:S(2)}, u32[]{:S(2)}) collective-permute-start(bf16[100,128]{1,0:T(8,128)(2,1)S(1)} %get-tuple-element.29), channel_id=1, source_target_pairs={{0,4},{4,0},{8,12},{12,8},{1,5},{5,1},{9,13},{13,9},{2,6},{6,2},{1... | collective-permute-start | bytes 76808 | tf_op jit(solution)/shard_map/ppermute | solution.py:386
  7.9 1.2 %collective-permute-done.refs_1_ = bf16[100,128]{1,0:T(8,128)(2,1)S(1)} collective-permute-done((bf16[100,128]{1,0:T(8,128)(2,1)S(1)}, bf16[100,128]{1,0:T(8,128)(2,1)S(1)}, u32[]{:S(2)}, u32[]{:S(2)}) %collective-permute-start) | collective-permute-done | bytes 25632 | tf_op jit(solution)/shard_map/ppermute | solution.py:386
  9.1 2.9 %collective-permute-done.1.refs_2_ = bf16[100,128]{1,0:T(8,128)(2,1)S(1)} collective-permute-done((bf16[100,128]{1,0:T(8,128)(2,1)S(1)}, bf16[100,128]{1,0:T(8,128)(2,1)S(1)}, u32[]{:S(2)}, u32[]{:S(2)}) %collective-permute-start.1) | collective-permute-done | bytes 25632 | tf_op jit(solution)/shard_map/ppermute | solution.py:386
  12.0 0.0 collective-permute-done.2.refs_3_
  12.0 0.0 copy-done
  12.0 0.0 copy-done.1
  12.0 0.0 copy-done.2
  12.1 0.5 %give.1 = (bf16[40,640]{1,0:T(8,128)(2,1)S(1)}, bf16[40,640]{1,0:T(8,128)(2,1)S(1)}, bf16[40,1152]{1,0:T(8,128)(2,1)S(1)}) custom-call(bf16[100,128]{1,0:T(8,128)(2,1)S(1)} %get-tuple-element.26.refs_0_, bf16[100,128]{1,0:T(8,128)(2,1)S(1)} %collective-permute-done.refs_1_, bf16[100,128]{1,0:T(8,128)(2,1)S(1)} %collective-permute-done.1.refs_2_, ...), custom_call_target="tpu_custom_call" | custom-call | flops 58982400 | bytes 3051520 | tf_op jit(solution)/shard_map/give/pallas_call | solution.py:259
  12.5 0.1 collective-permute-start.3
  12.6 0.4 %keep.1.left_ref = bf16[40,1152]{1,0:T(8,128)(2,1)S(1)} custom-call(bf16[40,640]{1,0:T(8,128)(2,1)S(1)} %get-tuple-element.30.rows_ref, bf16[40,640]{1,0:T(8,128)(2,1)S(1)} %get-tuple-element.31.cots_ref, bf16[640,768]{1,0:T(8,128)(2,1)S(1)} %bitcast.10, bf16[640,768]{1,0:T(8,128)(2,1)S(1)} %bitcast.14, bf16[768,640]{1,0:T(8,128)(2,1)S(1)} %bitcast.18), custom_call_target="tpu_custom_call" | custom-call | flops 58982400 | bytes 3051520 | tf_op jit(solution)/shard_map/keep/pallas_call | solution.py:259
  13.1 0.8 %collective-permute-done.3.right_ref = bf16[40,1152]{1,0:T(8,128)(2,1)S(1)} collective-permute-done((bf16[40,1152]{1,0:T(8,128)(2,1)S(1)}, bf16[40,1152]{1,0:T(8,128)(2,1)S(1)}, u32[]{:S(2)}, u32[]{:S(2)}) %collective-permute-start.3) | collective-permute-done | bytes 92192 | tf_op jit(solution)/shard_map/ppermute | solution.py:386
  13.9 1.6 %collective-permute-start.4 = (bf16[40,1152]{1,0:T(8,128)(2,1)S(1)}, bf16[40,1152]{1,0:T(8,128)(2,1)S(1)}, u32[]{:S(2)}, u32[]{:S(2)}) collective-permute-start(bf16[40,1152]{1,0:T(8,128)(2,1)S(1)} %add.1.near_ref), channel_id=1, source_target_pairs={{0,2},{1,3},{2,0},{3,1},{4,6},{5,7},{6,4},{7,5},{8,10},{9,11},{10,... | collective-permute-start | bytes 276488 | tf_op jit(solution)/shard_map/ppermute | solution.py:386
  15.5 3.2 %collective-permute-done.4.far_ref = bf16[40,1152]{1,0:T(8,128)(2,1)S(1)} collective-permute-done((bf16[40,1152]{1,0:T(8,128)(2,1)S(1)}, bf16[40,1152]{1,0:T(8,128)(2,1)S(1)}, u32[]{:S(2)}, u32[]{:S(2)}) %collective-permute-start.4) | collective-permute-done | bytes 92192 | tf_op jit(solution)/shard_map/ppermute | solution.py:386
  18.7 0.1 activate.1.mine_ref
  18.8 0.1 collective-permute-start.5
  18.8 0.5 %own.1 = (f32[40,640]{1,0:T(8,128)S(1)}, f32[40,640]{1,0:T(8,128)S(1)}, bf16[384,96]{1,0:T(8,128)(2,1)S(1)}) custom-call(bf16[40,1152]{1,0:T(8,128)(2,1)S(1)} %activate.1.mine_ref, f32[96,128]{1,0:T(8,128)S(1)} %get-tuple-element.33.scaled_ref, f32[96,128]{1,0:T(8,128)S(1)} %get-tuple-element.34.pick_ref, bf16[640,768]{1,0:T(8,128)(2,1)S(1)} %bitcast.11, ...), custom_call_target="tpu_custom_call" | custom-call | flops 58982400 | bytes 3139584 | tf_op jit(solution)/shard_map/own/pallas_call | solution.py:259
  19.3 0.8 %collective-permute-done.5.refs_0_.theirs_ref = bf16[40,1152]{1,0:T(8,128)(2,1)S(1)} collective-permute-done((bf16[40,1152]{1,0:T(8,128)(2,1)S(1)}, bf16[40,1152]{1,0:T(8,128)(2,1)S(1)}, u32[]{:S(2)}, u32[]{:S(2)}) %collective-permute-start.5) | collective-permute-done | bytes 92192 | tf_op jit(solution)/shard_map/ppermute | solution.py:386
  20.1 0.5 %back.1 = (bf16[100,128]{1,0:T(8,128)(2,1)S(1)}, bf16[100,128]{1,0:T(8,128)(2,1)S(1)}, bf16[100,128]{1,0:T(8,128)(2,1)S(1)}, bf16[100,128]{1,0:T(8,128)(2,1)S(1)}) custom-call(bf16[40,1152]{1,0:T(8,128)(2,1)S(1)} %collective-permute-done.5.refs_0_.theirs_ref, f32[40,640]{1,0:T(8,128)S(1)} %get-tuple-element.35.refs_1_, ...), custom_call_target="tpu_custom_call" | custom-call | flops 58982400 | bytes 3246080 | tf_op jit(solution)/shard_map/back/pallas_call | solution.py:259
  20.7 1.5 %collective-permute-start.6 = (bf16[100,128]{1,0:T(8,128)(2,1)S(1)}, bf16[100,128]{1,0:T(8,128)(2,1)S(1)}, u32[]{:S(2)}, u32[]{:S(2)}) collective-permute-start(bf16[100,128]{1,0:T(8,128)(2,1)S(1)} %get-tuple-element.38), channel_id=1, source_target_pairs={{0,12},{4,8},{8,4},{12,0},{1,13},{5,9},{9,5},{13,1},{2,14},{6,10},... | collective-permute-start | bytes 76808 | tf_op jit(solution)/shard_map/ppermute | solution.py:386
  22.2 0.6 %collective-permute-start.7 = (bf16[100,128]{1,0:T(8,128)(2,1)S(1)}, bf16[100,128]{1,0:T(8,128)(2,1)S(1)}, u32[]{:S(2)}, u32[]{:S(2)}) collective-permute-start(bf16[100,128]{1,0:T(8,128)(2,1)S(1)} %get-tuple-element.39), channel_id=1, source_target_pairs={{0,8},{4,12},{8,0},{12,4},{1,9},{5,13},{9,1},{13,5},{2,10},{6,14},... | collective-permute-start | bytes 76808 | tf_op jit(solution)/shard_map/ppermute | solution.py:386
  22.8 2.3 %collective-permute-start.8 = (bf16[100,128]{1,0:T(8,128)(2,1)S(1)}, bf16[100,128]{1,0:T(8,128)(2,1)S(1)}, u32[]{:S(2)}, u32[]{:S(2)}) collective-permute-start(bf16[100,128]{1,0:T(8,128)(2,1)S(1)} %get-tuple-element.40), channel_id=1, source_target_pairs={{0,4},{4,0},{8,12},{12,8},{1,5},{5,1},{9,13},{13,9},{2,6},{6,2},{1... | collective-permute-start | bytes 76808 | tf_op jit(solution)/shard_map/ppermute | solution.py:386
  25.1 2.0 %weight_grads.1 = (bf16[640,768]{1,0:T(8,128)(2,1)}, bf16[640,768]{1,0:T(8,128)(2,1)}, bf16[768,640]{1,0:T(8,128)(2,1)}) custom-call(bf16[40,640]{1,0:T(8,128)(2,1)S(1)} %get-tuple-element.30.rows_ref, bf16[40,640]{1,0:T(8,128)(2,1)S(1)} %get-tuple-element.31.cots_ref, bf16[40,1152]{1,0:T(8,128)(2,1)S(1)} %activate.1.mine_ref, ...), custom_call_target="tpu_custom_call" | custom-call | flops 117964800 | bytes 2949120 | tf_op jit(solution)/shard_map/weight_grads/pallas_call | solution.py:311
  27.1 0.0 collective-permute-done.6.refs_1_
  27.1 0.0 collective-permute-done.7.refs_2_
  27.1 0.1 collective-permute-done.8.refs_3_
  27.2 1.0 %combine.1 = (bf16[128,640]{1,0:T(8,128)(2,1)}, bf16[128,640]{1,0:T(8,128)(2,1)}) custom-call(bf16[100,128]{1,0:T(8,128)(2,1)S(1)} %get-tuple-element.37.refs_0_, bf16[100,128]{1,0:T(8,128)(2,1)S(1)} %collective-permute-done.6.refs_1_, bf16[100,128]{1,0:T(8,128)(2,1)S(1)} %collective-permute-done.7.refs_2_, ...), custom_call_target="tpu_custom_call" | custom-call | tf_op jit(solution)/shard_map/combine/pallas_call | solution.py:369
  (1 shorter events, 0.0 us)
Async XLA Ops:
  0.6 11.4 %copy-start = (bf16[1,640,768]{2,1,0:T(8,128)(2,1)S(1)}, bf16[1,640,768]{2,1,0:T(8,128)(2,1)}, u32[]{:S(2)}) copy-start(bf16[1,640,768]{2,1,0:T(8,128)(2,1)} %param.15) | copy-start | bytes 2949124
  0.6 11.4 %copy-start.1 = (bf16[1,640,768]{2,1,0:T(8,128)(2,1)S(1)}, bf16[1,640,768]{2,1,0:T(8,128)(2,1)}, u32[]{:S(2)}) copy-start(bf16[1,640,768]{2,1,0:T(8,128)(2,1)} %param.16) | copy-start | bytes 2949124
  0.7 11.4 %copy-start.2 = (bf16[1,768,640]{2,1,0:T(8,128)(2,1)S(1)}, bf16[1,768,640]{2,1,0:T(8,128)(2,1)}, u32[]{:S(2)}) copy-start(bf16[1,768,640]{2,1,0:T(8,128)(2,1)} %param.17) | copy-start | bytes 2949124
  2.2 6.9 %collective-permute-start = (bf16[100,128]{1,0:T(8,128)(2,1)S(1)}, bf16[100,128]{1,0:T(8,128)(2,1)S(1)}, u32[]{:S(2)}, u32[]{:S(2)}) collective-permute-start(bf16[100,128]{1,0:T(8,128)(2,1)S(1)} %get-tuple-element.27), channel_id=1, source_target_pairs={{0,12},{4,8},{8,4},{12,0},{1,13},{5,9},{9,5},{13,1},{2,14},{6,10},... | collective-permute-start | bytes 76808 | tf_op jit(solution)/shard_map/ppermute | solution.py:386
  7.3 4.7 %collective-permute-start.1 = (bf16[100,128]{1,0:T(8,128)(2,1)S(1)}, bf16[100,128]{1,0:T(8,128)(2,1)S(1)}, u32[]{:S(2)}, u32[]{:S(2)}) collective-permute-start(bf16[100,128]{1,0:T(8,128)(2,1)S(1)} %get-tuple-element.28), channel_id=1, source_target_pairs={{0,8},{4,12},{8,0},{12,4},{1,9},{5,13},{9,1},{13,5},{2,10},{6,14},... | collective-permute-start | bytes 76808 | tf_op jit(solution)/shard_map/ppermute | solution.py:386
  7.3 4.7 %collective-permute-start.2 = (bf16[100,128]{1,0:T(8,128)(2,1)S(1)}, bf16[100,128]{1,0:T(8,128)(2,1)S(1)}, u32[]{:S(2)}, u32[]{:S(2)}) collective-permute-start(bf16[100,128]{1,0:T(8,128)(2,1)S(1)} %get-tuple-element.29), channel_id=1, source_target_pairs={{0,4},{4,0},{8,12},{12,8},{1,5},{5,1},{9,13},{13,9},{2,6},{6,2},{1... | collective-permute-start | bytes 76808 | tf_op jit(solution)/shard_map/ppermute | solution.py:386
  12.5 1.4 %collective-permute-start.3 = (bf16[40,1152]{1,0:T(8,128)(2,1)S(1)}, bf16[40,1152]{1,0:T(8,128)(2,1)S(1)}, u32[]{:S(2)}, u32[]{:S(2)}) collective-permute-start(bf16[40,1152]{1,0:T(8,128)(2,1)S(1)} %get-tuple-element.32), channel_id=1, source_target_pairs={{0,1},{1,0},{2,3},{3,2},{4,5},{5,4},{6,7},{7,6},{8,9},{9,8},{10,11... | collective-permute-start | bytes 276488 | tf_op jit(solution)/shard_map/ppermute | solution.py:386
  13.9 4.8 %collective-permute-start.4 = (bf16[40,1152]{1,0:T(8,128)(2,1)S(1)}, bf16[40,1152]{1,0:T(8,128)(2,1)S(1)}, u32[]{:S(2)}, u32[]{:S(2)}) collective-permute-start(bf16[40,1152]{1,0:T(8,128)(2,1)S(1)} %add.1.near_ref), channel_id=1, source_target_pairs={{0,2},{1,3},{2,0},{3,1},{4,6},{5,7},{6,4},{7,5},{8,10},{9,11},{10,... | collective-permute-start | bytes 276488 | tf_op jit(solution)/shard_map/ppermute | solution.py:386
  18.8 1.4 %collective-permute-start.5 = (bf16[40,1152]{1,0:T(8,128)(2,1)S(1)}, bf16[40,1152]{1,0:T(8,128)(2,1)S(1)}, u32[]{:S(2)}, u32[]{:S(2)}) collective-permute-start(bf16[40,1152]{1,0:T(8,128)(2,1)S(1)} %activate.1.mine_ref), channel_id=1, source_target_pairs={{0,1},{1,0},{2,3},{3,2},{4,5},{5,4},{6,7},{7,6},{8,9},{9,8},{10,11... | collective-permute-start | bytes 276488 | tf_op jit(solution)/shard_map/ppermute | solution.py:386
  20.7 6.4 %collective-permute-start.6 = (bf16[100,128]{1,0:T(8,128)(2,1)S(1)}, bf16[100,128]{1,0:T(8,128)(2,1)S(1)}, u32[]{:S(2)}, u32[]{:S(2)}) collective-permute-start(bf16[100,128]{1,0:T(8,128)(2,1)S(1)} %get-tuple-element.38), channel_id=1, source_target_pairs={{0,12},{4,8},{8,4},{12,0},{1,13},{5,9},{9,5},{13,1},{2,14},{6,10},... | collective-permute-start | bytes 76808 | tf_op jit(solution)/shard_map/ppermute | solution.py:386
  22.2 4.9 %collective-permute-start.7 = (bf16[100,128]{1,0:T(8,128)(2,1)S(1)}, bf16[100,128]{1,0:T(8,128)(2,1)S(1)}, u32[]{:S(2)}, u32[]{:S(2)}) collective-permute-start(bf16[100,128]{1,0:T(8,128)(2,1)S(1)} %get-tuple-element.39), channel_id=1, source_target_pairs={{0,8},{4,12},{8,0},{12,4},{1,9},{5,13},{9,1},{13,5},{2,10},{6,14},... | collective-permute-start | bytes 76808 | tf_op jit(solution)/shard_map/ppermute | solution.py:386
  22.8 4.4 %collective-permute-start.8 = (bf16[100,128]{1,0:T(8,128)(2,1)S(1)}, bf16[100,128]{1,0:T(8,128)(2,1)S(1)}, u32[]{:S(2)}, u32[]{:S(2)}) collective-permute-start(bf16[100,128]{1,0:T(8,128)(2,1)S(1)} %get-tuple-element.40), channel_id=1, source_target_pairs={{0,4},{4,0},{8,12},{12,8},{1,5},{5,1},{9,13},{13,9},{2,6},{6,2},{1... | collective-permute-start | bytes 76808 | tf_op jit(solution)/shard_map/ppermute | solution.py:386

commit v12 on v9

--- a/solution.py
+++ b/solution.py
@@ -201,8 +201,8 @@
     width = gate_ref.shape[1]
     half = width // 2
     units = half_columns(which, width)
-    part_ref[:, :half] = matmul(rows, gate_ref[:, units], 1, 0).astype(BF16)
-    part_ref[:, half : 2 * half] = matmul(rows, up_ref[:, units], 1, 0).astype(BF16)
+    both = jnp.concatenate([gate_ref[:, units], up_ref[:, units]], axis=1)
+    part_ref[:, : 2 * half] = matmul(rows, both, 1, 0).astype(BF16)
     part_ref[:, 2 * half :] = matmul(cots, down_ref[units, :], 1, 1).astype(BF16)
 
 
@@ -250,8 +250,8 @@
     half = width // 2
     units = half_columns(which, width)
     outs = matmul(acts_ref[:, :half], down_ref[units, :], 1, 0)
-    ins = matmul(acts_ref[:, half : 2 * half], gate_ref[:, units], 1, 1)
-    return outs, ins + matmul(acts_ref[:, 2 * half :], up_ref[:, units], 1, 1)
+    both = jnp.concatenate([gate_ref[:, units], up_ref[:, units]], axis=1)
+    return outs, matmul(acts_ref[:, half:], both, 1, 1)
 
 
 def own_kernel(mine_ref, gate_ref, up_ref, down_ref, outs_ref, ins_ref):

time: 28.3 us -> 28.2 us (level)
  no operation moved by 1% of the time
where the time goes in v12:
time: 28.2 us; the launch traced here: 28 us
  starting transfers between devices  11.9 us (42%)
  Pallas kernels  8.26 us (29%)
  waiting for transfers between devices  7.1 us (25%)
  between operations  0.72 us (3%)
    ppermute x9, starting transfers between devices, swapped(): lax.ppermute(array, axis, [(i, i ^ distance) for i in range(lax.axis_size...  11.9 us
    ppermute x9, waiting for transfers between devices, swapped(): lax.ppermute(array, axis, [(i, i ^ distance) for i in range(lax.axis_size...  7.1 us
    pallas_call x1, Pallas kernels, load_weights(): pl.pallas_call(load_kernel, out_shape=tuple((pltpu.VMEM(w.shape, BF16) fo...  2.01 us
    pallas_call x1, Pallas kernels, weight_grads(): pl.pallas_call(grads_kernel, out_shape=tuple((jax.ShapeDtypeStruct(shape,...  1.95 us
    pallas_call x6, Pallas kernels, by_rows(): pl.pallas_call(kernel, grid=(steps,), out_shape=tuple((jax.ShapeDtypeStru...  1.92 us
    pallas_call x1, Pallas kernels, dispatch(): pl.pallas_call(functools.partial(dispatch_kernel, experts, plan.shape[1],...  1.39 us
    pallas_call x1, Pallas kernels, combine(): pl.pallas_call(functools.partial(combine_kernel, columns, slots, chunks,...  0.99 us
  transfers between devices with their start and end apart: 9, of which 5 were waited for; matrix products, arithmetic and copies ran while one was open for 0% of the time, Pallas kernels for 17%

profile of v12, /device:TPU:0, one launch (start us, length us, event | category | flops | bytes accessed | tf_op | source)
XLA Modules:
  0.0 28.0 jit_solution(13466705914567128745)
XLA Ops:
  0.6 1.4 %dispatch.1 = (bf16[100,128]{1,0:T(8,128)(2,1)S(1)}, bf16[100,128]{1,0:T(8,128)(2,1)S(1)}, bf16[100,128]{1,0:T(8,128)(2,1)S(1)}, bf16[100,128]{1,0:T(8,128)(2,1)...) custom-call(s32[2,2]{1,0:T(2,128)} %refs_0_.1, s32[4]{0:T(128)} %refs_1_.1, s32[2,128]{1,0:T(2,128)} %bitcast.11, ...), custom_call_target="tpu_custom_call" | custom-call | tf_op jit(solution)/shard_map/dispatch/pallas_call | solution.py:132
  2.0 5.1 %collective-permute-start = (bf16[100,128]{1,0:T(8,128)(2,1)S(1)}, bf16[100,128]{1,0:T(8,128)(2,1)S(1)}, u32[]{:S(2)}, u32[]{:S(2)}) collective-permute-start(bf16[100,128]{1,0:T(8,128)(2,1)S(1)} %get-tuple-element.30), channel_id=1, source_target_pairs={{0,12},{4,8},{8,4},{12,0},{1,13},{5,9},{9,5},{13,1},{2,14},{6,10},... | collective-permute-start | bytes 76808 | tf_op jit(solution)/shard_map/ppermute | solution.py:412
  7.1 0.0 collective-permute-start.1
  7.1 0.6 %collective-permute-start.2 = (bf16[100,128]{1,0:T(8,128)(2,1)S(1)}, bf16[100,128]{1,0:T(8,128)(2,1)S(1)}, u32[]{:S(2)}, u32[]{:S(2)}) collective-permute-start(bf16[100,128]{1,0:T(8,128)(2,1)S(1)} %get-tuple-element.32), channel_id=1, source_target_pairs={{0,4},{4,0},{8,12},{12,8},{1,5},{5,1},{9,13},{13,9},{2,6},{6,2},{1... | collective-permute-start | bytes 76808 | tf_op jit(solution)/shard_map/ppermute | solution.py:412
  7.8 2.0 %load_weights.1 = (bf16[640,768]{1,0:T(8,128)(2,1)S(1)}, bf16[640,768]{1,0:T(8,128)(2,1)S(1)}, bf16[768,640]{1,0:T(8,128)(2,1)S(1)}, bf16[384,96]{1,0:T(8,128)(2,1)S(1)}) custom-call(bf16[640,768]{1,0:T(8,128)(2,1)} %bitcast.8, bf16[640,768]{1,0:T(8,128)(2,1)} %bitcast.9, bf16[768,640]{1,0:T(8,128)(2,1)} %bitcast.10, ...), custom_call_target="tpu_custom_call" | custom-call | bytes 5898240 | tf_op jit(solution)/shard_map/load_weights/pallas_call | solution.py:180
  9.8 0.0 collective-permute-done.refs_1_
  9.8 2.1 %collective-permute-done.1.refs_2_ = bf16[100,128]{1,0:T(8,128)(2,1)S(1)} collective-permute-done((bf16[100,128]{1,0:T(8,128)(2,1)S(1)}, bf16[100,128]{1,0:T(8,128)(2,1)S(1)}, u32[]{:S(2)}, u32[]{:S(2)}) %collective-permute-start.1) | collective-permute-done | bytes 25632 | tf_op jit(solution)/shard_map/ppermute | solution.py:412
  11.9 0.0 collective-permute-done.2.refs_3_
  11.9 0.5 %give.1 = (bf16[40,640]{1,0:T(8,128)(2,1)S(1)}, bf16[40,640]{1,0:T(8,128)(2,1)S(1)}, bf16[40,1152]{1,0:T(8,128)(2,1)S(1)}) custom-call(bf16[100,128]{1,0:T(8,128)(2,1)S(1)} %get-tuple-element.29.refs_0_, bf16[100,128]{1,0:T(8,128)(2,1)S(1)} %collective-permute-done.refs_1_, bf16[100,128]{1,0:T(8,128)(2,1)S(1)} %collective-permute-done.1.refs_2_, ...), custom_call_target="tpu_custom_call" | custom-call | flops 58982400 | bytes 3051520 | tf_op jit(solution)/shard_map/give/pallas_call | solution.py:289
  12.4 0.1 collective-permute-start.3
  12.5 0.4 %keep.1.left_ref = bf16[40,1152]{1,0:T(8,128)(2,1)S(1)} custom-call(bf16[40,640]{1,0:T(8,128)(2,1)S(1)} %get-tuple-element.38.rows_ref, bf16[40,640]{1,0:T(8,128)(2,1)S(1)} %get-tuple-element.39.cots_ref, bf16[640,768]{1,0:T(8,128)(2,1)S(1)} %get-tuple-element.35.refs_4_.gate_ref.refs_3_, bf16[640,768]{1,0:T(8,128)(2,1)S(1)} %get-tuple-element.36.refs_5_.up_ref.refs_4_, ...), custom_call_target="tpu_custom_call" | custom-call | flops 58982400 | bytes 3051520 | tf_op jit(solution)/shard_map/keep/pallas_call | solution.py:289
  12.9 0.8 %collective-permute-done.3.right_ref = bf16[40,1152]{1,0:T(8,128)(2,1)S(1)} collective-permute-done((bf16[40,1152]{1,0:T(8,128)(2,1)S(1)}, bf16[40,1152]{1,0:T(8,128)(2,1)S(1)}, u32[]{:S(2)}, u32[]{:S(2)}) %collective-permute-start.3) | collective-permute-done | bytes 92192 | tf_op jit(solution)/shard_map/ppermute | solution.py:412
  13.8 1.6 %collective-permute-start.4 = (bf16[40,1152]{1,0:T(8,128)(2,1)S(1)}, bf16[40,1152]{1,0:T(8,128)(2,1)S(1)}, u32[]{:S(2)}, u32[]{:S(2)}) collective-permute-start(bf16[40,1152]{1,0:T(8,128)(2,1)S(1)} %add.1.near_ref), channel_id=1, source_target_pairs={{0,2},{1,3},{2,0},{3,1},{4,6},{5,7},{6,4},{7,5},{8,10},{9,11},{10,... | collective-permute-start | bytes 276488 | tf_op jit(solution)/shard_map/ppermute | solution.py:412
  15.3 3.2 %collective-permute-done.4.far_ref = bf16[40,1152]{1,0:T(8,128)(2,1)S(1)} collective-permute-done((bf16[40,1152]{1,0:T(8,128)(2,1)S(1)}, bf16[40,1152]{1,0:T(8,128)(2,1)S(1)}, u32[]{:S(2)}, u32[]{:S(2)}) %collective-permute-start.4) | collective-permute-done | bytes 92192 | tf_op jit(solution)/shard_map/ppermute | solution.py:412
  18.5 0.1 activate.1.mine_ref
  18.6 0.1 collective-permute-start.5
  18.7 0.5 %own.1 = (f32[40,640]{1,0:T(8,128)S(1)}, f32[40,640]{1,0:T(8,128)S(1)}) custom-call(bf16[40,1152]{1,0:T(8,128)(2,1)S(1)} %activate.1.mine_ref, bf16[640,768]{1,0:T(8,128)(2,1)S(1)} %get-tuple-element.35.refs_4_.gate_ref.refs_3_, bf16[640,768]{1,0:T(8,128)(2,1)S(1)} %get-tuple-element.36.refs_5_.up_ref.refs_4_, ...), custom_call_target="tpu_custom_call" | custom-call | flops 58982400 | bytes 3041280 | tf_op jit(solution)/shard_map/own/pallas_call | solution.py:289
  19.1 0.8 %collective-permute-done.5.refs_0_.theirs_ref = bf16[40,1152]{1,0:T(8,128)(2,1)S(1)} collective-permute-done((bf16[40,1152]{1,0:T(8,128)(2,1)S(1)}, bf16[40,1152]{1,0:T(8,128)(2,1)S(1)}, u32[]{:S(2)}, u32[]{:S(2)}) %collective-permute-start.5) | collective-permute-done | bytes 92192 | tf_op jit(solution)/shard_map/ppermute | solution.py:412
  20.0 0.5 %back.1 = (bf16[100,128]{1,0:T(8,128)(2,1)S(1)}, bf16[100,128]{1,0:T(8,128)(2,1)S(1)}, bf16[100,128]{1,0:T(8,128)(2,1)S(1)}, bf16[100,128]{1,0:T(8,128)(2,1)S(1)}) custom-call(bf16[40,1152]{1,0:T(8,128)(2,1)S(1)} %collective-permute-done.5.refs_0_.theirs_ref, f32[40,640]{1,0:T(8,128)S(1)} %get-tuple-element.41.refs_1_, ...), custom_call_target="tpu_custom_call" | custom-call | flops 58982400 | bytes 3246080 | tf_op jit(solution)/shard_map/back/pallas_call | solution.py:289
  20.4 1.7 %collective-permute-start.6 = (bf16[100,128]{1,0:T(8,128)(2,1)S(1)}, bf16[100,128]{1,0:T(8,128)(2,1)S(1)}, u32[]{:S(2)}, u32[]{:S(2)}) collective-permute-start(bf16[100,128]{1,0:T(8,128)(2,1)S(1)} %get-tuple-element.44), channel_id=1, source_target_pairs={{0,12},{4,8},{8,4},{12,0},{1,13},{5,9},{9,5},{13,1},{2,14},{6,10},... | collective-permute-start | bytes 76808 | tf_op jit(solution)/shard_map/ppermute | solution.py:412
  22.2 0.4 %collective-permute-start.7 = (bf16[100,128]{1,0:T(8,128)(2,1)S(1)}, bf16[100,128]{1,0:T(8,128)(2,1)S(1)}, u32[]{:S(2)}, u32[]{:S(2)}) collective-permute-start(bf16[100,128]{1,0:T(8,128)(2,1)S(1)} %get-tuple-element.45), channel_id=1, source_target_pairs={{0,8},{4,12},{8,0},{12,4},{1,9},{5,13},{9,1},{13,5},{2,10},{6,14},... | collective-permute-start | bytes 76808 | tf_op jit(solution)/shard_map/ppermute | solution.py:412
  22.6 2.3 %collective-permute-start.8 = (bf16[100,128]{1,0:T(8,128)(2,1)S(1)}, bf16[100,128]{1,0:T(8,128)(2,1)S(1)}, u32[]{:S(2)}, u32[]{:S(2)}) collective-permute-start(bf16[100,128]{1,0:T(8,128)(2,1)S(1)} %get-tuple-element.46), channel_id=1, source_target_pairs={{0,4},{4,0},{8,12},{12,8},{1,5},{5,1},{9,13},{13,9},{2,6},{6,2},{1... | collective-permute-start | bytes 76808 | tf_op jit(solution)/shard_map/ppermute | solution.py:412
  24.9 2.0 %weight_grads.1 = (bf16[640,768]{1,0:T(8,128)(2,1)}, bf16[640,768]{1,0:T(8,128)(2,1)}, bf16[768,640]{1,0:T(8,128)(2,1)}) custom-call(bf16[40,640]{1,0:T(8,128)(2,1)S(1)} %get-tuple-element.38.rows_ref, bf16[40,640]{1,0:T(8,128)(2,1)S(1)} %get-tuple-element.39.cots_ref, bf16[40,1152]{1,0:T(8,128)(2,1)S(1)} %activate.1.mine_ref, ...), custom_call_target="tpu_custom_call" | custom-call | flops 117964800 | bytes 2949120 | tf_op jit(solution)/shard_map/weight_grads/pallas_call | solution.py:341
  26.9 0.0 collective-permute-done.6.refs_1_
  26.9 0.1 collective-permute-done.7.refs_2_
  27.0 0.0 collective-permute-done.8.refs_3_
  27.0 1.0 %combine.1 = (bf16[128,640]{1,0:T(8,128)(2,1)}, bf16[128,640]{1,0:T(8,128)(2,1)}) custom-call(bf16[100,128]{1,0:T(8,128)(2,1)S(1)} %get-tuple-element.43.refs_0_, bf16[100,128]{1,0:T(8,128)(2,1)S(1)} %collective-permute-done.6.refs_1_, bf16[100,128]{1,0:T(8,128)(2,1)S(1)} %collective-permute-done.7.refs_2_, ...), custom_call_target="tpu_custom_call" | custom-call | tf_op jit(solution)/shard_map/combine/pallas_call | solution.py:395
  (1 shorter events, 0.0 us)
Async XLA Ops:
  2.0 7.8 %collective-permute-start = (bf16[100,128]{1,0:T(8,128)(2,1)S(1)}, bf16[100,128]{1,0:T(8,128)(2,1)S(1)}, u32[]{:S(2)}, u32[]{:S(2)}) collective-permute-start(bf16[100,128]{1,0:T(8,128)(2,1)S(1)} %get-tuple-element.30), channel_id=1, source_target_pairs={{0,12},{4,8},{8,4},{12,0},{1,13},{5,9},{9,5},{13,1},{2,14},{6,10},... | collective-permute-start | bytes 76808 | tf_op jit(solution)/shard_map/ppermute | solution.py:412
  7.1 4.7 %collective-permute-start.1 = (bf16[100,128]{1,0:T(8,128)(2,1)S(1)}, bf16[100,128]{1,0:T(8,128)(2,1)S(1)}, u32[]{:S(2)}, u32[]{:S(2)}) collective-permute-start(bf16[100,128]{1,0:T(8,128)(2,1)S(1)} %get-tuple-element.31), channel_id=1, source_target_pairs={{0,8},{4,12},{8,0},{12,4},{1,9},{5,13},{9,1},{13,5},{2,10},{6,14},... | collective-permute-start | bytes 76808 | tf_op jit(solution)/shard_map/ppermute | solution.py:412
  7.1 4.7 %collective-permute-start.2 = (bf16[100,128]{1,0:T(8,128)(2,1)S(1)}, bf16[100,128]{1,0:T(8,128)(2,1)S(1)}, u32[]{:S(2)}, u32[]{:S(2)}) collective-permute-start(bf16[100,128]{1,0:T(8,128)(2,1)S(1)} %get-tuple-element.32), channel_id=1, source_target_pairs={{0,4},{4,0},{8,12},{12,8},{1,5},{5,1},{9,13},{13,9},{2,6},{6,2},{1... | collective-permute-start | bytes 76808 | tf_op jit(solution)/shard_map/ppermute | solution.py:412
  12.4 1.4 %collective-permute-start.3 = (bf16[40,1152]{1,0:T(8,128)(2,1)S(1)}, bf16[40,1152]{1,0:T(8,128)(2,1)S(1)}, u32[]{:S(2)}, u32[]{:S(2)}) collective-permute-start(bf16[40,1152]{1,0:T(8,128)(2,1)S(1)} %get-tuple-element.40), channel_id=1, source_target_pairs={{0,1},{1,0},{2,3},{3,2},{4,5},{5,4},{6,7},{7,6},{8,9},{9,8},{10,11... | collective-permute-start | bytes 276488 | tf_op jit(solution)/shard_map/ppermute | solution.py:412
  13.8 4.8 %collective-permute-start.4 = (bf16[40,1152]{1,0:T(8,128)(2,1)S(1)}, bf16[40,1152]{1,0:T(8,128)(2,1)S(1)}, u32[]{:S(2)}, u32[]{:S(2)}) collective-permute-start(bf16[40,1152]{1,0:T(8,128)(2,1)S(1)} %add.1.near_ref), channel_id=1, source_target_pairs={{0,2},{1,3},{2,0},{3,1},{4,6},{5,7},{6,4},{7,5},{8,10},{9,11},{10,... | collective-permute-start | bytes 276488 | tf_op jit(solution)/shard_map/ppermute | solution.py:412
  18.6 1.4 %collective-permute-start.5 = (bf16[40,1152]{1,0:T(8,128)(2,1)S(1)}, bf16[40,1152]{1,0:T(8,128)(2,1)S(1)}, u32[]{:S(2)}, u32[]{:S(2)}) collective-permute-start(bf16[40,1152]{1,0:T(8,128)(2,1)S(1)} %activate.1.mine_ref), channel_id=1, source_target_pairs={{0,1},{1,0},{2,3},{3,2},{4,5},{5,4},{6,7},{7,6},{8,9},{9,8},{10,11... | collective-permute-start | bytes 276488 | tf_op jit(solution)/shard_map/ppermute | solution.py:412
  20.4 6.4 %collective-permute-start.6 = (bf16[100,128]{1,0:T(8,128)(2,1)S(1)}, bf16[100,128]{1,0:T(8,128)(2,1)S(1)}, u32[]{:S(2)}, u32[]{:S(2)}) collective-permute-start(bf16[100,128]{1,0:T(8,128)(2,1)S(1)} %get-tuple-element.44), channel_id=1, source_target_pairs={{0,12},{4,8},{8,4},{12,0},{1,13},{5,9},{9,5},{13,1},{2,14},{6,10},... | collective-permute-start | bytes 76808 | tf_op jit(solution)/shard_map/ppermute | solution.py:412
  22.2 4.8 %collective-permute-start.7 = (bf16[100,128]{1,0:T(8,128)(2,1)S(1)}, bf16[100,128]{1,0:T(8,128)(2,1)S(1)}, u32[]{:S(2)}, u32[]{:S(2)}) collective-permute-start(bf16[100,128]{1,0:T(8,128)(2,1)S(1)} %get-tuple-element.45), channel_id=1, source_target_pairs={{0,8},{4,12},{8,0},{12,4},{1,9},{5,13},{9,1},{13,5},{2,10},{6,14},... | collective-permute-start | bytes 76808 | tf_op jit(solution)/shard_map/ppermute | solution.py:412
  22.6 4.4 %collective-permute-start.8 = (bf16[100,128]{1,0:T(8,128)(2,1)S(1)}, bf16[100,128]{1,0:T(8,128)(2,1)S(1)}, u32[]{:S(2)}, u32[]{:S(2)}) collective-permute-start(bf16[100,128]{1,0:T(8,128)(2,1)S(1)} %get-tuple-element.46), channel_id=1, source_target_pairs={{0,4},{4,0},{8,12},{12,8},{1,5},{5,1},{9,13},{13,9},{2,6},{6,2},{1... | collective-permute-start | bytes 76808 | tf_op jit(solution)/shard_map/ppermute | solution.py:412

commit v13 on v12

--- a/solution.py
+++ b/solution.py
@@ -12,6 +12,7 @@
 SPARE = 2
 OWN = BLK * MAXB
 GROUP = 4
+ORDER = (0, 2, 3, 1)
 CHUNK = 128
 LOADS = 4
 VMEM_LIMIT = 32 * 1024 * 1024
@@ -43,8 +44,8 @@
     return -(-rows // 8) * 8
 
 
-def distance(index, experts):
-    return (experts - index) % experts
+def distance(index):
+    return ORDER[index]
 
 
 def dispatch_kernel(experts, hosts, slots, chunks, pieces, *refs):
@@ -84,7 +85,7 @@
         copy.wait()
     members, weights, limits = [], [], []
     for index in range(experts):
-        expert = index if pieces == 1 else me ^ distance(index, experts)
+        expert = index if pieces == 1 else me ^ distance(index)
         hot = (plan_ref[0, 0] == expert) | (plan_ref[1, 0] == expert)
         wanted = token_slot * hot.astype(I32)
         here = jnp.zeros((1, count), F32)
@@ -418,7 +419,7 @@
         blocks = array.reshape(experts, -1, array.shape[1])
         moved = lax.all_to_all(blocks, "expert", split_axis=0, concat_axis=0, tiled=True)
         return [moved.reshape(array.shape)]
-    moved = [swapped(arrays[i], "expert", distance(i, experts)) for i in range(1, experts)]
+    moved = [swapped(arrays[i], "expert", distance(i)) for i in range(1, experts)]
     return [arrays[0]] + moved
 
 

time: 28.2 us -> 28.5 us (1.011)
  waiting for transfers between devices: 7.1 us -> 8.35 us
  starting transfers between devices: 11.9 us -> 10.9 us
    ppermute x9, waiting for transfers between devices: 7.1 us -> 8.35 us  [swapped(): lax.ppermute(array, axis, [(i, i ^ distance) for i in range(lax.axis_size...]
    ppermute x9, starting transfers between devices: 11.9 us -> 10.9 us  [swapped(): lax.ppermute(array, axis, [(i, i ^ distance) for i in range(lax.axis_size...]
where the time goes in v13:
time: 28.5 us; the launch traced here: 28.3 us
  starting transfers between devices  10.9 us (38%)
  waiting for transfers between devices  8.35 us (29%)
  Pallas kernels  8.27 us (29%)
  between operations  0.72 us (3%)
    ppermute x9, starting transfers between devices, swapped(): lax.ppermute(array, axis, [(i, i ^ distance) for i in range(lax.axis_size...  10.9 us
    ppermute x9, waiting for transfers between devices, swapped(): lax.ppermute(array, axis, [(i, i ^ distance) for i in range(lax.axis_size...  8.35 us
    pallas_call x1, Pallas kernels, load_weights(): pl.pallas_call(load_kernel, out_shape=tuple((pltpu.VMEM(w.shape, BF16) fo...  2.01 us
    pallas_call x1, Pallas kernels, weight_grads(): pl.pallas_call(grads_kernel, out_shape=tuple((jax.ShapeDtypeStruct(shape,...  1.96 us
    pallas_call x6, Pallas kernels, by_rows(): pl.pallas_call(kernel, grid=(steps,), out_shape=tuple((jax.ShapeDtypeStru...  1.93 us
    pallas_call x1, Pallas kernels, dispatch(): pl.pallas_call(functools.partial(dispatch_kernel, experts, plan.shape[1],...  1.39 us
    pallas_call x1, Pallas kernels, combine(): pl.pallas_call(functools.partial(combine_kernel, columns, slots, chunks,...  0.99 us
  transfers between devices with their start and end apart: 9, of which 5 were waited for; matrix products, arithmetic and copies ran while one was open for 0% of the time, Pallas kernels for 17%

profile of v13, /device:TPU:0, one launch (start us, length us, event | category | flops | bytes accessed | tf_op | source)
XLA Modules:
  0.0 28.3 jit_solution(16893469483385868540)
XLA Ops:
  0.6 1.4 %dispatch.1 = (bf16[100,128]{1,0:T(8,128)(2,1)S(1)}, bf16[100,128]{1,0:T(8,128)(2,1)S(1)}, bf16[100,128]{1,0:T(8,128)(2,1)S(1)}, bf16[100,128]{1,0:T(8,128)(2,1)...) custom-call(s32[2,2]{1,0:T(2,128)} %refs_0_.1, s32[4]{0:T(128)} %refs_1_.1, s32[2,128]{1,0:T(2,128)} %bitcast.11, ...), custom_call_target="tpu_custom_call" | custom-call | tf_op jit(solution)/shard_map/dispatch/pallas_call | solution.py:133
  2.0 4.1 %collective-permute-start = (bf16[100,128]{1,0:T(8,128)(2,1)S(1)}, bf16[100,128]{1,0:T(8,128)(2,1)S(1)}, u32[]{:S(2)}, u32[]{:S(2)}) collective-permute-start(bf16[100,128]{1,0:T(8,128)(2,1)S(1)} %get-tuple-element.30), channel_id=1, source_target_pairs={{0,8},{4,12},{8,0},{12,4},{1,9},{5,13},{9,1},{13,5},{2,10},{6,14},... | collective-permute-start | bytes 76808 | tf_op jit(solution)/shard_map/ppermute | solution.py:413
  6.1 1.3 %collective-permute-start.1 = (bf16[100,128]{1,0:T(8,128)(2,1)S(1)}, bf16[100,128]{1,0:T(8,128)(2,1)S(1)}, u32[]{:S(2)}, u32[]{:S(2)}) collective-permute-start(bf16[100,128]{1,0:T(8,128)(2,1)S(1)} %get-tuple-element.31), channel_id=1, source_target_pairs={{0,12},{4,8},{8,4},{12,0},{1,13},{5,9},{9,5},{13,1},{2,14},{6,10},... | collective-permute-start | bytes 76808 | tf_op jit(solution)/shard_map/ppermute | solution.py:413
  7.5 0.2 collective-permute-start.2
  7.7 2.0 %load_weights.1 = (bf16[640,768]{1,0:T(8,128)(2,1)S(1)}, bf16[640,768]{1,0:T(8,128)(2,1)S(1)}, bf16[768,640]{1,0:T(8,128)(2,1)S(1)}, bf16[384,96]{1,0:T(8,128)(2,1)S(1)}) custom-call(bf16[640,768]{1,0:T(8,128)(2,1)} %bitcast.8, bf16[640,768]{1,0:T(8,128)(2,1)} %bitcast.9, bf16[768,640]{1,0:T(8,128)(2,1)} %bitcast.10, ...), custom_call_target="tpu_custom_call" | custom-call | bytes 5898240 | tf_op jit(solution)/shard_map/load_weights/pallas_call | solution.py:181
  9.7 0.0 collective-permute-done.refs_1_
  9.7 2.0 %collective-permute-done.1.refs_2_ = bf16[100,128]{1,0:T(8,128)(2,1)S(1)} collective-permute-done((bf16[100,128]{1,0:T(8,128)(2,1)S(1)}, bf16[100,128]{1,0:T(8,128)(2,1)S(1)}, u32[]{:S(2)}, u32[]{:S(2)}) %collective-permute-start.1) | collective-permute-done | bytes 25632 | tf_op jit(solution)/shard_map/ppermute | solution.py:413
  11.8 0.0 collective-permute-done.2.refs_3_
  11.8 0.5 %give.1 = (bf16[40,640]{1,0:T(8,128)(2,1)S(1)}, bf16[40,640]{1,0:T(8,128)(2,1)S(1)}, bf16[40,1152]{1,0:T(8,128)(2,1)S(1)}) custom-call(bf16[100,128]{1,0:T(8,128)(2,1)S(1)} %get-tuple-element.29.refs_0_, bf16[100,128]{1,0:T(8,128)(2,1)S(1)} %collective-permute-done.refs_1_, bf16[100,128]{1,0:T(8,128)(2,1)S(1)} %collective-permute-done.1.refs_2_, ...), custom_call_target="tpu_custom_call" | custom-call | flops 58982400 | bytes 3051520 | tf_op jit(solution)/shard_map/give/pallas_call | solution.py:290
  12.3 0.1 collective-permute-start.3
  12.3 0.4 %keep.1.left_ref = bf16[40,1152]{1,0:T(8,128)(2,1)S(1)} custom-call(bf16[40,640]{1,0:T(8,128)(2,1)S(1)} %get-tuple-element.38.rows_ref, bf16[40,640]{1,0:T(8,128)(2,1)S(1)} %get-tuple-element.39.cots_ref, bf16[640,768]{1,0:T(8,128)(2,1)S(1)} %get-tuple-element.35.refs_4_.gate_ref.refs_3_, bf16[640,768]{1,0:T(8,128)(2,1)S(1)} %get-tuple-element.36.refs_5_.up_ref.refs_4_, ...), custom_call_target="tpu_custom_call" | custom-call | flops 58982400 | bytes 3051520 | tf_op jit(solution)/shard_map/keep/pallas_call | solution.py:290
  12.8 0.8 %collective-permute-done.3.right_ref = bf16[40,1152]{1,0:T(8,128)(2,1)S(1)} collective-permute-done((bf16[40,1152]{1,0:T(8,128)(2,1)S(1)}, bf16[40,1152]{1,0:T(8,128)(2,1)S(1)}, u32[]{:S(2)}, u32[]{:S(2)}) %collective-permute-start.3) | collective-permute-done | bytes 92192 | tf_op jit(solution)/shard_map/ppermute | solution.py:413
  13.6 1.6 %collective-permute-start.4 = (bf16[40,1152]{1,0:T(8,128)(2,1)S(1)}, bf16[40,1152]{1,0:T(8,128)(2,1)S(1)}, u32[]{:S(2)}, u32[]{:S(2)}) collective-permute-start(bf16[40,1152]{1,0:T(8,128)(2,1)S(1)} %add.1.near_ref), channel_id=1, source_target_pairs={{0,2},{1,3},{2,0},{3,1},{4,6},{5,7},{6,4},{7,5},{8,10},{9,11},{10,... | collective-permute-start | bytes 276488 | tf_op jit(solution)/shard_map/ppermute | solution.py:413
  15.2 3.2 %collective-permute-done.4.far_ref = bf16[40,1152]{1,0:T(8,128)(2,1)S(1)} collective-permute-done((bf16[40,1152]{1,0:T(8,128)(2,1)S(1)}, bf16[40,1152]{1,0:T(8,128)(2,1)S(1)}, u32[]{:S(2)}, u32[]{:S(2)}) %collective-permute-start.4) | collective-permute-done | bytes 92192 | tf_op jit(solution)/shard_map/ppermute | solution.py:413
  18.4 0.1 activate.1.mine_ref
  18.5 0.1 collective-permute-start.5
  18.6 0.5 %own.1 = (f32[40,640]{1,0:T(8,128)S(1)}, f32[40,640]{1,0:T(8,128)S(1)}) custom-call(bf16[40,1152]{1,0:T(8,128)(2,1)S(1)} %activate.1.mine_ref, bf16[640,768]{1,0:T(8,128)(2,1)S(1)} %get-tuple-element.35.refs_4_.gate_ref.refs_3_, bf16[640,768]{1,0:T(8,128)(2,1)S(1)} %get-tuple-element.36.refs_5_.up_ref.refs_4_, ...), custom_call_target="tpu_custom_call" | custom-call | flops 58982400 | bytes 3041280 | tf_op jit(solution)/shard_map/own/pallas_call | solution.py:290
  19.0 0.8 %collective-permute-done.5.refs_0_.theirs_ref = bf16[40,1152]{1,0:T(8,128)(2,1)S(1)} collective-permute-done((bf16[40,1152]{1,0:T(8,128)(2,1)S(1)}, bf16[40,1152]{1,0:T(8,128)(2,1)S(1)}, u32[]{:S(2)}, u32[]{:S(2)}) %collective-permute-start.5) | collective-permute-done | bytes 92192 | tf_op jit(solution)/shard_map/ppermute | solution.py:413
  19.8 0.5 %back.1 = (bf16[100,128]{1,0:T(8,128)(2,1)S(1)}, bf16[100,128]{1,0:T(8,128)(2,1)S(1)}, bf16[100,128]{1,0:T(8,128)(2,1)S(1)}, bf16[100,128]{1,0:T(8,128)(2,1)S(1)}) custom-call(bf16[40,1152]{1,0:T(8,128)(2,1)S(1)} %collective-permute-done.5.refs_0_.theirs_ref, f32[40,640]{1,0:T(8,128)S(1)} %get-tuple-element.41.refs_1_, ...), custom_call_target="tpu_custom_call" | custom-call | flops 58982400 | bytes 3246080 | tf_op jit(solution)/shard_map/back/pallas_call | solution.py:290
  20.3 1.3 %collective-permute-start.6 = (bf16[100,128]{1,0:T(8,128)(2,1)S(1)}, bf16[100,128]{1,0:T(8,128)(2,1)S(1)}, u32[]{:S(2)}, u32[]{:S(2)}) collective-permute-start(bf16[100,128]{1,0:T(8,128)(2,1)S(1)} %get-tuple-element.44), channel_id=1, source_target_pairs={{0,8},{4,12},{8,0},{12,4},{1,9},{5,13},{9,1},{13,5},{2,10},{6,14},... | collective-permute-start | bytes 76808 | tf_op jit(solution)/shard_map/ppermute | solution.py:413
  21.6 1.0 %collective-permute-start.7 = (bf16[100,128]{1,0:T(8,128)(2,1)S(1)}, bf16[100,128]{1,0:T(8,128)(2,1)S(1)}, u32[]{:S(2)}, u32[]{:S(2)}) collective-permute-start(bf16[100,128]{1,0:T(8,128)(2,1)S(1)} %get-tuple-element.45), channel_id=1, source_target_pairs={{0,12},{4,8},{8,4},{12,0},{1,13},{5,9},{9,5},{13,1},{2,14},{6,10},... | collective-permute-start | bytes 76808 | tf_op jit(solution)/shard_map/ppermute | solution.py:413
  22.6 1.3 %collective-permute-start.8 = (bf16[100,128]{1,0:T(8,128)(2,1)S(1)}, bf16[100,128]{1,0:T(8,128)(2,1)S(1)}, u32[]{:S(2)}, u32[]{:S(2)}) collective-permute-start(bf16[100,128]{1,0:T(8,128)(2,1)S(1)} %get-tuple-element.46), channel_id=1, source_target_pairs={{0,4},{4,0},{8,12},{12,8},{1,5},{5,1},{9,13},{13,9},{2,6},{6,2},{1... | collective-permute-start | bytes 76808 | tf_op jit(solution)/shard_map/ppermute | solution.py:413
  23.9 2.0 %weight_grads.1 = (bf16[640,768]{1,0:T(8,128)(2,1)}, bf16[640,768]{1,0:T(8,128)(2,1)}, bf16[768,640]{1,0:T(8,128)(2,1)}) custom-call(bf16[40,640]{1,0:T(8,128)(2,1)S(1)} %get-tuple-element.38.rows_ref, bf16[40,640]{1,0:T(8,128)(2,1)S(1)} %get-tuple-element.39.cots_ref, bf16[40,1152]{1,0:T(8,128)(2,1)S(1)} %activate.1.mine_ref, ...), custom_call_target="tpu_custom_call" | custom-call | flops 117964800 | bytes 2949120 | tf_op jit(solution)/shard_map/weight_grads/pallas_call | solution.py:342
  25.8 0.0 collective-permute-done.6.refs_1_
  25.9 1.4 %collective-permute-done.7.refs_2_ = bf16[100,128]{1,0:T(8,128)(2,1)S(1)} collective-permute-done((bf16[100,128]{1,0:T(8,128)(2,1)S(1)}, bf16[100,128]{1,0:T(8,128)(2,1)S(1)}, u32[]{:S(2)}, u32[]{:S(2)}) %collective-permute-start.7) | collective-permute-done | bytes 25632 | tf_op jit(solution)/shard_map/ppermute | solution.py:413
  27.3 0.0 collective-permute-done.8.refs_3_
  27.3 1.0 %combine.1 = (bf16[128,640]{1,0:T(8,128)(2,1)}, bf16[128,640]{1,0:T(8,128)(2,1)}) custom-call(bf16[100,128]{1,0:T(8,128)(2,1)S(1)} %get-tuple-element.43.refs_0_, bf16[100,128]{1,0:T(8,128)(2,1)S(1)} %collective-permute-done.6.refs_1_, bf16[100,128]{1,0:T(8,128)(2,1)S(1)} %collective-permute-done.7.refs_2_, ...), custom_call_target="tpu_custom_call" | custom-call | tf_op jit(solution)/shard_map/combine/pallas_call | solution.py:396
  (1 shorter events, 0.0 us)
Async XLA Ops:
  2.0 7.7 %collective-permute-start = (bf16[100,128]{1,0:T(8,128)(2,1)S(1)}, bf16[100,128]{1,0:T(8,128)(2,1)S(1)}, u32[]{:S(2)}, u32[]{:S(2)}) collective-permute-start(bf16[100,128]{1,0:T(8,128)(2,1)S(1)} %get-tuple-element.30), channel_id=1, source_target_pairs={{0,8},{4,12},{8,0},{12,4},{1,9},{5,13},{9,1},{13,5},{2,10},{6,14},... | collective-permute-start | bytes 76808 | tf_op jit(solution)/shard_map/ppermute | solution.py:413
  6.1 5.6 %collective-permute-start.1 = (bf16[100,128]{1,0:T(8,128)(2,1)S(1)}, bf16[100,128]{1,0:T(8,128)(2,1)S(1)}, u32[]{:S(2)}, u32[]{:S(2)}) collective-permute-start(bf16[100,128]{1,0:T(8,128)(2,1)S(1)} %get-tuple-element.31), channel_id=1, source_target_pairs={{0,12},{4,8},{8,4},{12,0},{1,13},{5,9},{9,5},{13,1},{2,14},{6,10},... | collective-permute-start | bytes 76808 | tf_op jit(solution)/shard_map/ppermute | solution.py:413
  7.5 4.3 %collective-permute-start.2 = (bf16[100,128]{1,0:T(8,128)(2,1)S(1)}, bf16[100,128]{1,0:T(8,128)(2,1)S(1)}, u32[]{:S(2)}, u32[]{:S(2)}) collective-permute-start(bf16[100,128]{1,0:T(8,128)(2,1)S(1)} %get-tuple-element.32), channel_id=1, source_target_pairs={{0,4},{4,0},{8,12},{12,8},{1,5},{5,1},{9,13},{13,9},{2,6},{6,2},{1... | collective-permute-start | bytes 76808 | tf_op jit(solution)/shard_map/ppermute | solution.py:413
  12.3 1.4 %collective-permute-start.3 = (bf16[40,1152]{1,0:T(8,128)(2,1)S(1)}, bf16[40,1152]{1,0:T(8,128)(2,1)S(1)}, u32[]{:S(2)}, u32[]{:S(2)}) collective-permute-start(bf16[40,1152]{1,0:T(8,128)(2,1)S(1)} %get-tuple-element.40), channel_id=1, source_target_pairs={{0,1},{1,0},{2,3},{3,2},{4,5},{5,4},{6,7},{7,6},{8,9},{9,8},{10,11... | collective-permute-start | bytes 276488 | tf_op jit(solution)/shard_map/ppermute | solution.py:413
  13.6 4.8 %collective-permute-start.4 = (bf16[40,1152]{1,0:T(8,128)(2,1)S(1)}, bf16[40,1152]{1,0:T(8,128)(2,1)S(1)}, u32[]{:S(2)}, u32[]{:S(2)}) collective-permute-start(bf16[40,1152]{1,0:T(8,128)(2,1)S(1)} %add.1.near_ref), channel_id=1, source_target_pairs={{0,2},{1,3},{2,0},{3,1},{4,6},{5,7},{6,4},{7,5},{8,10},{9,11},{10,... | collective-permute-start | bytes 276488 | tf_op jit(solution)/shard_map/ppermute | solution.py:413
  18.5 1.4 %collective-permute-start.5 = (bf16[40,1152]{1,0:T(8,128)(2,1)S(1)}, bf16[40,1152]{1,0:T(8,128)(2,1)S(1)}, u32[]{:S(2)}, u32[]{:S(2)}) collective-permute-start(bf16[40,1152]{1,0:T(8,128)(2,1)S(1)} %activate.1.mine_ref), channel_id=1, source_target_pairs={{0,1},{1,0},{2,3},{3,2},{4,5},{5,4},{6,7},{7,6},{8,9},{9,8},{10,11... | collective-permute-start | bytes 276488 | tf_op jit(solution)/shard_map/ppermute | solution.py:413
  20.3 5.5 %collective-permute-start.6 = (bf16[100,128]{1,0:T(8,128)(2,1)S(1)}, bf16[100,128]{1,0:T(8,128)(2,1)S(1)}, u32[]{:S(2)}, u32[]{:S(2)}) collective-permute-start(bf16[100,128]{1,0:T(8,128)(2,1)S(1)} %get-tuple-element.44), channel_id=1, source_target_pairs={{0,8},{4,12},{8,0},{12,4},{1,9},{5,13},{9,1},{13,5},{2,10},{6,14},... | collective-permute-start | bytes 76808 | tf_op jit(solution)/shard_map/ppermute | solution.py:413
  21.6 5.6 %collective-permute-start.7 = (bf16[100,128]{1,0:T(8,128)(2,1)S(1)}, bf16[100,128]{1,0:T(8,128)(2,1)S(1)}, u32[]{:S(2)}, u32[]{:S(2)}) collective-permute-start(bf16[100,128]{1,0:T(8,128)(2,1)S(1)} %get-tuple-element.45), channel_id=1, source_target_pairs={{0,12},{4,8},{8,4},{12,0},{1,13},{5,9},{9,5},{13,1},{2,14},{6,10},... | collective-permute-start | bytes 76808 | tf_op jit(solution)/shard_map/ppermute | solution.py:413
  22.6 4.7 %collective-permute-start.8 = (bf16[100,128]{1,0:T(8,128)(2,1)S(1)}, bf16[100,128]{1,0:T(8,128)(2,1)S(1)}, u32[]{:S(2)}, u32[]{:S(2)}) collective-permute-start(bf16[100,128]{1,0:T(8,128)(2,1)S(1)} %get-tuple-element.46), channel_id=1, source_target_pairs={{0,4},{4,0},{8,12},{12,8},{1,5},{5,1},{9,13},{13,9},{2,6},{6,2},{1... | collective-permute-start | bytes 76808 | tf_op jit(solution)/shard_map/ppermute | solution.py:413

commit v14 on v12

--- a/solution.py
+++ b/solution.py
@@ -12,6 +12,8 @@
 SPARE = 2
 OWN = BLK * MAXB
 GROUP = 4
+SEND_ORDER = (0, 2, 3, 1)
+BACK_ORDER = (0, 3, 2, 1)
 CHUNK = 128
 LOADS = 4
 VMEM_LIMIT = 32 * 1024 * 1024
@@ -41,10 +43,6 @@
 
 def padded(rows):
     return -(-rows // 8) * 8
-
-
-def distance(index, experts):
-    return (experts - index) % experts
 
 
 def dispatch_kernel(experts, hosts, slots, chunks, pieces, *refs):
@@ -84,7 +82,7 @@
         copy.wait()
     members, weights, limits = [], [], []
     for index in range(experts):
-        expert = index if pieces == 1 else me ^ distance(index, experts)
+        expert = index if pieces == 1 else me ^ SEND_ORDER[index]
         hot = (plan_ref[0, 0] == expert) | (plan_ref[1, 0] == expert)
         wanted = token_slot * hot.astype(I32)
         here = jnp.zeros((1, count), F32)
@@ -274,7 +272,10 @@
             for kind in range(2):
                 place = (2 * j + kind) * slots
                 wide[s, place : place + slots, :] = flat[kind, s * slots : (s + 1) * slots, columns]
-        back_ref, start = (back_refs[0], s * block) if pieces == 1 else (back_refs[s], 0)
+        if pieces == 1:
+            back_ref, start = back_refs[0], s * block
+        else:
+            back_ref, start = back_refs[BACK_ORDER.index(SEND_ORDER[s])], 0
         back_ref[start : start + block, :] = wide[s].astype(BF16)
 
 
@@ -363,9 +364,10 @@
         rows, width, block = 2 * slots, back_refs[0].shape[1], padded(2 * slots)
         for i, back_ref in enumerate(back_refs):
             wide[i] = back_ref[...].astype(F32)
+            first = SEND_ORDER.index(BACK_ORDER[i]) * block
             for j in range(chunks):
                 part = pl.ds(j * width, width)
-                flat[i * block : i * block + rows, part] = wide[i, j * rows : (j + 1) * rows, :]
+                flat[first : first + rows, part] = wide[i, j * rows : (j + 1) * rows, :]
     count = mixed_ref.shape[0]
     copies = []
     for start, size in columns:
@@ -412,13 +414,13 @@
     return lax.ppermute(array, axis, [(i, i ^ distance) for i in range(lax.axis_size(axis))])
 
 
-def over_experts(arrays, experts):
+def over_experts(arrays, experts, order):
     if len(arrays) == 1:
         array = arrays[0]
         blocks = array.reshape(experts, -1, array.shape[1])
         moved = lax.all_to_all(blocks, "expert", split_axis=0, concat_axis=0, tiled=True)
         return [moved.reshape(array.shape)]
-    moved = [swapped(arrays[i], "expert", distance(i, experts)) for i in range(1, experts)]
+    moved = [swapped(arrays[i], "expert", order[i]) for i in range(1, experts)]
     return [arrays[0]] + moved
 
 
@@ -455,7 +457,7 @@
         chunks,
         pieces,
     )
-    recvs = over_experts(sends, experts)
+    recvs = over_experts(sends, experts, SEND_ORDER)
     *weights, merge = load_weights(gate, up, down, scaled, pick)
     steps, total, half = experts // GROUP, experts * slots, 3 * width // 2
     layout = (slots, chunks, pieces)
@@ -500,7 +502,7 @@
         scratch[::-1],
         flops,
     )
-    returned = over_experts(backs if pieces > 1 else [backs], experts)
+    returned = over_experts(backs if pieces > 1 else [backs], experts, BACK_ORDER)
     gate_grad, up_grad, down_grad = weight_grads(rows, cots, mine, theirs)
     mixed, token_grad = combine(returned, merge, slots, chunks)
     return mixed, token_grad, gate_grad[None], up_grad[None], down_grad[None]

time: 28.2 us -> 28.4 us (level)
  no operation moved by 1% of the time
where the time goes in v14:
time: 28.4 us; the launch traced here: 28.2 us
  starting transfers between devices  11.8 us (42%)
  Pallas kernels  8.29 us (29%)
  waiting for transfers between devices  7.33 us (26%)
  between operations  0.72 us (3%)
    ppermute x9, starting transfers between devices, swapped(): lax.ppermute(array, axis, [(i, i ^ distance) for i in range(lax.axis_size...  11.8 us
    ppermute x9, waiting for transfers between devices, swapped(): lax.ppermute(array, axis, [(i, i ^ distance) for i in range(lax.axis_size...  7.33 us
    pallas_call x1, Pallas kernels, load_weights(): pl.pallas_call(load_kernel, out_shape=tuple((pltpu.VMEM(w.shape, BF16) fo...  2.01 us
    pallas_call x1, Pallas kernels, weight_grads(): pl.pallas_call(grads_kernel, out_shape=tuple((jax.ShapeDtypeStruct(shape,...  1.97 us
    pallas_call x6, Pallas kernels, by_rows(): pl.pallas_call(kernel, grid=(steps,), out_shape=tuple((jax.ShapeDtypeStru...  1.93 us
    pallas_call x1, Pallas kernels, dispatch(): pl.pallas_call(functools.partial(dispatch_kernel, experts, plan.shape[1],...  1.39 us
    pallas_call x1, Pallas kernels, combine(): pl.pallas_call(functools.partial(combine_kernel, columns, slots, chunks,...  1 us
  transfers between devices with their start and end apart: 9, of which 5 were waited for; matrix products, arithmetic and copies ran while one was open for 0% of the time, Pallas kernels for 17%

profile of v14, /device:TPU:0, one launch (start us, length us, event | category | flops | bytes accessed | tf_op | source)
XLA Modules:
  0.0 28.2 jit_solution(196643965705523772)
XLA Ops:
  0.6 1.4 %dispatch.1 = (bf16[100,128]{1,0:T(8,128)(2,1)S(1)}, bf16[100,128]{1,0:T(8,128)(2,1)S(1)}, bf16[100,128]{1,0:T(8,128)(2,1)S(1)}, bf16[100,128]{1,0:T(8,128)(2,1)...) custom-call(s32[2,2]{1,0:T(2,128)} %refs_0_.1, s32[4]{0:T(128)} %refs_1_.1, s32[2,128]{1,0:T(2,128)} %bitcast.11, ...), custom_call_target="tpu_custom_call" | custom-call | tf_op jit(solution)/shard_map/dispatch/pallas_call | solution.py:130
  2.0 4.1 %collective-permute-start = (bf16[100,128]{1,0:T(8,128)(2,1)S(1)}, bf16[100,128]{1,0:T(8,128)(2,1)S(1)}, u32[]{:S(2)}, u32[]{:S(2)}) collective-permute-start(bf16[100,128]{1,0:T(8,128)(2,1)S(1)} %get-tuple-element.30), channel_id=1, source_target_pairs={{0,8},{4,12},{8,0},{12,4},{1,9},{5,13},{9,1},{13,5},{2,10},{6,14},... | collective-permute-start | bytes 76808 | tf_op jit(solution)/shard_map/ppermute | solution.py:414
  6.1 1.3 %collective-permute-start.1 = (bf16[100,128]{1,0:T(8,128)(2,1)S(1)}, bf16[100,128]{1,0:T(8,128)(2,1)S(1)}, u32[]{:S(2)}, u32[]{:S(2)}) collective-permute-start(bf16[100,128]{1,0:T(8,128)(2,1)S(1)} %get-tuple-element.31), channel_id=1, source_target_pairs={{0,12},{4,8},{8,4},{12,0},{1,13},{5,9},{9,5},{13,1},{2,14},{6,10},... | collective-permute-start | bytes 76808 | tf_op jit(solution)/shard_map/ppermute | solution.py:414
  7.5 0.2 collective-permute-start.2
  7.7 2.0 %load_weights.1 = (bf16[640,768]{1,0:T(8,128)(2,1)S(1)}, bf16[640,768]{1,0:T(8,128)(2,1)S(1)}, bf16[768,640]{1,0:T(8,128)(2,1)S(1)}, bf16[384,96]{1,0:T(8,128)(2,1)S(1)}) custom-call(bf16[640,768]{1,0:T(8,128)(2,1)} %bitcast.8, bf16[640,768]{1,0:T(8,128)(2,1)} %bitcast.9, bf16[768,640]{1,0:T(8,128)(2,1)} %bitcast.10, ...), custom_call_target="tpu_custom_call" | custom-call | bytes 5898240 | tf_op jit(solution)/shard_map/load_weights/pallas_call | solution.py:178
  9.7 0.0 collective-permute-done.refs_1_
  9.7 2.0 %collective-permute-done.1.refs_2_ = bf16[100,128]{1,0:T(8,128)(2,1)S(1)} collective-permute-done((bf16[100,128]{1,0:T(8,128)(2,1)S(1)}, bf16[100,128]{1,0:T(8,128)(2,1)S(1)}, u32[]{:S(2)}, u32[]{:S(2)}) %collective-permute-start.1) | collective-permute-done | bytes 25632 | tf_op jit(solution)/shard_map/ppermute | solution.py:414
  11.8 0.0 collective-permute-done.2.refs_3_
  11.8 0.5 %give.1 = (bf16[40,640]{1,0:T(8,128)(2,1)S(1)}, bf16[40,640]{1,0:T(8,128)(2,1)S(1)}, bf16[40,1152]{1,0:T(8,128)(2,1)S(1)}) custom-call(bf16[100,128]{1,0:T(8,128)(2,1)S(1)} %get-tuple-element.29.refs_0_, bf16[100,128]{1,0:T(8,128)(2,1)S(1)} %collective-permute-done.refs_1_, bf16[100,128]{1,0:T(8,128)(2,1)S(1)} %collective-permute-done.1.refs_2_, ...), custom_call_target="tpu_custom_call" | custom-call | flops 58982400 | bytes 3051520 | tf_op jit(solution)/shard_map/give/pallas_call | solution.py:290
  12.3 0.1 collective-permute-start.3
  12.3 0.4 %keep.1.left_ref = bf16[40,1152]{1,0:T(8,128)(2,1)S(1)} custom-call(bf16[40,640]{1,0:T(8,128)(2,1)S(1)} %get-tuple-element.38.rows_ref, bf16[40,640]{1,0:T(8,128)(2,1)S(1)} %get-tuple-element.39.cots_ref, bf16[640,768]{1,0:T(8,128)(2,1)S(1)} %get-tuple-element.35.refs_4_.gate_ref.refs_3_, bf16[640,768]{1,0:T(8,128)(2,1)S(1)} %get-tuple-element.36.refs_5_.up_ref.refs_4_, ...), custom_call_target="tpu_custom_call" | custom-call | flops 58982400 | bytes 3051520 | tf_op jit(solution)/shard_map/keep/pallas_call | solution.py:290
  12.8 0.8 %collective-permute-done.3.right_ref = bf16[40,1152]{1,0:T(8,128)(2,1)S(1)} collective-permute-done((bf16[40,1152]{1,0:T(8,128)(2,1)S(1)}, bf16[40,1152]{1,0:T(8,128)(2,1)S(1)}, u32[]{:S(2)}, u32[]{:S(2)}) %collective-permute-start.3) | collective-permute-done | bytes 92192 | tf_op jit(solution)/shard_map/ppermute | solution.py:414
  13.6 1.6 %collective-permute-start.4 = (bf16[40,1152]{1,0:T(8,128)(2,1)S(1)}, bf16[40,1152]{1,0:T(8,128)(2,1)S(1)}, u32[]{:S(2)}, u32[]{:S(2)}) collective-permute-start(bf16[40,1152]{1,0:T(8,128)(2,1)S(1)} %add.1.near_ref), channel_id=1, source_target_pairs={{0,2},{1,3},{2,0},{3,1},{4,6},{5,7},{6,4},{7,5},{8,10},{9,11},{10,... | collective-permute-start | bytes 276488 | tf_op jit(solution)/shard_map/ppermute | solution.py:414
  15.2 3.2 %collective-permute-done.4.far_ref = bf16[40,1152]{1,0:T(8,128)(2,1)S(1)} collective-permute-done((bf16[40,1152]{1,0:T(8,128)(2,1)S(1)}, bf16[40,1152]{1,0:T(8,128)(2,1)S(1)}, u32[]{:S(2)}, u32[]{:S(2)}) %collective-permute-start.4) | collective-permute-done | bytes 92192 | tf_op jit(solution)/shard_map/ppermute | solution.py:414
  18.4 0.1 activate.1.mine_ref
  18.5 0.1 collective-permute-start.5
  18.6 0.5 %own.1 = (f32[40,640]{1,0:T(8,128)S(1)}, f32[40,640]{1,0:T(8,128)S(1)}) custom-call(bf16[40,1152]{1,0:T(8,128)(2,1)S(1)} %activate.1.mine_ref, bf16[640,768]{1,0:T(8,128)(2,1)S(1)} %get-tuple-element.35.refs_4_.gate_ref.refs_3_, bf16[640,768]{1,0:T(8,128)(2,1)S(1)} %get-tuple-element.36.refs_5_.up_ref.refs_4_, ...), custom_call_target="tpu_custom_call" | custom-call | flops 58982400 | bytes 3041280 | tf_op jit(solution)/shard_map/own/pallas_call | solution.py:290
  19.0 0.8 %collective-permute-done.5.refs_0_.theirs_ref = bf16[40,1152]{1,0:T(8,128)(2,1)S(1)} collective-permute-done((bf16[40,1152]{1,0:T(8,128)(2,1)S(1)}, bf16[40,1152]{1,0:T(8,128)(2,1)S(1)}, u32[]{:S(2)}, u32[]{:S(2)}) %collective-permute-start.5) | collective-permute-done | bytes 92192 | tf_op jit(solution)/shard_map/ppermute | solution.py:414
  19.8 0.5 %back.1 = (bf16[100,128]{1,0:T(8,128)(2,1)S(1)}, bf16[100,128]{1,0:T(8,128)(2,1)S(1)}, bf16[100,128]{1,0:T(8,128)(2,1)S(1)}, bf16[100,128]{1,0:T(8,128)(2,1)S(1)}) custom-call(bf16[40,1152]{1,0:T(8,128)(2,1)S(1)} %collective-permute-done.5.refs_0_.theirs_ref, f32[40,640]{1,0:T(8,128)S(1)} %get-tuple-element.41.refs_1_, ...), custom_call_target="tpu_custom_call" | custom-call | flops 58982400 | bytes 3246080 | tf_op jit(solution)/shard_map/back/pallas_call | solution.py:290
  20.3 2.1 %collective-permute-start.6 = (bf16[100,128]{1,0:T(8,128)(2,1)S(1)}, bf16[100,128]{1,0:T(8,128)(2,1)S(1)}, u32[]{:S(2)}, u32[]{:S(2)}) collective-permute-start(bf16[100,128]{1,0:T(8,128)(2,1)S(1)} %get-tuple-element.44), channel_id=1, source_target_pairs={{0,12},{4,8},{8,4},{12,0},{1,13},{5,9},{9,5},{13,1},{2,14},{6,10},... | collective-permute-start | bytes 76808 | tf_op jit(solution)/shard_map/ppermute | solution.py:414
  22.4 0.0 collective-permute-start.7
  22.4 2.4 %collective-permute-start.8 = (bf16[100,128]{1,0:T(8,128)(2,1)S(1)}, bf16[100,128]{1,0:T(8,128)(2,1)S(1)}, u32[]{:S(2)}, u32[]{:S(2)}) collective-permute-start(bf16[100,128]{1,0:T(8,128)(2,1)S(1)} %get-tuple-element.46), channel_id=1, source_target_pairs={{0,4},{4,0},{8,12},{12,8},{1,5},{5,1},{9,13},{13,9},{2,6},{6,2},{1... | collective-permute-start | bytes 76808 | tf_op jit(solution)/shard_map/ppermute | solution.py:414
  24.8 2.0 %weight_grads.1 = (bf16[640,768]{1,0:T(8,128)(2,1)}, bf16[640,768]{1,0:T(8,128)(2,1)}, bf16[768,640]{1,0:T(8,128)(2,1)}) custom-call(bf16[40,640]{1,0:T(8,128)(2,1)S(1)} %get-tuple-element.38.rows_ref, bf16[40,640]{1,0:T(8,128)(2,1)S(1)} %get-tuple-element.39.cots_ref, bf16[40,1152]{1,0:T(8,128)(2,1)S(1)} %activate.1.mine_ref, ...), custom_call_target="tpu_custom_call" | custom-call | flops 117964800 | bytes 2949120 | tf_op jit(solution)/shard_map/weight_grads/pallas_call | solution.py:342
  26.8 0.0 collective-permute-done.6.refs_1_
  26.8 0.4 %collective-permute-done.7.refs_2_ = bf16[100,128]{1,0:T(8,128)(2,1)S(1)} collective-permute-done((bf16[100,128]{1,0:T(8,128)(2,1)S(1)}, bf16[100,128]{1,0:T(8,128)(2,1)S(1)}, u32[]{:S(2)}, u32[]{:S(2)}) %collective-permute-start.7) | collective-permute-done | bytes 25632 | tf_op jit(solution)/shard_map/ppermute | solution.py:414
  27.2 0.0 collective-permute-done.8.refs_3_
  27.2 1.0 %combine.1 = (bf16[128,640]{1,0:T(8,128)(2,1)}, bf16[128,640]{1,0:T(8,128)(2,1)}) custom-call(bf16[100,128]{1,0:T(8,128)(2,1)S(1)} %get-tuple-element.43.refs_0_, bf16[100,128]{1,0:T(8,128)(2,1)S(1)} %collective-permute-done.6.refs_1_, bf16[100,128]{1,0:T(8,128)(2,1)S(1)} %collective-permute-done.7.refs_2_, ...), custom_call_target="tpu_custom_call" | custom-call | tf_op jit(solution)/shard_map/combine/pallas_call | solution.py:397
  (1 shorter events, 0.0 us)
Async XLA Ops:
  2.0 7.7 %collective-permute-start = (bf16[100,128]{1,0:T(8,128)(2,1)S(1)}, bf16[100,128]{1,0:T(8,128)(2,1)S(1)}, u32[]{:S(2)}, u32[]{:S(2)}) collective-permute-start(bf16[100,128]{1,0:T(8,128)(2,1)S(1)} %get-tuple-element.30), channel_id=1, source_target_pairs={{0,8},{4,12},{8,0},{12,4},{1,9},{5,13},{9,1},{13,5},{2,10},{6,14},... | collective-permute-start | bytes 76808 | tf_op jit(solution)/shard_map/ppermute | solution.py:414
  6.1 5.6 %collective-permute-start.1 = (bf16[100,128]{1,0:T(8,128)(2,1)S(1)}, bf16[100,128]{1,0:T(8,128)(2,1)S(1)}, u32[]{:S(2)}, u32[]{:S(2)}) collective-permute-start(bf16[100,128]{1,0:T(8,128)(2,1)S(1)} %get-tuple-element.31), channel_id=1, source_target_pairs={{0,12},{4,8},{8,4},{12,0},{1,13},{5,9},{9,5},{13,1},{2,14},{6,10},... | collective-permute-start | bytes 76808 | tf_op jit(solution)/shard_map/ppermute | solution.py:414
  7.5 4.3 %collective-permute-start.2 = (bf16[100,128]{1,0:T(8,128)(2,1)S(1)}, bf16[100,128]{1,0:T(8,128)(2,1)S(1)}, u32[]{:S(2)}, u32[]{:S(2)}) collective-permute-start(bf16[100,128]{1,0:T(8,128)(2,1)S(1)} %get-tuple-element.32), channel_id=1, source_target_pairs={{0,4},{4,0},{8,12},{12,8},{1,5},{5,1},{9,13},{13,9},{2,6},{6,2},{1... | collective-permute-start | bytes 76808 | tf_op jit(solution)/shard_map/ppermute | solution.py:414
  12.3 1.4 %collective-permute-start.3 = (bf16[40,1152]{1,0:T(8,128)(2,1)S(1)}, bf16[40,1152]{1,0:T(8,128)(2,1)S(1)}, u32[]{:S(2)}, u32[]{:S(2)}) collective-permute-start(bf16[40,1152]{1,0:T(8,128)(2,1)S(1)} %get-tuple-element.40), channel_id=1, source_target_pairs={{0,1},{1,0},{2,3},{3,2},{4,5},{5,4},{6,7},{7,6},{8,9},{9,8},{10,11... | collective-permute-start | bytes 276488 | tf_op jit(solution)/shard_map/ppermute | solution.py:414
  13.6 4.8 %collective-permute-start.4 = (bf16[40,1152]{1,0:T(8,128)(2,1)S(1)}, bf16[40,1152]{1,0:T(8,128)(2,1)S(1)}, u32[]{:S(2)}, u32[]{:S(2)}) collective-permute-start(bf16[40,1152]{1,0:T(8,128)(2,1)S(1)} %add.1.near_ref), channel_id=1, source_target_pairs={{0,2},{1,3},{2,0},{3,1},{4,6},{5,7},{6,4},{7,5},{8,10},{9,11},{10,... | collective-permute-start | bytes 276488 | tf_op jit(solution)/shard_map/ppermute | solution.py:414
  18.5 1.4 %collective-permute-start.5 = (bf16[40,1152]{1,0:T(8,128)(2,1)S(1)}, bf16[40,1152]{1,0:T(8,128)(2,1)S(1)}, u32[]{:S(2)}, u32[]{:S(2)}) collective-permute-start(bf16[40,1152]{1,0:T(8,128)(2,1)S(1)} %activate.1.mine_ref), channel_id=1, source_target_pairs={{0,1},{1,0},{2,3},{3,2},{4,5},{5,4},{6,7},{7,6},{8,9},{9,8},{10,11... | collective-permute-start | bytes 276488 | tf_op jit(solution)/shard_map/ppermute | solution.py:414
  20.3 6.4 %collective-permute-start.6 = (bf16[100,128]{1,0:T(8,128)(2,1)S(1)}, bf16[100,128]{1,0:T(8,128)(2,1)S(1)}, u32[]{:S(2)}, u32[]{:S(2)}) collective-permute-start(bf16[100,128]{1,0:T(8,128)(2,1)S(1)} %get-tuple-element.44), channel_id=1, source_target_pairs={{0,12},{4,8},{8,4},{12,0},{1,13},{5,9},{9,5},{13,1},{2,14},{6,10},... | collective-permute-start | bytes 76808 | tf_op jit(solution)/shard_map/ppermute | solution.py:414
  22.4 4.7 %collective-permute-start.7 = (bf16[100,128]{1,0:T(8,128)(2,1)S(1)}, bf16[100,128]{1,0:T(8,128)(2,1)S(1)}, u32[]{:S(2)}, u32[]{:S(2)}) collective-permute-start(bf16[100,128]{1,0:T(8,128)(2,1)S(1)} %get-tuple-element.45), channel_id=1, source_target_pairs={{0,8},{4,12},{8,0},{12,4},{1,9},{5,13},{9,1},{13,5},{2,10},{6,14},... | collective-permute-start | bytes 76808 | tf_op jit(solution)/shard_map/ppermute | solution.py:414
  22.4 4.7 %collective-permute-start.8 = (bf16[100,128]{1,0:T(8,128)(2,1)S(1)}, bf16[100,128]{1,0:T(8,128)(2,1)S(1)}, u32[]{:S(2)}, u32[]{:S(2)}) collective-permute-start(bf16[100,128]{1,0:T(8,128)(2,1)S(1)} %get-tuple-element.46), channel_id=1, source_target_pairs={{0,4},{4,0},{8,12},{12,8},{1,5},{5,1},{9,13},{13,9},{2,6},{6,2},{1... | collective-permute-start | bytes 76808 | tf_op jit(solution)/shard_map/ppermute | solution.py:414

commit v15 on v12

--- a/solution.py
+++ b/solution.py
@@ -117,6 +117,9 @@
         send_refs[0][...] = send.astype(BF16)
         return
     width = send.shape[1] // chunks
+    used = 2 * slots * chunks
+    if wide.shape[0] > used:
+        wide[used:, :] = jnp.zeros((wide.shape[0] - used, width), F32)
     for i, send_ref in enumerate(send_refs):
         for j in range(chunks):
             rows = send[i * block : i * block + 2 * slots, j * width : (j + 1) * width]
@@ -128,7 +131,8 @@
     count, feature = tokens.shape
     vmem = pl.BlockSpec(memory_space=pltpu.VMEM)
     block = padded(2 * slots)
-    sent = (experts * block, feature) if pieces == 1 else (2 * slots * chunks, feature // chunks)
+    packed = (padded(2 * slots * chunks), feature // chunks)
+    sent = (experts * block, feature) if pieces == 1 else packed
     outs = pl.pallas_call(
         functools.partial(dispatch_kernel, experts, plan.shape[1], slots, chunks, pieces),
         out_shape=(jax.ShapeDtypeStruct(sent, BF16),) * pieces
@@ -141,7 +145,7 @@
             pltpu.VMEM(ids.shape, I32),
             pltpu.VMEM(gates.shape, F32),
             pltpu.VMEM((2 * count, feature), BF16),
-            pltpu.VMEM((2 * slots * chunks, feature // chunks), F32),
+            pltpu.VMEM(packed, F32),
             pltpu.SemaphoreType.DMA((4 + 2 * LOADS,)),
         ],
         compiler_params=params(),
@@ -266,8 +270,9 @@
     outs, ins = half_outputs(1, theirs_ref, gate_ref, up_ref, down_ref)
     flat[0] = outs_ref[...] + outs
     flat[1] = ins_ref[...] + ins
-    if block > 2 * slots * chunks:
-        wide[...] = jnp.zeros_like(wide)
+    used = 2 * slots * chunks
+    if block > used:
+        wide[:, used:, :] = jnp.zeros((group, block - used, width), F32)
     for s in range(group):
         for j in range(chunks):
             columns = pl.ds(j * width, width)
@@ -359,10 +364,12 @@
     back_refs = refs[:pieces]
     merge_ref, mixed_hbm, token_hbm, mixed_ref, token_ref, wide, flat, sems = refs[pieces:]
     if pieces > 1:
-        flat[...] = jnp.zeros_like(flat)
         rows, width, block = 2 * slots, back_refs[0].shape[1], padded(2 * slots)
         for i, back_ref in enumerate(back_refs):
             wide[i] = back_ref[...].astype(F32)
+            if block > rows:
+                gap = pl.ds(i * block + rows, block - rows)
+                flat[gap, :] = jnp.zeros((block - rows, flat.shape[1]), F32)
             for j in range(chunks):
                 part = pl.ds(j * width, width)
                 flat[i * block : i * block + rows, part] = wide[i, j * rows : (j + 1) * rows, :]
@@ -442,7 +449,7 @@
     feature, width = gate.shape
     pieces = experts if experts <= GROUP and feature % CHUNK == 0 else 1
     chunks = feature // CHUNK if pieces > 1 else 1
-    block = 2 * slots * chunks if pieces > 1 else padded(2 * slots)
+    block = padded(2 * slots * chunks)
     sends, (scaled, pick) = dispatch(
         replica_plan,
         cap_blocks,

time: 28.2 us -> 28.2 us (level)
  no operation moved by 1% of the time
where the time goes in v15:
time: 28.2 us; the launch traced here: 28 us
  starting transfers between devices  11.9 us (42%)
  Pallas kernels  8.27 us (29%)
  waiting for transfers between devices  7.1 us (25%)
  between operations  0.72 us (3%)
    ppermute x9, starting transfers between devices, swapped(): lax.ppermute(array, axis, [(i, i ^ distance) for i in range(lax.axis_size...  11.9 us
    ppermute x9, waiting for transfers between devices, swapped(): lax.ppermute(array, axis, [(i, i ^ distance) for i in range(lax.axis_size...  7.1 us
    pallas_call x1, Pallas kernels, load_weights(): pl.pallas_call(load_kernel, out_shape=tuple((pltpu.VMEM(w.shape, BF16) fo...  2.01 us
    pallas_call x1, Pallas kernels, weight_grads(): pl.pallas_call(grads_kernel, out_shape=tuple((jax.ShapeDtypeStruct(shape,...  1.96 us
    pallas_call x6, Pallas kernels, by_rows(): pl.pallas_call(kernel, grid=(steps,), out_shape=tuple((jax.ShapeDtypeStru...  1.92 us
    pallas_call x1, Pallas kernels, dispatch(): pl.pallas_call(functools.partial(dispatch_kernel, experts, plan.shape[1],...  1.39 us
    pallas_call x1, Pallas kernels, combine(): pl.pallas_call(functools.partial(combine_kernel, columns, slots, chunks,...  0.99 us
  transfers between devices with their start and end apart: 9, of which 5 were waited for; matrix products, arithmetic and copies ran while one was open for 0% of the time, Pallas kernels for 17%

profile of v15, /device:TPU:0, one launch (start us, length us, event | category | flops | bytes accessed | tf_op | source)
XLA Modules:
  0.0 28.0 jit_solution(9723575673339062493)
XLA Ops:
  0.6 1.4 %dispatch.1 = (bf16[104,128]{1,0:T(8,128)(2,1)S(1)}, bf16[104,128]{1,0:T(8,128)(2,1)S(1)}, bf16[104,128]{1,0:T(8,128)(2,1)S(1)}, bf16[104,128]{1,0:T(8,128)(2,1)...) custom-call(s32[2,2]{1,0:T(2,128)} %refs_0_.1, s32[4]{0:T(128)} %refs_1_.1, s32[2,128]{1,0:T(2,128)} %bitcast.11, ...), custom_call_target="tpu_custom_call" | custom-call | tf_op jit(solution)/shard_map/dispatch/pallas_call | solution.py:136
  2.0 5.1 %collective-permute-start = (bf16[104,128]{1,0:T(8,128)(2,1)S(1)}, bf16[104,128]{1,0:T(8,128)(2,1)S(1)}, u32[]{:S(2)}, u32[]{:S(2)}) collective-permute-start(bf16[104,128]{1,0:T(8,128)(2,1)S(1)} %get-tuple-element.30), channel_id=1, source_target_pairs={{0,12},{4,8},{8,4},{12,0},{1,13},{5,9},{9,5},{13,1},{2,14},{6,10},... | collective-permute-start | bytes 79880 | tf_op jit(solution)/shard_map/ppermute | solution.py:419
  7.1 0.0 collective-permute-start.1
  7.1 0.6 %collective-permute-start.2 = (bf16[104,128]{1,0:T(8,128)(2,1)S(1)}, bf16[104,128]{1,0:T(8,128)(2,1)S(1)}, u32[]{:S(2)}, u32[]{:S(2)}) collective-permute-start(bf16[104,128]{1,0:T(8,128)(2,1)S(1)} %get-tuple-element.32), channel_id=1, source_target_pairs={{0,4},{4,0},{8,12},{12,8},{1,5},{5,1},{9,13},{13,9},{2,6},{6,2},{1... | collective-permute-start | bytes 79880 | tf_op jit(solution)/shard_map/ppermute | solution.py:419
  7.8 2.0 %load_weights.1 = (bf16[640,768]{1,0:T(8,128)(2,1)S(1)}, bf16[640,768]{1,0:T(8,128)(2,1)S(1)}, bf16[768,640]{1,0:T(8,128)(2,1)S(1)}, bf16[384,96]{1,0:T(8,128)(2,1)S(1)}) custom-call(bf16[640,768]{1,0:T(8,128)(2,1)} %bitcast.8, bf16[640,768]{1,0:T(8,128)(2,1)} %bitcast.9, bf16[768,640]{1,0:T(8,128)(2,1)} %bitcast.10, ...), custom_call_target="tpu_custom_call" | custom-call | bytes 5898240 | tf_op jit(solution)/shard_map/load_weights/pallas_call | solution.py:184
  9.8 0.0 collective-permute-done.refs_1_
  9.8 2.1 %collective-permute-done.1.refs_2_ = bf16[104,128]{1,0:T(8,128)(2,1)S(1)} collective-permute-done((bf16[104,128]{1,0:T(8,128)(2,1)S(1)}, bf16[104,128]{1,0:T(8,128)(2,1)S(1)}, u32[]{:S(2)}, u32[]{:S(2)}) %collective-permute-start.1) | collective-permute-done | bytes 26656 | tf_op jit(solution)/shard_map/ppermute | solution.py:419
  11.9 0.0 collective-permute-done.2.refs_3_
  11.9 0.5 %give.1 = (bf16[40,640]{1,0:T(8,128)(2,1)S(1)}, bf16[40,640]{1,0:T(8,128)(2,1)S(1)}, bf16[40,1152]{1,0:T(8,128)(2,1)S(1)}) custom-call(bf16[104,128]{1,0:T(8,128)(2,1)S(1)} %get-tuple-element.29.refs_0_, bf16[104,128]{1,0:T(8,128)(2,1)S(1)} %collective-permute-done.refs_1_, bf16[104,128]{1,0:T(8,128)(2,1)S(1)} %collective-permute-done.1.refs_2_, ...), custom_call_target="tpu_custom_call" | custom-call | flops 58982400 | bytes 3055616 | tf_op jit(solution)/shard_map/give/pallas_call | solution.py:294
  12.4 0.1 collective-permute-start.3
  12.5 0.4 %keep.1.left_ref = bf16[40,1152]{1,0:T(8,128)(2,1)S(1)} custom-call(bf16[40,640]{1,0:T(8,128)(2,1)S(1)} %get-tuple-element.38.rows_ref, bf16[40,640]{1,0:T(8,128)(2,1)S(1)} %get-tuple-element.39.cots_ref, bf16[640,768]{1,0:T(8,128)(2,1)S(1)} %get-tuple-element.35.refs_4_.gate_ref.refs_3_, bf16[640,768]{1,0:T(8,128)(2,1)S(1)} %get-tuple-element.36.refs_5_.up_ref.refs_4_, ...), custom_call_target="tpu_custom_call" | custom-call | flops 58982400 | bytes 3051520 | tf_op jit(solution)/shard_map/keep/pallas_call | solution.py:294
  12.9 0.8 %collective-permute-done.3.right_ref = bf16[40,1152]{1,0:T(8,128)(2,1)S(1)} collective-permute-done((bf16[40,1152]{1,0:T(8,128)(2,1)S(1)}, bf16[40,1152]{1,0:T(8,128)(2,1)S(1)}, u32[]{:S(2)}, u32[]{:S(2)}) %collective-permute-start.3) | collective-permute-done | bytes 92192 | tf_op jit(solution)/shard_map/ppermute | solution.py:419
  13.8 1.6 %collective-permute-start.4 = (bf16[40,1152]{1,0:T(8,128)(2,1)S(1)}, bf16[40,1152]{1,0:T(8,128)(2,1)S(1)}, u32[]{:S(2)}, u32[]{:S(2)}) collective-permute-start(bf16[40,1152]{1,0:T(8,128)(2,1)S(1)} %add.1.near_ref), channel_id=1, source_target_pairs={{0,2},{1,3},{2,0},{3,1},{4,6},{5,7},{6,4},{7,5},{8,10},{9,11},{10,... | collective-permute-start | bytes 276488 | tf_op jit(solution)/shard_map/ppermute | solution.py:419
  15.3 3.2 %collective-permute-done.4.far_ref = bf16[40,1152]{1,0:T(8,128)(2,1)S(1)} collective-permute-done((bf16[40,1152]{1,0:T(8,128)(2,1)S(1)}, bf16[40,1152]{1,0:T(8,128)(2,1)S(1)}, u32[]{:S(2)}, u32[]{:S(2)}) %collective-permute-start.4) | collective-permute-done | bytes 92192 | tf_op jit(solution)/shard_map/ppermute | solution.py:419
  18.5 0.1 activate.1.mine_ref
  18.6 0.1 collective-permute-start.5
  18.7 0.5 %own.1 = (f32[40,640]{1,0:T(8,128)S(1)}, f32[40,640]{1,0:T(8,128)S(1)}) custom-call(bf16[40,1152]{1,0:T(8,128)(2,1)S(1)} %activate.1.mine_ref, bf16[640,768]{1,0:T(8,128)(2,1)S(1)} %get-tuple-element.35.refs_4_.gate_ref.refs_3_, bf16[640,768]{1,0:T(8,128)(2,1)S(1)} %get-tuple-element.36.refs_5_.up_ref.refs_4_, ...), custom_call_target="tpu_custom_call" | custom-call | flops 58982400 | bytes 3041280 | tf_op jit(solution)/shard_map/own/pallas_call | solution.py:294
  19.1 0.8 %collective-permute-done.5.refs_0_.theirs_ref = bf16[40,1152]{1,0:T(8,128)(2,1)S(1)} collective-permute-done((bf16[40,1152]{1,0:T(8,128)(2,1)S(1)}, bf16[40,1152]{1,0:T(8,128)(2,1)S(1)}, u32[]{:S(2)}, u32[]{:S(2)}) %collective-permute-start.5) | collective-permute-done | bytes 92192 | tf_op jit(solution)/shard_map/ppermute | solution.py:419
  20.0 0.5 %back.1 = (bf16[104,128]{1,0:T(8,128)(2,1)S(1)}, bf16[104,128]{1,0:T(8,128)(2,1)S(1)}, bf16[104,128]{1,0:T(8,128)(2,1)S(1)}, bf16[104,128]{1,0:T(8,128)(2,1)S(1)}) custom-call(bf16[40,1152]{1,0:T(8,128)(2,1)S(1)} %collective-permute-done.5.refs_0_.theirs_ref, f32[40,640]{1,0:T(8,128)S(1)} %get-tuple-element.41.refs_1_, ...), custom_call_target="tpu_custom_call" | custom-call | flops 58982400 | bytes 3246080 | tf_op jit(solution)/shard_map/back/pallas_call | solution.py:294
  20.4 1.7 %collective-permute-start.6 = (bf16[104,128]{1,0:T(8,128)(2,1)S(1)}, bf16[104,128]{1,0:T(8,128)(2,1)S(1)}, u32[]{:S(2)}, u32[]{:S(2)}) collective-permute-start(bf16[104,128]{1,0:T(8,128)(2,1)S(1)} %get-tuple-element.44), channel_id=1, source_target_pairs={{0,12},{4,8},{8,4},{12,0},{1,13},{5,9},{9,5},{13,1},{2,14},{6,10},... | collective-permute-start | bytes 79880 | tf_op jit(solution)/shard_map/ppermute | solution.py:419
  22.2 0.4 %collective-permute-start.7 = (bf16[104,128]{1,0:T(8,128)(2,1)S(1)}, bf16[104,128]{1,0:T(8,128)(2,1)S(1)}, u32[]{:S(2)}, u32[]{:S(2)}) collective-permute-start(bf16[104,128]{1,0:T(8,128)(2,1)S(1)} %get-tuple-element.45), channel_id=1, source_target_pairs={{0,8},{4,12},{8,0},{12,4},{1,9},{5,13},{9,1},{13,5},{2,10},{6,14},... | collective-permute-start | bytes 79880 | tf_op jit(solution)/shard_map/ppermute | solution.py:419
  22.6 2.3 %collective-permute-start.8 = (bf16[104,128]{1,0:T(8,128)(2,1)S(1)}, bf16[104,128]{1,0:T(8,128)(2,1)S(1)}, u32[]{:S(2)}, u32[]{:S(2)}) collective-permute-start(bf16[104,128]{1,0:T(8,128)(2,1)S(1)} %get-tuple-element.46), channel_id=1, source_target_pairs={{0,4},{4,0},{8,12},{12,8},{1,5},{5,1},{9,13},{13,9},{2,6},{6,2},{1... | collective-permute-start | bytes 79880 | tf_op jit(solution)/shard_map/ppermute | solution.py:419
  24.9 2.0 %weight_grads.1 = (bf16[640,768]{1,0:T(8,128)(2,1)}, bf16[640,768]{1,0:T(8,128)(2,1)}, bf16[768,640]{1,0:T(8,128)(2,1)}) custom-call(bf16[40,640]{1,0:T(8,128)(2,1)S(1)} %get-tuple-element.38.rows_ref, bf16[40,640]{1,0:T(8,128)(2,1)S(1)} %get-tuple-element.39.cots_ref, bf16[40,1152]{1,0:T(8,128)(2,1)S(1)} %activate.1.mine_ref, ...), custom_call_target="tpu_custom_call" | custom-call | flops 117964800 | bytes 2949120 | tf_op jit(solution)/shard_map/weight_grads/pallas_call | solution.py:346
  26.9 0.0 collective-permute-done.6.refs_1_
  26.9 0.1 collective-permute-done.7.refs_2_
  27.0 0.0 collective-permute-done.8.refs_3_
  27.0 1.0 %combine.1 = (bf16[128,640]{1,0:T(8,128)(2,1)}, bf16[128,640]{1,0:T(8,128)(2,1)}) custom-call(bf16[104,128]{1,0:T(8,128)(2,1)S(1)} %get-tuple-element.43.refs_0_, bf16[104,128]{1,0:T(8,128)(2,1)S(1)} %collective-permute-done.6.refs_1_, bf16[104,128]{1,0:T(8,128)(2,1)S(1)} %collective-permute-done.7.refs_2_, ...), custom_call_target="tpu_custom_call" | custom-call | tf_op jit(solution)/shard_map/combine/pallas_call | solution.py:402
  (1 shorter events, 0.0 us)
Async XLA Ops:
  2.0 7.8 %collective-permute-start = (bf16[104,128]{1,0:T(8,128)(2,1)S(1)}, bf16[104,128]{1,0:T(8,128)(2,1)S(1)}, u32[]{:S(2)}, u32[]{:S(2)}) collective-permute-start(bf16[104,128]{1,0:T(8,128)(2,1)S(1)} %get-tuple-element.30), channel_id=1, source_target_pairs={{0,12},{4,8},{8,4},{12,0},{1,13},{5,9},{9,5},{13,1},{2,14},{6,10},... | collective-permute-start | bytes 79880 | tf_op jit(solution)/shard_map/ppermute | solution.py:419
  7.1 4.7 %collective-permute-start.1 = (bf16[104,128]{1,0:T(8,128)(2,1)S(1)}, bf16[104,128]{1,0:T(8,128)(2,1)S(1)}, u32[]{:S(2)}, u32[]{:S(2)}) collective-permute-start(bf16[104,128]{1,0:T(8,128)(2,1)S(1)} %get-tuple-element.31), channel_id=1, source_target_pairs={{0,8},{4,12},{8,0},{12,4},{1,9},{5,13},{9,1},{13,5},{2,10},{6,14},... | collective-permute-start | bytes 79880 | tf_op jit(solution)/shard_map/ppermute | solution.py:419
  7.1 4.7 %collective-permute-start.2 = (bf16[104,128]{1,0:T(8,128)(2,1)S(1)}, bf16[104,128]{1,0:T(8,128)(2,1)S(1)}, u32[]{:S(2)}, u32[]{:S(2)}) collective-permute-start(bf16[104,128]{1,0:T(8,128)(2,1)S(1)} %get-tuple-element.32), channel_id=1, source_target_pairs={{0,4},{4,0},{8,12},{12,8},{1,5},{5,1},{9,13},{13,9},{2,6},{6,2},{1... | collective-permute-start | bytes 79880 | tf_op jit(solution)/shard_map/ppermute | solution.py:419
  12.4 1.4 %collective-permute-start.3 = (bf16[40,1152]{1,0:T(8,128)(2,1)S(1)}, bf16[40,1152]{1,0:T(8,128)(2,1)S(1)}, u32[]{:S(2)}, u32[]{:S(2)}) collective-permute-start(bf16[40,1152]{1,0:T(8,128)(2,1)S(1)} %get-tuple-element.40), channel_id=1, source_target_pairs={{0,1},{1,0},{2,3},{3,2},{4,5},{5,4},{6,7},{7,6},{8,9},{9,8},{10,11... | collective-permute-start | bytes 276488 | tf_op jit(solution)/shard_map/ppermute | solution.py:419
  13.8 4.8 %collective-permute-start.4 = (bf16[40,1152]{1,0:T(8,128)(2,1)S(1)}, bf16[40,1152]{1,0:T(8,128)(2,1)S(1)}, u32[]{:S(2)}, u32[]{:S(2)}) collective-permute-start(bf16[40,1152]{1,0:T(8,128)(2,1)S(1)} %add.1.near_ref), channel_id=1, source_target_pairs={{0,2},{1,3},{2,0},{3,1},{4,6},{5,7},{6,4},{7,5},{8,10},{9,11},{10,... | collective-permute-start | bytes 276488 | tf_op jit(solution)/shard_map/ppermute | solution.py:419
  18.6 1.4 %collective-permute-start.5 = (bf16[40,1152]{1,0:T(8,128)(2,1)S(1)}, bf16[40,1152]{1,0:T(8,128)(2,1)S(1)}, u32[]{:S(2)}, u32[]{:S(2)}) collective-permute-start(bf16[40,1152]{1,0:T(8,128)(2,1)S(1)} %activate.1.mine_ref), channel_id=1, source_target_pairs={{0,1},{1,0},{2,3},{3,2},{4,5},{5,4},{6,7},{7,6},{8,9},{9,8},{10,11... | collective-permute-start | bytes 276488 | tf_op jit(solution)/shard_map/ppermute | solution.py:419
  20.4 6.4 %collective-permute-start.6 = (bf16[104,128]{1,0:T(8,128)(2,1)S(1)}, bf16[104,128]{1,0:T(8,128)(2,1)S(1)}, u32[]{:S(2)}, u32[]{:S(2)}) collective-permute-start(bf16[104,128]{1,0:T(8,128)(2,1)S(1)} %get-tuple-element.44), channel_id=1, source_target_pairs={{0,12},{4,8},{8,4},{12,0},{1,13},{5,9},{9,5},{13,1},{2,14},{6,10},... | collective-permute-start | bytes 79880 | tf_op jit(solution)/shard_map/ppermute | solution.py:419
  22.2 4.8 %collective-permute-start.7 = (bf16[104,128]{1,0:T(8,128)(2,1)S(1)}, bf16[104,128]{1,0:T(8,128)(2,1)S(1)}, u32[]{:S(2)}, u32[]{:S(2)}) collective-permute-start(bf16[104,128]{1,0:T(8,128)(2,1)S(1)} %get-tuple-element.45), channel_id=1, source_target_pairs={{0,8},{4,12},{8,0},{12,4},{1,9},{5,13},{9,1},{13,5},{2,10},{6,14},... | collective-permute-start | bytes 79880 | tf_op jit(solution)/shard_map/ppermute | solution.py:419
  22.6 4.4 %collective-permute-start.8 = (bf16[104,128]{1,0:T(8,128)(2,1)S(1)}, bf16[104,128]{1,0:T(8,128)(2,1)S(1)}, u32[]{:S(2)}, u32[]{:S(2)}) collective-permute-start(bf16[104,128]{1,0:T(8,128)(2,1)S(1)} %get-tuple-element.46), channel_id=1, source_target_pairs={{0,4},{4,0},{8,12},{12,8},{1,5},{5,1},{9,13},{13,9},{2,6},{6,2},{1... | collective-permute-start | bytes 79880 | tf_op jit(solution)/shard_map/ppermute | solution.py:419

commit v16 on v15

--- a/solution.py
+++ b/solution.py
@@ -325,13 +325,14 @@
             hidden = acts_ref[:, start : start + size]
             down_ref[rows, :] = matmul(hidden, cots_ref[...], 0, 0).astype(BF16)
             send(down_ref, down_hbm, rows)
-    for place, out_ref, out_hbm in ((1, gate_ref, gate_hbm), (2, up_ref, up_hbm)):
-        for start, size in spans(out_ref.shape[0], CHUNK):
-            rows = pl.ds(start, size)
-            for acts_ref, units in sides:
-                grad = acts_ref[:, place * half : (place + 1) * half]
-                out_ref[rows, units] = matmul(rows_ref[:, rows], grad, 0, 0).astype(BF16)
-            send(out_ref, out_hbm, rows)
+    for start, size in spans(gate_ref.shape[0], CHUNK):
+        rows = pl.ds(start, size)
+        for acts_ref, units in sides:
+            grads = matmul(rows_ref[:, rows], acts_ref[:, half:], 0, 0).astype(BF16)
+            gate_ref[rows, units] = grads[:, :half]
+            up_ref[rows, units] = grads[:, half:]
+        send(gate_ref, gate_hbm, rows)
+        send(up_ref, up_hbm, rows)
     for copy in copies:
         copy.wait()
 

time: 28.2 us -> 28.2 us (level)
  no operation moved by 1% of the time
where the time goes in v16:
time: 28.2 us; the launch traced here: 28 us
  starting transfers between devices  11.9 us (42%)
  Pallas kernels  8.27 us (29%)
  waiting for transfers between devices  7.11 us (25%)
  between operations  0.72 us (3%)
    ppermute x9, starting transfers between devices, swapped(): lax.ppermute(array, axis, [(i, i ^ distance) for i in range(lax.axis_size...  11.9 us
    ppermute x9, waiting for transfers between devices, swapped(): lax.ppermute(array, axis, [(i, i ^ distance) for i in range(lax.axis_size...  7.11 us
    pallas_call x1, Pallas kernels, load_weights(): pl.pallas_call(load_kernel, out_shape=tuple((pltpu.VMEM(w.shape, BF16) fo...  2.01 us
    pallas_call x1, Pallas kernels, weight_grads(): pl.pallas_call(grads_kernel, out_shape=tuple((jax.ShapeDtypeStruct(shape,...  1.95 us
    pallas_call x6, Pallas kernels, by_rows(): pl.pallas_call(kernel, grid=(steps,), out_shape=tuple((jax.ShapeDtypeStru...  1.92 us
    pallas_call x1, Pallas kernels, dispatch(): pl.pallas_call(functools.partial(dispatch_kernel, experts, plan.shape[1],...  1.39 us
    pallas_call x1, Pallas kernels, combine(): pl.pallas_call(functools.partial(combine_kernel, columns, slots, chunks,...  0.99 us
  transfers between devices with their start and end apart: 9, of which 5 were waited for; matrix products, arithmetic and copies ran while one was open for 0% of the time, Pallas kernels for 17%

profile of v16, /device:TPU:0, one launch (start us, length us, event | category | flops | bytes accessed | tf_op | source)
XLA Modules:
  0.0 28.0 jit_solution(15365860109067032353)
XLA Ops:
  0.6 1.4 %dispatch.1 = (bf16[104,128]{1,0:T(8,128)(2,1)S(1)}, bf16[104,128]{1,0:T(8,128)(2,1)S(1)}, bf16[104,128]{1,0:T(8,128)(2,1)S(1)}, bf16[104,128]{1,0:T(8,128)(2,1)...) custom-call(s32[2,2]{1,0:T(2,128)} %refs_0_.1, s32[4]{0:T(128)} %refs_1_.1, s32[2,128]{1,0:T(2,128)} %bitcast.11, ...), custom_call_target="tpu_custom_call" | custom-call | tf_op jit(solution)/shard_map/dispatch/pallas_call | solution.py:136
  2.0 5.1 %collective-permute-start = (bf16[104,128]{1,0:T(8,128)(2,1)S(1)}, bf16[104,128]{1,0:T(8,128)(2,1)S(1)}, u32[]{:S(2)}, u32[]{:S(2)}) collective-permute-start(bf16[104,128]{1,0:T(8,128)(2,1)S(1)} %get-tuple-element.30), channel_id=1, source_target_pairs={{0,12},{4,8},{8,4},{12,0},{1,13},{5,9},{9,5},{13,1},{2,14},{6,10},... | collective-permute-start | bytes 79880 | tf_op jit(solution)/shard_map/ppermute | solution.py:420
  7.1 0.0 collective-permute-start.1
  7.1 0.6 %collective-permute-start.2 = (bf16[104,128]{1,0:T(8,128)(2,1)S(1)}, bf16[104,128]{1,0:T(8,128)(2,1)S(1)}, u32[]{:S(2)}, u32[]{:S(2)}) collective-permute-start(bf16[104,128]{1,0:T(8,128)(2,1)S(1)} %get-tuple-element.32), channel_id=1, source_target_pairs={{0,4},{4,0},{8,12},{12,8},{1,5},{5,1},{9,13},{13,9},{2,6},{6,2},{1... | collective-permute-start | bytes 79880 | tf_op jit(solution)/shard_map/ppermute | solution.py:420
  7.8 2.0 %load_weights.1 = (bf16[640,768]{1,0:T(8,128)(2,1)S(1)}, bf16[640,768]{1,0:T(8,128)(2,1)S(1)}, bf16[768,640]{1,0:T(8,128)(2,1)S(1)}, bf16[384,96]{1,0:T(8,128)(2,1)S(1)}) custom-call(bf16[640,768]{1,0:T(8,128)(2,1)} %bitcast.8, bf16[640,768]{1,0:T(8,128)(2,1)} %bitcast.9, bf16[768,640]{1,0:T(8,128)(2,1)} %bitcast.10, ...), custom_call_target="tpu_custom_call" | custom-call | bytes 5898240 | tf_op jit(solution)/shard_map/load_weights/pallas_call | solution.py:184
  9.8 0.0 collective-permute-done.refs_1_
  9.8 2.1 %collective-permute-done.1.refs_2_ = bf16[104,128]{1,0:T(8,128)(2,1)S(1)} collective-permute-done((bf16[104,128]{1,0:T(8,128)(2,1)S(1)}, bf16[104,128]{1,0:T(8,128)(2,1)S(1)}, u32[]{:S(2)}, u32[]{:S(2)}) %collective-permute-start.1) | collective-permute-done | bytes 26656 | tf_op jit(solution)/shard_map/ppermute | solution.py:420
  11.9 0.0 collective-permute-done.2.refs_3_
  11.9 0.5 %give.1 = (bf16[40,640]{1,0:T(8,128)(2,1)S(1)}, bf16[40,640]{1,0:T(8,128)(2,1)S(1)}, bf16[40,1152]{1,0:T(8,128)(2,1)S(1)}) custom-call(bf16[104,128]{1,0:T(8,128)(2,1)S(1)} %get-tuple-element.29.refs_0_, bf16[104,128]{1,0:T(8,128)(2,1)S(1)} %collective-permute-done.refs_1_, bf16[104,128]{1,0:T(8,128)(2,1)S(1)} %collective-permute-done.1.refs_2_, ...), custom_call_target="tpu_custom_call" | custom-call | flops 58982400 | bytes 3055616 | tf_op jit(solution)/shard_map/give/pallas_call | solution.py:294
  12.4 0.1 collective-permute-start.3
  12.5 0.4 %keep.1.left_ref = bf16[40,1152]{1,0:T(8,128)(2,1)S(1)} custom-call(bf16[40,640]{1,0:T(8,128)(2,1)S(1)} %get-tuple-element.38.rows_ref, bf16[40,640]{1,0:T(8,128)(2,1)S(1)} %get-tuple-element.39.cots_ref, bf16[640,768]{1,0:T(8,128)(2,1)S(1)} %get-tuple-element.35.refs_4_.gate_ref.refs_3_, bf16[640,768]{1,0:T(8,128)(2,1)S(1)} %get-tuple-element.36.refs_5_.up_ref.refs_4_, ...), custom_call_target="tpu_custom_call" | custom-call | flops 58982400 | bytes 3051520 | tf_op jit(solution)/shard_map/keep/pallas_call | solution.py:294
  12.9 0.8 %collective-permute-done.3.right_ref = bf16[40,1152]{1,0:T(8,128)(2,1)S(1)} collective-permute-done((bf16[40,1152]{1,0:T(8,128)(2,1)S(1)}, bf16[40,1152]{1,0:T(8,128)(2,1)S(1)}, u32[]{:S(2)}, u32[]{:S(2)}) %collective-permute-start.3) | collective-permute-done | bytes 92192 | tf_op jit(solution)/shard_map/ppermute | solution.py:420
  13.8 1.6 %collective-permute-start.4 = (bf16[40,1152]{1,0:T(8,128)(2,1)S(1)}, bf16[40,1152]{1,0:T(8,128)(2,1)S(1)}, u32[]{:S(2)}, u32[]{:S(2)}) collective-permute-start(bf16[40,1152]{1,0:T(8,128)(2,1)S(1)} %add.1.near_ref), channel_id=1, source_target_pairs={{0,2},{1,3},{2,0},{3,1},{4,6},{5,7},{6,4},{7,5},{8,10},{9,11},{10,... | collective-permute-start | bytes 276488 | tf_op jit(solution)/shard_map/ppermute | solution.py:420
  15.3 3.2 %collective-permute-done.4.far_ref = bf16[40,1152]{1,0:T(8,128)(2,1)S(1)} collective-permute-done((bf16[40,1152]{1,0:T(8,128)(2,1)S(1)}, bf16[40,1152]{1,0:T(8,128)(2,1)S(1)}, u32[]{:S(2)}, u32[]{:S(2)}) %collective-permute-start.4) | collective-permute-done | bytes 92192 | tf_op jit(solution)/shard_map/ppermute | solution.py:420
  18.5 0.1 activate.1.mine_ref
  18.6 0.1 collective-permute-start.5
  18.7 0.5 %own.1 = (f32[40,640]{1,0:T(8,128)S(1)}, f32[40,640]{1,0:T(8,128)S(1)}) custom-call(bf16[40,1152]{1,0:T(8,128)(2,1)S(1)} %activate.1.mine_ref, bf16[640,768]{1,0:T(8,128)(2,1)S(1)} %get-tuple-element.35.refs_4_.gate_ref.refs_3_, bf16[640,768]{1,0:T(8,128)(2,1)S(1)} %get-tuple-element.36.refs_5_.up_ref.refs_4_, ...), custom_call_target="tpu_custom_call" | custom-call | flops 58982400 | bytes 3041280 | tf_op jit(solution)/shard_map/own/pallas_call | solution.py:294
  19.1 0.8 %collective-permute-done.5.refs_0_.theirs_ref = bf16[40,1152]{1,0:T(8,128)(2,1)S(1)} collective-permute-done((bf16[40,1152]{1,0:T(8,128)(2,1)S(1)}, bf16[40,1152]{1,0:T(8,128)(2,1)S(1)}, u32[]{:S(2)}, u32[]{:S(2)}) %collective-permute-start.5) | collective-permute-done | bytes 92192 | tf_op jit(solution)/shard_map/ppermute | solution.py:420
  20.0 0.5 %back.1 = (bf16[104,128]{1,0:T(8,128)(2,1)S(1)}, bf16[104,128]{1,0:T(8,128)(2,1)S(1)}, bf16[104,128]{1,0:T(8,128)(2,1)S(1)}, bf16[104,128]{1,0:T(8,128)(2,1)S(1)}) custom-call(bf16[40,1152]{1,0:T(8,128)(2,1)S(1)} %collective-permute-done.5.refs_0_.theirs_ref, f32[40,640]{1,0:T(8,128)S(1)} %get-tuple-element.41.refs_1_, ...), custom_call_target="tpu_custom_call" | custom-call | flops 58982400 | bytes 3246080 | tf_op jit(solution)/shard_map/back/pallas_call | solution.py:294
  20.4 1.7 %collective-permute-start.6 = (bf16[104,128]{1,0:T(8,128)(2,1)S(1)}, bf16[104,128]{1,0:T(8,128)(2,1)S(1)}, u32[]{:S(2)}, u32[]{:S(2)}) collective-permute-start(bf16[104,128]{1,0:T(8,128)(2,1)S(1)} %get-tuple-element.44), channel_id=1, source_target_pairs={{0,12},{4,8},{8,4},{12,0},{1,13},{5,9},{9,5},{13,1},{2,14},{6,10},... | collective-permute-start | bytes 79880 | tf_op jit(solution)/shard_map/ppermute | solution.py:420
  22.2 0.4 %collective-permute-start.7 = (bf16[104,128]{1,0:T(8,128)(2,1)S(1)}, bf16[104,128]{1,0:T(8,128)(2,1)S(1)}, u32[]{:S(2)}, u32[]{:S(2)}) collective-permute-start(bf16[104,128]{1,0:T(8,128)(2,1)S(1)} %get-tuple-element.45), channel_id=1, source_target_pairs={{0,8},{4,12},{8,0},{12,4},{1,9},{5,13},{9,1},{13,5},{2,10},{6,14},... | collective-permute-start | bytes 79880 | tf_op jit(solution)/shard_map/ppermute | solution.py:420
  22.6 2.3 %collective-permute-start.8 = (bf16[104,128]{1,0:T(8,128)(2,1)S(1)}, bf16[104,128]{1,0:T(8,128)(2,1)S(1)}, u32[]{:S(2)}, u32[]{:S(2)}) collective-permute-start(bf16[104,128]{1,0:T(8,128)(2,1)S(1)} %get-tuple-element.46), channel_id=1, source_target_pairs={{0,4},{4,0},{8,12},{12,8},{1,5},{5,1},{9,13},{13,9},{2,6},{6,2},{1... | collective-permute-start | bytes 79880 | tf_op jit(solution)/shard_map/ppermute | solution.py:420
  24.9 2.0 %weight_grads.1 = (bf16[640,768]{1,0:T(8,128)(2,1)}, bf16[640,768]{1,0:T(8,128)(2,1)}, bf16[768,640]{1,0:T(8,128)(2,1)}) custom-call(bf16[40,640]{1,0:T(8,128)(2,1)S(1)} %get-tuple-element.38.rows_ref, bf16[40,640]{1,0:T(8,128)(2,1)S(1)} %get-tuple-element.39.cots_ref, bf16[40,1152]{1,0:T(8,128)(2,1)S(1)} %activate.1.mine_ref, ...), custom_call_target="tpu_custom_call" | custom-call | flops 117964800 | bytes 2949120 | tf_op jit(solution)/shard_map/weight_grads/pallas_call | solution.py:347
  26.9 0.0 collective-permute-done.6.refs_1_
  26.9 0.1 collective-permute-done.7.refs_2_
  27.0 0.0 collective-permute-done.8.refs_3_
  27.0 1.0 %combine.1 = (bf16[128,640]{1,0:T(8,128)(2,1)}, bf16[128,640]{1,0:T(8,128)(2,1)}) custom-call(bf16[104,128]{1,0:T(8,128)(2,1)S(1)} %get-tuple-element.43.refs_0_, bf16[104,128]{1,0:T(8,128)(2,1)S(1)} %collective-permute-done.6.refs_1_, bf16[104,128]{1,0:T(8,128)(2,1)S(1)} %collective-permute-done.7.refs_2_, ...), custom_call_target="tpu_custom_call" | custom-call | tf_op jit(solution)/shard_map/combine/pallas_call | solution.py:403
  (1 shorter events, 0.0 us)
Async XLA Ops:
  2.0 7.8 %collective-permute-start = (bf16[104,128]{1,0:T(8,128)(2,1)S(1)}, bf16[104,128]{1,0:T(8,128)(2,1)S(1)}, u32[]{:S(2)}, u32[]{:S(2)}) collective-permute-start(bf16[104,128]{1,0:T(8,128)(2,1)S(1)} %get-tuple-element.30), channel_id=1, source_target_pairs={{0,12},{4,8},{8,4},{12,0},{1,13},{5,9},{9,5},{13,1},{2,14},{6,10},... | collective-permute-start | bytes 79880 | tf_op jit(solution)/shard_map/ppermute | solution.py:420
  7.1 4.7 %collective-permute-start.1 = (bf16[104,128]{1,0:T(8,128)(2,1)S(1)}, bf16[104,128]{1,0:T(8,128)(2,1)S(1)}, u32[]{:S(2)}, u32[]{:S(2)}) collective-permute-start(bf16[104,128]{1,0:T(8,128)(2,1)S(1)} %get-tuple-element.31), channel_id=1, source_target_pairs={{0,8},{4,12},{8,0},{12,4},{1,9},{5,13},{9,1},{13,5},{2,10},{6,14},... | collective-permute-start | bytes 79880 | tf_op jit(solution)/shard_map/ppermute | solution.py:420
  7.1 4.7 %collective-permute-start.2 = (bf16[104,128]{1,0:T(8,128)(2,1)S(1)}, bf16[104,128]{1,0:T(8,128)(2,1)S(1)}, u32[]{:S(2)}, u32[]{:S(2)}) collective-permute-start(bf16[104,128]{1,0:T(8,128)(2,1)S(1)} %get-tuple-element.32), channel_id=1, source_target_pairs={{0,4},{4,0},{8,12},{12,8},{1,5},{5,1},{9,13},{13,9},{2,6},{6,2},{1... | collective-permute-start | bytes 79880 | tf_op jit(solution)/shard_map/ppermute | solution.py:420
  12.4 1.4 %collective-permute-start.3 = (bf16[40,1152]{1,0:T(8,128)(2,1)S(1)}, bf16[40,1152]{1,0:T(8,128)(2,1)S(1)}, u32[]{:S(2)}, u32[]{:S(2)}) collective-permute-start(bf16[40,1152]{1,0:T(8,128)(2,1)S(1)} %get-tuple-element.40), channel_id=1, source_target_pairs={{0,1},{1,0},{2,3},{3,2},{4,5},{5,4},{6,7},{7,6},{8,9},{9,8},{10,11... | collective-permute-start | bytes 276488 | tf_op jit(solution)/shard_map/ppermute | solution.py:420
  13.8 4.8 %collective-permute-start.4 = (bf16[40,1152]{1,0:T(8,128)(2,1)S(1)}, bf16[40,1152]{1,0:T(8,128)(2,1)S(1)}, u32[]{:S(2)}, u32[]{:S(2)}) collective-permute-start(bf16[40,1152]{1,0:T(8,128)(2,1)S(1)} %add.1.near_ref), channel_id=1, source_target_pairs={{0,2},{1,3},{2,0},{3,1},{4,6},{5,7},{6,4},{7,5},{8,10},{9,11},{10,... | collective-permute-start | bytes 276488 | tf_op jit(solution)/shard_map/ppermute | solution.py:420
  18.6 1.4 %collective-permute-start.5 = (bf16[40,1152]{1,0:T(8,128)(2,1)S(1)}, bf16[40,1152]{1,0:T(8,128)(2,1)S(1)}, u32[]{:S(2)}, u32[]{:S(2)}) collective-permute-start(bf16[40,1152]{1,0:T(8,128)(2,1)S(1)} %activate.1.mine_ref), channel_id=1, source_target_pairs={{0,1},{1,0},{2,3},{3,2},{4,5},{5,4},{6,7},{7,6},{8,9},{9,8},{10,11... | collective-permute-start | bytes 276488 | tf_op jit(solution)/shard_map/ppermute | solution.py:420
  20.4 6.4 %collective-permute-start.6 = (bf16[104,128]{1,0:T(8,128)(2,1)S(1)}, bf16[104,128]{1,0:T(8,128)(2,1)S(1)}, u32[]{:S(2)}, u32[]{:S(2)}) collective-permute-start(bf16[104,128]{1,0:T(8,128)(2,1)S(1)} %get-tuple-element.44), channel_id=1, source_target_pairs={{0,12},{4,8},{8,4},{12,0},{1,13},{5,9},{9,5},{13,1},{2,14},{6,10},... | collective-permute-start | bytes 79880 | tf_op jit(solution)/shard_map/ppermute | solution.py:420
  22.2 4.8 %collective-permute-start.7 = (bf16[104,128]{1,0:T(8,128)(2,1)S(1)}, bf16[104,128]{1,0:T(8,128)(2,1)S(1)}, u32[]{:S(2)}, u32[]{:S(2)}) collective-permute-start(bf16[104,128]{1,0:T(8,128)(2,1)S(1)} %get-tuple-element.45), channel_id=1, source_target_pairs={{0,8},{4,12},{8,0},{12,4},{1,9},{5,13},{9,1},{13,5},{2,10},{6,14},... | collective-permute-start | bytes 79880 | tf_op jit(solution)/shard_map/ppermute | solution.py:420
  22.6 4.4 %collective-permute-start.8 = (bf16[104,128]{1,0:T(8,128)(2,1)S(1)}, bf16[104,128]{1,0:T(8,128)(2,1)S(1)}, u32[]{:S(2)}, u32[]{:S(2)}) collective-permute-start(bf16[104,128]{1,0:T(8,128)(2,1)S(1)} %get-tuple-element.46), channel_id=1, source_target_pairs={{0,4},{4,0},{8,12},{12,8},{1,5},{5,1},{9,13},{13,9},{2,6},{6,2},{1... | collective-permute-start | bytes 79880 | tf_op jit(solution)/shard_map/ppermute | solution.py:420

commit v17 on v15

--- a/solution.py
+++ b/solution.py
@@ -55,9 +55,7 @@
     block = padded(2 * slots)
     pairs = [(ids_hbm, ids_ref), (plan_hbm, plan_ref), (caps_hbm, caps_ref), (gates_hbm, gates_ref)]
     for place, source in enumerate((tok_hbm, grad_hbm)):
-        for start, size in spans(count, count // LOADS):
-            target = both_ref.at[pl.ds(place * count + start, size)]
-            pairs.append((source.at[pl.ds(start, size)], target))
+        pairs.append((source, both_ref.at[pl.ds(place * count, count)]))
     copies = [
         pltpu.make_async_copy(source, target, sems.at[i])
         for i, (source, target) in enumerate(pairs)
@@ -146,7 +144,7 @@
             pltpu.VMEM(gates.shape, F32),
             pltpu.VMEM((2 * count, feature), BF16),
             pltpu.VMEM(packed, F32),
-            pltpu.SemaphoreType.DMA((4 + 2 * LOADS,)),
+            pltpu.SemaphoreType.DMA((6,)),
         ],
         compiler_params=params(),
         name="dispatch",

time: 28.2 us -> 28.1 us (level)
  no operation moved by 1% of the time
where the time goes in v17:
time: 28.1 us; the launch traced here: 27.9 us
  starting transfers between devices  11.9 us (42%)
  Pallas kernels  8.21 us (29%)
  waiting for transfers between devices  7.1 us (25%)
  between operations  0.72 us (3%)
    ppermute x9, starting transfers between devices, swapped(): lax.ppermute(array, axis, [(i, i ^ distance) for i in range(lax.axis_size...  11.9 us
    ppermute x9, waiting for transfers between devices, swapped(): lax.ppermute(array, axis, [(i, i ^ distance) for i in range(lax.axis_size...  7.1 us
    pallas_call x1, Pallas kernels, load_weights(): pl.pallas_call(load_kernel, out_shape=tuple((pltpu.VMEM(w.shape, BF16) fo...  2.01 us
    pallas_call x1, Pallas kernels, weight_grads(): pl.pallas_call(grads_kernel, out_shape=tuple((jax.ShapeDtypeStruct(shape,...  1.96 us
    pallas_call x6, Pallas kernels, by_rows(): pl.pallas_call(kernel, grid=(steps,), out_shape=tuple((jax.ShapeDtypeStru...  1.93 us
    pallas_call x1, Pallas kernels, dispatch(): pl.pallas_call(functools.partial(dispatch_kernel, experts, plan.shape[1],...  1.33 us
    pallas_call x1, Pallas kernels, combine(): pl.pallas_call(functools.partial(combine_kernel, columns, slots, chunks,...  0.99 us
  transfers between devices with their start and end apart: 9, of which 5 were waited for; matrix products, arithmetic and copies ran while one was open for 0% of the time, Pallas kernels for 17%

profile of v17, /device:TPU:0, one launch (start us, length us, event | category | flops | bytes accessed | tf_op | source)
XLA Modules:
  0.0 27.9 jit_solution(3058022498738405565)
XLA Ops:
  0.6 1.3 %dispatch.1 = (bf16[104,128]{1,0:T(8,128)(2,1)S(1)}, bf16[104,128]{1,0:T(8,128)(2,1)S(1)}, bf16[104,128]{1,0:T(8,128)(2,1)S(1)}, bf16[104,128]{1,0:T(8,128)(2,1)...) custom-call(s32[2,2]{1,0:T(2,128)} %refs_0_.1, s32[4]{0:T(128)} %refs_1_.1, s32[2,128]{1,0:T(2,128)} %bitcast.11, ...), custom_call_target="tpu_custom_call" | custom-call | tf_op jit(solution)/shard_map/dispatch/pallas_call | solution.py:134
  2.0 5.1 %collective-permute-start = (bf16[104,128]{1,0:T(8,128)(2,1)S(1)}, bf16[104,128]{1,0:T(8,128)(2,1)S(1)}, u32[]{:S(2)}, u32[]{:S(2)}) collective-permute-start(bf16[104,128]{1,0:T(8,128)(2,1)S(1)} %get-tuple-element.30), channel_id=1, source_target_pairs={{0,12},{4,8},{8,4},{12,0},{1,13},{5,9},{9,5},{13,1},{2,14},{6,10},... | collective-permute-start | bytes 79880 | tf_op jit(solution)/shard_map/ppermute | solution.py:417
  7.1 0.0 collective-permute-start.1
  7.1 0.6 %collective-permute-start.2 = (bf16[104,128]{1,0:T(8,128)(2,1)S(1)}, bf16[104,128]{1,0:T(8,128)(2,1)S(1)}, u32[]{:S(2)}, u32[]{:S(2)}) collective-permute-start(bf16[104,128]{1,0:T(8,128)(2,1)S(1)} %get-tuple-element.32), channel_id=1, source_target_pairs={{0,4},{4,0},{8,12},{12,8},{1,5},{5,1},{9,13},{13,9},{2,6},{6,2},{1... | collective-permute-start | bytes 79880 | tf_op jit(solution)/shard_map/ppermute | solution.py:417
  7.7 2.0 %load_weights.1 = (bf16[640,768]{1,0:T(8,128)(2,1)S(1)}, bf16[640,768]{1,0:T(8,128)(2,1)S(1)}, bf16[768,640]{1,0:T(8,128)(2,1)S(1)}, bf16[384,96]{1,0:T(8,128)(2,1)S(1)}) custom-call(bf16[640,768]{1,0:T(8,128)(2,1)} %bitcast.8, bf16[640,768]{1,0:T(8,128)(2,1)} %bitcast.9, bf16[768,640]{1,0:T(8,128)(2,1)} %bitcast.10, ...), custom_call_target="tpu_custom_call" | custom-call | bytes 5898240 | tf_op jit(solution)/shard_map/load_weights/pallas_call | solution.py:182
  9.7 0.0 collective-permute-done.refs_1_
  9.8 2.1 %collective-permute-done.1.refs_2_ = bf16[104,128]{1,0:T(8,128)(2,1)S(1)} collective-permute-done((bf16[104,128]{1,0:T(8,128)(2,1)S(1)}, bf16[104,128]{1,0:T(8,128)(2,1)S(1)}, u32[]{:S(2)}, u32[]{:S(2)}) %collective-permute-start.1) | collective-permute-done | bytes 26656 | tf_op jit(solution)/shard_map/ppermute | solution.py:417
  11.8 0.0 collective-permute-done.2.refs_3_
  11.8 0.5 %give.1 = (bf16[40,640]{1,0:T(8,128)(2,1)S(1)}, bf16[40,640]{1,0:T(8,128)(2,1)S(1)}, bf16[40,1152]{1,0:T(8,128)(2,1)S(1)}) custom-call(bf16[104,128]{1,0:T(8,128)(2,1)S(1)} %get-tuple-element.29.refs_0_, bf16[104,128]{1,0:T(8,128)(2,1)S(1)} %collective-permute-done.refs_1_, bf16[104,128]{1,0:T(8,128)(2,1)S(1)} %collective-permute-done.1.refs_2_, ...), custom_call_target="tpu_custom_call" | custom-call | flops 58982400 | bytes 3055616 | tf_op jit(solution)/shard_map/give/pallas_call | solution.py:292
  12.3 0.1 collective-permute-start.3
  12.4 0.4 %keep.1.left_ref = bf16[40,1152]{1,0:T(8,128)(2,1)S(1)} custom-call(bf16[40,640]{1,0:T(8,128)(2,1)S(1)} %get-tuple-element.38.rows_ref, bf16[40,640]{1,0:T(8,128)(2,1)S(1)} %get-tuple-element.39.cots_ref, bf16[640,768]{1,0:T(8,128)(2,1)S(1)} %get-tuple-element.35.refs_4_.gate_ref.refs_3_, bf16[640,768]{1,0:T(8,128)(2,1)S(1)} %get-tuple-element.36.refs_5_.up_ref.refs_4_, ...), custom_call_target="tpu_custom_call" | custom-call | flops 58982400 | bytes 3051520 | tf_op jit(solution)/shard_map/keep/pallas_call | solution.py:292
  12.8 0.8 %collective-permute-done.3.right_ref = bf16[40,1152]{1,0:T(8,128)(2,1)S(1)} collective-permute-done((bf16[40,1152]{1,0:T(8,128)(2,1)S(1)}, bf16[40,1152]{1,0:T(8,128)(2,1)S(1)}, u32[]{:S(2)}, u32[]{:S(2)}) %collective-permute-start.3) | collective-permute-done | bytes 92192 | tf_op jit(solution)/shard_map/ppermute | solution.py:417
  13.7 1.6 %collective-permute-start.4 = (bf16[40,1152]{1,0:T(8,128)(2,1)S(1)}, bf16[40,1152]{1,0:T(8,128)(2,1)S(1)}, u32[]{:S(2)}, u32[]{:S(2)}) collective-permute-start(bf16[40,1152]{1,0:T(8,128)(2,1)S(1)} %add.1.near_ref), channel_id=1, source_target_pairs={{0,2},{1,3},{2,0},{3,1},{4,6},{5,7},{6,4},{7,5},{8,10},{9,11},{10,... | collective-permute-start | bytes 276488 | tf_op jit(solution)/shard_map/ppermute | solution.py:417
  15.3 3.2 %collective-permute-done.4.far_ref = bf16[40,1152]{1,0:T(8,128)(2,1)S(1)} collective-permute-done((bf16[40,1152]{1,0:T(8,128)(2,1)S(1)}, bf16[40,1152]{1,0:T(8,128)(2,1)S(1)}, u32[]{:S(2)}, u32[]{:S(2)}) %collective-permute-start.4) | collective-permute-done | bytes 92192 | tf_op jit(solution)/shard_map/ppermute | solution.py:417
  18.5 0.1 activate.1.mine_ref
  18.5 0.1 collective-permute-start.5
  18.6 0.5 %own.1 = (f32[40,640]{1,0:T(8,128)S(1)}, f32[40,640]{1,0:T(8,128)S(1)}) custom-call(bf16[40,1152]{1,0:T(8,128)(2,1)S(1)} %activate.1.mine_ref, bf16[640,768]{1,0:T(8,128)(2,1)S(1)} %get-tuple-element.35.refs_4_.gate_ref.refs_3_, bf16[640,768]{1,0:T(8,128)(2,1)S(1)} %get-tuple-element.36.refs_5_.up_ref.refs_4_, ...), custom_call_target="tpu_custom_call" | custom-call | flops 58982400 | bytes 3041280 | tf_op jit(solution)/shard_map/own/pallas_call | solution.py:292
  19.1 0.8 %collective-permute-done.5.refs_0_.theirs_ref = bf16[40,1152]{1,0:T(8,128)(2,1)S(1)} collective-permute-done((bf16[40,1152]{1,0:T(8,128)(2,1)S(1)}, bf16[40,1152]{1,0:T(8,128)(2,1)S(1)}, u32[]{:S(2)}, u32[]{:S(2)}) %collective-permute-start.5) | collective-permute-done | bytes 92192 | tf_op jit(solution)/shard_map/ppermute | solution.py:417
  19.9 0.5 %back.1 = (bf16[104,128]{1,0:T(8,128)(2,1)S(1)}, bf16[104,128]{1,0:T(8,128)(2,1)S(1)}, bf16[104,128]{1,0:T(8,128)(2,1)S(1)}, bf16[104,128]{1,0:T(8,128)(2,1)S(1)}) custom-call(bf16[40,1152]{1,0:T(8,128)(2,1)S(1)} %collective-permute-done.5.refs_0_.theirs_ref, f32[40,640]{1,0:T(8,128)S(1)} %get-tuple-element.41.refs_1_, ...), custom_call_target="tpu_custom_call" | custom-call | flops 58982400 | bytes 3246080 | tf_op jit(solution)/shard_map/back/pallas_call | solution.py:292
  20.4 1.7 %collective-permute-start.6 = (bf16[104,128]{1,0:T(8,128)(2,1)S(1)}, bf16[104,128]{1,0:T(8,128)(2,1)S(1)}, u32[]{:S(2)}, u32[]{:S(2)}) collective-permute-start(bf16[104,128]{1,0:T(8,128)(2,1)S(1)} %get-tuple-element.44), channel_id=1, source_target_pairs={{0,12},{4,8},{8,4},{12,0},{1,13},{5,9},{9,5},{13,1},{2,14},{6,10},... | collective-permute-start | bytes 79880 | tf_op jit(solution)/shard_map/ppermute | solution.py:417
  22.1 0.4 %collective-permute-start.7 = (bf16[104,128]{1,0:T(8,128)(2,1)S(1)}, bf16[104,128]{1,0:T(8,128)(2,1)S(1)}, u32[]{:S(2)}, u32[]{:S(2)}) collective-permute-start(bf16[104,128]{1,0:T(8,128)(2,1)S(1)} %get-tuple-element.45), channel_id=1, source_target_pairs={{0,8},{4,12},{8,0},{12,4},{1,9},{5,13},{9,1},{13,5},{2,10},{6,14},... | collective-permute-start | bytes 79880 | tf_op jit(solution)/shard_map/ppermute | solution.py:417
  22.5 2.3 %collective-permute-start.8 = (bf16[104,128]{1,0:T(8,128)(2,1)S(1)}, bf16[104,128]{1,0:T(8,128)(2,1)S(1)}, u32[]{:S(2)}, u32[]{:S(2)}) collective-permute-start(bf16[104,128]{1,0:T(8,128)(2,1)S(1)} %get-tuple-element.46), channel_id=1, source_target_pairs={{0,4},{4,0},{8,12},{12,8},{1,5},{5,1},{9,13},{13,9},{2,6},{6,2},{1... | collective-permute-start | bytes 79880 | tf_op jit(solution)/shard_map/ppermute | solution.py:417
  24.8 2.0 %weight_grads.1 = (bf16[640,768]{1,0:T(8,128)(2,1)}, bf16[640,768]{1,0:T(8,128)(2,1)}, bf16[768,640]{1,0:T(8,128)(2,1)}) custom-call(bf16[40,640]{1,0:T(8,128)(2,1)S(1)} %get-tuple-element.38.rows_ref, bf16[40,640]{1,0:T(8,128)(2,1)S(1)} %get-tuple-element.39.cots_ref, bf16[40,1152]{1,0:T(8,128)(2,1)S(1)} %activate.1.mine_ref, ...), custom_call_target="tpu_custom_call" | custom-call | flops 117964800 | bytes 2949120 | tf_op jit(solution)/shard_map/weight_grads/pallas_call | solution.py:344
  26.8 0.0 collective-permute-done.6.refs_1_
  26.8 0.1 collective-permute-done.7.refs_2_
  26.9 0.0 collective-permute-done.8.refs_3_
  26.9 1.0 %combine.1 = (bf16[128,640]{1,0:T(8,128)(2,1)}, bf16[128,640]{1,0:T(8,128)(2,1)}) custom-call(bf16[104,128]{1,0:T(8,128)(2,1)S(1)} %get-tuple-element.43.refs_0_, bf16[104,128]{1,0:T(8,128)(2,1)S(1)} %collective-permute-done.6.refs_1_, bf16[104,128]{1,0:T(8,128)(2,1)S(1)} %collective-permute-done.7.refs_2_, ...), custom_call_target="tpu_custom_call" | custom-call | tf_op jit(solution)/shard_map/combine/pallas_call | solution.py:400
  (1 shorter events, 0.0 us)
Async XLA Ops:
  2.0 7.8 %collective-permute-start = (bf16[104,128]{1,0:T(8,128)(2,1)S(1)}, bf16[104,128]{1,0:T(8,128)(2,1)S(1)}, u32[]{:S(2)}, u32[]{:S(2)}) collective-permute-start(bf16[104,128]{1,0:T(8,128)(2,1)S(1)} %get-tuple-element.30), channel_id=1, source_target_pairs={{0,12},{4,8},{8,4},{12,0},{1,13},{5,9},{9,5},{13,1},{2,14},{6,10},... | collective-permute-start | bytes 79880 | tf_op jit(solution)/shard_map/ppermute | solution.py:417
  7.1 4.7 %collective-permute-start.1 = (bf16[104,128]{1,0:T(8,128)(2,1)S(1)}, bf16[104,128]{1,0:T(8,128)(2,1)S(1)}, u32[]{:S(2)}, u32[]{:S(2)}) collective-permute-start(bf16[104,128]{1,0:T(8,128)(2,1)S(1)} %get-tuple-element.31), channel_id=1, source_target_pairs={{0,8},{4,12},{8,0},{12,4},{1,9},{5,13},{9,1},{13,5},{2,10},{6,14},... | collective-permute-start | bytes 79880 | tf_op jit(solution)/shard_map/ppermute | solution.py:417
  7.1 4.7 %collective-permute-start.2 = (bf16[104,128]{1,0:T(8,128)(2,1)S(1)}, bf16[104,128]{1,0:T(8,128)(2,1)S(1)}, u32[]{:S(2)}, u32[]{:S(2)}) collective-permute-start(bf16[104,128]{1,0:T(8,128)(2,1)S(1)} %get-tuple-element.32), channel_id=1, source_target_pairs={{0,4},{4,0},{8,12},{12,8},{1,5},{5,1},{9,13},{13,9},{2,6},{6,2},{1... | collective-permute-start | bytes 79880 | tf_op jit(solution)/shard_map/ppermute | solution.py:417
  12.3 1.4 %collective-permute-start.3 = (bf16[40,1152]{1,0:T(8,128)(2,1)S(1)}, bf16[40,1152]{1,0:T(8,128)(2,1)S(1)}, u32[]{:S(2)}, u32[]{:S(2)}) collective-permute-start(bf16[40,1152]{1,0:T(8,128)(2,1)S(1)} %get-tuple-element.40), channel_id=1, source_target_pairs={{0,1},{1,0},{2,3},{3,2},{4,5},{5,4},{6,7},{7,6},{8,9},{9,8},{10,11... | collective-permute-start | bytes 276488 | tf_op jit(solution)/shard_map/ppermute | solution.py:417
  13.7 4.8 %collective-permute-start.4 = (bf16[40,1152]{1,0:T(8,128)(2,1)S(1)}, bf16[40,1152]{1,0:T(8,128)(2,1)S(1)}, u32[]{:S(2)}, u32[]{:S(2)}) collective-permute-start(bf16[40,1152]{1,0:T(8,128)(2,1)S(1)} %add.1.near_ref), channel_id=1, source_target_pairs={{0,2},{1,3},{2,0},{3,1},{4,6},{5,7},{6,4},{7,5},{8,10},{9,11},{10,... | collective-permute-start | bytes 276488 | tf_op jit(solution)/shard_map/ppermute | solution.py:417
  18.5 1.4 %collective-permute-start.5 = (bf16[40,1152]{1,0:T(8,128)(2,1)S(1)}, bf16[40,1152]{1,0:T(8,128)(2,1)S(1)}, u32[]{:S(2)}, u32[]{:S(2)}) collective-permute-start(bf16[40,1152]{1,0:T(8,128)(2,1)S(1)} %activate.1.mine_ref), channel_id=1, source_target_pairs={{0,1},{1,0},{2,3},{3,2},{4,5},{5,4},{6,7},{7,6},{8,9},{9,8},{10,11... | collective-permute-start | bytes 276488 | tf_op jit(solution)/shard_map/ppermute | solution.py:417
  20.4 6.4 %collective-permute-start.6 = (bf16[104,128]{1,0:T(8,128)(2,1)S(1)}, bf16[104,128]{1,0:T(8,128)(2,1)S(1)}, u32[]{:S(2)}, u32[]{:S(2)}) collective-permute-start(bf16[104,128]{1,0:T(8,128)(2,1)S(1)} %get-tuple-element.44), channel_id=1, source_target_pairs={{0,12},{4,8},{8,4},{12,0},{1,13},{5,9},{9,5},{13,1},{2,14},{6,10},... | collective-permute-start | bytes 79880 | tf_op jit(solution)/shard_map/ppermute | solution.py:417
  22.1 4.8 %collective-permute-start.7 = (bf16[104,128]{1,0:T(8,128)(2,1)S(1)}, bf16[104,128]{1,0:T(8,128)(2,1)S(1)}, u32[]{:S(2)}, u32[]{:S(2)}) collective-permute-start(bf16[104,128]{1,0:T(8,128)(2,1)S(1)} %get-tuple-element.45), channel_id=1, source_target_pairs={{0,8},{4,12},{8,0},{12,4},{1,9},{5,13},{9,1},{13,5},{2,10},{6,14},... | collective-permute-start | bytes 79880 | tf_op jit(solution)/shard_map/ppermute | solution.py:417
  22.5 4.4 %collective-permute-start.8 = (bf16[104,128]{1,0:T(8,128)(2,1)S(1)}, bf16[104,128]{1,0:T(8,128)(2,1)S(1)}, u32[]{:S(2)}, u32[]{:S(2)}) collective-permute-start(bf16[104,128]{1,0:T(8,128)(2,1)S(1)} %get-tuple-element.46), channel_id=1, source_target_pairs={{0,4},{4,0},{8,12},{12,8},{1,5},{5,1},{9,13},{13,9},{2,6},{6,2},{1... | collective-permute-start | bytes 79880 | tf_op jit(solution)/shard_map/ppermute | solution.py:417
